TPU v7x, 32 devices: a whole 2x2x4 slice. The times are simulated.
32 devices in a mesh: clip: 2 (over x), row: 16 (over z, y, core).
Axes of the slice: x: 2, y: 2, z: 4, core: 2. Of those that a mesh axis runs over, the one named last changes fastest.
Arguments:
- source: bfloat16 [32768, 256], P(('clip', 'row')), parts along dimension 0, may hold values from -6 to 6
- near_blocks: bfloat16 [128, 16, 256, 256], P(('clip', 'row')), parts along dimension 0, may hold values from -0.125 to 0.125
- near_list: int32 [128, 16], P(('clip', 'row')), parts along dimension 0, may hold values from 0 to 63, as said below
- near_count: int32 [128], P(('clip', 'row')), parts along dimension 0, may hold values from 1 to 16
- col_basis: bfloat16 [128, 256, 128], P(('clip', 'row')), parts along dimension 0, may hold values from -0.375 to 0.375
- row_basis: bfloat16 [128, 256, 128], P(('clip', 'row')), parts along dimension 0, may hold values from -0.5 to 0.5
- transfer: bfloat16 [128, 128, 128], P(('clip', 'row')), parts along dimension 0, may hold values from -0.25 to 0.25
- far_list: int32 [128, 16], P(('clip', 'row')), parts along dimension 0, may hold values from 0 to 63, as said below
- far_coupling: bfloat16 [128, 16, 128, 128], P(('clip', 'row')), parts along dimension 0, may hold values from -0.125 to 0.125
- coarse_list: int32 [32, 8], P(('clip', 'row')), parts along dimension 0, may hold values from 0 to 15, as said below
- coarse_coupling: bfloat16 [32, 8, 128, 128], P(('clip', 'row')), parts along dimension 0, may hold values from -0.375 to 0.375
Outputs:
- product: bfloat16 [32768, 256], P(('clip', 'row')), parts along dimension 0
There are 2 independent parts, one for each index of `clip`. A program takes and returns all parts, laid end to end along the dimension named above; each array names one. Nothing has to cross between parts.
Inputs may be any that keep to these rules, and one draw needn't show every extreme that they name: near_list[i, 0] = i; the other entries lie within 4 leaves of i. far_list[i, f] lies in a coarse cluster one or two clusters away from that of leaf i. coarse_list[d, m] lies in the same aligned group of 16 coarse clusters as d, and its position in the group differs from that of d by three or more modulo 16.
All inputs are finite; a program needn't handle non-finite values.
Results may differ from a plain program's by a relative error of at most 0.0057.
Values may be sent and summed in bfloat16 or wider, within the bound.
No kernel may reach another device: no remote copies, remote signals or barrier semaphores. Data moves between devices by JAX's collectives and lax.ppermute only.
A program may use at most 128 MiB of HBM per device.

v0:
```python
import jax
import jax.numpy as jnp
from jax import lax
from jax.sharding import PartitionSpec as P


def padded_2(block, sides, width):
    for axis, dim in sides:
        count = lax.axis_size(axis)
        forward = [(i, i + 1) for i in range(count - 1)]
        backward = [(target, source) for source, target in forward]
        low = lax.ppermute(
            lax.slice_in_dim(block, block.shape[dim] - width, None, axis=dim), axis, forward
        )
        high = lax.ppermute(lax.slice_in_dim(block, 0, width, axis=dim), axis, backward)
        block = jnp.concatenate([low, block, high], axis=dim)
    return block


def body(
    source,
    near_blocks,
    near_list,
    near_count,
    col_basis,
    row_basis,
    transfer,
    far_list,
    far_coupling,
    coarse_list,
    coarse_coupling,
):
    leaf_dev = near_blocks.shape[0]
    slots = near_blocks.shape[1]
    leaf_rows = near_blocks.shape[2]
    width = source.shape[1]
    tree_height = source.shape[0]
    place = lax.axis_index("row")
    padded = padded_2(source, (("row", 0),), tree_height)
    panels = padded.reshape(3 * leaf_dev, leaf_rows, width)
    local = near_list - (place * leaf_dev - leaf_dev)
    selected_entries = panels[local]
    live = lax.broadcasted_iota(jnp.int32, (leaf_dev, slots), 1) < near_count[:, None]
    selected_entries = jnp.where(
        live[:, :, None, None], selected_entries, jnp.zeros_like(selected_entries)
    )
    near = jnp.einsum(
        "lsab,lsbr->lar", near_blocks, selected_entries, preferred_element_type=jnp.float32
    )
    own = source.reshape(leaf_dev, leaf_rows, width)
    coef = jnp.einsum("lak,lar->lkr", col_basis, own, preferred_element_type=jnp.float32).astype(
        jnp.bfloat16
    )
    parent = jnp.einsum("lab,lar->br", transfer, coef, preferred_element_type=jnp.float32).astype(
        jnp.bfloat16
    )
    every_coef, every_parent = (
        lax.all_gather(coef, "row", axis=0, tiled=True),
        lax.all_gather(parent[None], "row", axis=0, tiled=True),
    )
    far_picked = every_coef[far_list]
    coarse_picked = every_parent[coarse_list[0]]
    leaf_far = jnp.einsum(
        "lfab,lfbr->lar", far_coupling, far_picked, preferred_element_type=jnp.float32
    )
    coarse = jnp.einsum(
        "mab,mbr->ar", coarse_coupling[0], coarse_picked, preferred_element_type=jnp.float32
    )
    spread = jnp.einsum(
        "lab,br->lar", transfer.astype(jnp.float32), coarse, precision=lax.Precision.HIGHEST
    )
    down = (leaf_far + spread).astype(jnp.bfloat16)
    result = near + jnp.einsum("lka,lar->lkr", row_basis, down, preferred_element_type=jnp.float32)
    return result.reshape(tree_height, width).astype(jnp.bfloat16)


def solution(mesh):
    placed = (
        P(("clip", "row"), None),
        P(("clip", "row"), None, None, None),
        P(("clip", "row"), None),
        P(("clip", "row")),
        P(("clip", "row"), None, None),
        P(("clip", "row"), None, None),
        P(("clip", "row"), None, None),
        P(("clip", "row"), None),
        P(("clip", "row"), None, None, None),
        P(("clip", "row"), None),
        P(("clip", "row"), None, None, None),
    )
    return jax.shard_map(
        body, mesh=mesh, in_specs=placed, out_specs=P(("clip", "row"), None), check_vma=False
    )
```

profile of v0, /device:TPU:1, one launch (start us, length us, event | category | flops | bytes accessed | tf_op | source)
XLA Modules:
  0.0 131.0 jit_solution(409917974796687169)
XLA Ops:
  6.5 0.0 copy-start
  6.5 0.0 all-gather.6.cloned.1.call-start
  6.5 1.5 %convolution_convert_fusion = bf16[4,128,256]{2,1,0:T(8,128)(2,1)S(1)} fusion(bf16[4,256,128]{2,1,0:T(8,128)(2,1)} %param.15, bf16[4,256,256]{2,1,0:T(8,128)(2,1)} %bitcast.58), kind=kOutput, calls=%fused_computation.15 | convolution fusion | flops 67239936 | bytes 1048576 | tf_op jit(solution)/shard_map/lak,lar->lkr/dot_general | solution.py:51
  8.1 0.0 copy-start.1
  8.1 1.9 %fusion.16 = bf16[128,256]{0,1:T(8,128)(2,1)} fusion(bf16[4,128,256]{2,1,0:T(8,128)(2,1)S(1)} %convolution_convert_fusion, bf16[4,128,128]{2,1,0:T(8,128)(2,1)} %param.17), kind=kOutput, calls=%fused_computation.18 | convolution fusion | flops 33587200 | bytes 458752 | tf_op jit(solution)/shard_map/lab,lar->br/dot_general | solution.py:54
  10.0 0.0 all-gather.6.cloned.1.call-update
  10.0 0.0 all-gather.4.cloned.1.call-start
  10.1 0.0 copy-done.1
  10.1 0.7 all-gather.4.cloned.1.call-update
  10.8 4.5 %collective-permute-start = (bf16[1024,256]{1,0:T(8,128)(2,1)}, bf16[1024,256]{1,0:T(8,128)(2,1)S(1)}, u32[]{:S(2)}, u32[]{:S(2)}) collective-permute-start(bf16[1024,256]{1,0:T(8,128)(2,1)} %param.11), channel_id=1, source_target_pairs={{0,1},{1,2},{2,3},{3,4},{4,5},{5,6},{6,7},{7,8},{8,9},{9,10},{10,1... | collective-permute-start | bytes 1572872 | tf_op jit(solution)/shard_map/ppermute | solution.py:12
  15.3 1.9 %collective-permute-start.1 = (bf16[1024,256]{1,0:T(8,128)(2,1)}, bf16[1024,256]{1,0:T(8,128)(2,1)S(1)}, u32[]{:S(2)}, u32[]{:S(2)}) collective-permute-start(bf16[1024,256]{1,0:T(8,128)(2,1)} %param.11), channel_id=1, source_target_pairs={{1,0},{2,1},{3,2},{4,3},{5,4},{6,5},{7,6},{8,7},{9,8},{10,9},{11,1... | collective-permute-start | bytes 1572872 | tf_op jit(solution)/shard_map/ppermute | solution.py:15
  17.3 0.7 compare_select_fusion
  17.9 0.1 reshape.67
  18.0 0.7 compare_select_fusion.1
  18.7 0.1 reshape.59
  18.8 0.7 fusion.19
  19.5 0.7 iota_compare_fusion
  20.2 7.8 %collective-permute-done = bf16[1024,256]{1,0:T(8,128)(2,1)S(1)} collective-permute-done((bf16[1024,256]{1,0:T(8,128)(2,1)}, bf16[1024,256]{1,0:T(8,128)(2,1)S(1)}, u32[]{:S(2)}, u32[]{:S(2)}) %collective-permute-start) | collective-permute-done | bytes 524320 | tf_op jit(solution)/shard_map/ppermute | solution.py:12
  28.1 0.0 collective-permute-done.1
  28.1 2.3 %pad_maximum_fusion = bf16[3072,256]{1,0:T(8,128)(2,1)} fusion(bf16[1024,256]{1,0:T(8,128)(2,1)S(1)} %collective-permute-done.1, bf16[1024,256]{1,0:T(8,128)(2,1)} %param.11, bf16[1024,256]{1,0:T(8,128)(2,1)S(1)} %collective-permute-done), kind=kLoop, calls=%fused_computation.7 | loop fusion | flops 4718592 | bytes 3145728 | tf_op jit(solution)/shard_map/concatenate | solution.py:16
  30.4 0.0 copy-start.3
  30.4 7.0 %gather_fusion = bf16[64,256,256]{2,1,0:T(8,128)(2,1)} fusion(bf16[12,256,256]{2,1,0:T(8,128)(2,1)} %bitcast.54, s32[1024]{0:T(1024)S(1)} %pad_clamp_fusion.2), kind=kCustom, calls=%fused_computation | custom fusion | bytes 16777472 | tf_op jit(solution)/shard_map/gather | solution.py:42
  37.3 16.2 %all-gather.6.cloned.1.call-done = bf16[2048,256]{0,1:T(8,128)(2,1)} async-done(((bf16[128,256]{0,1:T(8,128)(2,1)}), bf16[2048,256]{0,1:T(8,128)(2,1)}) %all-gather.6.cloned.1.call-update) | async-done | bytes 1048592 | tf_op jit(solution)/shard_map/all_gather | solution.py:59
  53.5 1.5 %copy.30 = bf16[2048,256]{1,0:T(8,128)(2,1)S(1)} copy(bf16[2048,256]{0,1:T(8,128)(2,1)} %all-gather.6.cloned.1.call-done) | data formatting | bytes 2097152 | tf_op jit(solution)/shard_map/all_gather | solution.py:59
  55.0 1.4 %gather_fusion.2 = bf16[8,128,256]{2,1,0:T(8,128)(2,1)} fusion(bf16[16,128,256]{2,1,0:T(8,128)(2,1)S(1)} %bitcast.57, s32[1024]{0:T(1024)S(1)} %pad_clamp_fusion), kind=kCustom, calls=%fused_computation.2 | custom fusion | bytes 1048608 | tf_op jit(solution)/shard_map/gather | solution.py:62
  56.4 0.0 copy-done.3
  56.4 1.4 %fusion.17 = f32[256,128,1]{1,0,2:T(8,128)S(1)} fusion(bf16[8,128,256]{2,1,0:T(8,128)(2,1)} %gather_fusion.2, bf16[1,8,128,128]{3,2,1,0:T(8,128)(2,1)S(1)} %copy-done.3), kind=kOutput, calls=%fused_computation.19 | convolution fusion | flops 67108864 | bytes 917504 | tf_op jit(solution)/shard_map/mab,mbr->ar/dot_general | solution.py:66
  57.7 48.0 %all-gather.4.cloned.1.call-done = bf16[64,128,256]{2,1,0:T(8,128)(2,1)} async-done(((bf16[4,128,256]{2,1,0:T(8,128)(2,1)}), bf16[64,128,256]{2,1,0:T(8,128)(2,1)}) %all-gather.4.cloned.1.call-update) | async-done | bytes 4194320 | tf_op jit(solution)/shard_map/all_gather | solution.py:58
  105.8 4.9 %gather_fusion.1 = bf16[64,128,256]{2,1,0:T(8,128)(2,1)} fusion(bf16[64,128,256]{2,1,0:T(8,128)(2,1)} %all-gather.4.cloned.1.call-done, s32[1024]{0:T(1024)S(1)} %pad_clamp_fusion.1), kind=kCustom, calls=%fused_computation.1 | custom fusion | bytes 8388864 | tf_op jit(solution)/shard_map/gather | solution.py:61
  110.7 0.0 copy-done
  110.7 0.0 copy-start.2
  110.7 0.0 copy-start.4
  110.7 3.8 %convolution_bitcast_fusion.1 = f32[4,128,256]{1,2,0:T(8,128)S(1)} fusion(bf16[4,16,128,256]{3,2,1,0:T(8,128)(2,1)} %bitcast.55, bf16[4,16,128,128]{3,2,1,0:T(8,128)(2,1)S(1)} %copy-done), kind=kOutput, calls=%fused_computation.13 | convolution fusion | flops 536870912 | bytes 6815744 | tf_op jit(solution)/shard_map/lfab,lfbr->lar/dot_general | solution.py:63
  114.5 0.0 copy-done.2
  114.5 0.4 fusion.14
  114.9 0.0 copy-done.4
  114.9 0.3 fusion.21
  115.2 9.0 %fusion.10 = bf16[4,256,256]{1,2,0:T(8,128)(2,1)} fusion(f32[4,256,256]{1,2,0:T(8,128)S(1)} %fusion.21, bf16[4,16,256,256]{3,2,1,0:T(8,128)(2,1)} %param.12, bf16[4,16,256,256]{3,2,1,0:T(8,128)(2,1)} %bitcast.56, pred[4,16]{1,0:T(4,128)(4,1)S(1)} %iota_compare_fusion), kind=kOutput, calls=%fused_computation.10 | convolution fusion | flops 2152202240 | bytes 18350144 | tf_op jit(solution)/shard_map/lsab,lsbr->lar/dot_general | solution.py:47
  (3 shorter events, 0.0 us)
Async XLA Ops:
  6.5 104.1 %copy-start = (bf16[4,16,128,128]{3,2,1,0:T(8,128)(2,1)S(1)}, bf16[4,16,128,128]{3,2,1,0:T(8,128)(2,1)}, u32[]{:S(2)}) copy-start(bf16[4,16,128,128]{3,2,1,0:T(8,128)(2,1)} %param.19) | copy-start | bytes 6291460
  6.5 47.0 %all-gather.6.cloned.1.call-start = ((), (), s32[]{:S(2)}) async-start(), calls=%async_computation.1 | async-start | bytes 1114112 | tf_op jit(solution)/shard_map/all_gather | solution.py:59
  8.1 2.0 %copy-start.1 = (bf16[4,128,256]{2,1,0:T(8,128)(2,1)}, bf16[4,128,256]{2,1,0:T(8,128)(2,1)S(1)}, u32[]{:S(2)}) copy-start(bf16[4,128,256]{2,1,0:T(8,128)(2,1)S(1)} %convolution_convert_fusion) | copy-start | bytes 786436
  10.0 95.7 %all-gather.4.cloned.1.call-start = ((), (), s32[]{:S(2)}) async-start(), calls=%async_computation | async-start | bytes 4456448 | tf_op jit(solution)/shard_map/all_gather | solution.py:58
  10.8 17.3 %collective-permute-start = (bf16[1024,256]{1,0:T(8,128)(2,1)}, bf16[1024,256]{1,0:T(8,128)(2,1)S(1)}, u32[]{:S(2)}, u32[]{:S(2)}) collective-permute-start(bf16[1024,256]{1,0:T(8,128)(2,1)} %param.11), channel_id=1, source_target_pairs={{0,1},{1,2},{2,3},{3,4},{4,5},{5,6},{6,7},{7,8},{8,9},{9,10},{10,1... | collective-permute-start | bytes 1572872 | tf_op jit(solution)/shard_map/ppermute | solution.py:12
  15.3 12.7 %collective-permute-start.1 = (bf16[1024,256]{1,0:T(8,128)(2,1)}, bf16[1024,256]{1,0:T(8,128)(2,1)S(1)}, u32[]{:S(2)}, u32[]{:S(2)}) collective-permute-start(bf16[1024,256]{1,0:T(8,128)(2,1)} %param.11), channel_id=1, source_target_pairs={{1,0},{2,1},{3,2},{4,3},{5,4},{6,5},{7,6},{8,7},{9,8},{10,9},{11,1... | collective-permute-start | bytes 1572872 | tf_op jit(solution)/shard_map/ppermute | solution.py:15
  30.4 26.0 %copy-start.3 = (bf16[1,8,128,128]{3,2,1,0:T(8,128)(2,1)S(1)}, bf16[1,8,128,128]{3,2,1,0:T(8,128)(2,1)}, u32[]{:S(2)}) copy-start(bf16[1,8,128,128]{3,2,1,0:T(8,128)(2,1)} %param.21) | copy-start | bytes 786436
  110.7 3.8 %copy-start.2 = (bf16[4,128,128]{2,1,0:T(8,128)(2,1)S(1)}, bf16[4,128,128]{2,1,0:T(8,128)(2,1)}, u32[]{:S(2)}) copy-start(bf16[4,128,128]{2,1,0:T(8,128)(2,1)} %param.17) | copy-start | bytes 393220
  110.7 4.2 %copy-start.4 = (bf16[4,256,128]{2,1,0:T(8,128)(2,1)S(1)}, bf16[4,256,128]{2,1,0:T(8,128)(2,1)}, u32[]{:S(2)}) copy-start(bf16[4,256,128]{2,1,0:T(8,128)(2,1)} %param.16) | copy-start | bytes 786436
Sparse Core Ops, SparseCore 0:
  10.1 43.3 all-gather.5
  55.7 50.0 all-gather.3
where the time goes:
time: 132 us; the launch traced here: 131 us
  waiting for transfers between devices  72.7 us (55%)
  matrix products  18.3 us (14%)
  local copies, waits for them, and re-layouts  14.9 us (11%)
  between operations  13.5 us (10%)
  starting transfers between devices  6.51 us (5%)
  other arithmetic  5.09 us (4%)
    all_gather x1, waiting for transfers between devices, body(): lax.all_gather(coef, 'row', axis=0, tiled=True)  48 us
    all_gather x1, waiting for transfers between devices, body(): lax.all_gather(parent[None], 'row', axis=0, tiled=True)  16.2 us
    dot_general x1, matrix products, body(): jnp.einsum('lsab,lsbr->lar', near_blocks, selected_entries, preferred_ele...  8.98 us
    ppermute x1, waiting for transfers between devices, padded_2(): lax.ppermute(lax.slice_in_dim(block, block.shape[dim] - width, None, axis...  7.84 us
    gather x1, local copies, waits for them, and re-layouts, body(): selected_entries = panels[local]  6.97 us
    gather x1, local copies, waits for them, and re-layouts, body(): far_picked = every_coef[far_list]  4.92 us
    ppermute x1, starting transfers between devices, padded_2(): lax.ppermute(lax.slice_in_dim(block, block.shape[dim] - width, None, axis...  4.54 us
    dot_general x1, matrix products, body(): jnp.einsum('lfab,lfbr->lar', far_coupling, far_picked, preferred_element_...  3.76 us
  transfers between devices with their start and end apart: 4, of which 3 were waited for; matrix products, arithmetic and copies ran while one was open for 13% of the time, Pallas kernels for 0%

commit v1 on v0

v1 whole, which is shorter than its diff:
```python
import jax
import jax.numpy as jnp
from jax import lax
from jax.experimental import pallas as pl
from jax.experimental.pallas import tpu as pltpu
from jax.sharding import PartitionSpec as P

GROUP = 16
CHUNK = 4


def dot(a, b):
    return jnp.dot(a, b, preferred_element_type=jnp.float32)


def dot_t(a, b):
    return lax.dot_general(
        a, b, (((0,), (0,)), ((), ())), preferred_element_type=jnp.float32
    )


def up_kernel(source_ref, col_ref, transfer_ref, coef_ref, parent_ref):
    leaves, rows, rank = col_ref.shape
    total = None
    for leaf in range(leaves):
        coef = dot_t(col_ref[leaf], source_ref[pl.ds(leaf * rows, rows), :]).astype(jnp.bfloat16)
        coef_ref[leaf] = coef
        term = dot_t(transfer_ref[leaf], coef)
        total = term if total is None else total + term
    parent_ref[...] = total.astype(jnp.bfloat16)


def near_kernel(
    list_ref, count_ref, blocks_hbm, own_hbm, other_hbm, across_hbm, near_ref,
    blocks, panels, block_sems, panel_sems,
):
    leaves, slots, rows, _ = blocks.shape
    chunks = slots // CHUNK
    place = list_ref[0, 0] // leaves
    pairs = [
        pltpu.make_async_copy(
            ref, panels.at[pl.ds(which * leaves, leaves)], panel_sems.at[which]
        )
        for which, ref in enumerate((own_hbm, other_hbm, across_hbm))
    ]
    for copy in pairs:
        copy.start()

    def block_copy(leaf, chunk):
        where = pl.ds(chunk * CHUNK, CHUNK)
        return pltpu.make_async_copy(
            blocks_hbm.at[leaf, where], blocks.at[leaf, where], block_sems.at[leaf, chunk]
        )

    for leaf in range(leaves):
        for chunk in range(chunks):
            @pl.when(chunk * CHUNK < count_ref[leaf])
            def _():
                block_copy(leaf, chunk).start()

    panels[3 * leaves] = jnp.zeros(panels.shape[1:], panels.dtype)
    for copy in pairs:
        copy.wait()

    def panel_of(leaf, slot):
        column = list_ref[leaf, slot]
        cluster = column // leaves
        which = jnp.where(cluster == place, 0, jnp.where(cluster == (place ^ 1), 1, 2))
        index = which * leaves + column - cluster * leaves
        return panels[jnp.where(slot < count_ref[leaf], index, 3 * leaves)]

    for leaf in range(leaves):
        for chunk in range(chunks):
            @pl.when(chunk * CHUNK < count_ref[leaf])
            def _():
                block_copy(leaf, chunk).wait()
                total = None if chunk == 0 else near_ref[leaf]
                for slot in range(chunk * CHUNK, (chunk + 1) * CHUNK):
                    term = dot(blocks[leaf, slot], panel_of(leaf, slot))
                    total = term if total is None else total + term
                near_ref[leaf] = total


def down_kernel(
    near_list_ref, far_list_ref, coarse_list_ref,
    near_hbm, row_ref, transfer_ref, coupling_hbm, coarse_coupling_ref,
    skip_hbm, across_hbm, other_hbm, passed_hbm, mine_hbm, theirs_hbm,
    out_ref,
    near, coupling, coefs, parents, sems,
):
    leaves, slots, rank, _ = coupling.shape
    place = near_list_ref[0, 0] // leaves
    copies = [
        pltpu.make_async_copy(ref, coefs.at[pl.ds(n * leaves, leaves)], sems.at[n])
        for n, ref in enumerate((skip_hbm, across_hbm, other_hbm, passed_hbm))
    ]
    half = GROUP // 2
    copies += [
        pltpu.make_async_copy(ref, parents.at[pl.ds(n * half, half)], sems.at[4 + n])
        for n, ref in enumerate((mine_hbm, theirs_hbm))
    ]
    copies.append(pltpu.make_async_copy(coupling_hbm, coupling, sems.at[6]))
    near_copy = pltpu.make_async_copy(near_hbm, near, sems.at[7])
    for copy in copies:
        copy.start()
    near_copy.start()
    for copy in copies:
        copy.wait()

    local = place % GROUP
    total = None
    for slot in range(coarse_list_ref.shape[1]):
        step = (coarse_list_ref[0, slot] % GROUP) ^ local
        index = (step & 1) * half + (step >> 1)
        term = dot(coarse_coupling_ref[0, slot], parents[index])
        total = term if total is None else total + term
    high = total.astype(jnp.bfloat16)
    low = (total - high.astype(jnp.float32)).astype(jnp.bfloat16)
    coarse = jnp.concatenate([high, low], axis=0)

    odd = place % 2 == 1
    near_copy.wait()
    for leaf in range(leaves):
        matrix = transfer_ref[leaf]
        total = dot(jnp.concatenate([matrix, matrix], axis=1), coarse)
        for slot in range(slots):
            column = far_list_ref[leaf, slot]
            cluster = column // leaves
            away = jnp.where(odd, place - cluster, cluster - place)
            which = jnp.where(away < 0, away + 2, away + 1)
            index = which * leaves + column - cluster * leaves
            total = total + dot(coupling[leaf, slot], coefs[index])
        down = total.astype(jnp.bfloat16)
        result = near[leaf] + dot(row_ref[leaf], down)
        out_ref[leaf] = result.astype(jnp.bfloat16)


VMEM = pl.BlockSpec(memory_space=pltpu.VMEM)
SMEM = pl.BlockSpec(memory_space=pltpu.SMEM)
ANY = pl.BlockSpec(memory_space=pl.ANY)


def body(
    source,
    near_blocks,
    near_list,
    near_count,
    col_basis,
    row_basis,
    transfer,
    far_list,
    far_coupling,
    coarse_list,
    coarse_coupling,
):
    leaves, slots, rows, _ = near_blocks.shape
    rank = col_basis.shape[2]
    width = source.shape[1]
    count = lax.axis_size("row")
    far_slots = far_coupling.shape[1]
    coarse_slots = coarse_coupling.shape[1]

    def pairs_of(target):
        return [(d, target(d)) for d in range(count) if 0 <= target(d) < count]

    across = pairs_of(lambda d: d + 1 if d % 2 else d - 1)
    skip = pairs_of(lambda d: d - 2 if d % 2 else d + 2)

    def flip(bit):
        return pairs_of(lambda d: d ^ bit)

    def send(value, pairs):
        return lax.ppermute(value, "row", pairs)

    panels = source.reshape(leaves, rows, width)
    source_across = send(panels, across)
    source_other = send(panels, flip(1))

    coef, parent = pl.pallas_call(
        up_kernel,
        out_shape=(
            jax.ShapeDtypeStruct((leaves, rank, width), jnp.bfloat16),
            jax.ShapeDtypeStruct((rank, width), jnp.bfloat16),
        ),
        in_specs=[VMEM] * 3,
        out_specs=(VMEM, VMEM),
        cost_estimate=pl.CostEstimate(
            flops=2 * leaves * rank * width * (rows + rank),
            bytes_accessed=2 * leaves * rows * (width + rank),
            transcendentals=0,
        ),
        name="up",
    )(source, col_basis, transfer)

    parent = parent[None]
    pair = jnp.concatenate([parent, send(parent, flip(2))], axis=0)
    mine = jnp.concatenate([pair] + [send(pair, flip(bit)) for bit in (4, 8, 12)], axis=0)
    theirs = send(mine, flip(1))

    coef_across = send(coef, across)
    coef_other = send(coef, flip(1))
    coef_passed = send(coef_across, flip(1))
    coef_skip = send(coef, skip)

    near = pl.pallas_call(
        near_kernel,
        out_shape=jax.ShapeDtypeStruct((leaves, rows, width), jnp.float32),
        in_specs=[SMEM, SMEM, ANY, ANY, ANY, ANY],
        out_specs=VMEM,
        scratch_shapes=[
            pltpu.VMEM((leaves, slots, rows, rows), jnp.bfloat16),
            pltpu.VMEM((3 * leaves + 1, rows, width), jnp.bfloat16),
            pltpu.SemaphoreType.DMA((leaves, slots // CHUNK)),
            pltpu.SemaphoreType.DMA((3,)),
        ],
        cost_estimate=pl.CostEstimate(
            flops=2 * leaves * slots * rows * rows * width,
            bytes_accessed=2 * leaves * slots * rows * rows,
            transcendentals=0,
        ),
        compiler_params=pltpu.CompilerParams(vmem_limit_bytes=24 * 2**20),
        name="near",
    )(near_list, near_count, near_blocks, panels, source_other, source_across)

    result = pl.pallas_call(
        down_kernel,
        out_shape=jax.ShapeDtypeStruct((leaves, rows, width), jnp.bfloat16),
        in_specs=[SMEM] * 3 + [ANY, VMEM, VMEM, ANY, VMEM] + [ANY] * 6,
        out_specs=VMEM,
        scratch_shapes=[
            pltpu.VMEM((leaves, rows, width), jnp.float32),
            pltpu.VMEM((leaves, far_slots, rank, rank), jnp.bfloat16),
            pltpu.VMEM((4 * leaves, rank, width), jnp.bfloat16),
            pltpu.VMEM((GROUP, rank, width), jnp.bfloat16),
            pltpu.SemaphoreType.DMA((8,)),
        ],
        cost_estimate=pl.CostEstimate(
            flops=2 * leaves * (far_slots + 4) * rank * rank * width,
            bytes_accessed=2 * leaves * far_slots * rank * rank,
            transcendentals=0,
        ),
        compiler_params=pltpu.CompilerParams(vmem_limit_bytes=16 * 2**20),
        name="down",
    )(
        near_list, far_list, coarse_list, near, row_basis, transfer, far_coupling,
        coarse_coupling, coef_skip, coef_across, coef_other, coef_passed, mine, theirs,
    )
    return result.reshape(source.shape)


def solution(mesh):
    placed = (
        P(("clip", "row"), None),
        P(("clip", "row"), None, None, None),
        P(("clip", "row"), None),
        P(("clip", "row")),
        P(("clip", "row"), None, None),
        P(("clip", "row"), None, None),
        P(("clip", "row"), None, None),
        P(("clip", "row"), None),
        P(("clip", "row"), None, None, None),
        P(("clip", "row"), None),
        P(("clip", "row"), None, None, None),
    )
    return jax.shard_map(
        body, mesh=mesh, in_specs=placed, out_specs=P(("clip", "row"), None), check_vma=False
    )
```

time: 132 us -> 49.9 us (0.38)
  the two profiles are of different devices: /device:TPU:1 before, /device:TPU:6 now
where the time goes in v1:
time: 49.9 us; the launch traced here: 49.4 us
  starting transfers between devices  25 us (50%)
  Pallas kernels  12.2 us (24%)
  local copies, waits for them, and re-layouts  6.66 us (13%)
  waiting for transfers between devices  4.59 us (9%)
  other arithmetic  0.85 us (2%)
    ppermute x11, starting transfers between devices, send(): return lax.ppermute(value, 'row', pairs)  25 us
    unnamed x24, local copies, waits for them, and re-layouts  6.65 us
    pallas_call x1, Pallas kernels, body(): pl.pallas_call(near_kernel, out_shape=jax.ShapeDtypeStruct((leaves, rows,...  5.7 us
    ppermute x11, waiting for transfers between devices, send(): return lax.ppermute(value, 'row', pairs)  4.59 us
    pallas_call x1, Pallas kernels, body(): pl.pallas_call(down_kernel, out_shape=jax.ShapeDtypeStruct((leaves, rows,...  4.07 us
    pallas_call x1, Pallas kernels, body(): pl.pallas_call(up_kernel, out_shape=(jax.ShapeDtypeStruct((leaves, rank,...  2.41 us
  transfers between devices with their start and end apart: 11, of which 3 were waited for; matrix products, arithmetic and copies ran while one was open for 4% of the time, Pallas kernels for 12%

profile of v1, /device:TPU:6, one launch (start us, length us, event | category | flops | bytes accessed | tf_op | source)
XLA Modules:
  0.0 49.4 jit_solution(8775201457199261827)
XLA Ops:
  0.0 0.0 copy-start.3
  0.0 0.0 copy-start.7
  0.0 0.0 copy-start.1
  0.0 0.0 copy-start.9
  0.0 2.4 %up.1 = (bf16[4,128,256]{2,1,0:T(8,128)(2,1)}, bf16[128,256]{1,0:T(8,128)(2,1)}) custom-call(bf16[1024,256]{1,0:T(8,128)(2,1)} %source_ref.1, bf16[4,256,128]{2,1,0:T(8,128)(2,1)} %col_ref.1, bf16[4,128,128]{2,1,0:T(8,128)(2,1)} %transfer_ref.3), custom_call_target="tpu_custom_call" | custom-call | flops 100663296 | bytes 786432 | tf_op jit(solution)/shard_map/up/pallas_call | solution.py:179
  2.4 0.5 %collective-permute-start.6 = (bf16[1,128,256]{2,1,0:T(8,128)(2,1)}, bf16[1,128,256]{2,1,0:T(8,128)(2,1)S(1)}, u32[]{:S(2)}, u32[]{:S(2)}) collective-permute-start(bf16[1,128,256]{2,1,0:T(8,128)(2,1)} %bitcast.7), channel_id=1, source_target_pairs={{0,2},{1,3},{2,0},{3,1},{4,6},{5,7},{6,4},{7,5},{8,10},{9,11},{10,... | collective-permute-start | bytes 196616 | tf_op jit(solution)/shard_map/ppermute | solution.py:173
  2.9 0.0 collective-permute-start
  2.9 3.5 %collective-permute-start.1 = (bf16[4,256,256]{2,1,0:T(8,128)(2,1)}, bf16[4,256,256]{2,1,0:T(8,128)(2,1)S(1)}, u32[]{:S(2)}, u32[]{:S(2)}) collective-permute-start(bf16[4,256,256]{2,1,0:T(8,128)(2,1)} %bitcast.5), channel_id=1, source_target_pairs={{1,2},{2,1},{3,4},{4,3},{5,6},{6,5},{7,8},{8,7},{9,10},{10,9},{11,... | collective-permute-start | bytes 1572872 | tf_op jit(solution)/shard_map/ppermute | solution.py:173
  6.5 2.0 %collective-permute-start.3 = (bf16[4,128,256]{2,1,0:T(8,128)(2,1)}, bf16[4,128,256]{2,1,0:T(8,128)(2,1)S(1)}, u32[]{:S(2)}, u32[]{:S(2)}) collective-permute-start(bf16[4,128,256]{2,1,0:T(8,128)(2,1)} %get-tuple-element.7), channel_id=1, source_target_pairs={{1,2},{2,1},{3,4},{4,3},{5,6},{6,5},{7,8},{8,7},{9,10},{10,9},{11,... | collective-permute-start | bytes 786440 | tf_op jit(solution)/shard_map/ppermute | solution.py:173
  8.5 0.0 collective-permute-done.6
  8.5 0.9 %pad_maximum_fusion = bf16[2,128,256]{2,1,0:T(8,128)(2,1)S(1)} fusion(bf16[1,128,256]{2,1,0:T(8,128)(2,1)S(1)} %collective-permute-done.6, bf16[1,128,256]{2,1,0:T(8,128)(2,1)} %bitcast.8), kind=kLoop, calls=%fused_computation | loop fusion | flops 65536 | bytes 262144 | tf_op jit(solution)/shard_map/concatenate | solution.py:196
  9.4 1.6 %collective-permute-start.7 = (bf16[2,128,256]{2,1,0:T(8,128)(2,1)S(1)}, bf16[2,128,256]{2,1,0:T(8,128)(2,1)S(1)}, u32[]{:S(2)}, u32[]{:S(2)}) collective-permute-start(bf16[2,128,256]{2,1,0:T(8,128)(2,1)S(1)} %pad_maximum_fusion), channel_id=1, source_target_pairs={{0,4},{1,5},{2,6},{3,7},{4,0},{5,1},{6,2},{7,3},{8,12},{9,13},{10,... | collective-permute-start | bytes 393224 | tf_op jit(solution)/shard_map/ppermute | solution.py:173
  11.0 0.8 %constant_dynamic-update-slice_fusion.4 = bf16[8,128,256]{2,1,0:T(8,128)(2,1)S(1)} fusion(bf16[128,256]{1,0:T(8,128)(2,1)} %get-tuple-element.8), kind=kLoop, calls=%fused_computation.5 | loop fusion | bytes 131072
  11.9 2.6 %collective-permute-start.8 = (bf16[2,128,256]{2,1,0:T(8,128)(2,1)S(1)}, bf16[2,128,256]{2,1,0:T(8,128)(2,1)S(1)}, u32[]{:S(2)}, u32[]{:S(2)}) collective-permute-start(bf16[2,128,256]{2,1,0:T(8,128)(2,1)S(1)} %pad_maximum_fusion), channel_id=1, source_target_pairs={{0,8},{1,9},{2,10},{3,11},{4,12},{5,13},{6,14},{7,15},{8,0},{9,1},... | collective-permute-start | bytes 393224 | tf_op jit(solution)/shard_map/ppermute | solution.py:173
  14.5 1.0 %collective-permute-done.7 = bf16[2,128,256]{2,1,0:T(8,128)(2,1)S(1)} collective-permute-done((bf16[2,128,256]{2,1,0:T(8,128)(2,1)S(1)}, bf16[2,128,256]{2,1,0:T(8,128)(2,1)S(1)}, u32[]{:S(2)}, u32[]{:S(2)}) %collective-permute-start.7) | collective-permute-done | bytes 131104 | tf_op jit(solution)/shard_map/ppermute | solution.py:173
  15.5 4.6 %collective-permute-start.9 = (bf16[2,128,256]{2,1,0:T(8,128)(2,1)S(1)}, bf16[2,128,256]{2,1,0:T(8,128)(2,1)S(1)}, u32[]{:S(2)}, u32[]{:S(2)}) collective-permute-start(bf16[2,128,256]{2,1,0:T(8,128)(2,1)S(1)} %pad_maximum_fusion), channel_id=1, source_target_pairs={{0,12},{1,13},{2,14},{3,15},{4,8},{5,9},{6,10},{7,11},{8,4},{9,5},... | collective-permute-start | bytes 393224 | tf_op jit(solution)/shard_map/ppermute | solution.py:173
  20.0 3.2 %collective-permute-done.8 = bf16[2,128,256]{2,1,0:T(8,128)(2,1)S(1)} collective-permute-done((bf16[2,128,256]{2,1,0:T(8,128)(2,1)S(1)}, bf16[2,128,256]{2,1,0:T(8,128)(2,1)S(1)}, u32[]{:S(2)}, u32[]{:S(2)}) %collective-permute-start.8) | collective-permute-done | bytes 131104 | tf_op jit(solution)/shard_map/ppermute | solution.py:173
  23.2 0.4 collective-permute-done.9
  23.6 4.5 %collective-permute-start.10 = (bf16[8,128,256]{2,1,0:T(8,128)(2,1)S(1)}, bf16[8,128,256]{2,1,0:T(8,128)(2,1)S(1)}, u32[]{:S(2)}, u32[]{:S(2)}) collective-permute-start(bf16[8,128,256]{2,1,0:T(8,128)(2,1)S(1)} %constant_dynamic-update-slice_fusion.mine_hbm), channel_id=1, source_target_pairs={{0,1},{1,0},{2,3},{3,2},{4,5},{5,4},{6,7},{7,6},{8,9},{9,8},{10,11... | collective-permute-start | bytes 1572872 | tf_op jit(solution)/shard_map/ppermute | solution.py:173
  28.1 5.1 %collective-permute-start.2 = (bf16[4,128,256]{2,1,0:T(8,128)(2,1)}, bf16[4,128,256]{2,1,0:T(8,128)(2,1)S(1)}, u32[]{:S(2)}, u32[]{:S(2)}) collective-permute-start(bf16[4,128,256]{2,1,0:T(8,128)(2,1)} %get-tuple-element.7), channel_id=1, source_target_pairs={{0,2},{2,4},{3,1},{4,6},{5,3},{6,8},{7,5},{8,10},{9,7},{10,12},{11... | collective-permute-start | bytes 786440 | tf_op jit(solution)/shard_map/ppermute | solution.py:173
  33.2 0.0 collective-permute-done.3.across_hbm
  33.2 0.1 collective-permute-start.4
  33.3 0.0 collective-permute-done.other_hbm
  33.3 0.5 collective-permute-start.5
  33.8 0.0 collective-permute-done.1.across_hbm
  33.8 0.0 copy-start
  33.8 3.4 %copy-done = bf16[4,16,256,256]{3,2,1,0:T(8,128)(2,1)S(1)} copy-done((bf16[4,16,256,256]{3,2,1,0:T(8,128)(2,1)S(1)}, bf16[4,16,256,256]{3,2,1,0:T(8,128)(2,1)}, u32[]{:S(2)}) %copy-start) | copy-done | bytes 8388632
  37.2 0.0 copy-start.2
  37.2 1.0 %copy-done.2 = bf16[1024,256]{1,0:T(8,128)(2,1)S(1)} copy-done((bf16[1024,256]{1,0:T(8,128)(2,1)S(1)}, bf16[1024,256]{1,0:T(8,128)(2,1)}, u32[]{:S(2)}) %copy-start.2) | copy-done | bytes 524312
  38.2 0.0 copy-start.6
  38.2 0.7 %copy-done.6 = s32[4,16]{1,0:T(4,128)S(1)} copy-done((s32[4,16]{1,0:T(4,128)S(1)}, s32[4,16]{1,0:T(4,128)}, u32[]{:S(2)}) %copy-start.6) | copy-done | bytes 280
  38.9 0.0 copy-start.8
  38.9 0.7 %copy-done.8 = s32[4]{0:T(128)S(1)} copy-done((s32[4]{0:T(128)S(1)}, s32[4]{0:T(128)}, u32[]{:S(2)}) %copy-start.8) | copy-done | bytes 40
  39.6 0.0 copy-start.4
  39.6 0.0 copy-start.5
  39.6 5.7 %near.1.near_hbm = f32[4,256,256]{2,1,0:T(8,128)S(1)} custom-call(s32[4,16]{1,0:T(4,128)S(1)} %copy-done.6, s32[4]{0:T(128)S(1)} %copy-done.8, bf16[4,16,256,256]{3,2,1,0:T(8,128)(2,1)S(1)} %copy-done, bf16[4,256,256]{2,1,0:T(8,128)(2,1)S(1)} %bitcast.6, bf16[4,256,256]{2,1,0:T(8,128)(2,1)S(1)} %collective-permute-done.other_hbm, ...), custom_call_target="tpu_custom_call" | custom-call | flops 2147483648 | bytes 8388608 | tf_op jit(solution)/shard_map/near/pallas_call | solution.py:205
  45.3 0.0 collective-permute-done.2.skip_hbm
  45.3 0.0 collective-permute-done.4.other_hbm
  45.3 0.0 collective-permute-done.5.passed_hbm
  45.3 0.0 collective-permute-done.10.theirs_hbm
  45.3 0.0 copy-done.3
  45.3 0.0 copy-done.7
  45.3 0.0 copy-done.1
  45.3 0.0 copy-done.9
  45.4 0.0 copy-done.4
  45.4 0.0 copy-done.5
  45.4 4.1 %down.1 = bf16[4,256,256]{2,1,0:T(8,128)(2,1)} custom-call(s32[4,16]{1,0:T(4,128)S(1)} %copy-done.6, s32[4,16]{1,0:T(4,128)S(1)} %copy-done.7, s32[1,8]{1,0:T(1,128)S(1)} %copy-done.9, f32[4,256,256]{2,1,0:T(8,128)S(1)} %near.1.near_hbm, bf16[4,256,128]{2,1,0:T(8,128)(2,1)S(1)} %copy-done.4, bf16[4,128,128]{2,1,0:T(8,128)(2,1)S(1)} %copy-done.3, ...), custom_call_target="tpu_custom_call" | custom-call | flops 671088640 | bytes 2097152 | tf_op jit(solution)/shard_map/down/pallas_call | solution.py:225
  (4 shorter events, 0.0 us)
Async XLA Ops:
  0.0 45.3 %copy-start.3 = (bf16[4,128,128]{2,1,0:T(8,128)(2,1)S(1)}, bf16[4,128,128]{2,1,0:T(8,128)(2,1)}, u32[]{:S(2)}) copy-start(bf16[4,128,128]{2,1,0:T(8,128)(2,1)} %transfer_ref.3) | copy-start | bytes 393220
  0.0 45.3 %copy-start.7 = (s32[4,16]{1,0:T(4,128)S(1)}, s32[4,16]{1,0:T(4,128)}, u32[]{:S(2)}) copy-start(s32[4,16]{1,0:T(4,128)} %far_list_ref.1) | copy-start | bytes 772
  0.0 45.3 %copy-start.1 = (bf16[4,16,128,128]{3,2,1,0:T(8,128)(2,1)S(1)}, bf16[4,16,128,128]{3,2,1,0:T(8,128)(2,1)}, u32[]{:S(2)}) copy-start(bf16[4,16,128,128]{3,2,1,0:T(8,128)(2,1)} %coupling_hbm.1) | copy-start | bytes 6291460
  0.0 45.3 %copy-start.9 = (s32[1,8]{1,0:T(1,128)S(1)}, s32[1,8]{1,0:T(1,128)}, u32[]{:S(2)}) copy-start(s32[1,8]{1,0:T(1,128)} %coarse_list_ref.1) | copy-start | bytes 100
  2.4 6.1 %collective-permute-start.6 = (bf16[1,128,256]{2,1,0:T(8,128)(2,1)}, bf16[1,128,256]{2,1,0:T(8,128)(2,1)S(1)}, u32[]{:S(2)}, u32[]{:S(2)}) collective-permute-start(bf16[1,128,256]{2,1,0:T(8,128)(2,1)} %bitcast.7), channel_id=1, source_target_pairs={{0,2},{1,3},{2,0},{3,1},{4,6},{5,7},{6,4},{7,5},{8,10},{9,11},{10,... | collective-permute-start | bytes 196616 | tf_op jit(solution)/shard_map/ppermute | solution.py:173
  2.9 30.4 %collective-permute-start = (bf16[4,256,256]{2,1,0:T(8,128)(2,1)}, bf16[4,256,256]{2,1,0:T(8,128)(2,1)S(1)}, u32[]{:S(2)}, u32[]{:S(2)}) collective-permute-start(bf16[4,256,256]{2,1,0:T(8,128)(2,1)} %bitcast.4), channel_id=1, source_target_pairs={{0,1},{1,0},{2,3},{3,2},{4,5},{5,4},{6,7},{7,6},{8,9},{9,8},{10,11... | collective-permute-start | bytes 1572872 | tf_op jit(solution)/shard_map/ppermute | solution.py:173
  2.9 30.9 %collective-permute-start.1 = (bf16[4,256,256]{2,1,0:T(8,128)(2,1)}, bf16[4,256,256]{2,1,0:T(8,128)(2,1)S(1)}, u32[]{:S(2)}, u32[]{:S(2)}) collective-permute-start(bf16[4,256,256]{2,1,0:T(8,128)(2,1)} %bitcast.5), channel_id=1, source_target_pairs={{1,2},{2,1},{3,4},{4,3},{5,6},{6,5},{7,8},{8,7},{9,10},{10,9},{11,... | collective-permute-start | bytes 1572872 | tf_op jit(solution)/shard_map/ppermute | solution.py:173
  6.5 26.7 %collective-permute-start.3 = (bf16[4,128,256]{2,1,0:T(8,128)(2,1)}, bf16[4,128,256]{2,1,0:T(8,128)(2,1)S(1)}, u32[]{:S(2)}, u32[]{:S(2)}) collective-permute-start(bf16[4,128,256]{2,1,0:T(8,128)(2,1)} %get-tuple-element.7), channel_id=1, source_target_pairs={{1,2},{2,1},{3,4},{4,3},{5,6},{6,5},{7,8},{8,7},{9,10},{10,9},{11,... | collective-permute-start | bytes 786440 | tf_op jit(solution)/shard_map/ppermute | solution.py:173
  9.4 6.1 %collective-permute-start.7 = (bf16[2,128,256]{2,1,0:T(8,128)(2,1)S(1)}, bf16[2,128,256]{2,1,0:T(8,128)(2,1)S(1)}, u32[]{:S(2)}, u32[]{:S(2)}) collective-permute-start(bf16[2,128,256]{2,1,0:T(8,128)(2,1)S(1)} %pad_maximum_fusion), channel_id=1, source_target_pairs={{0,4},{1,5},{2,6},{3,7},{4,0},{5,1},{6,2},{7,3},{8,12},{9,13},{10,... | collective-permute-start | bytes 393224 | tf_op jit(solution)/shard_map/ppermute | solution.py:173
  11.9 11.3 %collective-permute-start.8 = (bf16[2,128,256]{2,1,0:T(8,128)(2,1)S(1)}, bf16[2,128,256]{2,1,0:T(8,128)(2,1)S(1)}, u32[]{:S(2)}, u32[]{:S(2)}) collective-permute-start(bf16[2,128,256]{2,1,0:T(8,128)(2,1)S(1)} %pad_maximum_fusion), channel_id=1, source_target_pairs={{0,8},{1,9},{2,10},{3,11},{4,12},{5,13},{6,14},{7,15},{8,0},{9,1},... | collective-permute-start | bytes 393224 | tf_op jit(solution)/shard_map/ppermute | solution.py:173
  15.5 8.2 %collective-permute-start.9 = (bf16[2,128,256]{2,1,0:T(8,128)(2,1)S(1)}, bf16[2,128,256]{2,1,0:T(8,128)(2,1)S(1)}, u32[]{:S(2)}, u32[]{:S(2)}) collective-permute-start(bf16[2,128,256]{2,1,0:T(8,128)(2,1)S(1)} %pad_maximum_fusion), channel_id=1, source_target_pairs={{0,12},{1,13},{2,14},{3,15},{4,8},{5,9},{6,10},{7,11},{8,4},{9,5},... | collective-permute-start | bytes 393224 | tf_op jit(solution)/shard_map/ppermute | solution.py:173
  23.6 21.7 %collective-permute-start.10 = (bf16[8,128,256]{2,1,0:T(8,128)(2,1)S(1)}, bf16[8,128,256]{2,1,0:T(8,128)(2,1)S(1)}, u32[]{:S(2)}, u32[]{:S(2)}) collective-permute-start(bf16[8,128,256]{2,1,0:T(8,128)(2,1)S(1)} %constant_dynamic-update-slice_fusion.mine_hbm), channel_id=1, source_target_pairs={{0,1},{1,0},{2,3},{3,2},{4,5},{5,4},{6,7},{7,6},{8,9},{9,8},{10,11... | collective-permute-start | bytes 1572872 | tf_op jit(solution)/shard_map/ppermute | solution.py:173
  28.1 17.2 %collective-permute-start.2 = (bf16[4,128,256]{2,1,0:T(8,128)(2,1)}, bf16[4,128,256]{2,1,0:T(8,128)(2,1)S(1)}, u32[]{:S(2)}, u32[]{:S(2)}) collective-permute-start(bf16[4,128,256]{2,1,0:T(8,128)(2,1)} %get-tuple-element.7), channel_id=1, source_target_pairs={{0,2},{2,4},{3,1},{4,6},{5,3},{6,8},{7,5},{8,10},{9,7},{10,12},{11... | collective-permute-start | bytes 786440 | tf_op jit(solution)/shard_map/ppermute | solution.py:173
  33.2 12.1 %collective-permute-start.4 = (bf16[4,128,256]{2,1,0:T(8,128)(2,1)}, bf16[4,128,256]{2,1,0:T(8,128)(2,1)S(1)}, u32[]{:S(2)}, u32[]{:S(2)}) collective-permute-start(bf16[4,128,256]{2,1,0:T(8,128)(2,1)} %get-tuple-element.7), channel_id=1, source_target_pairs={{0,1},{1,0},{2,3},{3,2},{4,5},{5,4},{6,7},{7,6},{8,9},{9,8},{10,11... | collective-permute-start | bytes 786440 | tf_op jit(solution)/shard_map/ppermute | solution.py:173
  33.3 12.0 %collective-permute-start.5 = (bf16[4,128,256]{2,1,0:T(8,128)(2,1)S(1)}, bf16[4,128,256]{2,1,0:T(8,128)(2,1)S(1)}, u32[]{:S(2)}, u32[]{:S(2)}) collective-permute-start(bf16[4,128,256]{2,1,0:T(8,128)(2,1)S(1)} %collective-permute-done.3.across_hbm), channel_id=1, source_target_pairs={{0,1},{1,0},{2,3},{3,2},{4,5},{5,4},{6,7},{7,6},{8,9},{9,8},{10,11... | collective-permute-start | bytes 786440 | tf_op jit(solution)/shard_map/ppermute | solution.py:173
  33.8 3.4 %copy-start = (bf16[4,16,256,256]{3,2,1,0:T(8,128)(2,1)S(1)}, bf16[4,16,256,256]{3,2,1,0:T(8,128)(2,1)}, u32[]{:S(2)}) copy-start(bf16[4,16,256,256]{3,2,1,0:T(8,128)(2,1)} %blocks_hbm.1) | copy-start | bytes 25165828
  37.2 1.0 %copy-start.2 = (bf16[1024,256]{1,0:T(8,128)(2,1)S(1)}, bf16[1024,256]{1,0:T(8,128)(2,1)}, u32[]{:S(2)}) copy-start(bf16[1024,256]{1,0:T(8,128)(2,1)} %source_ref.1) | copy-start | bytes 1572868
  38.2 0.7 %copy-start.6 = (s32[4,16]{1,0:T(4,128)S(1)}, s32[4,16]{1,0:T(4,128)}, u32[]{:S(2)}) copy-start(s32[4,16]{1,0:T(4,128)} %near_list_ref.1) | copy-start | bytes 772
  38.9 0.7 %copy-start.8 = (s32[4]{0:T(128)S(1)}, s32[4]{0:T(128)}, u32[]{:S(2)}) copy-start(s32[4]{0:T(128)} %count_ref.1) | copy-start | bytes 52
  39.6 5.8 %copy-start.4 = (bf16[4,256,128]{2,1,0:T(8,128)(2,1)S(1)}, bf16[4,256,128]{2,1,0:T(8,128)(2,1)}, u32[]{:S(2)}) copy-start(bf16[4,256,128]{2,1,0:T(8,128)(2,1)} %row_ref.1) | copy-start | bytes 786436
  39.6 5.8 %copy-start.5 = (bf16[1,8,128,128]{3,2,1,0:T(8,128)(2,1)S(1)}, bf16[1,8,128,128]{3,2,1,0:T(8,128)(2,1)}, u32[]{:S(2)}) copy-start(bf16[1,8,128,128]{3,2,1,0:T(8,128)(2,1)} %coarse_coupling_ref.1) | copy-start | bytes 786436

commit v2 on v1

v2 whole, which is shorter than its diff:
```python
import jax
import jax.numpy as jnp
from jax import lax
from jax.experimental import pallas as pl
from jax.experimental.pallas import tpu as pltpu
from jax.sharding import PartitionSpec as P

GROUP = 16
CHUNK = 4


def dot(a, b):
    return jnp.dot(a, b, preferred_element_type=jnp.float32)


def dot_t(a, b):
    return lax.dot_general(
        a, b, (((0,), (0,)), ((), ())), preferred_element_type=jnp.float32
    )


def up_kernel(source_ref, col_ref, transfer_ref, share_ref, coef_ref, parent_ref):
    leaves, rows, rank = col_ref.shape
    total = None
    for leaf in range(leaves):
        panel = source_ref[pl.ds(leaf * rows, rows), :]
        share_ref[pl.ds(leaf * rows, rows), :] = panel
        coef = dot_t(col_ref[leaf], panel).astype(jnp.bfloat16)
        coef_ref[pl.ds(leaf * rank, rank), :] = coef
        share_ref[pl.ds(leaves * rows + leaf * rank, rank), :] = coef
        term = dot_t(transfer_ref[leaf], coef)
        total = term if total is None else total + term
    parent_ref[...] = total.astype(jnp.bfloat16)


def near_kernel(
    list_ref, count_ref, blocks_hbm, own_ref, share_ref, across_ref, near_ref,
    blocks, panels, block_sems, panel_sems,
):
    leaves, slots, rows, _ = blocks.shape
    chunks = slots // CHUNK
    size = leaves * rows
    place = list_ref[0, 0] // leaves
    pairs = [
        pltpu.make_async_copy(
            ref.at[pl.ds(0, size)], panels.at[pl.ds(which * size, size)], panel_sems.at[which]
        )
        for which, ref in enumerate((own_ref, share_ref, across_ref))
    ]
    for copy in pairs:
        copy.start()

    def block_copy(leaf, chunk):
        where = pl.ds(chunk * CHUNK, CHUNK)
        return pltpu.make_async_copy(
            blocks_hbm.at[leaf, where], blocks.at[leaf, where], block_sems.at[leaf, chunk]
        )

    for leaf in range(leaves):
        for chunk in range(chunks):
            @pl.when(chunk * CHUNK < count_ref[leaf])
            def _():
                block_copy(leaf, chunk).start()

    panels[pl.ds(3 * size, rows), :] = jnp.zeros((rows, panels.shape[1]), panels.dtype)
    for copy in pairs:
        copy.wait()

    def panel_of(leaf, slot):
        column = list_ref[leaf, slot]
        cluster = column // leaves
        which = jnp.where(cluster == place, 0, jnp.where(cluster == (place ^ 1), 1, 2))
        index = which * leaves + column - cluster * leaves
        index = jnp.where(slot < count_ref[leaf], index, 3 * leaves)
        return panels[pl.ds(pl.multiple_of(index * rows, rows), rows), :]

    for leaf in range(leaves):
        for chunk in range(chunks):
            @pl.when(chunk * CHUNK < count_ref[leaf])
            def _():
                block_copy(leaf, chunk).wait()
                total = None if chunk == 0 else near_ref[leaf]
                for slot in range(chunk * CHUNK, (chunk + 1) * CHUNK):
                    term = dot(blocks[leaf, slot], panel_of(leaf, slot))
                    total = term if total is None else total + term
                near_ref[leaf] = total


def down_kernel(
    near_list_ref, far_list_ref, coarse_list_ref,
    near_ref, row_ref, transfer_ref, coupling_ref, coarse_coupling_ref,
    skip_ref, across_ref, share_ref, passed_ref, mine_ref, theirs_ref,
    out_ref,
    coefs, sems,
):
    leaves, slots, rank, _ = coupling_ref.shape
    rows = row_ref.shape[1]
    size = leaves * rank
    place = near_list_ref[0, 0] // leaves
    copies = [
        pltpu.make_async_copy(
            ref.at[pl.ds(start, size)], coefs.at[pl.ds(n * size, size)], sems.at[n]
        )
        for n, (ref, start) in enumerate(
            ((skip_ref, 0), (across_ref, 0), (share_ref, leaves * rows), (passed_ref, 0))
        )
    ]
    for copy in copies:
        copy.start()

    local = place % GROUP
    total = None
    for slot in range(coarse_list_ref.shape[1]):
        cluster = coarse_list_ref[0, slot] % GROUP
        flip = cluster ^ local
        index = (cluster >> 2) * 2 + ((flip >> 1) & 1)
        panel = jnp.where((flip & 1) == 0, mine_ref[index], theirs_ref[index])
        term = dot(coarse_coupling_ref[0, slot], panel)
        total = term if total is None else total + term
    high = total.astype(jnp.bfloat16)
    low = (total - high.astype(jnp.float32)).astype(jnp.bfloat16)
    coarse = jnp.concatenate([high, low], axis=0)

    odd = place % 2 == 1
    for copy in copies:
        copy.wait()
    for leaf in range(leaves):
        matrix = transfer_ref[leaf]
        total = dot(jnp.concatenate([matrix, matrix], axis=1), coarse)
        for slot in range(slots):
            column = far_list_ref[leaf, slot]
            cluster = column // leaves
            away = jnp.where(odd, place - cluster, cluster - place)
            which = jnp.where(away < 0, away + 2, away + 1)
            index = which * leaves + column - cluster * leaves
            panel = coefs[pl.ds(pl.multiple_of(index * rank, rank), rank), :]
            total = total + dot(coupling_ref[leaf, slot], panel)
        down = total.astype(jnp.bfloat16)
        result = near_ref[leaf] + dot(row_ref[leaf], down)
        out_ref[pl.ds(leaf * rows, rows), :] = result.astype(jnp.bfloat16)


VMEM = pl.BlockSpec(memory_space=pltpu.VMEM)
SMEM = pl.BlockSpec(memory_space=pltpu.SMEM)
ANY = pl.BlockSpec(memory_space=pl.ANY)
HBM = pl.BlockSpec(memory_space=pltpu.HBM)


def body(
    source,
    near_blocks,
    near_list,
    near_count,
    col_basis,
    row_basis,
    transfer,
    far_list,
    far_coupling,
    coarse_list,
    coarse_coupling,
):
    leaves, slots, rows, _ = near_blocks.shape
    rank = col_basis.shape[2]
    width = source.shape[1]
    count = lax.axis_size("row")
    far_slots = far_coupling.shape[1]

    def pairs_of(target):
        return [(d, target(d)) for d in range(count) if 0 <= target(d) < count]

    across = pairs_of(lambda d: d + 1 if d % 2 else d - 1)
    skip = pairs_of(lambda d: d - 2 if d % 2 else d + 2)

    def flip(bit):
        return pairs_of(lambda d: d ^ bit)

    def send(value, pairs):
        return lax.ppermute(value, "row", pairs)

    across_source = send(source, across)

    share, coef, parent = pl.pallas_call(
        up_kernel,
        out_shape=(
            jax.ShapeDtypeStruct((leaves * (rows + rank), width), jnp.bfloat16),
            jax.ShapeDtypeStruct((leaves * rank, width), jnp.bfloat16),
            jax.ShapeDtypeStruct((rank, width), jnp.bfloat16),
        ),
        in_specs=[VMEM] * 3,
        out_specs=(VMEM,) * 3,
        cost_estimate=pl.CostEstimate(
            flops=2 * leaves * rank * width * (rows + rank),
            bytes_accessed=2 * leaves * rows * (width + rank),
            transcendentals=0,
        ),
        name="up",
    )(source, col_basis, transfer)

    parent = parent[None]
    pair = jnp.concatenate([parent, send(parent, flip(2))], axis=0)
    layers = [
        [base + step * 4 for step in range(GROUP // 4)]
        for start in range(0, count, GROUP)
        for base in range(start, start + 4)
    ]
    copies = jnp.broadcast_to(pair[None], (GROUP // 4,) + pair.shape)
    mine = lax.all_to_all(
        copies, "row", split_axis=0, concat_axis=0, axis_index_groups=layers
    ).reshape(GROUP // 2, rank, width)
    theirs = send(mine, flip(1))

    share_other = send(share, flip(1))
    coef_across = send(coef, across)
    coef_passed = send(coef_across, flip(1))
    coef_skip = send(coef, skip)

    near = pl.pallas_call(
        near_kernel,
        out_shape=jax.ShapeDtypeStruct((leaves, rows, width), jnp.float32),
        in_specs=[SMEM, SMEM, HBM, ANY, ANY, ANY],
        out_specs=VMEM,
        scratch_shapes=[
            pltpu.VMEM((leaves, slots, rows, rows), jnp.bfloat16),
            pltpu.VMEM(((3 * leaves + 1) * rows, width), jnp.bfloat16),
            pltpu.SemaphoreType.DMA((leaves, slots // CHUNK)),
            pltpu.SemaphoreType.DMA((3,)),
        ],
        cost_estimate=pl.CostEstimate(
            flops=2 * leaves * slots * rows * rows * width,
            bytes_accessed=2 * leaves * slots * rows * rows,
            transcendentals=0,
        ),
        compiler_params=pltpu.CompilerParams(vmem_limit_bytes=50 * 2**20),
        name="near",
    )(near_list, near_count, near_blocks, share, share_other, across_source)

    return pl.pallas_call(
        down_kernel,
        out_shape=jax.ShapeDtypeStruct(source.shape, jnp.bfloat16),
        in_specs=[SMEM] * 3 + [VMEM] * 5 + [ANY] * 4 + [VMEM] * 2,
        out_specs=VMEM,
        scratch_shapes=[
            pltpu.VMEM((4 * leaves * rank, width), jnp.bfloat16),
            pltpu.SemaphoreType.DMA((4,)),
        ],
        cost_estimate=pl.CostEstimate(
            flops=2 * leaves * (far_slots + 4) * rank * rank * width,
            bytes_accessed=2 * leaves * far_slots * rank * rank,
            transcendentals=0,
        ),
        compiler_params=pltpu.CompilerParams(vmem_limit_bytes=16 * 2**20),
        name="down",
    )(
        near_list, far_list, coarse_list, near, row_basis, transfer, far_coupling,
        coarse_coupling, coef_skip, coef_across, share_other, coef_passed, mine, theirs,
    )


def solution(mesh):
    placed = (
        P(("clip", "row"), None),
        P(("clip", "row"), None, None, None),
        P(("clip", "row"), None),
        P(("clip", "row")),
        P(("clip", "row"), None, None),
        P(("clip", "row"), None, None),
        P(("clip", "row"), None, None),
        P(("clip", "row"), None),
        P(("clip", "row"), None, None, None),
        P(("clip", "row"), None),
        P(("clip", "row"), None, None, None),
    )
    return jax.shard_map(
        body, mesh=mesh, in_specs=placed, out_specs=P(("clip", "row"), None), check_vma=False
    )
```

time: 49.9 us -> 57.5 us (1.15)
  the two profiles are of different devices: /device:TPU:6 before, /device:TPU:23 now
where the time goes in v2:
time: 57.5 us; the launch traced here: 57.1 us
  starting transfers between devices  27 us (47%)
  Pallas kernels  14.8 us (26%)
  waiting for transfers between devices  11 us (19%)
  local copies, waits for them, and re-layouts  3.32 us (6%)
  other arithmetic  0.85 us (1%)
    ppermute x7, starting transfers between devices, send(): return lax.ppermute(value, 'row', pairs)  22.4 us
    ppermute x7, waiting for transfers between devices, send(): return lax.ppermute(value, 'row', pairs)  9.15 us
    pallas_call x1, Pallas kernels, body(): pl.pallas_call(near_kernel, out_shape=jax.ShapeDtypeStruct((leaves, rows,...  7.99 us
    all_to_all x1, starting transfers between devices, body(): lax.all_to_all(copies, 'row', split_axis=0, concat_axis=0, axis_index_gro...  4.64 us
    pallas_call x1, Pallas kernels, body(): pl.pallas_call(down_kernel, out_shape=jax.ShapeDtypeStruct(source.shape,...  4.22 us
    pallas_call x1, Pallas kernels, body(): pl.pallas_call(up_kernel, out_shape=(jax.ShapeDtypeStruct((leaves * (rows...  2.59 us
    unnamed x20, local copies, waits for them, and re-layouts  2.49 us
    all_to_all x1, waiting for transfers between devices, body(): lax.all_to_all(copies, 'row', split_axis=0, concat_axis=0, axis_index_gro...  1.83 us
  transfers between devices with their start and end apart: 8, of which 3 were waited for; matrix products, arithmetic and copies ran while one was open for 0% of the time, Pallas kernels for 14%

profile of v2, /device:TPU:23, one launch (start us, length us, event | category | flops | bytes accessed | tf_op | source)
XLA Modules:
  0.0 57.1 jit_solution(7181323126098290272)
XLA Ops:
  0.0 0.0 copy-start.2
  0.0 0.0 copy-start.6
  0.0 0.0 copy-start.7
  0.0 0.0 copy-start.9
  0.0 0.0 copy-start
  0.0 2.6 %up.1 = (bf16[1536,256]{1,0:T(8,128)(2,1)}, bf16[512,256]{1,0:T(8,128)(2,1)}, bf16[128,256]{1,0:T(8,128)(2,1)}) custom-call(bf16[1024,256]{1,0:T(8,128)(2,1)} %source_ref.1, bf16[4,256,128]{2,1,0:T(8,128)(2,1)} %col_ref.1, bf16[4,128,128]{2,1,0:T(8,128)(2,1)} %transfer_ref.3), custom_call_target="tpu_custom_call" | custom-call | flops 100663296 | bytes 786432 | tf_op jit(solution)/shard_map/up/pallas_call | solution.py:182
  2.6 0.2 collective-permute-start.5
  2.8 3.1 %collective-permute-done.5 = bf16[1,128,256]{2,1,0:T(8,128)(2,1)S(1)} collective-permute-done((bf16[1,128,256]{2,1,0:T(8,128)(2,1)}, bf16[1,128,256]{2,1,0:T(8,128)(2,1)S(1)}, u32[]{:S(2)}, u32[]{:S(2)}) %collective-permute-start.5) | collective-permute-done | bytes 65568 | tf_op jit(solution)/shard_map/ppermute | solution.py:178
  5.9 0.9 %pad_maximum_fusion = bf16[2,128,256]{2,1,0:T(8,128)(2,1)S(1)} fusion(bf16[1,128,256]{2,1,0:T(8,128)(2,1)S(1)} %collective-permute-done.5, bf16[1,128,256]{2,1,0:T(8,128)(2,1)} %bitcast.5), kind=kLoop, calls=%fused_computation | loop fusion | flops 65536 | bytes 262144 | tf_op jit(solution)/shard_map/concatenate | solution.py:200
  6.8 0.8 %broadcast_in_dim.10 = bf16[4,2,128,256]{3,2,1,0:T(8,128)(2,1)} broadcast(bf16[2,128,256]{2,1,0:T(8,128)(2,1)S(1)} %pad_maximum_fusion), dimensions={1,2,3} | broadcast | bytes 655360 | tf_op jit(solution)/shard_map/broadcast_in_dim | solution.py:206
  7.6 4.6 %all-to-all-start = ((bf16[4,2,128,256]{3,2,1,0:T(8,128)(2,1)}), bf16[4,2,128,256]{3,2,1,0:T(8,128)(2,1)S(1)}, u32[]{:S(2)}, u32[]{:S(2)}) async-start(bf16[4,2,128,256]{3,2,1,0:T(8,128)(2,1)} %broadcast_in_dim.10), calls=%async_computation | async-start | bytes 1048576 | tf_op jit(solution)/shard_map/all_to_all | solution.py:207
  12.3 2.4 %collective-permute-start = (bf16[1536,256]{1,0:T(8,128)(2,1)}, bf16[1536,256]{1,0:T(8,128)(2,1)S(1)}, u32[]{:S(2)}, u32[]{:S(2)}) collective-permute-start(bf16[1536,256]{1,0:T(8,128)(2,1)} %get-tuple-element.8.own_ref), channel_id=1, source_target_pairs={{0,1},{1,0},{2,3},{3,2},{4,5},{5,4},{6,7},{7,6},{8,9},{9,8},{10,11... | collective-permute-start | bytes 2359304 | tf_op jit(solution)/shard_map/ppermute | solution.py:178
  14.7 2.9 %collective-permute-start.1 = (bf16[1024,256]{1,0:T(8,128)(2,1)}, bf16[1024,256]{1,0:T(8,128)(2,1)}, u32[]{:S(2)}, u32[]{:S(2)}) collective-permute-start(bf16[1024,256]{1,0:T(8,128)(2,1)} %source_ref.1), channel_id=1, source_target_pairs={{1,2},{2,1},{3,4},{4,3},{5,6},{6,5},{7,8},{8,7},{9,10},{10,9},{11,... | collective-permute-start | bytes 1572872 | tf_op jit(solution)/shard_map/ppermute | solution.py:178
  17.6 3.5 %collective-permute-start.3 = (bf16[512,256]{1,0:T(8,128)(2,1)}, bf16[512,256]{1,0:T(8,128)(2,1)}, u32[]{:S(2)}, u32[]{:S(2)}) collective-permute-start(bf16[512,256]{1,0:T(8,128)(2,1)} %get-tuple-element.9), channel_id=1, source_target_pairs={{1,2},{2,1},{3,4},{4,3},{5,6},{6,5},{7,8},{8,7},{9,10},{10,9},{11,... | collective-permute-start | bytes 786440 | tf_op jit(solution)/shard_map/ppermute | solution.py:178
  21.1 1.8 %all-to-all-done = bf16[4,2,128,256]{3,2,1,0:T(8,128)(2,1)S(1)} async-done(((bf16[4,2,128,256]{3,2,1,0:T(8,128)(2,1)}), bf16[4,2,128,256]{3,2,1,0:T(8,128)(2,1)S(1)}, u32[]{:S(2)}, u32[]{:S(2)}) %all-to-all-start) | async-done | bytes 524320 | tf_op jit(solution)/shard_map/all_to_all | solution.py:207
  23.0 2.0 %collective-permute-start.6 = (bf16[8,128,256]{2,1,0:T(8,128)(2,1)S(1)}, bf16[8,128,256]{2,1,0:T(8,128)(2,1)S(1)}, u32[]{:S(2)}, u32[]{:S(2)}) collective-permute-start(bf16[8,128,256]{2,1,0:T(8,128)(2,1)S(1)} %bitcast.2), channel_id=1, source_target_pairs={{0,1},{1,0},{2,3},{3,2},{4,5},{5,4},{6,7},{7,6},{8,9},{9,8},{10,11... | collective-permute-start | bytes 1572872 | tf_op jit(solution)/shard_map/ppermute | solution.py:178
  24.9 2.0 %collective-permute-start.2 = (bf16[512,256]{1,0:T(8,128)(2,1)}, bf16[512,256]{1,0:T(8,128)(2,1)S(1)}, u32[]{:S(2)}, u32[]{:S(2)}) collective-permute-start(bf16[512,256]{1,0:T(8,128)(2,1)} %get-tuple-element.9), channel_id=1, source_target_pairs={{0,2},{2,4},{3,1},{4,6},{5,3},{6,8},{7,5},{8,10},{9,7},{10,12},{11... | collective-permute-start | bytes 786440 | tf_op jit(solution)/shard_map/ppermute | solution.py:178
  26.9 6.0 %collective-permute-done.3.across_ref = bf16[512,256]{1,0:T(8,128)(2,1)} collective-permute-done((bf16[512,256]{1,0:T(8,128)(2,1)}, bf16[512,256]{1,0:T(8,128)(2,1)}, u32[]{:S(2)}, u32[]{:S(2)}) %collective-permute-start.3) | collective-permute-done | bytes 262176 | tf_op jit(solution)/shard_map/ppermute | solution.py:178
  32.9 9.4 %collective-permute-start.4 = (bf16[512,256]{1,0:T(8,128)(2,1)}, bf16[512,256]{1,0:T(8,128)(2,1)S(1)}, u32[]{:S(2)}, u32[]{:S(2)}) collective-permute-start(bf16[512,256]{1,0:T(8,128)(2,1)} %collective-permute-done.3.across_ref), channel_id=1, source_target_pairs={{0,1},{1,0},{2,3},{3,2},{4,5},{5,4},{6,7},{7,6},{8,9},{9,8},{10,11... | collective-permute-start | bytes 786440 | tf_op jit(solution)/shard_map/ppermute | solution.py:178
  42.3 0.0 collective-permute-done.1.across_ref
  42.3 0.0 collective-permute-done.share_ref
  42.3 0.0 copy-start.1
  42.3 1.1 %copy-done.1 = bf16[1536,256]{1,0:T(8,128)(2,1)S(1)} copy-done((bf16[1536,256]{1,0:T(8,128)(2,1)S(1)}, bf16[1536,256]{1,0:T(8,128)(2,1)}, u32[]{:S(2)}) %copy-start.1) | copy-done | bytes 786456
  43.5 0.0 copy-start.5
  43.5 0.7 %copy-done.5 = s32[4,16]{1,0:T(4,128)S(1)} copy-done((s32[4,16]{1,0:T(4,128)S(1)}, s32[4,16]{1,0:T(4,128)}, u32[]{:S(2)}) %copy-start.5) | copy-done | bytes 280
  44.1 0.0 copy-start.8
  44.1 0.7 %copy-done.8 = s32[4]{0:T(128)S(1)} copy-done((s32[4]{0:T(128)S(1)}, s32[4]{0:T(128)}, u32[]{:S(2)}) %copy-start.8) | copy-done | bytes 40
  44.8 0.0 copy-start.3
  44.8 0.0 copy-start.4
  44.8 8.0 %near.1.near_ref = f32[4,256,256]{2,1,0:T(8,128)S(1)} custom-call(s32[4,16]{1,0:T(4,128)S(1)} %copy-done.5, s32[4]{0:T(128)S(1)} %copy-done.8, bf16[4,16,256,256]{3,2,1,0:T(8,128)(2,1)} %blocks_hbm.1, bf16[1536,256]{1,0:T(8,128)(2,1)S(1)} %copy-done.1, bf16[1536,256]{1,0:T(8,128)(2,1)S(1)} %collective-permute-done.share_ref, ...), custom_call_target="tpu_custom_call" | custom-call | flops 2147483648 | bytes 8388608 | tf_op jit(solution)/shard_map/near/pallas_call | solution.py:217
  52.8 0.0 collective-permute-done.2.skip_ref
  52.8 0.0 collective-permute-done.4.passed_ref
  52.8 0.0 collective-permute-done.6.theirs_ref
  52.8 0.0 copy-done.2
  52.8 0.0 copy-done.6
  52.9 0.0 copy-done.7
  52.9 0.0 copy-done.9
  52.9 0.0 copy-done
  52.9 0.0 copy-done.3
  52.9 0.0 copy-done.4
  52.9 4.2 %down.1 = bf16[1024,256]{1,0:T(8,128)(2,1)} custom-call(s32[4,16]{1,0:T(4,128)S(1)} %copy-done.6, s32[4,16]{1,0:T(4,128)S(1)} %copy-done.7, s32[1,8]{1,0:T(1,128)S(1)} %copy-done.9, f32[4,256,256]{2,1,0:T(8,128)S(1)} %near.1.near_ref, bf16[4,256,128]{2,1,0:T(8,128)(2,1)S(1)} %copy-done.3, bf16[4,128,128]{2,1,0:T(8,128)(2,1)S(1)} %copy-done.2, ...), custom_call_target="tpu_custom_call" | custom-call | flops 671088640 | bytes 2097152 | tf_op jit(solution)/shard_map/down/pallas_call | solution.py:237
Async XLA Ops:
  0.0 52.8 %copy-start.2 = (bf16[4,128,128]{2,1,0:T(8,128)(2,1)S(1)}, bf16[4,128,128]{2,1,0:T(8,128)(2,1)}, u32[]{:S(2)}) copy-start(bf16[4,128,128]{2,1,0:T(8,128)(2,1)} %transfer_ref.3) | copy-start | bytes 393220
  0.0 52.8 %copy-start.6 = (s32[4,16]{1,0:T(4,128)S(1)}, s32[4,16]{1,0:T(4,128)}, u32[]{:S(2)}) copy-start(s32[4,16]{1,0:T(4,128)} %near_list_ref.1) | copy-start | bytes 772
  0.0 52.9 %copy-start.7 = (s32[4,16]{1,0:T(4,128)S(1)}, s32[4,16]{1,0:T(4,128)}, u32[]{:S(2)}) copy-start(s32[4,16]{1,0:T(4,128)} %far_list_ref.1) | copy-start | bytes 772
  0.0 52.9 %copy-start.9 = (s32[1,8]{1,0:T(1,128)S(1)}, s32[1,8]{1,0:T(1,128)}, u32[]{:S(2)}) copy-start(s32[1,8]{1,0:T(1,128)} %coarse_list_ref.1) | copy-start | bytes 100
  0.0 52.9 %copy-start = (bf16[4,16,128,128]{3,2,1,0:T(8,128)(2,1)S(1)}, bf16[4,16,128,128]{3,2,1,0:T(8,128)(2,1)}, u32[]{:S(2)}) copy-start(bf16[4,16,128,128]{3,2,1,0:T(8,128)(2,1)} %coupling_ref.1) | copy-start | bytes 6291460
  2.6 3.3 %collective-permute-start.5 = (bf16[1,128,256]{2,1,0:T(8,128)(2,1)}, bf16[1,128,256]{2,1,0:T(8,128)(2,1)S(1)}, u32[]{:S(2)}, u32[]{:S(2)}) collective-permute-start(bf16[1,128,256]{2,1,0:T(8,128)(2,1)} %bitcast.4), channel_id=1, source_target_pairs={{0,2},{1,3},{2,0},{3,1},{4,6},{5,7},{6,4},{7,5},{8,10},{9,11},{10,... | collective-permute-start | bytes 196616 | tf_op jit(solution)/shard_map/ppermute | solution.py:178
  7.6 15.3 %all-to-all-start = ((bf16[4,2,128,256]{3,2,1,0:T(8,128)(2,1)}), bf16[4,2,128,256]{3,2,1,0:T(8,128)(2,1)S(1)}, u32[]{:S(2)}, u32[]{:S(2)}) async-start(bf16[4,2,128,256]{3,2,1,0:T(8,128)(2,1)} %broadcast_in_dim.10), calls=%async_computation | async-start | bytes 1048576 | tf_op jit(solution)/shard_map/all_to_all | solution.py:207
  12.3 30.1 %collective-permute-start = (bf16[1536,256]{1,0:T(8,128)(2,1)}, bf16[1536,256]{1,0:T(8,128)(2,1)S(1)}, u32[]{:S(2)}, u32[]{:S(2)}) collective-permute-start(bf16[1536,256]{1,0:T(8,128)(2,1)} %get-tuple-element.8.own_ref), channel_id=1, source_target_pairs={{0,1},{1,0},{2,3},{3,2},{4,5},{5,4},{6,7},{7,6},{8,9},{9,8},{10,11... | collective-permute-start | bytes 2359304 | tf_op jit(solution)/shard_map/ppermute | solution.py:178
  14.7 27.7 %collective-permute-start.1 = (bf16[1024,256]{1,0:T(8,128)(2,1)}, bf16[1024,256]{1,0:T(8,128)(2,1)}, u32[]{:S(2)}, u32[]{:S(2)}) collective-permute-start(bf16[1024,256]{1,0:T(8,128)(2,1)} %source_ref.1), channel_id=1, source_target_pairs={{1,2},{2,1},{3,4},{4,3},{5,6},{6,5},{7,8},{8,7},{9,10},{10,9},{11,... | collective-permute-start | bytes 1572872 | tf_op jit(solution)/shard_map/ppermute | solution.py:178
  17.6 15.4 %collective-permute-start.3 = (bf16[512,256]{1,0:T(8,128)(2,1)}, bf16[512,256]{1,0:T(8,128)(2,1)}, u32[]{:S(2)}, u32[]{:S(2)}) collective-permute-start(bf16[512,256]{1,0:T(8,128)(2,1)} %get-tuple-element.9), channel_id=1, source_target_pairs={{1,2},{2,1},{3,4},{4,3},{5,6},{6,5},{7,8},{8,7},{9,10},{10,9},{11,... | collective-permute-start | bytes 786440 | tf_op jit(solution)/shard_map/ppermute | solution.py:178
  23.0 29.9 %collective-permute-start.6 = (bf16[8,128,256]{2,1,0:T(8,128)(2,1)S(1)}, bf16[8,128,256]{2,1,0:T(8,128)(2,1)S(1)}, u32[]{:S(2)}, u32[]{:S(2)}) collective-permute-start(bf16[8,128,256]{2,1,0:T(8,128)(2,1)S(1)} %bitcast.2), channel_id=1, source_target_pairs={{0,1},{1,0},{2,3},{3,2},{4,5},{5,4},{6,7},{7,6},{8,9},{9,8},{10,11... | collective-permute-start | bytes 1572872 | tf_op jit(solution)/shard_map/ppermute | solution.py:178
  24.9 27.9 %collective-permute-start.2 = (bf16[512,256]{1,0:T(8,128)(2,1)}, bf16[512,256]{1,0:T(8,128)(2,1)S(1)}, u32[]{:S(2)}, u32[]{:S(2)}) collective-permute-start(bf16[512,256]{1,0:T(8,128)(2,1)} %get-tuple-element.9), channel_id=1, source_target_pairs={{0,2},{2,4},{3,1},{4,6},{5,3},{6,8},{7,5},{8,10},{9,7},{10,12},{11... | collective-permute-start | bytes 786440 | tf_op jit(solution)/shard_map/ppermute | solution.py:178
  32.9 19.9 %collective-permute-start.4 = (bf16[512,256]{1,0:T(8,128)(2,1)}, bf16[512,256]{1,0:T(8,128)(2,1)S(1)}, u32[]{:S(2)}, u32[]{:S(2)}) collective-permute-start(bf16[512,256]{1,0:T(8,128)(2,1)} %collective-permute-done.3.across_ref), channel_id=1, source_target_pairs={{0,1},{1,0},{2,3},{3,2},{4,5},{5,4},{6,7},{7,6},{8,9},{9,8},{10,11... | collective-permute-start | bytes 786440 | tf_op jit(solution)/shard_map/ppermute | solution.py:178
  42.3 1.1 %copy-start.1 = (bf16[1536,256]{1,0:T(8,128)(2,1)S(1)}, bf16[1536,256]{1,0:T(8,128)(2,1)}, u32[]{:S(2)}) copy-start(bf16[1536,256]{1,0:T(8,128)(2,1)} %get-tuple-element.8.own_ref) | copy-start | bytes 2359300
  43.5 0.7 %copy-start.5 = (s32[4,16]{1,0:T(4,128)S(1)}, s32[4,16]{1,0:T(4,128)}, u32[]{:S(2)}) copy-start(s32[4,16]{1,0:T(4,128)} %near_list_ref.1) | copy-start | bytes 772
  44.1 0.7 %copy-start.8 = (s32[4]{0:T(128)S(1)}, s32[4]{0:T(128)}, u32[]{:S(2)}) copy-start(s32[4]{0:T(128)} %count_ref.1) | copy-start | bytes 52
  44.8 8.1 %copy-start.3 = (bf16[4,256,128]{2,1,0:T(8,128)(2,1)S(1)}, bf16[4,256,128]{2,1,0:T(8,128)(2,1)}, u32[]{:S(2)}) copy-start(bf16[4,256,128]{2,1,0:T(8,128)(2,1)} %row_ref.1) | copy-start | bytes 786436
  44.8 8.1 %copy-start.4 = (bf16[1,8,128,128]{3,2,1,0:T(8,128)(2,1)S(1)}, bf16[1,8,128,128]{3,2,1,0:T(8,128)(2,1)}, u32[]{:S(2)}) copy-start(bf16[1,8,128,128]{3,2,1,0:T(8,128)(2,1)} %coarse_coupling_ref.1) | copy-start | bytes 786436

commit v3 on v2

--- a/solution.py
+++ b/solution.py
@@ -7,6 +7,7 @@
 
 GROUP = 16
 CHUNK = 4
+AHEAD = 4
 
 
 def dot(a, b):
@@ -33,14 +34,52 @@
     parent_ref[...] = total.astype(jnp.bfloat16)
 
 
+def join(pieces, starts):
+    sizes = [piece.shape[0] - start for piece, start in zip(pieces, starts)]
+
+    def join_kernel(*refs):
+        at = 0
+        for ref, start, size in zip(refs, starts, sizes):
+            refs[-1][pl.ds(at, size), :] = ref[pl.ds(start, size), :]
+            at += size
+
+    return pl.pallas_call(
+        join_kernel,
+        out_shape=jax.ShapeDtypeStruct((sum(sizes), pieces[0].shape[1]), pieces[0].dtype),
+        in_specs=[VMEM] * len(pieces),
+        out_specs=VMEM,
+        name="join",
+    )(*pieces)
+
+
 def near_kernel(
-    list_ref, count_ref, blocks_hbm, own_ref, share_ref, across_ref, near_ref,
+    list_ref, count_ref, blocks_hbm, own_ref, share_ref, across_ref,
+    near_ref,
     blocks, panels, block_sems, panel_sems,
 ):
     leaves, slots, rows, _ = blocks.shape
     chunks = slots // CHUNK
     size = leaves * rows
     place = list_ref[0, 0] // leaves
+
+    def live(step):
+        return step % chunks * CHUNK < count_ref[step // chunks]
+
+    def block_copy(step):
+        leaf, chunk = step // chunks, step % chunks
+        where = pl.ds(chunk * CHUNK, CHUNK)
+        return pltpu.make_async_copy(
+            blocks_hbm.at[leaf, where], blocks.at[leaf, where], block_sems.at[leaf, chunk]
+        )
+
+    def start(step):
+        if step < leaves * chunks:
+            @pl.when(live(step))
+            def _():
+                block_copy(step).start()
+
+    for step in range(AHEAD):
+        start(step)
     pairs = [
         pltpu.make_async_copy(
             ref.at[pl.ds(0, size)], panels.at[pl.ds(which * size, size)], panel_sems.at[which]
@@ -49,18 +88,6 @@
     ]
     for copy in pairs:
         copy.start()
-
-    def block_copy(leaf, chunk):
-        where = pl.ds(chunk * CHUNK, CHUNK)
-        return pltpu.make_async_copy(
-            blocks_hbm.at[leaf, where], blocks.at[leaf, where], block_sems.at[leaf, chunk]
-        )
-
-    for leaf in range(leaves):
-        for chunk in range(chunks):
-            @pl.when(chunk * CHUNK < count_ref[leaf])
-            def _():
-                block_copy(leaf, chunk).start()
 
     panels[pl.ds(3 * size, rows), :] = jnp.zeros((rows, panels.shape[1]), panels.dtype)
     for copy in pairs:
@@ -74,22 +101,24 @@
         index = jnp.where(slot < count_ref[leaf], index, 3 * leaves)
         return panels[pl.ds(pl.multiple_of(index * rows, rows), rows), :]
 
-    for leaf in range(leaves):
-        for chunk in range(chunks):
-            @pl.when(chunk * CHUNK < count_ref[leaf])
-            def _():
-                block_copy(leaf, chunk).wait()
-                total = None if chunk == 0 else near_ref[leaf]
-                for slot in range(chunk * CHUNK, (chunk + 1) * CHUNK):
-                    term = dot(blocks[leaf, slot], panel_of(leaf, slot))
-                    total = term if total is None else total + term
-                near_ref[leaf] = total
+    for step in range(leaves * chunks):
+        leaf, chunk = step // chunks, step % chunks
+        start(step + AHEAD)
+
+        @pl.when(live(step))
+        def _():
+            block_copy(step).wait()
+            total = None if chunk == 0 else near_ref[leaf]
+            for slot in range(chunk * CHUNK, (chunk + 1) * CHUNK):
+                term = dot(blocks[leaf, slot], panel_of(leaf, slot))
+                total = term if total is None else total + term
+            near_ref[leaf] = total
 
 
 def down_kernel(
     near_list_ref, far_list_ref, coarse_list_ref,
     near_ref, row_ref, transfer_ref, coupling_ref, coarse_coupling_ref,
-    skip_ref, across_ref, share_ref, passed_ref, mine_ref, theirs_ref,
+    skip_ref, across_ref, share_ref, mine_ref, theirs_ref,
     out_ref,
     coefs, sems,
 ):
@@ -102,7 +131,7 @@
             ref.at[pl.ds(start, size)], coefs.at[pl.ds(n * size, size)], sems.at[n]
         )
         for n, (ref, start) in enumerate(
-            ((skip_ref, 0), (across_ref, 0), (share_ref, leaves * rows), (passed_ref, 0))
+            ((skip_ref, 0), (across_ref, leaves * rows), (share_ref, leaves * rows), (theirs_ref, GROUP // 2 * rank))
         )
     ]
     for copy in copies:
@@ -111,10 +140,9 @@
     local = place % GROUP
     total = None
     for slot in range(coarse_list_ref.shape[1]):
-        cluster = coarse_list_ref[0, slot] % GROUP
-        flip = cluster ^ local
-        index = (cluster >> 2) * 2 + ((flip >> 1) & 1)
-        panel = jnp.where((flip & 1) == 0, mine_ref[index], theirs_ref[index])
+        flip = coarse_list_ref[0, slot] % GROUP ^ local
+        where = pl.ds(pl.multiple_of((flip >> 1) * rank, rank), rank)
+        panel = jnp.where((flip & 1) == 0, mine_ref[where, :], theirs_ref[where, :])
         term = dot(coarse_coupling_ref[0, slot], panel)
         total = term if total is None else total + term
     high = total.astype(jnp.bfloat16)
@@ -177,8 +205,6 @@
     def send(value, pairs):
         return lax.ppermute(value, "row", pairs)
 
-    across_source = send(source, across)
-
     share, coef, parent = pl.pallas_call(
         up_kernel,
         out_shape=(
@@ -196,28 +222,18 @@
         name="up",
     )(source, col_basis, transfer)
 
-    parent = parent[None]
-    pair = jnp.concatenate([parent, send(parent, flip(2))], axis=0)
-    layers = [
-        [base + step * 4 for step in range(GROUP // 4)]
-        for start in range(0, count, GROUP)
-        for base in range(start, start + 4)
-    ]
-    copies = jnp.broadcast_to(pair[None], (GROUP // 4,) + pair.shape)
-    mine = lax.all_to_all(
-        copies, "row", split_axis=0, concat_axis=0, axis_index_groups=layers
-    ).reshape(GROUP // 2, rank, width)
-    theirs = send(mine, flip(1))
-
+    share_across = send(share, across)
     share_other = send(share, flip(1))
-    coef_across = send(coef, across)
-    coef_passed = send(coef_across, flip(1))
     coef_skip = send(coef, skip)
+    pair = join([parent, send(parent, flip(2))], [0, 0])
+    layers = [send(pair, flip(bit)) for bit in (4, 8, 12)]
+    passed = join([pair, *layers, share_across], [0] * 4 + [leaves * rows])
+    passed_other = send(passed, flip(1))
 
     near = pl.pallas_call(
         near_kernel,
         out_shape=jax.ShapeDtypeStruct((leaves, rows, width), jnp.float32),
-        in_specs=[SMEM, SMEM, HBM, ANY, ANY, ANY],
+        in_specs=[SMEM, SMEM, HBM] + [ANY] * 3,
         out_specs=VMEM,
         scratch_shapes=[
             pltpu.VMEM((leaves, slots, rows, rows), jnp.bfloat16),
@@ -230,14 +246,14 @@
             bytes_accessed=2 * leaves * slots * rows * rows,
             transcendentals=0,
         ),
-        compiler_params=pltpu.CompilerParams(vmem_limit_bytes=50 * 2**20),
+        compiler_params=pltpu.CompilerParams(vmem_limit_bytes=48 * 2**20),
         name="near",
-    )(near_list, near_count, near_blocks, share, share_other, across_source)
+    )(near_list, near_count, near_blocks, share, share_other, share_across)
 
     return pl.pallas_call(
         down_kernel,
         out_shape=jax.ShapeDtypeStruct(source.shape, jnp.bfloat16),
-        in_specs=[SMEM] * 3 + [VMEM] * 5 + [ANY] * 4 + [VMEM] * 2,
+        in_specs=[SMEM] * 3 + [VMEM] * 5 + [ANY] * 3 + [VMEM] * 2,
         out_specs=VMEM,
         scratch_shapes=[
             pltpu.VMEM((4 * leaves * rank, width), jnp.bfloat16),
@@ -252,7 +268,7 @@
         name="down",
     )(
         near_list, far_list, coarse_list, near, row_basis, transfer, far_coupling,
-        coarse_coupling, coef_skip, coef_across, share_other, coef_passed, mine, theirs,
+        coarse_coupling, coef_skip, share_across, share_other, passed, passed_other,
     )
 
 

time: 57.5 us -> 64.9 us (1.13)
  the two profiles are of different devices: /device:TPU:23 before, /device:TPU:25 now
where the time goes in v3:
time: 64.9 us; the launch traced here: 64.7 us
  waiting for transfers between devices  21.3 us (33%)
  starting transfers between devices  20.2 us (31%)
  Pallas kernels  17.3 us (27%)
  local copies, waits for them, and re-layouts  5.84 us (9%)
    ppermute x8, waiting for transfers between devices, send(): return lax.ppermute(value, 'row', pairs)  21.3 us
    ppermute x8, starting transfers between devices, send(): return lax.ppermute(value, 'row', pairs)  20.2 us
    pallas_call x1, Pallas kernels, body(): pl.pallas_call(near_kernel, out_shape=jax.ShapeDtypeStruct((leaves, rows,...  7.13 us
    unnamed x32, local copies, waits for them, and re-layouts  5.84 us
    pallas_call x2, Pallas kernels, join(): pl.pallas_call(join_kernel, out_shape=jax.ShapeDtypeStruct((sum(sizes), p...  3.89 us
    pallas_call x1, Pallas kernels, body(): pl.pallas_call(down_kernel, out_shape=jax.ShapeDtypeStruct(source.shape,...  3.75 us
    pallas_call x1, Pallas kernels, body(): pl.pallas_call(up_kernel, out_shape=(jax.ShapeDtypeStruct((leaves * (rows...  2.49 us
  transfers between devices with their start and end apart: 8, of which 3 were waited for; matrix products, arithmetic and copies ran while one was open for 0% of the time, Pallas kernels for 17%

profile of v3, /device:TPU:25, one launch (start us, length us, event | category | flops | bytes accessed | tf_op | source)
XLA Modules:
  0.0 64.7 jit_solution(5865745123357318308)
XLA Ops:
  0.0 0.0 copy-start.5
  0.0 0.0 copy-start.9
  0.0 0.0 copy-start.11
  0.0 0.0 copy-start.6
  0.0 0.0 copy-start.7
  0.0 2.5 %up.1 = (bf16[1536,256]{1,0:T(8,128)(2,1)}, bf16[512,256]{1,0:T(8,128)(2,1)}, bf16[128,256]{1,0:T(8,128)(2,1)}) custom-call(bf16[1024,256]{1,0:T(8,128)(2,1)} %source_ref.1, bf16[4,256,128]{2,1,0:T(8,128)(2,1)} %col_ref.1, bf16[4,128,128]{2,1,0:T(8,128)(2,1)} %transfer_ref.3), custom_call_target="tpu_custom_call" | custom-call | flops 100663296 | bytes 786432 | tf_op jit(solution)/shard_map/up/pallas_call | solution.py:208
  2.5 3.7 %collective-permute-start.1 = (bf16[1536,256]{1,0:T(8,128)(2,1)}, bf16[1536,256]{1,0:T(8,128)(2,1)S(1)}, u32[]{:S(2)}, u32[]{:S(2)}) collective-permute-start(bf16[1536,256]{1,0:T(8,128)(2,1)} %get-tuple-element.8.own_ref), channel_id=1, source_target_pairs={{1,2},{2,1},{3,4},{4,3},{5,6},{6,5},{7,8},{8,7},{9,10},{10,9},{11,... | collective-permute-start | bytes 2359304 | tf_op jit(solution)/shard_map/ppermute | solution.py:206
  6.2 0.1 collective-permute-start
  6.3 0.1 collective-permute-start.3
  6.4 12.0 %collective-permute-done.3.refs_1_ = bf16[128,256]{1,0:T(8,128)(2,1)S(1)} collective-permute-done((bf16[128,256]{1,0:T(8,128)(2,1)}, bf16[128,256]{1,0:T(8,128)(2,1)S(1)}, u32[]{:S(2)}, u32[]{:S(2)}) %collective-permute-start.3) | collective-permute-done | bytes 65568 | tf_op jit(solution)/shard_map/ppermute | solution.py:206
  18.5 0.0 copy-start.15
  18.5 0.6 copy-done.15
  19.1 1.5 %join.2.refs_0_ = bf16[256,256]{1,0:T(8,128)(2,1)} custom-call(bf16[128,256]{1,0:T(8,128)(2,1)} %get-tuple-element.10.refs_0_, bf16[128,256]{1,0:T(8,128)(2,1)} %copy-done.15), custom_call_target="tpu_custom_call" | custom-call | tf_op jit(solution)/shard_map/join/pallas_call | solution.py:46
  20.6 7.0 %collective-permute-start.4 = (bf16[256,256]{1,0:T(8,128)(2,1)}, bf16[256,256]{1,0:T(8,128)(2,1)S(1)}, u32[]{:S(2)}, u32[]{:S(2)}) collective-permute-start(bf16[256,256]{1,0:T(8,128)(2,1)} %join.2.refs_0_), channel_id=1, source_target_pairs={{0,4},{1,5},{2,6},{3,7},{4,0},{5,1},{6,2},{7,3},{8,12},{9,13},{10,... | collective-permute-start | bytes 393224 | tf_op jit(solution)/shard_map/ppermute | solution.py:206
  27.6 0.1 collective-permute-start.5
  27.7 2.0 %collective-permute-start.6 = (bf16[256,256]{1,0:T(8,128)(2,1)}, bf16[256,256]{1,0:T(8,128)(2,1)S(1)}, u32[]{:S(2)}, u32[]{:S(2)}) collective-permute-start(bf16[256,256]{1,0:T(8,128)(2,1)} %join.2.refs_0_), channel_id=1, source_target_pairs={{0,12},{1,13},{2,14},{3,15},{4,8},{5,9},{6,10},{7,11},{8,4},{9,5},... | collective-permute-start | bytes 393224 | tf_op jit(solution)/shard_map/ppermute | solution.py:206
  29.7 0.5 collective-permute-done.4.refs_1_
  30.2 0.0 copy-start.12
  30.2 8.7 %collective-permute-done.5.refs_2_ = bf16[256,256]{1,0:T(8,128)(2,1)S(1)} collective-permute-done((bf16[256,256]{1,0:T(8,128)(2,1)}, bf16[256,256]{1,0:T(8,128)(2,1)S(1)}, u32[]{:S(2)}, u32[]{:S(2)}) %collective-permute-start.5) | collective-permute-done | bytes 131104 | tf_op jit(solution)/shard_map/ppermute | solution.py:206
  38.9 0.0 copy-start.13
  38.9 0.0 collective-permute-done.6.refs_3_
  38.9 0.0 copy-start.14
  38.9 0.0 collective-permute-done.1.across_ref.refs_4_
  38.9 0.0 copy-done.12
  38.9 0.6 copy-done.13
  39.6 0.0 copy-done.14
  39.6 0.0 copy-start
  39.6 0.9 %copy-done = bf16[1536,256]{1,0:T(8,128)(2,1)} copy-done((bf16[1536,256]{1,0:T(8,128)(2,1)}, bf16[1536,256]{1,0:T(8,128)(2,1)S(1)}, u32[]{:S(2)}) %copy-start) | copy-done | bytes 786456
  40.5 2.4 %join.3.mine_ref = bf16[1536,256]{1,0:T(8,128)(2,1)} custom-call(bf16[256,256]{1,0:T(8,128)(2,1)} %join.2.refs_0_, bf16[256,256]{1,0:T(8,128)(2,1)} %copy-done.12, bf16[256,256]{1,0:T(8,128)(2,1)} %copy-done.13, bf16[256,256]{1,0:T(8,128)(2,1)} %copy-done.14, bf16[1536,256]{1,0:T(8,128)(2,1)} %copy-done), custom_call_target="tpu_custom_call" | custom-call | tf_op jit(solution)/shard_map/join/pallas_call | solution.py:46
  42.9 2.3 %collective-permute-start.7 = (bf16[1536,256]{1,0:T(8,128)(2,1)}, bf16[1536,256]{1,0:T(8,128)(2,1)S(1)}, u32[]{:S(2)}, u32[]{:S(2)}) collective-permute-start(bf16[1536,256]{1,0:T(8,128)(2,1)} %join.3.mine_ref), channel_id=1, source_target_pairs={{0,1},{1,0},{2,3},{3,2},{4,5},{5,4},{6,7},{7,6},{8,9},{9,8},{10,11... | collective-permute-start | bytes 2359304 | tf_op jit(solution)/shard_map/ppermute | solution.py:206
  45.1 4.9 %collective-permute-start.2 = (bf16[512,256]{1,0:T(8,128)(2,1)}, bf16[512,256]{1,0:T(8,128)(2,1)S(1)}, u32[]{:S(2)}, u32[]{:S(2)}) collective-permute-start(bf16[512,256]{1,0:T(8,128)(2,1)} %get-tuple-element.9), channel_id=1, source_target_pairs={{0,2},{2,4},{3,1},{4,6},{5,3},{6,8},{7,5},{8,10},{9,7},{10,12},{11... | collective-permute-start | bytes 786440 | tf_op jit(solution)/shard_map/ppermute | solution.py:206
  50.1 0.0 collective-permute-done.share_ref
  50.1 0.0 copy-start.1
  50.1 1.1 %copy-done.1 = bf16[1536,256]{1,0:T(8,128)(2,1)S(1)} copy-done((bf16[1536,256]{1,0:T(8,128)(2,1)S(1)}, bf16[1536,256]{1,0:T(8,128)(2,1)}, u32[]{:S(2)}) %copy-start.1) | copy-done | bytes 786456
  51.2 0.0 copy-start.4
  51.2 1.1 %copy-done.4 = bf16[1536,256]{1,0:T(8,128)(2,1)S(1)} copy-done((bf16[1536,256]{1,0:T(8,128)(2,1)S(1)}, bf16[1536,256]{1,0:T(8,128)(2,1)}, u32[]{:S(2)}) %copy-start.4) | copy-done | bytes 786456
  52.4 0.0 copy-start.8
  52.4 0.7 %copy-done.8 = s32[4,16]{1,0:T(4,128)S(1)} copy-done((s32[4,16]{1,0:T(4,128)S(1)}, s32[4,16]{1,0:T(4,128)}, u32[]{:S(2)}) %copy-start.8) | copy-done | bytes 280
  53.1 0.0 copy-start.10
  53.1 0.7 %copy-done.10 = s32[4]{0:T(128)S(1)} copy-done((s32[4]{0:T(128)S(1)}, s32[4]{0:T(128)}, u32[]{:S(2)}) %copy-start.10) | copy-done | bytes 40
  53.7 0.0 copy-start.2
  53.7 0.0 copy-start.3
  53.7 7.1 %near.1.near_ref = f32[4,256,256]{2,1,0:T(8,128)S(1)} custom-call(s32[4,16]{1,0:T(4,128)S(1)} %copy-done.8, s32[4]{0:T(128)S(1)} %copy-done.10, bf16[4,16,256,256]{3,2,1,0:T(8,128)(2,1)} %blocks_hbm.1, bf16[1536,256]{1,0:T(8,128)(2,1)S(1)} %copy-done.4, bf16[1536,256]{1,0:T(8,128)(2,1)S(1)} %collective-permute-done.share_ref, bf16[1536,256]{1,0:T(8,128)(2,1)S(1)} %copy-done.1), custom_call_target="tpu_custom_call" | custom-call | flops 2147483648 | bytes 8388608 | tf_op jit(solution)/shard_map/near/pallas_call | solution.py:233
  60.8 0.0 collective-permute-done.2.skip_ref
  60.9 0.0 collective-permute-done.7.theirs_ref
  60.9 0.0 copy-done.5
  60.9 0.0 copy-done.9
  60.9 0.0 copy-done.11
  60.9 0.0 copy-done.6
  60.9 0.0 copy-done.7
  60.9 0.0 copy-done.2
  60.9 0.0 copy-done.3
  60.9 3.8 %down.1 = bf16[1024,256]{1,0:T(8,128)(2,1)} custom-call(s32[4,16]{1,0:T(4,128)S(1)} %copy-done.8, s32[4,16]{1,0:T(4,128)S(1)} %copy-done.9, s32[1,8]{1,0:T(1,128)S(1)} %copy-done.11, f32[4,256,256]{2,1,0:T(8,128)S(1)} %near.1.near_ref, bf16[4,256,128]{2,1,0:T(8,128)(2,1)S(1)} %copy-done.6, bf16[4,128,128]{2,1,0:T(8,128)(2,1)S(1)} %copy-done.5, ...), custom_call_target="tpu_custom_call" | custom-call | flops 671088640 | bytes 2097152 | tf_op jit(solution)/shard_map/down/pallas_call | solution.py:253
Async XLA Ops:
  0.0 60.9 %copy-start.5 = (bf16[4,128,128]{2,1,0:T(8,128)(2,1)S(1)}, bf16[4,128,128]{2,1,0:T(8,128)(2,1)}, u32[]{:S(2)}) copy-start(bf16[4,128,128]{2,1,0:T(8,128)(2,1)} %transfer_ref.3) | copy-start | bytes 393220
  0.0 60.9 %copy-start.9 = (s32[4,16]{1,0:T(4,128)S(1)}, s32[4,16]{1,0:T(4,128)}, u32[]{:S(2)}) copy-start(s32[4,16]{1,0:T(4,128)} %far_list_ref.1) | copy-start | bytes 772
  0.0 60.9 %copy-start.11 = (s32[1,8]{1,0:T(1,128)S(1)}, s32[1,8]{1,0:T(1,128)}, u32[]{:S(2)}) copy-start(s32[1,8]{1,0:T(1,128)} %coarse_list_ref.1) | copy-start | bytes 100
  0.0 60.9 %copy-start.6 = (bf16[4,256,128]{2,1,0:T(8,128)(2,1)S(1)}, bf16[4,256,128]{2,1,0:T(8,128)(2,1)}, u32[]{:S(2)}) copy-start(bf16[4,256,128]{2,1,0:T(8,128)(2,1)} %row_ref.1) | copy-start | bytes 786436
  0.0 60.9 %copy-start.7 = (bf16[1,8,128,128]{3,2,1,0:T(8,128)(2,1)S(1)}, bf16[1,8,128,128]{3,2,1,0:T(8,128)(2,1)}, u32[]{:S(2)}) copy-start(bf16[1,8,128,128]{3,2,1,0:T(8,128)(2,1)} %coarse_coupling_ref.1) | copy-start | bytes 786436
  2.5 36.4 %collective-permute-start.1 = (bf16[1536,256]{1,0:T(8,128)(2,1)}, bf16[1536,256]{1,0:T(8,128)(2,1)S(1)}, u32[]{:S(2)}, u32[]{:S(2)}) collective-permute-start(bf16[1536,256]{1,0:T(8,128)(2,1)} %get-tuple-element.8.own_ref), channel_id=1, source_target_pairs={{1,2},{2,1},{3,4},{4,3},{5,6},{6,5},{7,8},{8,7},{9,10},{10,9},{11,... | collective-permute-start | bytes 2359304 | tf_op jit(solution)/shard_map/ppermute | solution.py:206
  6.2 43.9 %collective-permute-start = (bf16[1536,256]{1,0:T(8,128)(2,1)}, bf16[1536,256]{1,0:T(8,128)(2,1)S(1)}, u32[]{:S(2)}, u32[]{:S(2)}) collective-permute-start(bf16[1536,256]{1,0:T(8,128)(2,1)} %get-tuple-element.8.own_ref), channel_id=1, source_target_pairs={{0,1},{1,0},{2,3},{3,2},{4,5},{5,4},{6,7},{7,6},{8,9},{9,8},{10,11... | collective-permute-start | bytes 2359304 | tf_op jit(solution)/shard_map/ppermute | solution.py:206
  6.3 12.2 %collective-permute-start.3 = (bf16[128,256]{1,0:T(8,128)(2,1)}, bf16[128,256]{1,0:T(8,128)(2,1)S(1)}, u32[]{:S(2)}, u32[]{:S(2)}) collective-permute-start(bf16[128,256]{1,0:T(8,128)(2,1)} %get-tuple-element.10.refs_0_), channel_id=1, source_target_pairs={{0,2},{1,3},{2,0},{3,1},{4,6},{5,7},{6,4},{7,5},{8,10},{9,11},{10,... | collective-permute-start | bytes 196616 | tf_op jit(solution)/shard_map/ppermute | solution.py:206
  18.5 0.6 copy-start.15
  20.6 9.6 %collective-permute-start.4 = (bf16[256,256]{1,0:T(8,128)(2,1)}, bf16[256,256]{1,0:T(8,128)(2,1)S(1)}, u32[]{:S(2)}, u32[]{:S(2)}) collective-permute-start(bf16[256,256]{1,0:T(8,128)(2,1)} %join.2.refs_0_), channel_id=1, source_target_pairs={{0,4},{1,5},{2,6},{3,7},{4,0},{5,1},{6,2},{7,3},{8,12},{9,13},{10,... | collective-permute-start | bytes 393224 | tf_op jit(solution)/shard_map/ppermute | solution.py:206
  27.6 11.3 %collective-permute-start.5 = (bf16[256,256]{1,0:T(8,128)(2,1)}, bf16[256,256]{1,0:T(8,128)(2,1)S(1)}, u32[]{:S(2)}, u32[]{:S(2)}) collective-permute-start(bf16[256,256]{1,0:T(8,128)(2,1)} %join.2.refs_0_), channel_id=1, source_target_pairs={{0,8},{1,9},{2,10},{3,11},{4,12},{5,13},{6,14},{7,15},{8,0},{9,1},... | collective-permute-start | bytes 393224 | tf_op jit(solution)/shard_map/ppermute | solution.py:206
  27.7 11.3 %collective-permute-start.6 = (bf16[256,256]{1,0:T(8,128)(2,1)}, bf16[256,256]{1,0:T(8,128)(2,1)S(1)}, u32[]{:S(2)}, u32[]{:S(2)}) collective-permute-start(bf16[256,256]{1,0:T(8,128)(2,1)} %join.2.refs_0_), channel_id=1, source_target_pairs={{0,12},{1,13},{2,14},{3,15},{4,8},{5,9},{6,10},{7,11},{8,4},{9,5},... | collective-permute-start | bytes 393224 | tf_op jit(solution)/shard_map/ppermute | solution.py:206
  30.2 8.8 %copy-start.12 = (bf16[256,256]{1,0:T(8,128)(2,1)}, bf16[256,256]{1,0:T(8,128)(2,1)S(1)}, u32[]{:S(2)}) copy-start(bf16[256,256]{1,0:T(8,128)(2,1)S(1)} %collective-permute-done.4.refs_1_) | copy-start | bytes 393220
  38.9 0.7 %copy-start.13 = (bf16[256,256]{1,0:T(8,128)(2,1)}, bf16[256,256]{1,0:T(8,128)(2,1)S(1)}, u32[]{:S(2)}) copy-start(bf16[256,256]{1,0:T(8,128)(2,1)S(1)} %collective-permute-done.5.refs_2_) | copy-start | bytes 393220
  38.9 0.7 %copy-start.14 = (bf16[256,256]{1,0:T(8,128)(2,1)}, bf16[256,256]{1,0:T(8,128)(2,1)S(1)}, u32[]{:S(2)}) copy-start(bf16[256,256]{1,0:T(8,128)(2,1)S(1)} %collective-permute-done.6.refs_3_) | copy-start | bytes 393220
  39.6 0.9 %copy-start = (bf16[1536,256]{1,0:T(8,128)(2,1)}, bf16[1536,256]{1,0:T(8,128)(2,1)S(1)}, u32[]{:S(2)}) copy-start(bf16[1536,256]{1,0:T(8,128)(2,1)S(1)} %collective-permute-done.1.across_ref.refs_4_) | copy-start | bytes 2359300
  42.9 18.0 %collective-permute-start.7 = (bf16[1536,256]{1,0:T(8,128)(2,1)}, bf16[1536,256]{1,0:T(8,128)(2,1)S(1)}, u32[]{:S(2)}, u32[]{:S(2)}) collective-permute-start(bf16[1536,256]{1,0:T(8,128)(2,1)} %join.3.mine_ref), channel_id=1, source_target_pairs={{0,1},{1,0},{2,3},{3,2},{4,5},{5,4},{6,7},{7,6},{8,9},{9,8},{10,11... | collective-permute-start | bytes 2359304 | tf_op jit(solution)/shard_map/ppermute | solution.py:206
  45.1 15.7 %collective-permute-start.2 = (bf16[512,256]{1,0:T(8,128)(2,1)}, bf16[512,256]{1,0:T(8,128)(2,1)S(1)}, u32[]{:S(2)}, u32[]{:S(2)}) collective-permute-start(bf16[512,256]{1,0:T(8,128)(2,1)} %get-tuple-element.9), channel_id=1, source_target_pairs={{0,2},{2,4},{3,1},{4,6},{5,3},{6,8},{7,5},{8,10},{9,7},{10,12},{11... | collective-permute-start | bytes 786440 | tf_op jit(solution)/shard_map/ppermute | solution.py:206
  50.1 1.1 %copy-start.1 = (bf16[1536,256]{1,0:T(8,128)(2,1)S(1)}, bf16[1536,256]{1,0:T(8,128)(2,1)}, u32[]{:S(2)}) copy-start(bf16[1536,256]{1,0:T(8,128)(2,1)} %copy-done) | copy-start | bytes 2359300
  51.2 1.1 %copy-start.4 = (bf16[1536,256]{1,0:T(8,128)(2,1)S(1)}, bf16[1536,256]{1,0:T(8,128)(2,1)}, u32[]{:S(2)}) copy-start(bf16[1536,256]{1,0:T(8,128)(2,1)} %get-tuple-element.8.own_ref) | copy-start | bytes 2359300
  52.4 0.7 %copy-start.8 = (s32[4,16]{1,0:T(4,128)S(1)}, s32[4,16]{1,0:T(4,128)}, u32[]{:S(2)}) copy-start(s32[4,16]{1,0:T(4,128)} %near_list_ref.1) | copy-start | bytes 772
  53.1 0.7 %copy-start.10 = (s32[4]{0:T(128)S(1)}, s32[4]{0:T(128)}, u32[]{:S(2)}) copy-start(s32[4]{0:T(128)} %count_ref.1) | copy-start | bytes 52
  53.7 7.2 %copy-start.2 = (bf16[1536,256]{1,0:T(8,128)(2,1)S(1)}, bf16[1536,256]{1,0:T(8,128)(2,1)}, u32[]{:S(2)}) copy-start(bf16[1536,256]{1,0:T(8,128)(2,1)} %join.3.mine_ref) | copy-start | bytes 2359300
  53.7 7.2 %copy-start.3 = (bf16[4,16,128,128]{3,2,1,0:T(8,128)(2,1)S(1)}, bf16[4,16,128,128]{3,2,1,0:T(8,128)(2,1)}, u32[]{:S(2)}) copy-start(bf16[4,16,128,128]{3,2,1,0:T(8,128)(2,1)} %coupling_ref.1) | copy-start | bytes 6291460

commit v4 on v0

v4 whole, which is shorter than its diff:
```python
import jax
import jax.numpy as jnp
from jax import lax
from jax.experimental import pallas as pl
from jax.experimental.pallas import tpu as pltpu
from jax.sharding import PartitionSpec as P

GROUP = 16
MIB = 2**20

VMEM = pl.BlockSpec(memory_space=pltpu.VMEM)
SMEM = pl.BlockSpec(memory_space=pltpu.SMEM)
ANY = pl.BlockSpec(memory_space=pl.ANY)


def dot(a, b):
    return jnp.dot(a, b, preferred_element_type=jnp.float32)


def dot_t(a, b):
    return lax.dot_general(
        a, b, (((0,), (0,)), ((), ())), preferred_element_type=jnp.float32
    )


def rows_at(index, rows):
    return pl.ds(pl.multiple_of(index * rows, rows), rows)


def up_kernel(source_ref, col_ref, transfer_ref, share_ref, lift_ref):
    leaves, rows, rank = col_ref.shape
    total = None
    for leaf in range(leaves):
        panel = source_ref[pl.ds(leaf * rows, rows), :]
        share_ref[pl.ds(leaf * rows, rows), :] = panel
        coef = dot_t(col_ref[leaf], panel).astype(jnp.bfloat16)
        lift_ref[pl.ds(leaf * rank, rank), :] = coef
        share_ref[pl.ds(leaves * rows + leaf * rank, rank), :] = coef
        term = dot_t(transfer_ref[leaf], coef)
        total = term if total is None else total + term
    lift_ref[pl.ds(leaves * rank, rank), :] = total.astype(jnp.bfloat16)


def pair_kernel(own_ref, lift_ref, _, level_ref, pair_ref):
    size = level_ref.shape[0]
    rank = own_ref.shape[0] - size
    level_ref[...] = lift_ref[pl.ds(0, size), :]
    pair_ref[pl.ds(0, rank), :] = own_ref[pl.ds(size, rank), :]
    pair_ref[pl.ds(rank, rank), :] = lift_ref[pl.ds(size, rank), :]


def pass_kernel(list_ref, *refs):
    *layers, level_ref, layer_ref, out_ref = refs
    at = 0
    for ref in layers:
        out_ref[pl.ds(at, ref.shape[0]), :] = ref[...]
        at += ref.shape[0]
    place = lax.div(list_ref[0, 0], list_ref.shape[0])
    corner = place & 3
    level = (corner == 0) | (corner == 3)
    out_ref[pl.ds(at, level_ref.shape[0]), :] = jnp.where(level, level_ref[...], layer_ref[...])


def pick_slots(list_ref, count_ref, blocks_hbm, blocks, sems, order_ref, leaf, keep):
    leaves, _ = list_ref.shape

    def step(slot, found):
        column = list_ref[leaf, slot]
        kept = keep(lax.div(column, leaves))

        @pl.when(kept)
        def _():
            order_ref[leaf, found] = column
            pltpu.make_async_copy(
                blocks_hbm.at[leaf, slot], blocks.at[leaf, found], sems.at[leaf, found]
            ).start()

        return found + kept.astype(jnp.int32)

    return lax.fori_loop(0, count_ref[leaf], step, 0)


def add_slots(total_ref, blocks_hbm, blocks, sems, order_ref, leaf, found, panel_of):
    def term(n):
        pltpu.make_async_copy(blocks_hbm.at[leaf, 0], blocks.at[leaf, n], sems.at[leaf, n]).wait()
        return dot(blocks[leaf, n], panel_of(order_ref[leaf, n]))

    def pair(n, _):
        total_ref[leaf] = total_ref[leaf] + term(2 * n) + term(2 * n + 1)
        return 0

    lax.fori_loop(0, found >> 1, pair, 0)

    @pl.when((found & 1) == 1)
    def _():
        total_ref[leaf] = total_ref[leaf] + term(found - 1)


def near_kernel(
    list_ref, count_ref, blocks_hbm, own_ref, share_ref,
    near_ref,
    blocks, panels, order, block_sems, panel_sems,
):
    leaves, _, rows, _ = blocks.shape
    size = leaves * rows
    place = lax.div(list_ref[0, 0], leaves)
    pairs = [
        pltpu.make_async_copy(
            ref.at[pl.ds(0, size)], panels.at[pl.ds(which * size, size)], panel_sems.at[which]
        )
        for which, ref in enumerate((own_ref, share_ref))
    ]
    for copy in pairs:
        copy.start()
    found = [
        pick_slots(
            list_ref, count_ref, blocks_hbm, blocks, block_sems, order, leaf,
            lambda cluster: (cluster ^ place) <= 1,
        )
        for leaf in range(leaves)
    ]
    near_ref[...] = jnp.zeros(near_ref.shape, near_ref.dtype)
    for copy in pairs:
        copy.wait()

    def panel_of(column):
        other = lax.div(column, leaves) ^ place
        return panels[rows_at(other * leaves + (column & (leaves - 1)), rows), :]

    for leaf in range(leaves):
        add_slots(near_ref, blocks_hbm, blocks, block_sems, order, leaf, found[leaf], panel_of)


def down_kernel(
    far_list_ref, coarse_list_ref, near_list_ref,
    transfer_ref, coupling_ref, coarse_coupling_ref, row_ref, near_ref,
    level_ref, layer_ref, share_ref, mine_ref, theirs_ref,
    out_ref,
    coefs, sems,
):
    leaves, slots, rank, _ = coupling_ref.shape
    rows = row_ref.shape[1]
    size = leaves * rank
    place = lax.div(near_list_ref[0, 0], leaves)
    copies = [
        pltpu.make_async_copy(
            ref.at[pl.ds(ref.shape[0] - size, size)], coefs.at[pl.ds(n * size, size)], sems.at[n]
        )
        for n, ref in enumerate((level_ref, layer_ref, share_ref, theirs_ref))
    ]
    for copy in copies:
        copy.start()

    local = place & (GROUP - 1)
    total = None
    for slot in range(coarse_list_ref.shape[1]):
        flip = (coarse_list_ref[0, slot] & (GROUP - 1)) ^ local
        where = rows_at(flip >> 1, rank)
        panel = jnp.where((flip & 1) == 0, mine_ref[where, :], theirs_ref[where, :])
        term = dot(coarse_coupling_ref[0, slot], panel)
        total = term if total is None else total + term
    high = total.astype(jnp.bfloat16)
    low = (total - high.astype(jnp.float32)).astype(jnp.bfloat16)
    coarse = jnp.concatenate([high, low], axis=0)

    beyond = jnp.where((place & 2) == 0, place - 2, place + 2)
    for copy in copies:
        copy.wait()

    def panel_of(leaf, slot):
        column = far_list_ref[leaf, slot]
        cluster = lax.div(column, leaves)
        which = jnp.where(
            cluster == (place ^ 2), 0,
            jnp.where(cluster == beyond, 1, jnp.where(cluster == (place ^ 1), 2, 3)),
        )
        return coefs[rows_at(which * leaves + column - cluster * leaves, rank), :]

    for leaf in range(leaves):
        matrix = transfer_ref[leaf]
        total = dot(jnp.concatenate([matrix, matrix], axis=1), coarse)
        for slot in range(0, slots, 2):
            both = jnp.concatenate([coupling_ref[leaf, slot], coupling_ref[leaf, slot + 1]], axis=1)
            panels = jnp.concatenate([panel_of(leaf, slot), panel_of(leaf, slot + 1)], axis=0)
            total = total + dot(both, panels)
        result = near_ref[leaf] + dot(row_ref[leaf], total.astype(jnp.bfloat16))
        out_ref[pl.ds(leaf * rows, rows), :] = result.astype(jnp.bfloat16)


def across_kernel(
    list_ref, count_ref, blocks_hbm, near_ref, across_ref,
    total_ref,
    blocks, order, sems,
):
    leaves, _, rows, _ = blocks.shape
    place = lax.div(list_ref[0, 0], leaves)
    found = [
        pick_slots(
            list_ref, count_ref, blocks_hbm, blocks, sems, order, leaf,
            lambda cluster: (cluster ^ place) > 1,
        )
        for leaf in range(leaves)
    ]
    total_ref[...] = near_ref[...]

    def panel_of(column):
        return across_ref[rows_at(column & (leaves - 1), rows), :]

    for leaf in range(leaves):
        add_slots(total_ref, blocks_hbm, blocks, sems, order, leaf, found[leaf], panel_of)


def call(kernel, name, outs, specs, args, scratch=(), flops=0, moved=0, limit=4):
    many = isinstance(outs, tuple)
    return pl.pallas_call(
        kernel,
        out_shape=outs,
        in_specs=specs,
        out_specs=(VMEM,) * len(outs) if many else VMEM,
        scratch_shapes=list(scratch),
        cost_estimate=pl.CostEstimate(flops=flops, bytes_accessed=moved, transcendentals=0),
        compiler_params=pltpu.CompilerParams(vmem_limit_bytes=limit * MIB),
        name=name,
    )(*args)


def body(
    source,
    near_blocks,
    near_list,
    near_count,
    col_basis,
    row_basis,
    transfer,
    far_list,
    far_coupling,
    coarse_list,
    coarse_coupling,
):
    leaves, slots, rows, _ = near_blocks.shape
    rank = col_basis.shape[2]
    width = source.shape[1]
    count = lax.axis_size("row")
    far_slots = far_coupling.shape[1]

    def send(value, target):
        pairs = [(d, target(d)) for d in range(count) if 0 <= target(d) < count]
        return lax.ppermute(value, "row", pairs)

    def panel(blocks, dtype=jnp.bfloat16):
        return jax.ShapeDtypeStruct((blocks * rank, width), dtype)

    share, lift = call(
        up_kernel, "up",
        (jax.ShapeDtypeStruct((leaves * (rows + rank), width), jnp.bfloat16), panel(leaves + 1)),
        [VMEM] * 3, (source, col_basis, transfer),
        flops=2 * leaves * rank * width * (rows + rank),
        moved=2 * leaves * rows * (width + rank), limit=8,
    )
    lift_level = send(lift, lambda d: d ^ 2)
    across = send(source, lambda d: d + 1 if d & 1 else d - 1)
    share_other = send(share, lambda d: d ^ 1)

    level, pair = call(
        pair_kernel, "pair", (panel(leaves), panel(2)),
        [VMEM] * 2 + [ANY], (lift, lift_level, share_other),
    )
    layers = [send(pair, lambda d, bit=bit: d ^ bit) for bit in (4, 8, 12)]
    layer = send(level, lambda d: d - 4 if d & 2 else d + 4)
    mine = call(
        pass_kernel, "pass", panel(GROUP // 2 + leaves), [SMEM] + [VMEM] * 6,
        (near_list, pair, *layers, level, layer),
    )
    theirs = send(mine, lambda d: d ^ 1)

    picked = [
        pltpu.VMEM(near_blocks.shape, jnp.bfloat16),
        pltpu.SMEM((leaves, slots), jnp.int32),
        pltpu.SemaphoreType.DMA((leaves, slots)),
    ]
    near = call(
        near_kernel, "near", jax.ShapeDtypeStruct((leaves, rows, width), jnp.float32),
        [SMEM, SMEM] + [ANY] * 3, (near_list, near_count, near_blocks, share, share_other),
        scratch=[
            picked[0],
            pltpu.VMEM((2 * leaves * rows, width), jnp.bfloat16),
            *picked[1:],
            pltpu.SemaphoreType.DMA((2,)),
        ],
        limit=48,
    )
    near = call(
        across_kernel, "across", jax.ShapeDtypeStruct((leaves, rows, width), jnp.float32),
        [SMEM] * 2 + [ANY] + [VMEM] * 2, (near_list, near_count, near_blocks, near, across),
        scratch=picked,
        flops=16 * leaves * slots * rows * rows * width,
        moved=2 * leaves * slots * rows * rows, limit=48,
    )
    return call(
        down_kernel, "down", jax.ShapeDtypeStruct(source.shape, jnp.bfloat16),
        [SMEM] * 3 + [VMEM] * 5 + [ANY] * 3 + [VMEM] * 2,
        (
            far_list, coarse_list, near_list, transfer, far_coupling, coarse_coupling, row_basis,
            near, level, layer, share_other, mine, theirs,
        ),
        scratch=[
            pltpu.VMEM((4 * leaves * rank, width), jnp.bfloat16),
            pltpu.SemaphoreType.DMA((4,)),
        ],
        flops=2 * leaves * (far_slots + 4) * rank * rank * width,
        moved=2 * leaves * far_slots * rank * rank, limit=12,
    )


def solution(mesh):
    placed = (
        P(("clip", "row"), None),
        P(("clip", "row"), None, None, None),
        P(("clip", "row"), None),
        P(("clip", "row")),
        P(("clip", "row"), None, None),
        P(("clip", "row"), None, None),
        P(("clip", "row"), None, None),
        P(("clip", "row"), None),
        P(("clip", "row"), None, None, None),
        P(("clip", "row"), None),
        P(("clip", "row"), None, None, None),
    )
    return jax.shard_map(
        body, mesh=mesh, in_specs=placed, out_specs=P(("clip", "row"), None), check_vma=False
    )
```

time: 132 us -> 52.4 us (0.40)
  the two profiles are of different devices: /device:TPU:1 before, /device:TPU:6 now
where the time goes in v4:
time: 52.4 us; the launch traced here: 52 us
  Pallas kernels  22.6 us (43%)
  waiting for transfers between devices  15.4 us (29%)
  starting transfers between devices  10.6 us (20%)
  local copies, waits for them, and re-layouts  3.23 us (6%)
    pallas_call x6, Pallas kernels, call(): pl.pallas_call(kernel, out_shape=outs, in_specs=specs, out_specs=(VMEM,)...  22.6 us
    ppermute x8, waiting for transfers between devices, send(): return lax.ppermute(value, 'row', pairs)  15.4 us
    ppermute x8, starting transfers between devices, send(): return lax.ppermute(value, 'row', pairs)  10.6 us
    unnamed x20, local copies, waits for them, and re-layouts  3.23 us
  transfers between devices with their start and end apart: 8, of which 2 were waited for; matrix products, arithmetic and copies ran while one was open for 0% of the time, Pallas kernels for 34%

profile of v4, /device:TPU:6, one launch (start us, length us, event | category | flops | bytes accessed | tf_op | source)
XLA Modules:
  0.0 52.0 jit_solution(6659847775400539201)
XLA Ops:
  0.0 0.0 copy-start.1
  0.0 0.9 %copy-done.1 = bf16[4,128,128]{2,1,0:T(8,128)(2,1)S(1)} copy-done((bf16[4,128,128]{2,1,0:T(8,128)(2,1)S(1)}, bf16[4,128,128]{2,1,0:T(8,128)(2,1)}, u32[]{:S(2)}) %copy-start.1) | copy-done | bytes 131096
  0.9 0.0 copy-start.3
  0.9 0.9 %copy-done.3 = bf16[4,256,128]{2,1,0:T(8,128)(2,1)S(1)} copy-done((bf16[4,256,128]{2,1,0:T(8,128)(2,1)S(1)}, bf16[4,256,128]{2,1,0:T(8,128)(2,1)}, u32[]{:S(2)}) %copy-start.3) | copy-done | bytes 262168
  1.9 1.5 %up.1 = (bf16[1536,256]{1,0:T(8,128)(2,1)S(1)}, bf16[640,256]{1,0:T(8,128)(2,1)S(1)}) custom-call(bf16[1024,256]{1,0:T(8,128)(2,1)} %source_ref.1, bf16[4,256,128]{2,1,0:T(8,128)(2,1)S(1)} %copy-done.3, bf16[4,128,128]{2,1,0:T(8,128)(2,1)S(1)} %copy-done.1), custom_call_target="tpu_custom_call" | custom-call | flops 100663296 | bytes 786432 | tf_op jit(solution)/shard_map/up/pallas_call | solution.py:215
  3.4 0.1 collective-permute-start
  3.5 0.6 %collective-permute-start.2 = (bf16[640,256]{1,0:T(8,128)(2,1)S(1)}, bf16[640,256]{1,0:T(8,128)(2,1)S(1)}, u32[]{:S(2)}, u32[]{:S(2)}) collective-permute-start(bf16[640,256]{1,0:T(8,128)(2,1)S(1)} %get-tuple-element.10.own_ref), channel_id=1, source_target_pairs={{0,2},{1,3},{2,0},{3,1},{4,6},{5,7},{6,4},{7,5},{8,10},{9,11},{10,... | collective-permute-start | bytes 983048 | tf_op jit(solution)/shard_map/ppermute | solution.py:248
  4.0 3.2 %collective-permute-start.1 = (bf16[1024,256]{1,0:T(8,128)(2,1)}, bf16[1024,256]{1,0:T(8,128)(2,1)S(1)}, u32[]{:S(2)}, u32[]{:S(2)}) collective-permute-start(bf16[1024,256]{1,0:T(8,128)(2,1)} %source_ref.1), channel_id=1, source_target_pairs={{1,2},{2,1},{3,4},{4,3},{5,6},{6,5},{7,8},{8,7},{9,10},{10,9},{11,... | collective-permute-start | bytes 1572872 | tf_op jit(solution)/shard_map/ppermute | solution.py:248
  7.2 12.4 %collective-permute-done.2.lift_ref = bf16[640,256]{1,0:T(8,128)(2,1)S(1)} collective-permute-done((bf16[640,256]{1,0:T(8,128)(2,1)S(1)}, bf16[640,256]{1,0:T(8,128)(2,1)S(1)}, u32[]{:S(2)}, u32[]{:S(2)}) %collective-permute-start.2) | collective-permute-done | bytes 327712 | tf_op jit(solution)/shard_map/ppermute | solution.py:248
  19.7 0.0 collective-permute-done.share_ref._
  19.7 1.3 %collective-permute-start.3 = (bf16[512,256]{1,0:T(8,128)(2,1)S(1)}, bf16[512,256]{1,0:T(8,128)(2,1)S(1)}, u32[]{:S(2)}, u32[]{:S(2)}) collective-permute-start(bf16[512,256]{1,0:T(8,128)(2,1)S(1)} %get-tuple-element.11.refs_4_.level_ref), channel_id=1, source_target_pairs={{0,4},{1,5},{4,8},{5,9},{6,2},{7,3},{8,12},{9,13},{10,6},{11,7},{1... | collective-permute-start | bytes 786440 | tf_op jit(solution)/shard_map/ppermute | solution.py:248
  21.0 4.7 %collective-permute-start.6 = (bf16[256,256]{1,0:T(8,128)(2,1)S(1)}, bf16[256,256]{1,0:T(8,128)(2,1)S(1)}, u32[]{:S(2)}, u32[]{:S(2)}) collective-permute-start(bf16[256,256]{1,0:T(8,128)(2,1)S(1)} %get-tuple-element.12.refs_0_), channel_id=1, source_target_pairs={{0,12},{1,13},{2,14},{3,15},{4,8},{5,9},{6,10},{7,11},{8,4},{9,5},... | collective-permute-start | bytes 393224 | tf_op jit(solution)/shard_map/ppermute | solution.py:248
  25.7 0.0 collective-permute-start.5
  25.7 0.6 %collective-permute-start.4 = (bf16[256,256]{1,0:T(8,128)(2,1)S(1)}, bf16[256,256]{1,0:T(8,128)(2,1)S(1)}, u32[]{:S(2)}, u32[]{:S(2)}) collective-permute-start(bf16[256,256]{1,0:T(8,128)(2,1)S(1)} %get-tuple-element.12.refs_0_), channel_id=1, source_target_pairs={{0,4},{1,5},{2,6},{3,7},{4,0},{5,1},{6,2},{7,3},{8,12},{9,13},{10,... | collective-permute-start | bytes 393224 | tf_op jit(solution)/shard_map/ppermute | solution.py:248
  26.4 0.0 copy-start.6
  26.4 0.7 %copy-done.6 = s32[4,16]{1,0:T(4,128)S(1)} copy-done((s32[4,16]{1,0:T(4,128)S(1)}, s32[4,16]{1,0:T(4,128)}, u32[]{:S(2)}) %copy-start.6) | copy-done | bytes 280
  27.1 0.0 copy-start.8
  27.1 0.7 %copy-done.8 = s32[4]{0:T(128)S(1)} copy-done((s32[4]{0:T(128)S(1)}, s32[4]{0:T(128)}, u32[]{:S(2)}) %copy-start.8) | copy-done | bytes 40
  27.7 10.5 %near.1.near_ref = f32[4,256,256]{2,1,0:T(8,128)S(1)} custom-call(s32[4,16]{1,0:T(4,128)S(1)} %copy-done.6, s32[4]{0:T(128)S(1)} %copy-done.8, bf16[4,16,256,256]{3,2,1,0:T(8,128)(2,1)} %blocks_hbm.3, bf16[1536,256]{1,0:T(8,128)(2,1)S(1)} %get-tuple-element.9.own_ref, bf16[1536,256]{1,0:T(8,128)(2,1)S(1)} %collective-permute-done.share_ref._), custom_call_target="tpu_custom_call" | custom-call | tf_op jit(solution)/shard_map/near/pallas_call | solution.py:215
  38.3 0.0 collective-permute-done.6.refs_3_
  38.3 3.0 %collective-permute-done.5.refs_2_ = bf16[256,256]{1,0:T(8,128)(2,1)S(1)} collective-permute-done((bf16[256,256]{1,0:T(8,128)(2,1)S(1)}, bf16[256,256]{1,0:T(8,128)(2,1)S(1)}, u32[]{:S(2)}, u32[]{:S(2)}) %collective-permute-start.5) | collective-permute-done | bytes 131104 | tf_op jit(solution)/shard_map/ppermute | solution.py:248
  41.3 0.0 collective-permute-done.4.refs_1_
  41.3 0.0 collective-permute-done.3.refs_5_.layer_ref
  41.3 0.6 %pass.1.mine_ref = bf16[1536,256]{1,0:T(8,128)(2,1)S(1)} custom-call(s32[4,16]{1,0:T(4,128)S(1)} %copy-done.6, bf16[256,256]{1,0:T(8,128)(2,1)S(1)} %get-tuple-element.12.refs_0_, bf16[256,256]{1,0:T(8,128)(2,1)S(1)} %collective-permute-done.4.refs_1_, bf16[256,256]{1,0:T(8,128)(2,1)S(1)} %collective-permute-done.5.refs_2_, ...), custom_call_target="tpu_custom_call" | custom-call | tf_op jit(solution)/shard_map/pass/pallas_call | solution.py:215
  41.9 0.0 copy-start
  41.9 0.0 copy-start.2
  41.9 0.0 copy-start.4
  41.9 0.0 copy-start.5
  42.0 0.0 copy-start.7
  42.0 0.0 copy-start.9
  42.0 0.1 collective-permute-start.7
  42.1 0.0 collective-permute-done.1.across_ref
  42.1 6.4 %across.1.near_ref = f32[4,256,256]{2,1,0:T(8,128)S(1)} custom-call(s32[4,16]{1,0:T(4,128)S(1)} %copy-done.6, s32[4]{0:T(128)S(1)} %copy-done.8, bf16[4,16,256,256]{3,2,1,0:T(8,128)(2,1)} %blocks_hbm.3, f32[4,256,256]{2,1,0:T(8,128)S(1)} %near.1.near_ref, bf16[1024,256]{1,0:T(8,128)(2,1)S(1)} %collective-permute-done.1.across_ref), custom_call_target="tpu_custom_call" | custom-call | flops 17179869184 | bytes 8388608 | tf_op jit(solution)/shard_map/across/pallas_call | solution.py:215
  48.5 0.0 collective-permute-done.7.theirs_ref
  48.5 0.0 copy-done
  48.5 0.0 copy-done.2
  48.5 0.0 copy-done.4
  48.5 0.0 copy-done.5
  48.5 0.0 copy-done.7
  48.5 0.0 copy-done.9
  48.5 3.5 %down.1 = bf16[1024,256]{1,0:T(8,128)(2,1)} custom-call(s32[4,16]{1,0:T(4,128)S(1)} %copy-done.7, s32[1,8]{1,0:T(1,128)S(1)} %copy-done.9, s32[4,16]{1,0:T(4,128)S(1)} %copy-done.6, bf16[4,128,128]{2,1,0:T(8,128)(2,1)S(1)} %copy-done.2, bf16[4,16,128,128]{3,2,1,0:T(8,128)(2,1)S(1)} %copy-done, bf16[1,8,128,128]{3,2,1,0:T(8,128)(2,1)S(1)} %copy-done.4, ...), custom_call_target="tpu_custom_call" | custom-call | flops 671088640 | bytes 2097152 | tf_op jit(solution)/shard_map/down/pallas_call | solution.py:215
  (1 shorter events, 0.0 us)
Async XLA Ops:
  0.0 0.9 %copy-start.1 = (bf16[4,128,128]{2,1,0:T(8,128)(2,1)S(1)}, bf16[4,128,128]{2,1,0:T(8,128)(2,1)}, u32[]{:S(2)}) copy-start(bf16[4,128,128]{2,1,0:T(8,128)(2,1)} %transfer_ref.3) | copy-start | bytes 393220
  0.9 0.9 %copy-start.3 = (bf16[4,256,128]{2,1,0:T(8,128)(2,1)S(1)}, bf16[4,256,128]{2,1,0:T(8,128)(2,1)}, u32[]{:S(2)}) copy-start(bf16[4,256,128]{2,1,0:T(8,128)(2,1)} %col_ref.1) | copy-start | bytes 786436
  3.4 16.3 %collective-permute-start = (bf16[1536,256]{1,0:T(8,128)(2,1)S(1)}, bf16[1536,256]{1,0:T(8,128)(2,1)S(1)}, u32[]{:S(2)}, u32[]{:S(2)}) collective-permute-start(bf16[1536,256]{1,0:T(8,128)(2,1)S(1)} %get-tuple-element.9.own_ref), channel_id=1, source_target_pairs={{0,1},{1,0},{2,3},{3,2},{4,5},{5,4},{6,7},{7,6},{8,9},{9,8},{10,11... | collective-permute-start | bytes 2359304 | tf_op jit(solution)/shard_map/ppermute | solution.py:248
  3.5 16.2 %collective-permute-start.2 = (bf16[640,256]{1,0:T(8,128)(2,1)S(1)}, bf16[640,256]{1,0:T(8,128)(2,1)S(1)}, u32[]{:S(2)}, u32[]{:S(2)}) collective-permute-start(bf16[640,256]{1,0:T(8,128)(2,1)S(1)} %get-tuple-element.10.own_ref), channel_id=1, source_target_pairs={{0,2},{1,3},{2,0},{3,1},{4,6},{5,7},{6,4},{7,5},{8,10},{9,11},{10,... | collective-permute-start | bytes 983048 | tf_op jit(solution)/shard_map/ppermute | solution.py:248
  4.0 38.0 %collective-permute-start.1 = (bf16[1024,256]{1,0:T(8,128)(2,1)}, bf16[1024,256]{1,0:T(8,128)(2,1)S(1)}, u32[]{:S(2)}, u32[]{:S(2)}) collective-permute-start(bf16[1024,256]{1,0:T(8,128)(2,1)} %source_ref.1), channel_id=1, source_target_pairs={{1,2},{2,1},{3,4},{4,3},{5,6},{6,5},{7,8},{8,7},{9,10},{10,9},{11,... | collective-permute-start | bytes 1572872 | tf_op jit(solution)/shard_map/ppermute | solution.py:248
  19.7 21.6 %collective-permute-start.3 = (bf16[512,256]{1,0:T(8,128)(2,1)S(1)}, bf16[512,256]{1,0:T(8,128)(2,1)S(1)}, u32[]{:S(2)}, u32[]{:S(2)}) collective-permute-start(bf16[512,256]{1,0:T(8,128)(2,1)S(1)} %get-tuple-element.11.refs_4_.level_ref), channel_id=1, source_target_pairs={{0,4},{1,5},{4,8},{5,9},{6,2},{7,3},{8,12},{9,13},{10,6},{11,7},{1... | collective-permute-start | bytes 786440 | tf_op jit(solution)/shard_map/ppermute | solution.py:248
  21.0 17.3 %collective-permute-start.6 = (bf16[256,256]{1,0:T(8,128)(2,1)S(1)}, bf16[256,256]{1,0:T(8,128)(2,1)S(1)}, u32[]{:S(2)}, u32[]{:S(2)}) collective-permute-start(bf16[256,256]{1,0:T(8,128)(2,1)S(1)} %get-tuple-element.12.refs_0_), channel_id=1, source_target_pairs={{0,12},{1,13},{2,14},{3,15},{4,8},{5,9},{6,10},{7,11},{8,4},{9,5},... | collective-permute-start | bytes 393224 | tf_op jit(solution)/shard_map/ppermute | solution.py:248
  25.7 15.5 %collective-permute-start.5 = (bf16[256,256]{1,0:T(8,128)(2,1)S(1)}, bf16[256,256]{1,0:T(8,128)(2,1)S(1)}, u32[]{:S(2)}, u32[]{:S(2)}) collective-permute-start(bf16[256,256]{1,0:T(8,128)(2,1)S(1)} %get-tuple-element.12.refs_0_), channel_id=1, source_target_pairs={{0,8},{1,9},{2,10},{3,11},{4,12},{5,13},{6,14},{7,15},{8,0},{9,1},... | collective-permute-start | bytes 393224 | tf_op jit(solution)/shard_map/ppermute | solution.py:248
  25.7 15.5 %collective-permute-start.4 = (bf16[256,256]{1,0:T(8,128)(2,1)S(1)}, bf16[256,256]{1,0:T(8,128)(2,1)S(1)}, u32[]{:S(2)}, u32[]{:S(2)}) collective-permute-start(bf16[256,256]{1,0:T(8,128)(2,1)S(1)} %get-tuple-element.12.refs_0_), channel_id=1, source_target_pairs={{0,4},{1,5},{2,6},{3,7},{4,0},{5,1},{6,2},{7,3},{8,12},{9,13},{10,... | collective-permute-start | bytes 393224 | tf_op jit(solution)/shard_map/ppermute | solution.py:248
  26.4 0.7 %copy-start.6 = (s32[4,16]{1,0:T(4,128)S(1)}, s32[4,16]{1,0:T(4,128)}, u32[]{:S(2)}) copy-start(s32[4,16]{1,0:T(4,128)} %near_list_ref.1) | copy-start | bytes 772
  27.1 0.7 %copy-start.8 = (s32[4]{0:T(128)S(1)}, s32[4]{0:T(128)}, u32[]{:S(2)}) copy-start(s32[4]{0:T(128)} %count_ref.3) | copy-start | bytes 52
  41.9 6.6 %copy-start = (bf16[4,16,128,128]{3,2,1,0:T(8,128)(2,1)S(1)}, bf16[4,16,128,128]{3,2,1,0:T(8,128)(2,1)}, u32[]{:S(2)}) copy-start(bf16[4,16,128,128]{3,2,1,0:T(8,128)(2,1)} %coupling_ref.1) | copy-start | bytes 6291460
  41.9 6.6 %copy-start.2 = (bf16[4,128,128]{2,1,0:T(8,128)(2,1)S(1)}, bf16[4,128,128]{2,1,0:T(8,128)(2,1)}, u32[]{:S(2)}) copy-start(bf16[4,128,128]{2,1,0:T(8,128)(2,1)} %transfer_ref.3) | copy-start | bytes 393220
  41.9 6.6 %copy-start.4 = (bf16[1,8,128,128]{3,2,1,0:T(8,128)(2,1)S(1)}, bf16[1,8,128,128]{3,2,1,0:T(8,128)(2,1)}, u32[]{:S(2)}) copy-start(bf16[1,8,128,128]{3,2,1,0:T(8,128)(2,1)} %coarse_coupling_ref.1) | copy-start | bytes 786436
  41.9 6.6 %copy-start.5 = (bf16[4,256,128]{2,1,0:T(8,128)(2,1)S(1)}, bf16[4,256,128]{2,1,0:T(8,128)(2,1)}, u32[]{:S(2)}) copy-start(bf16[4,256,128]{2,1,0:T(8,128)(2,1)} %row_ref.1) | copy-start | bytes 786436
  42.0 6.6 %copy-start.7 = (s32[4,16]{1,0:T(4,128)S(1)}, s32[4,16]{1,0:T(4,128)}, u32[]{:S(2)}) copy-start(s32[4,16]{1,0:T(4,128)} %far_list_ref.1) | copy-start | bytes 772
  42.0 6.6 %copy-start.9 = (s32[1,8]{1,0:T(1,128)S(1)}, s32[1,8]{1,0:T(1,128)}, u32[]{:S(2)}) copy-start(s32[1,8]{1,0:T(1,128)} %coarse_list_ref.1) | copy-start | bytes 100
  42.0 6.5 %collective-permute-start.7 = (bf16[1536,256]{1,0:T(8,128)(2,1)S(1)}, bf16[1536,256]{1,0:T(8,128)(2,1)S(1)}, u32[]{:S(2)}, u32[]{:S(2)}) collective-permute-start(bf16[1536,256]{1,0:T(8,128)(2,1)S(1)} %pass.1.mine_ref), channel_id=1, source_target_pairs={{0,1},{1,0},{2,3},{3,2},{4,5},{5,4},{6,7},{7,6},{8,9},{9,8},{10,11... | collective-permute-start | bytes 2359304 | tf_op jit(solution)/shard_map/ppermute | solution.py:248

commit v5 on v4

--- a/solution.py
+++ b/solution.py
@@ -6,6 +6,7 @@
 from jax.sharding import PartitionSpec as P
 
 GROUP = 16
+CHUNK = 4
 MIB = 2**20
 
 VMEM = pl.BlockSpec(memory_space=pltpu.VMEM)
@@ -41,12 +42,13 @@
     lift_ref[pl.ds(leaves * rank, rank), :] = total.astype(jnp.bfloat16)
 
 
-def pair_kernel(own_ref, lift_ref, _, level_ref, pair_ref):
+def pair_kernel(own_ref, lift_ref, share_ref, _, level_ref, pair_ref, source_ref):
     size = level_ref.shape[0]
     rank = own_ref.shape[0] - size
     level_ref[...] = lift_ref[pl.ds(0, size), :]
     pair_ref[pl.ds(0, rank), :] = own_ref[pl.ds(size, rank), :]
     pair_ref[pl.ds(rank, rank), :] = lift_ref[pl.ds(size, rank), :]
+    source_ref[...] = share_ref[pl.ds(0, source_ref.shape[0]), :]
 
 
 def pass_kernel(list_ref, *refs):
@@ -77,23 +79,27 @@
 
         return found + kept.astype(jnp.int32)
 
-    return lax.fori_loop(0, count_ref[leaf], step, 0)
+    found = lax.fori_loop(0, count_ref[leaf], step, 0)
+    for pad in range(CHUNK):
+        order_ref[leaf, found + pad] = -1
+    return found
 
 
 def add_slots(total_ref, blocks_hbm, blocks, sems, order_ref, leaf, found, panel_of):
-    def term(n):
-        pltpu.make_async_copy(blocks_hbm.at[leaf, 0], blocks.at[leaf, n], sems.at[leaf, n]).wait()
-        return dot(blocks[leaf, n], panel_of(order_ref[leaf, n]))
-
-    def pair(n, _):
-        total_ref[leaf] = total_ref[leaf] + term(2 * n) + term(2 * n + 1)
-        return 0
-
-    lax.fori_loop(0, found >> 1, pair, 0)
-
-    @pl.when((found & 1) == 1)
-    def _():
-        total_ref[leaf] = total_ref[leaf] + term(found - 1)
+    for first in range(0, blocks.shape[1], CHUNK):
+        @pl.when(first < found)
+        def _():
+            for n in range(first, first + CHUNK):
+                @pl.when(n < found)
+                def _():
+                    pltpu.make_async_copy(
+                        blocks_hbm.at[leaf, 0], blocks.at[leaf, n], sems.at[leaf, n]
+                    ).wait()
+            total = total_ref[leaf]
+            for n in range(first, first + CHUNK):
+                block = blocks[leaf, jnp.where(n < found, n, 0)]
+                total = total + dot(block, panel_of(order_ref[leaf, n]))
+            total_ref[leaf] = total
 
 
 def near_kernel(
@@ -120,12 +126,13 @@
         for leaf in range(leaves)
     ]
     near_ref[...] = jnp.zeros(near_ref.shape, near_ref.dtype)
+    panels[pl.ds(2 * size, rows), :] = jnp.zeros((rows, panels.shape[1]), panels.dtype)
     for copy in pairs:
         copy.wait()
 
     def panel_of(column):
-        other = lax.div(column, leaves) ^ place
-        return panels[rows_at(other * leaves + (column & (leaves - 1)), rows), :]
+        index = (lax.div(column, leaves) ^ place) * leaves + (column & (leaves - 1))
+        return panels[rows_at(jnp.where(column < 0, 2 * leaves, index), rows), :]
 
     for leaf in range(leaves):
         add_slots(near_ref, blocks_hbm, blocks, block_sems, order, leaf, found[leaf], panel_of)
@@ -204,7 +211,8 @@
     total_ref[...] = near_ref[...]
 
     def panel_of(column):
-        return across_ref[rows_at(column & (leaves - 1), rows), :]
+        panel = across_ref[rows_at(column & (leaves - 1), rows), :]
+        return jnp.where(column < 0, jnp.zeros_like(panel), panel)
 
     for leaf in range(leaves):
         add_slots(total_ref, blocks_hbm, blocks, sems, order, leaf, found[leaf], panel_of)
@@ -258,13 +266,29 @@
         moved=2 * leaves * rows * (width + rank), limit=8,
     )
     lift_level = send(lift, lambda d: d ^ 2)
-    across = send(source, lambda d: d + 1 if d & 1 else d - 1)
     share_other = send(share, lambda d: d ^ 1)
 
-    level, pair = call(
-        pair_kernel, "pair", (panel(leaves), panel(2)),
-        [VMEM] * 2 + [ANY], (lift, lift_level, share_other),
-    )
+    picked = [
+        pltpu.VMEM(near_blocks.shape, jnp.bfloat16),
+        pltpu.SMEM((leaves, slots + CHUNK), jnp.int32),
+        pltpu.SemaphoreType.DMA((leaves, slots)),
+    ]
+    near = call(
+        near_kernel, "near", jax.ShapeDtypeStruct((leaves, rows, width), jnp.float32),
+        [SMEM, SMEM] + [ANY] * 3, (near_list, near_count, near_blocks, share, share_other),
+        scratch=[
+            picked[0],
+            pltpu.VMEM(((2 * leaves + 1) * rows, width), jnp.bfloat16),
+            *picked[1:],
+            pltpu.SemaphoreType.DMA((2,)),
+        ],
+        limit=48,
+    )
+    level, pair, source_own = call(
+        pair_kernel, "pair", (panel(leaves), panel(2), jax.ShapeDtypeStruct(source.shape, jnp.bfloat16)),
+        [VMEM] * 3 + [ANY], (lift, lift_level, share, near),
+    )
+    across = send(source_own, lambda d: d + 1 if d & 1 else d - 1)
     layers = [send(pair, lambda d, bit=bit: d ^ bit) for bit in (4, 8, 12)]
     layer = send(level, lambda d: d - 4 if d & 2 else d + 4)
     mine = call(
@@ -273,22 +297,6 @@
     )
     theirs = send(mine, lambda d: d ^ 1)
 
-    picked = [
-        pltpu.VMEM(near_blocks.shape, jnp.bfloat16),
-        pltpu.SMEM((leaves, slots), jnp.int32),
-        pltpu.SemaphoreType.DMA((leaves, slots)),
-    ]
-    near = call(
-        near_kernel, "near", jax.ShapeDtypeStruct((leaves, rows, width), jnp.float32),
-        [SMEM, SMEM] + [ANY] * 3, (near_list, near_count, near_blocks, share, share_other),
-        scratch=[
-            picked[0],
-            pltpu.VMEM((2 * leaves * rows, width), jnp.bfloat16),
-            *picked[1:],
-            pltpu.SemaphoreType.DMA((2,)),
-        ],
-        limit=48,
-    )
     near = call(
         across_kernel, "across", jax.ShapeDtypeStruct((leaves, rows, width), jnp.float32),
         [SMEM] * 2 + [ANY] + [VMEM] * 2, (near_list, near_count, near_blocks, near, across),

time: 52.4 us -> 47.5 us (0.906)
  the two profiles are of different devices: /device:TPU:6 before, /device:TPU:19 now
where the time goes in v5:
time: 47.5 us; the launch traced here: 47.4 us
  waiting for transfers between devices  17.3 us (36%)
  Pallas kernels  13.3 us (28%)
  starting transfers between devices  12.3 us (26%)
  local copies, waits for them, and re-layouts  4.28 us (9%)
    ppermute x8, waiting for transfers between devices, send(): return lax.ppermute(value, 'row', pairs)  17.3 us
    pallas_call x6, Pallas kernels, call(): pl.pallas_call(kernel, out_shape=outs, in_specs=specs, out_specs=(VMEM,)...  13.3 us
    ppermute x8, starting transfers between devices, send(): return lax.ppermute(value, 'row', pairs)  12.3 us
    unnamed x26, local copies, waits for them, and re-layouts  4.28 us
  transfers between devices with their start and end apart: 8, of which 5 were waited for; matrix products, arithmetic and copies ran while one was open for 0% of the time, Pallas kernels for 20%

profile of v5, /device:TPU:19, one launch (start us, length us, event | category | flops | bytes accessed | tf_op | source)
XLA Modules:
  0.0 47.4 jit_solution(424100817024153044)
XLA Ops:
  0.0 0.0 copy-start.1
  0.0 0.9 %copy-done.1 = bf16[4,128,128]{2,1,0:T(8,128)(2,1)S(1)} copy-done((bf16[4,128,128]{2,1,0:T(8,128)(2,1)S(1)}, bf16[4,128,128]{2,1,0:T(8,128)(2,1)}, u32[]{:S(2)}) %copy-start.1) | copy-done | bytes 131096
  0.9 0.0 copy-start.3
  0.9 1.0 %copy-done.3 = bf16[1024,256]{1,0:T(8,128)(2,1)S(1)} copy-done((bf16[1024,256]{1,0:T(8,128)(2,1)S(1)}, bf16[1024,256]{1,0:T(8,128)(2,1)}, u32[]{:S(2)}) %copy-start.3) | copy-done | bytes 524312
  1.9 0.0 copy-start.4
  1.9 0.9 %copy-done.4 = bf16[4,256,128]{2,1,0:T(8,128)(2,1)S(1)} copy-done((bf16[4,256,128]{2,1,0:T(8,128)(2,1)S(1)}, bf16[4,256,128]{2,1,0:T(8,128)(2,1)}, u32[]{:S(2)}) %copy-start.4) | copy-done | bytes 262168
  2.9 0.0 copy-start.8
  2.9 0.0 copy-start.11
  2.9 0.5 %up.1 = (bf16[1536,256]{1,0:T(8,128)(2,1)S(1)}, bf16[640,256]{1,0:T(8,128)(2,1)S(1)}) custom-call(bf16[1024,256]{1,0:T(8,128)(2,1)S(1)} %copy-done.3, bf16[4,256,128]{2,1,0:T(8,128)(2,1)S(1)} %copy-done.4, bf16[4,128,128]{2,1,0:T(8,128)(2,1)S(1)} %copy-done.1), custom_call_target="tpu_custom_call" | custom-call | flops 100663296 | bytes 786432 | tf_op jit(solution)/shard_map/up/pallas_call | solution.py:223
  3.4 0.7 %collective-permute-start = (bf16[1536,256]{1,0:T(8,128)(2,1)S(1)}, bf16[1536,256]{1,0:T(8,128)(2,1)S(1)}, u32[]{:S(2)}, u32[]{:S(2)}) collective-permute-start(bf16[1536,256]{1,0:T(8,128)(2,1)S(1)} %get-tuple-element.10.own_ref.share_ref), channel_id=1, source_target_pairs={{0,1},{1,0},{2,3},{3,2},{4,5},{5,4},{6,7},{7,6},{8,9},{9,8},{10,11... | collective-permute-start | bytes 2359304 | tf_op jit(solution)/shard_map/ppermute | solution.py:256
  4.1 1.3 %collective-permute-start.1 = (bf16[640,256]{1,0:T(8,128)(2,1)S(1)}, bf16[640,256]{1,0:T(8,128)(2,1)S(1)}, u32[]{:S(2)}, u32[]{:S(2)}) collective-permute-start(bf16[640,256]{1,0:T(8,128)(2,1)S(1)} %get-tuple-element.11.own_ref), channel_id=1, source_target_pairs={{0,2},{1,3},{2,0},{3,1},{4,6},{5,7},{6,4},{7,5},{8,10},{9,11},{10,... | collective-permute-start | bytes 983048 | tf_op jit(solution)/shard_map/ppermute | solution.py:256
  5.4 0.7 %collective-permute-done.share_ref = bf16[1536,256]{1,0:T(8,128)(2,1)S(1)} collective-permute-done((bf16[1536,256]{1,0:T(8,128)(2,1)S(1)}, bf16[1536,256]{1,0:T(8,128)(2,1)S(1)}, u32[]{:S(2)}, u32[]{:S(2)}) %collective-permute-start) | collective-permute-done | bytes 786464 | tf_op jit(solution)/shard_map/ppermute | solution.py:256
  6.0 0.0 copy-start.7
  6.0 0.7 %copy-done.7 = s32[4,16]{1,0:T(4,128)S(1)} copy-done((s32[4,16]{1,0:T(4,128)S(1)}, s32[4,16]{1,0:T(4,128)}, u32[]{:S(2)}) %copy-start.7) | copy-done | bytes 280
  6.7 0.0 copy-start.10
  6.7 0.7 %copy-done.10 = s32[4]{0:T(128)S(1)} copy-done((s32[4]{0:T(128)S(1)}, s32[4]{0:T(128)}, u32[]{:S(2)}) %copy-start.10) | copy-done | bytes 40
  7.4 4.9 %near.1._.near_ref = f32[4,256,256]{2,1,0:T(8,128)S(1)} custom-call(s32[4,16]{1,0:T(4,128)S(1)} %copy-done.7, s32[4]{0:T(128)S(1)} %copy-done.10, bf16[4,16,256,256]{3,2,1,0:T(8,128)(2,1)} %blocks_hbm.3, bf16[1536,256]{1,0:T(8,128)(2,1)S(1)} %get-tuple-element.10.own_ref.share_ref, bf16[1536,256]{1,0:T(8,128)(2,1)S(1)} %collective-permute-done.share_ref), custom_call_target="tpu_custom_call" | custom-call | tf_op jit(solution)/shard_map/near/pallas_call | solution.py:223
  12.3 1.1 %collective-permute-done.1.lift_ref = bf16[640,256]{1,0:T(8,128)(2,1)S(1)} collective-permute-done((bf16[640,256]{1,0:T(8,128)(2,1)S(1)}, bf16[640,256]{1,0:T(8,128)(2,1)S(1)}, u32[]{:S(2)}, u32[]{:S(2)}) %collective-permute-start.1) | collective-permute-done | bytes 327712 | tf_op jit(solution)/shard_map/ppermute | solution.py:256
  13.4 0.1 pair.1
  13.5 3.9 %collective-permute-start.2 = (bf16[1024,256]{1,0:T(8,128)(2,1)S(1)}, bf16[1024,256]{1,0:T(8,128)(2,1)S(1)}, u32[]{:S(2)}, u32[]{:S(2)}) collective-permute-start(bf16[1024,256]{1,0:T(8,128)(2,1)S(1)} %get-tuple-element.12), channel_id=1, source_target_pairs={{1,2},{2,1},{3,4},{4,3},{5,6},{6,5},{7,8},{8,7},{9,10},{10,9},{11,... | collective-permute-start | bytes 1572872 | tf_op jit(solution)/shard_map/ppermute | solution.py:256
  17.4 3.2 %collective-permute-start.3 = (bf16[512,256]{1,0:T(8,128)(2,1)S(1)}, bf16[512,256]{1,0:T(8,128)(2,1)S(1)}, u32[]{:S(2)}, u32[]{:S(2)}) collective-permute-start(bf16[512,256]{1,0:T(8,128)(2,1)S(1)} %get-tuple-element.13.refs_4_.level_ref), channel_id=1, source_target_pairs={{0,4},{1,5},{4,8},{5,9},{6,2},{7,3},{8,12},{9,13},{10,6},{11,7},{1... | collective-permute-start | bytes 786440 | tf_op jit(solution)/shard_map/ppermute | solution.py:256
  20.6 0.1 collective-permute-start.4
  20.7 1.4 %collective-permute-start.5 = (bf16[256,256]{1,0:T(8,128)(2,1)S(1)}, bf16[256,256]{1,0:T(8,128)(2,1)S(1)}, u32[]{:S(2)}, u32[]{:S(2)}) collective-permute-start(bf16[256,256]{1,0:T(8,128)(2,1)S(1)} %get-tuple-element.14.refs_0_), channel_id=1, source_target_pairs={{0,8},{1,9},{2,10},{3,11},{4,12},{5,13},{6,14},{7,15},{8,0},{9,1},... | collective-permute-start | bytes 393224 | tf_op jit(solution)/shard_map/ppermute | solution.py:256
  22.0 1.3 %collective-permute-start.6 = (bf16[256,256]{1,0:T(8,128)(2,1)S(1)}, bf16[256,256]{1,0:T(8,128)(2,1)S(1)}, u32[]{:S(2)}, u32[]{:S(2)}) collective-permute-start(bf16[256,256]{1,0:T(8,128)(2,1)S(1)} %get-tuple-element.14.refs_0_), channel_id=1, source_target_pairs={{0,12},{1,13},{2,14},{3,15},{4,8},{5,9},{6,10},{7,11},{8,4},{9,5},... | collective-permute-start | bytes 393224 | tf_op jit(solution)/shard_map/ppermute | solution.py:256
  23.3 8.9 %collective-permute-done.4.refs_1_ = bf16[256,256]{1,0:T(8,128)(2,1)S(1)} collective-permute-done((bf16[256,256]{1,0:T(8,128)(2,1)S(1)}, bf16[256,256]{1,0:T(8,128)(2,1)S(1)}, u32[]{:S(2)}, u32[]{:S(2)}) %collective-permute-start.4) | collective-permute-done | bytes 131104 | tf_op jit(solution)/shard_map/ppermute | solution.py:256
  32.2 0.9 %collective-permute-done.5.refs_2_ = bf16[256,256]{1,0:T(8,128)(2,1)S(1)} collective-permute-done((bf16[256,256]{1,0:T(8,128)(2,1)S(1)}, bf16[256,256]{1,0:T(8,128)(2,1)S(1)}, u32[]{:S(2)}, u32[]{:S(2)}) %collective-permute-start.5) | collective-permute-done | bytes 131104 | tf_op jit(solution)/shard_map/ppermute | solution.py:256
  33.1 5.7 %collective-permute-done.6.refs_3_ = bf16[256,256]{1,0:T(8,128)(2,1)S(1)} collective-permute-done((bf16[256,256]{1,0:T(8,128)(2,1)S(1)}, bf16[256,256]{1,0:T(8,128)(2,1)S(1)}, u32[]{:S(2)}, u32[]{:S(2)}) %collective-permute-start.6) | collective-permute-done | bytes 131104 | tf_op jit(solution)/shard_map/ppermute | solution.py:256
  38.9 0.0 collective-permute-done.3.refs_5_.layer_ref
  38.9 0.0 copy-done.8
  38.9 0.6 %pass.1.mine_ref = bf16[1536,256]{1,0:T(8,128)(2,1)S(1)} custom-call(s32[4,16]{1,0:T(4,128)S(1)} %copy-done.8, bf16[256,256]{1,0:T(8,128)(2,1)S(1)} %get-tuple-element.14.refs_0_, bf16[256,256]{1,0:T(8,128)(2,1)S(1)} %collective-permute-done.4.refs_1_, bf16[256,256]{1,0:T(8,128)(2,1)S(1)} %collective-permute-done.5.refs_2_, ...), custom_call_target="tpu_custom_call" | custom-call | tf_op jit(solution)/shard_map/pass/pallas_call | solution.py:223
  39.5 0.0 copy-start
  39.5 0.0 copy-start.2
  39.6 0.0 copy-start.5
  39.6 0.0 copy-start.6
  39.6 0.0 copy-start.9
  39.6 0.0 copy-start.12
  39.6 0.5 collective-permute-start.7
  40.1 0.0 collective-permute-done.2.across_ref
  40.1 0.0 copy-done.11
  40.1 3.8 %across.1.near_ref = f32[4,256,256]{2,1,0:T(8,128)S(1)} custom-call(s32[4,16]{1,0:T(4,128)S(1)} %copy-done.8, s32[4]{0:T(128)S(1)} %copy-done.11, bf16[4,16,256,256]{3,2,1,0:T(8,128)(2,1)} %blocks_hbm.3, f32[4,256,256]{2,1,0:T(8,128)S(1)} %near.1._.near_ref, bf16[1024,256]{1,0:T(8,128)(2,1)S(1)} %collective-permute-done.2.across_ref), custom_call_target="tpu_custom_call" | custom-call | flops 17179869184 | bytes 8388608 | tf_op jit(solution)/shard_map/across/pallas_call | solution.py:223
  43.8 0.0 collective-permute-done.7.theirs_ref
  43.9 0.0 copy-done
  43.9 0.0 copy-done.2
  43.9 0.0 copy-done.5
  43.9 0.0 copy-done.6
  43.9 0.0 copy-done.9
  43.9 0.0 copy-done.12
  43.9 3.5 %down.1 = bf16[1024,256]{1,0:T(8,128)(2,1)} custom-call(s32[4,16]{1,0:T(4,128)S(1)} %copy-done.9, s32[1,8]{1,0:T(1,128)S(1)} %copy-done.12, s32[4,16]{1,0:T(4,128)S(1)} %copy-done.8, bf16[4,128,128]{2,1,0:T(8,128)(2,1)S(1)} %copy-done.2, bf16[4,16,128,128]{3,2,1,0:T(8,128)(2,1)S(1)} %copy-done, bf16[1,8,128,128]{3,2,1,0:T(8,128)(2,1)S(1)} %copy-done.5, ...), custom_call_target="tpu_custom_call" | custom-call | flops 671088640 | bytes 2097152 | tf_op jit(solution)/shard_map/down/pallas_call | solution.py:223
Async XLA Ops:
  0.0 0.9 %copy-start.1 = (bf16[4,128,128]{2,1,0:T(8,128)(2,1)S(1)}, bf16[4,128,128]{2,1,0:T(8,128)(2,1)}, u32[]{:S(2)}) copy-start(bf16[4,128,128]{2,1,0:T(8,128)(2,1)} %transfer_ref.3) | copy-start | bytes 393220
  0.9 1.0 %copy-start.3 = (bf16[1024,256]{1,0:T(8,128)(2,1)S(1)}, bf16[1024,256]{1,0:T(8,128)(2,1)}, u32[]{:S(2)}) copy-start(bf16[1024,256]{1,0:T(8,128)(2,1)} %source_ref.1) | copy-start | bytes 1572868
  1.9 0.9 %copy-start.4 = (bf16[4,256,128]{2,1,0:T(8,128)(2,1)S(1)}, bf16[4,256,128]{2,1,0:T(8,128)(2,1)}, u32[]{:S(2)}) copy-start(bf16[4,256,128]{2,1,0:T(8,128)(2,1)} %col_ref.1) | copy-start | bytes 786436
  2.9 36.0 %copy-start.8 = (s32[4,16]{1,0:T(4,128)S(1)}, s32[4,16]{1,0:T(4,128)}, u32[]{:S(2)}) copy-start(s32[4,16]{1,0:T(4,128)} %near_list_ref.1) | copy-start | bytes 772
  2.9 37.2 %copy-start.11 = (s32[4]{0:T(128)S(1)}, s32[4]{0:T(128)}, u32[]{:S(2)}) copy-start(s32[4]{0:T(128)} %count_ref.3) | copy-start | bytes 52
  3.4 2.7 %collective-permute-start = (bf16[1536,256]{1,0:T(8,128)(2,1)S(1)}, bf16[1536,256]{1,0:T(8,128)(2,1)S(1)}, u32[]{:S(2)}, u32[]{:S(2)}) collective-permute-start(bf16[1536,256]{1,0:T(8,128)(2,1)S(1)} %get-tuple-element.10.own_ref.share_ref), channel_id=1, source_target_pairs={{0,1},{1,0},{2,3},{3,2},{4,5},{5,4},{6,7},{7,6},{8,9},{9,8},{10,11... | collective-permute-start | bytes 2359304 | tf_op jit(solution)/shard_map/ppermute | solution.py:256
  4.1 9.3 %collective-permute-start.1 = (bf16[640,256]{1,0:T(8,128)(2,1)S(1)}, bf16[640,256]{1,0:T(8,128)(2,1)S(1)}, u32[]{:S(2)}, u32[]{:S(2)}) collective-permute-start(bf16[640,256]{1,0:T(8,128)(2,1)S(1)} %get-tuple-element.11.own_ref), channel_id=1, source_target_pairs={{0,2},{1,3},{2,0},{3,1},{4,6},{5,7},{6,4},{7,5},{8,10},{9,11},{10,... | collective-permute-start | bytes 983048 | tf_op jit(solution)/shard_map/ppermute | solution.py:256
  6.0 0.7 %copy-start.7 = (s32[4,16]{1,0:T(4,128)S(1)}, s32[4,16]{1,0:T(4,128)}, u32[]{:S(2)}) copy-start(s32[4,16]{1,0:T(4,128)} %near_list_ref.1) | copy-start | bytes 772
  6.7 0.7 %copy-start.10 = (s32[4]{0:T(128)S(1)}, s32[4]{0:T(128)}, u32[]{:S(2)}) copy-start(s32[4]{0:T(128)} %count_ref.3) | copy-start | bytes 52
  13.5 26.6 %collective-permute-start.2 = (bf16[1024,256]{1,0:T(8,128)(2,1)S(1)}, bf16[1024,256]{1,0:T(8,128)(2,1)S(1)}, u32[]{:S(2)}, u32[]{:S(2)}) collective-permute-start(bf16[1024,256]{1,0:T(8,128)(2,1)S(1)} %get-tuple-element.12), channel_id=1, source_target_pairs={{1,2},{2,1},{3,4},{4,3},{5,6},{6,5},{7,8},{8,7},{9,10},{10,9},{11,... | collective-permute-start | bytes 1572872 | tf_op jit(solution)/shard_map/ppermute | solution.py:256
  17.4 21.5 %collective-permute-start.3 = (bf16[512,256]{1,0:T(8,128)(2,1)S(1)}, bf16[512,256]{1,0:T(8,128)(2,1)S(1)}, u32[]{:S(2)}, u32[]{:S(2)}) collective-permute-start(bf16[512,256]{1,0:T(8,128)(2,1)S(1)} %get-tuple-element.13.refs_4_.level_ref), channel_id=1, source_target_pairs={{0,4},{1,5},{4,8},{5,9},{6,2},{7,3},{8,12},{9,13},{10,6},{11,7},{1... | collective-permute-start | bytes 786440 | tf_op jit(solution)/shard_map/ppermute | solution.py:256
  20.6 11.7 %collective-permute-start.4 = (bf16[256,256]{1,0:T(8,128)(2,1)S(1)}, bf16[256,256]{1,0:T(8,128)(2,1)S(1)}, u32[]{:S(2)}, u32[]{:S(2)}) collective-permute-start(bf16[256,256]{1,0:T(8,128)(2,1)S(1)} %get-tuple-element.14.refs_0_), channel_id=1, source_target_pairs={{0,4},{1,5},{2,6},{3,7},{4,0},{5,1},{6,2},{7,3},{8,12},{9,13},{10,... | collective-permute-start | bytes 393224 | tf_op jit(solution)/shard_map/ppermute | solution.py:256
  20.7 12.5 %collective-permute-start.5 = (bf16[256,256]{1,0:T(8,128)(2,1)S(1)}, bf16[256,256]{1,0:T(8,128)(2,1)S(1)}, u32[]{:S(2)}, u32[]{:S(2)}) collective-permute-start(bf16[256,256]{1,0:T(8,128)(2,1)S(1)} %get-tuple-element.14.refs_0_), channel_id=1, source_target_pairs={{0,8},{1,9},{2,10},{3,11},{4,12},{5,13},{6,14},{7,15},{8,0},{9,1},... | collective-permute-start | bytes 393224 | tf_op jit(solution)/shard_map/ppermute | solution.py:256
  22.0 16.9 %collective-permute-start.6 = (bf16[256,256]{1,0:T(8,128)(2,1)S(1)}, bf16[256,256]{1,0:T(8,128)(2,1)S(1)}, u32[]{:S(2)}, u32[]{:S(2)}) collective-permute-start(bf16[256,256]{1,0:T(8,128)(2,1)S(1)} %get-tuple-element.14.refs_0_), channel_id=1, source_target_pairs={{0,12},{1,13},{2,14},{3,15},{4,8},{5,9},{6,10},{7,11},{8,4},{9,5},... | collective-permute-start | bytes 393224 | tf_op jit(solution)/shard_map/ppermute | solution.py:256
  39.5 4.3 %copy-start = (bf16[4,16,128,128]{3,2,1,0:T(8,128)(2,1)S(1)}, bf16[4,16,128,128]{3,2,1,0:T(8,128)(2,1)}, u32[]{:S(2)}) copy-start(bf16[4,16,128,128]{3,2,1,0:T(8,128)(2,1)} %coupling_ref.1) | copy-start | bytes 6291460
  39.5 4.3 %copy-start.2 = (bf16[4,128,128]{2,1,0:T(8,128)(2,1)S(1)}, bf16[4,128,128]{2,1,0:T(8,128)(2,1)}, u32[]{:S(2)}) copy-start(bf16[4,128,128]{2,1,0:T(8,128)(2,1)} %transfer_ref.3) | copy-start | bytes 393220
  39.6 4.3 %copy-start.5 = (bf16[1,8,128,128]{3,2,1,0:T(8,128)(2,1)S(1)}, bf16[1,8,128,128]{3,2,1,0:T(8,128)(2,1)}, u32[]{:S(2)}) copy-start(bf16[1,8,128,128]{3,2,1,0:T(8,128)(2,1)} %coarse_coupling_ref.1) | copy-start | bytes 786436
  39.6 4.3 %copy-start.6 = (bf16[4,256,128]{2,1,0:T(8,128)(2,1)S(1)}, bf16[4,256,128]{2,1,0:T(8,128)(2,1)}, u32[]{:S(2)}) copy-start(bf16[4,256,128]{2,1,0:T(8,128)(2,1)} %row_ref.1) | copy-start | bytes 786436
  39.6 4.3 %copy-start.9 = (s32[4,16]{1,0:T(4,128)S(1)}, s32[4,16]{1,0:T(4,128)}, u32[]{:S(2)}) copy-start(s32[4,16]{1,0:T(4,128)} %far_list_ref.1) | copy-start | bytes 772
  39.6 4.3 %copy-start.12 = (s32[1,8]{1,0:T(1,128)S(1)}, s32[1,8]{1,0:T(1,128)}, u32[]{:S(2)}) copy-start(s32[1,8]{1,0:T(1,128)} %coarse_list_ref.1) | copy-start | bytes 100
  39.6 4.2 %collective-permute-start.7 = (bf16[1536,256]{1,0:T(8,128)(2,1)S(1)}, bf16[1536,256]{1,0:T(8,128)(2,1)S(1)}, u32[]{:S(2)}, u32[]{:S(2)}) collective-permute-start(bf16[1536,256]{1,0:T(8,128)(2,1)S(1)} %pass.1.mine_ref), channel_id=1, source_target_pairs={{0,1},{1,0},{2,3},{3,2},{4,5},{5,4},{6,7},{7,6},{8,9},{9,8},{10,11... | collective-permute-start | bytes 2359304 | tf_op jit(solution)/shard_map/ppermute | solution.py:256

commit v6 on v4

v6 whole, which is shorter than its diff:
```python
import jax
import jax.numpy as jnp
from jax import lax
from jax.experimental import pallas as pl
from jax.experimental.pallas import tpu as pltpu
from jax.sharding import PartitionSpec as P

GROUP = 16
CHUNK = 4
AHEAD = 4
MIB = 2**20

VMEM = pl.BlockSpec(memory_space=pltpu.VMEM)
SMEM = pl.BlockSpec(memory_space=pltpu.SMEM)
ANY = pl.BlockSpec(memory_space=pl.ANY)


def dot(a, b):
    return jnp.dot(a, b, preferred_element_type=jnp.float32)


def dot_t(a, b):
    return lax.dot_general(
        a, b, (((0,), (0,)), ((), ())), preferred_element_type=jnp.float32
    )


def rows_at(index, rows):
    return pl.ds(pl.multiple_of(index * rows, rows), rows)


def up_kernel(
    source_hbm, col_hbm, transfer_hbm,
    share_ref, parent_ref,
    col, transfer, sems,
):
    leaves, rows, rank = col.shape
    copies = []
    for leaf in range(leaves):
        panel = pl.ds(leaf * rows, rows)
        for n, (source, target) in enumerate((
            (source_hbm.at[panel], share_ref.at[panel]),
            (col_hbm.at[leaf], col.at[leaf]),
            (transfer_hbm.at[leaf], transfer.at[leaf]),
        )):
            copies.append(pltpu.make_async_copy(source, target, sems.at[leaf, n]))
            copies[-1].start()
    total = None
    for leaf in range(leaves):
        for copy in copies[3 * leaf:3 * leaf + 3]:
            copy.wait()
        coef = dot_t(col[leaf], share_ref[pl.ds(leaf * rows, rows), :]).astype(jnp.bfloat16)
        share_ref[pl.ds(leaves * rows + leaf * rank, rank), :] = coef
        term = dot_t(transfer[leaf], coef)
        total = term if total is None else total + term
    parent_ref[...] = total.astype(jnp.bfloat16)


def pair_kernel(own_ref, other_ref, share_ref, _, pair_ref, coef_ref, source_ref):
    rank = own_ref.shape[0]
    rows = source_ref.shape[0]
    coef_ref[...] = share_ref[pl.ds(rows, coef_ref.shape[0]), :]
    source_ref[...] = share_ref[pl.ds(0, rows), :]
    pair_ref[pl.ds(0, rank), :] = own_ref[...]
    pair_ref[pl.ds(rank, rank), :] = other_ref[...]


def join_kernel(*refs):
    *pieces, _, out_ref = refs
    at = 0
    for ref in pieces:
        out_ref[pl.ds(at, ref.shape[0]), :] = ref[...]
        at += ref.shape[0]


def pick_kernel(list_ref, level_ref, layer_ref, out_ref):
    place = lax.div(list_ref[0, 0], list_ref.shape[0])
    corner = place & 3
    level = (corner == 0) | (corner == 3)
    out_ref[...] = jnp.where(level, level_ref[...], layer_ref[...])


def near_kernel(
    list_ref, count_ref, blocks_hbm, own_ref, share_ref, across_ref,
    near_ref,
    blocks, panels, block_sems, panel_sems,
):
    leaves, slots, rows, _ = blocks.shape
    chunks = slots // CHUNK
    size = leaves * rows
    place = lax.div(list_ref[0, 0], leaves)

    def live(step):
        return step % chunks * CHUNK < count_ref[step // chunks]

    def block_copy(step):
        leaf, chunk = step // chunks, step % chunks
        where = pl.ds(chunk * CHUNK, CHUNK)
        return pltpu.make_async_copy(
            blocks_hbm.at[leaf, where], blocks.at[leaf, where], block_sems.at[leaf, chunk]
        )

    def start(step):
        if step < leaves * chunks:
            @pl.when(live(step))
            def _():
                block_copy(step).start()

    pairs = [
        pltpu.make_async_copy(
            ref.at[pl.ds(0, size)], panels.at[pl.ds(which * size, size)], panel_sems.at[which]
        )
        for which, ref in enumerate((own_ref, share_ref, across_ref))
    ]
    for copy in pairs:
        copy.start()
    for step in range(AHEAD):
        start(step)
    panels[pl.ds(3 * size, rows), :] = jnp.zeros((rows, panels.shape[1]), panels.dtype)
    for copy in pairs:
        copy.wait()

    def panel_of(leaf, slot):
        column = list_ref[leaf, slot]
        which = jnp.minimum(lax.div(column, leaves) ^ place, 2)
        index = which * leaves + (column & (leaves - 1))
        index = jnp.where(slot < count_ref[leaf], index, 3 * leaves)
        return panels[rows_at(index, rows), :]

    for step in range(leaves * chunks):
        leaf, chunk = step // chunks, step % chunks
        start(step + AHEAD)

        @pl.when(live(step))
        def _():
            block_copy(step).wait()
            total = None if chunk == 0 else near_ref[leaf]
            for slot in range(chunk * CHUNK, (chunk + 1) * CHUNK):
                term = dot(blocks[leaf, slot], panel_of(leaf, slot))
                total = term if total is None else total + term
            near_ref[leaf] = total


def down_kernel(
    far_list_ref, coarse_list_ref, near_list_ref,
    transfer_ref, coupling_ref, coarse_coupling_ref, row_ref, near_ref,
    level_ref, layer_ref, share_ref, passed_ref, mine_ref, theirs_ref,
    out_ref,
    coefs, sems,
):
    leaves, slots, rank, _ = coupling_ref.shape
    rows = row_ref.shape[1]
    size = leaves * rank
    place = lax.div(near_list_ref[0, 0], leaves)
    copies = [
        pltpu.make_async_copy(
            ref.at[pl.ds(ref.shape[0] - size, size)], coefs.at[pl.ds(n * size, size)], sems.at[n]
        )
        for n, ref in enumerate((level_ref, layer_ref, share_ref, passed_ref))
    ]
    for copy in copies:
        copy.start()

    local = place & (GROUP - 1)
    total = None
    for slot in range(coarse_list_ref.shape[1]):
        flip = (coarse_list_ref[0, slot] & (GROUP - 1)) ^ local
        where = rows_at(flip >> 1, rank)
        panel = jnp.where((flip & 1) == 0, mine_ref[where, :], theirs_ref[where, :])
        term = dot(coarse_coupling_ref[0, slot], panel)
        total = term if total is None else total + term
    high = total.astype(jnp.bfloat16)
    low = (total - high.astype(jnp.float32)).astype(jnp.bfloat16)
    coarse = jnp.concatenate([high, low], axis=0)

    beyond = jnp.where((place & 2) == 0, place - 2, place + 2)
    for copy in copies:
        copy.wait()

    def panel_of(leaf, slot):
        column = far_list_ref[leaf, slot]
        cluster = lax.div(column, leaves)
        which = jnp.where(
            cluster == (place ^ 2), 0,
            jnp.where(cluster == beyond, 1, jnp.where(cluster == (place ^ 1), 2, 3)),
        )
        return coefs[rows_at(which * leaves + column - cluster * leaves, rank), :]

    for leaf in range(leaves):
        matrix = transfer_ref[leaf]
        total = dot(jnp.concatenate([matrix, matrix], axis=1), coarse)
        for slot in range(0, slots, 2):
            both = jnp.concatenate([coupling_ref[leaf, slot], coupling_ref[leaf, slot + 1]], axis=1)
            panels = jnp.concatenate([panel_of(leaf, slot), panel_of(leaf, slot + 1)], axis=0)
            total = total + dot(both, panels)
        result = near_ref[leaf] + dot(row_ref[leaf], total.astype(jnp.bfloat16))
        out_ref[pl.ds(leaf * rows, rows), :] = result.astype(jnp.bfloat16)


def call(kernel, name, outs, specs, args, scratch=(), flops=0, moved=0, limit=4):
    many = isinstance(outs, tuple)
    return pl.pallas_call(
        kernel,
        out_shape=outs,
        in_specs=specs,
        out_specs=(VMEM,) * len(outs) if many else VMEM,
        scratch_shapes=list(scratch),
        cost_estimate=pl.CostEstimate(flops=flops, bytes_accessed=moved, transcendentals=0),
        compiler_params=pltpu.CompilerParams(vmem_limit_bytes=limit * MIB),
        name=name,
    )(*args)


def body(
    source,
    near_blocks,
    near_list,
    near_count,
    col_basis,
    row_basis,
    transfer,
    far_list,
    far_coupling,
    coarse_list,
    coarse_coupling,
):
    leaves, slots, rows, _ = near_blocks.shape
    rank = col_basis.shape[2]
    width = source.shape[1]
    count = lax.axis_size("row")
    far_slots = far_coupling.shape[1]

    def send(value, target):
        pairs = [(d, target(d)) for d in range(count) if 0 <= target(d) < count]
        return lax.ppermute(value, "row", pairs)

    def panel(blocks, dtype=jnp.bfloat16):
        return jax.ShapeDtypeStruct((blocks * rank, width), dtype)

    share, parent = call(
        up_kernel, "up",
        (jax.ShapeDtypeStruct((leaves * (rows + rank), width), jnp.bfloat16), panel(1)),
        [ANY] * 3, (source, col_basis, transfer),
        scratch=[
            pltpu.VMEM(col_basis.shape, jnp.bfloat16),
            pltpu.VMEM(transfer.shape, jnp.bfloat16),
            pltpu.SemaphoreType.DMA((leaves, 3)),
        ],
        flops=2 * leaves * rank * width * (rows + rank),
        moved=2 * leaves * rows * (width + rank), limit=16,
    )
    parent_level = send(parent, lambda d: d ^ 2)
    share_other = send(share, lambda d: d ^ 1)

    pair, coef, panels = call(
        pair_kernel, "pair",
        (panel(2), panel(leaves), jax.ShapeDtypeStruct(source.shape, jnp.bfloat16)),
        [VMEM] * 3 + [ANY], (parent, parent_level, share, share_other),
    )
    level = send(coef, lambda d: d ^ 2)
    across = send(panels, lambda d: d + 1 if d & 1 else d - 1)
    layers = [send(pair, lambda d, bit=bit: d ^ bit) for bit in (4, 8, 12)]

    layer = send(level, lambda d: d - 4 if d & 2 else d + 4)
    near = call(
        near_kernel, "near", jax.ShapeDtypeStruct((leaves, rows, width), jnp.float32),
        [SMEM, SMEM] + [ANY] * 4,
        (near_list, near_count, near_blocks, share, share_other, across),
        scratch=[
            pltpu.VMEM(near_blocks.shape, jnp.bfloat16),
            pltpu.VMEM(((3 * leaves + 1) * rows, width), jnp.bfloat16),
            pltpu.SemaphoreType.DMA((leaves, slots // CHUNK)),
            pltpu.SemaphoreType.DMA((3,)),
        ],
        flops=0,
        limit=48,
    )
    mine = call(join_kernel, "mine", panel(GROUP // 2), [VMEM] * 4 + [ANY], (pair, *layers, near))
    theirs = send(mine, lambda d: d ^ 1)
    picked = call(
        pick_kernel, "pick", panel(leaves), [SMEM] + [VMEM] * 2, (near_list, level, layer)
    )
    passed = send(picked, lambda d: d ^ 1)
    return call(
        down_kernel, "down", jax.ShapeDtypeStruct(source.shape, jnp.bfloat16),
        [SMEM] * 3 + [VMEM] * 5 + [ANY] * 4 + [VMEM] * 2,
        (
            far_list, coarse_list, near_list, transfer, far_coupling, coarse_coupling, row_basis,
            near, level, layer, share_other, passed, mine, theirs,
        ),
        scratch=[
            pltpu.VMEM((4 * leaves * rank, width), jnp.bfloat16),
            pltpu.SemaphoreType.DMA((4,)),
        ],
        flops=2 * leaves * (far_slots + 4) * rank * rank * width,
        moved=2 * leaves * far_slots * rank * rank, limit=12,
    )


def solution(mesh):
    placed = (
        P(("clip", "row"), None),
        P(("clip", "row"), None, None, None),
        P(("clip", "row"), None),
        P(("clip", "row")),
        P(("clip", "row"), None, None),
        P(("clip", "row"), None, None),
        P(("clip", "row"), None, None),
        P(("clip", "row"), None),
        P(("clip", "row"), None, None, None),
        P(("clip", "row"), None),
        P(("clip", "row"), None, None, None),
    )
    return jax.shard_map(
        body, mesh=mesh, in_specs=placed, out_specs=P(("clip", "row"), None), check_vma=False
    )
```

time: 52.4 us -> 50.3 us (0.960)
  the two profiles are of different devices: /device:TPU:6 before, /device:TPU:1 now
where the time goes in v6:
time: 50.3 us; the launch traced here: 50 us
  waiting for transfers between devices  16.4 us (33%)
  starting transfers between devices  16 us (32%)
  Pallas kernels  13.1 us (26%)
  local copies, waits for them, and re-layouts  4.4 us (9%)
    ppermute x10, waiting for transfers between devices, send(): return lax.ppermute(value, 'row', pairs)  16.4 us
    ppermute x10, starting transfers between devices, send(): return lax.ppermute(value, 'row', pairs)  16 us
    pallas_call x6, Pallas kernels, call(): pl.pallas_call(kernel, out_shape=outs, in_specs=specs, out_specs=(VMEM,)...  13.1 us
    unnamed x22, local copies, waits for them, and re-layouts  4.4 us
  transfers between devices with their start and end apart: 10, of which 3 were waited for; matrix products, arithmetic and copies ran while one was open for 0% of the time, Pallas kernels for 14%

profile of v6, /device:TPU:1, one launch (start us, length us, event | category | flops | bytes accessed | tf_op | source)
XLA Modules:
  0.0 50.0 jit_solution(13257149975662432050)
XLA Ops:
  0.0 0.0 copy-start
  0.0 0.0 copy-start.1
  0.0 1.1 %copy-done.1 = bf16[4,128,128]{2,1,0:T(8,128)(2,1)S(1)} copy-done((bf16[4,128,128]{2,1,0:T(8,128)(2,1)S(1)}, bf16[4,128,128]{2,1,0:T(8,128)(2,1)}, u32[]{:S(2)}) %copy-start.1) | copy-done | bytes 131096
  1.1 0.0 copy-start.3
  1.1 1.0 %copy-done.3 = bf16[1024,256]{1,0:T(8,128)(2,1)S(1)} copy-done((bf16[1024,256]{1,0:T(8,128)(2,1)S(1)}, bf16[1024,256]{1,0:T(8,128)(2,1)}, u32[]{:S(2)}) %copy-start.3) | copy-done | bytes 524312
  2.1 0.0 copy-start.4
  2.1 0.9 %copy-done.4 = bf16[4,256,128]{2,1,0:T(8,128)(2,1)S(1)} copy-done((bf16[4,256,128]{2,1,0:T(8,128)(2,1)S(1)}, bf16[4,256,128]{2,1,0:T(8,128)(2,1)}, u32[]{:S(2)}) %copy-start.4) | copy-done | bytes 262168
  3.0 0.0 copy-start.2
  3.1 0.0 copy-start.5
  3.1 0.0 copy-start.6
  3.1 2.4 %up.1 = (bf16[1536,256]{1,0:T(8,128)(2,1)S(1)}, bf16[128,256]{1,0:T(8,128)(2,1)S(1)}) custom-call(bf16[1024,256]{1,0:T(8,128)(2,1)S(1)} %copy-done.3, bf16[4,256,128]{2,1,0:T(8,128)(2,1)S(1)} %copy-done.4, bf16[4,128,128]{2,1,0:T(8,128)(2,1)S(1)} %copy-done.1), custom_call_target="tpu_custom_call" | custom-call | flops 100663296 | bytes 786432 | tf_op jit(solution)/shard_map/up/pallas_call | solution.py:202
  5.4 0.1 collective-permute-start
  5.5 2.7 %collective-permute-start.1 = (bf16[128,256]{1,0:T(8,128)(2,1)S(1)}, bf16[128,256]{1,0:T(8,128)(2,1)S(1)}, u32[]{:S(2)}, u32[]{:S(2)}) collective-permute-start(bf16[128,256]{1,0:T(8,128)(2,1)S(1)} %get-tuple-element.11.own_ref), channel_id=1, source_target_pairs={{0,2},{1,3},{2,0},{3,1},{4,6},{5,7},{6,4},{7,5},{8,10},{9,11},{10,... | collective-permute-start | bytes 196616 | tf_op jit(solution)/shard_map/ppermute | solution.py:235
  8.2 2.4 %collective-permute-done.1.other_ref = bf16[128,256]{1,0:T(8,128)(2,1)S(1)} collective-permute-done((bf16[128,256]{1,0:T(8,128)(2,1)S(1)}, bf16[128,256]{1,0:T(8,128)(2,1)S(1)}, u32[]{:S(2)}, u32[]{:S(2)}) %collective-permute-start.1) | collective-permute-done | bytes 65568 | tf_op jit(solution)/shard_map/ppermute | solution.py:235
  10.6 0.0 collective-permute-done._.share_ref
  10.6 0.1 pair.1
  10.7 3.9 %collective-permute-start.2 = (bf16[1024,256]{1,0:T(8,128)(2,1)S(1)}, bf16[1024,256]{1,0:T(8,128)(2,1)S(1)}, u32[]{:S(2)}, u32[]{:S(2)}) collective-permute-start(bf16[1024,256]{1,0:T(8,128)(2,1)S(1)} %get-tuple-element.12), channel_id=1, source_target_pairs={{1,2},{2,1},{3,4},{4,3},{5,6},{6,5},{7,8},{8,7},{9,10},{10,9},{11,... | collective-permute-start | bytes 1572872 | tf_op jit(solution)/shard_map/ppermute | solution.py:235
  14.6 1.3 %collective-permute-start.3 = (bf16[512,256]{1,0:T(8,128)(2,1)S(1)}, bf16[512,256]{1,0:T(8,128)(2,1)S(1)}, u32[]{:S(2)}, u32[]{:S(2)}) collective-permute-start(bf16[512,256]{1,0:T(8,128)(2,1)S(1)} %get-tuple-element.13), channel_id=1, source_target_pairs={{0,2},{1,3},{2,0},{3,1},{4,6},{5,7},{6,4},{7,5},{8,10},{9,11},{10,... | collective-permute-start | bytes 786440 | tf_op jit(solution)/shard_map/ppermute | solution.py:235
  15.9 1.3 %collective-permute-start.6 = (bf16[256,256]{1,0:T(8,128)(2,1)S(1)}, bf16[256,256]{1,0:T(8,128)(2,1)S(1)}, u32[]{:S(2)}, u32[]{:S(2)}) collective-permute-start(bf16[256,256]{1,0:T(8,128)(2,1)S(1)} %get-tuple-element.14.refs_0_), channel_id=1, source_target_pairs={{0,4},{1,5},{2,6},{3,7},{4,0},{5,1},{6,2},{7,3},{8,12},{9,13},{10,... | collective-permute-start | bytes 393224 | tf_op jit(solution)/shard_map/ppermute | solution.py:235
  17.2 1.1 %collective-permute-start.7 = (bf16[256,256]{1,0:T(8,128)(2,1)S(1)}, bf16[256,256]{1,0:T(8,128)(2,1)S(1)}, u32[]{:S(2)}, u32[]{:S(2)}) collective-permute-start(bf16[256,256]{1,0:T(8,128)(2,1)S(1)} %get-tuple-element.14.refs_0_), channel_id=1, source_target_pairs={{0,8},{1,9},{2,10},{3,11},{4,12},{5,13},{6,14},{7,15},{8,0},{9,1},... | collective-permute-start | bytes 393224 | tf_op jit(solution)/shard_map/ppermute | solution.py:235
  18.4 1.1 %collective-permute-start.8 = (bf16[256,256]{1,0:T(8,128)(2,1)S(1)}, bf16[256,256]{1,0:T(8,128)(2,1)S(1)}, u32[]{:S(2)}, u32[]{:S(2)}) collective-permute-start(bf16[256,256]{1,0:T(8,128)(2,1)S(1)} %get-tuple-element.14.refs_0_), channel_id=1, source_target_pairs={{0,12},{1,13},{2,14},{3,15},{4,8},{5,9},{6,10},{7,11},{8,4},{9,5},... | collective-permute-start | bytes 393224 | tf_op jit(solution)/shard_map/ppermute | solution.py:235
  19.5 12.5 %collective-permute-done.3.level_ref = bf16[512,256]{1,0:T(8,128)(2,1)S(1)} collective-permute-done((bf16[512,256]{1,0:T(8,128)(2,1)S(1)}, bf16[512,256]{1,0:T(8,128)(2,1)S(1)}, u32[]{:S(2)}, u32[]{:S(2)}) %collective-permute-start.3) | collective-permute-done | bytes 262176 | tf_op jit(solution)/shard_map/ppermute | solution.py:235
  32.0 3.2 %collective-permute-start.4 = (bf16[512,256]{1,0:T(8,128)(2,1)S(1)}, bf16[512,256]{1,0:T(8,128)(2,1)S(1)}, u32[]{:S(2)}, u32[]{:S(2)}) collective-permute-start(bf16[512,256]{1,0:T(8,128)(2,1)S(1)} %collective-permute-done.3.level_ref), channel_id=1, source_target_pairs={{0,4},{1,5},{4,8},{5,9},{6,2},{7,3},{8,12},{9,13},{10,6},{11,7},{1... | collective-permute-start | bytes 786440 | tf_op jit(solution)/shard_map/ppermute | solution.py:235
  35.2 0.0 collective-permute-done.2.across_ref
  35.2 0.0 copy-start.7
  35.2 0.7 %copy-done.7 = s32[4,16]{1,0:T(4,128)S(1)} copy-done((s32[4,16]{1,0:T(4,128)S(1)}, s32[4,16]{1,0:T(4,128)}, u32[]{:S(2)}) %copy-start.7) | copy-done | bytes 280
  35.9 0.0 copy-start.9
  35.9 0.7 %copy-done.9 = s32[4]{0:T(128)S(1)} copy-done((s32[4]{0:T(128)S(1)}, s32[4]{0:T(128)}, u32[]{:S(2)}) %copy-start.9) | copy-done | bytes 40
  36.5 0.0 copy-start.8
  36.5 0.0 copy-start.10
  36.5 6.6 %near.1.refs_4_.near_ref = f32[4,256,256]{2,1,0:T(8,128)S(1)} custom-call(s32[4,16]{1,0:T(4,128)S(1)} %copy-done.7, s32[4]{0:T(128)S(1)} %copy-done.9, bf16[4,16,256,256]{3,2,1,0:T(8,128)(2,1)} %blocks_hbm.1, bf16[1536,256]{1,0:T(8,128)(2,1)S(1)} %get-tuple-element.10.share_ref.own_ref, bf16[1536,256]{1,0:T(8,128)(2,1)S(1)} %collective-permute-done._.share_ref, ...), custom_call_target="tpu_custom_call" | custom-call | tf_op jit(solution)/shard_map/near/pallas_call | solution.py:202
  43.2 0.0 collective-permute-done.6.refs_1_
  43.2 0.0 collective-permute-done.7.refs_2_
  43.2 0.0 collective-permute-done.8.refs_3_
  43.2 1.1 %collective-permute-start.9 = (bf16[1024,256]{1,0:T(8,128)(2,1)S(1)}, bf16[1024,256]{1,0:T(8,128)(2,1)S(1)}, u32[]{:S(2)}, u32[]{:S(2)}) collective-permute-start(bf16[1024,256]{1,0:T(8,128)(2,1)S(1)} %mine.1.mine_ref), channel_id=1, source_target_pairs={{0,1},{1,0},{2,3},{3,2},{4,5},{5,4},{6,7},{7,6},{8,9},{9,8},{10,11... | collective-permute-start | bytes 1572872 | tf_op jit(solution)/shard_map/ppermute | solution.py:235
  44.3 0.0 collective-permute-done.4.layer_ref
  44.3 0.6 %pick.1 = bf16[512,256]{1,0:T(8,128)(2,1)S(1)} custom-call(s32[4,16]{1,0:T(4,128)S(1)} %copy-done.7, bf16[512,256]{1,0:T(8,128)(2,1)S(1)} %collective-permute-done.3.level_ref, bf16[512,256]{1,0:T(8,128)(2,1)S(1)} %collective-permute-done.4.layer_ref), custom_call_target="tpu_custom_call" | custom-call | tf_op jit(solution)/shard_map/pick/pallas_call | solution.py:202
  44.9 0.1 collective-permute-start.5
  45.0 1.5 %collective-permute-done.5.passed_ref = bf16[512,256]{1,0:T(8,128)(2,1)S(1)} collective-permute-done((bf16[512,256]{1,0:T(8,128)(2,1)S(1)}, bf16[512,256]{1,0:T(8,128)(2,1)S(1)}, u32[]{:S(2)}, u32[]{:S(2)}) %collective-permute-start.5) | collective-permute-done | bytes 262176 | tf_op jit(solution)/shard_map/ppermute | solution.py:235
  46.5 0.0 collective-permute-done.9.theirs_ref
  46.5 0.0 copy-done
  46.5 0.0 copy-done.2
  46.5 0.0 copy-done.5
  46.6 0.0 copy-done.6
  46.6 0.0 copy-done.8
  46.6 0.0 copy-done.10
  46.6 3.5 %down.1 = bf16[1024,256]{1,0:T(8,128)(2,1)} custom-call(s32[4,16]{1,0:T(4,128)S(1)} %copy-done.8, s32[1,8]{1,0:T(1,128)S(1)} %copy-done.10, s32[4,16]{1,0:T(4,128)S(1)} %copy-done.7, bf16[4,128,128]{2,1,0:T(8,128)(2,1)S(1)} %copy-done.2, bf16[4,16,128,128]{3,2,1,0:T(8,128)(2,1)S(1)} %copy-done, bf16[1,8,128,128]{3,2,1,0:T(8,128)(2,1)S(1)} %copy-done.5, ...), custom_call_target="tpu_custom_call" | custom-call | flops 671088640 | bytes 2097152 | tf_op jit(solution)/shard_map/down/pallas_call | solution.py:202
  (1 shorter events, 0.0 us)
Async XLA Ops:
  0.0 46.5 %copy-start = (bf16[4,16,128,128]{3,2,1,0:T(8,128)(2,1)S(1)}, bf16[4,16,128,128]{3,2,1,0:T(8,128)(2,1)}, u32[]{:S(2)}) copy-start(bf16[4,16,128,128]{3,2,1,0:T(8,128)(2,1)} %coupling_ref.1) | copy-start | bytes 6291460
  0.0 1.1 %copy-start.1 = (bf16[4,128,128]{2,1,0:T(8,128)(2,1)S(1)}, bf16[4,128,128]{2,1,0:T(8,128)(2,1)}, u32[]{:S(2)}) copy-start(bf16[4,128,128]{2,1,0:T(8,128)(2,1)} %transfer_ref.1) | copy-start | bytes 393220
  1.1 1.0 %copy-start.3 = (bf16[1024,256]{1,0:T(8,128)(2,1)S(1)}, bf16[1024,256]{1,0:T(8,128)(2,1)}, u32[]{:S(2)}) copy-start(bf16[1024,256]{1,0:T(8,128)(2,1)} %source_hbm.1) | copy-start | bytes 1572868
  2.1 0.9 %copy-start.4 = (bf16[4,256,128]{2,1,0:T(8,128)(2,1)S(1)}, bf16[4,256,128]{2,1,0:T(8,128)(2,1)}, u32[]{:S(2)}) copy-start(bf16[4,256,128]{2,1,0:T(8,128)(2,1)} %col_hbm.1) | copy-start | bytes 786436
  3.0 43.5 %copy-start.2 = (bf16[4,128,128]{2,1,0:T(8,128)(2,1)S(1)}, bf16[4,128,128]{2,1,0:T(8,128)(2,1)}, u32[]{:S(2)}) copy-start(bf16[4,128,128]{2,1,0:T(8,128)(2,1)} %transfer_ref.1) | copy-start | bytes 393220
  3.1 43.5 %copy-start.5 = (bf16[1,8,128,128]{3,2,1,0:T(8,128)(2,1)S(1)}, bf16[1,8,128,128]{3,2,1,0:T(8,128)(2,1)}, u32[]{:S(2)}) copy-start(bf16[1,8,128,128]{3,2,1,0:T(8,128)(2,1)} %coarse_coupling_ref.1) | copy-start | bytes 786436
  3.1 43.5 %copy-start.6 = (bf16[4,256,128]{2,1,0:T(8,128)(2,1)S(1)}, bf16[4,256,128]{2,1,0:T(8,128)(2,1)}, u32[]{:S(2)}) copy-start(bf16[4,256,128]{2,1,0:T(8,128)(2,1)} %row_ref.1) | copy-start | bytes 786436
  5.4 5.2 %collective-permute-start = (bf16[1536,256]{1,0:T(8,128)(2,1)S(1)}, bf16[1536,256]{1,0:T(8,128)(2,1)S(1)}, u32[]{:S(2)}, u32[]{:S(2)}) collective-permute-start(bf16[1536,256]{1,0:T(8,128)(2,1)S(1)} %get-tuple-element.10.share_ref.own_ref), channel_id=1, source_target_pairs={{0,1},{1,0},{2,3},{3,2},{4,5},{5,4},{6,7},{7,6},{8,9},{9,8},{10,11... | collective-permute-start | bytes 2359304 | tf_op jit(solution)/shard_map/ppermute | solution.py:235
  5.5 5.1 %collective-permute-start.1 = (bf16[128,256]{1,0:T(8,128)(2,1)S(1)}, bf16[128,256]{1,0:T(8,128)(2,1)S(1)}, u32[]{:S(2)}, u32[]{:S(2)}) collective-permute-start(bf16[128,256]{1,0:T(8,128)(2,1)S(1)} %get-tuple-element.11.own_ref), channel_id=1, source_target_pairs={{0,2},{1,3},{2,0},{3,1},{4,6},{5,7},{6,4},{7,5},{8,10},{9,11},{10,... | collective-permute-start | bytes 196616 | tf_op jit(solution)/shard_map/ppermute | solution.py:235
  10.7 24.5 %collective-permute-start.2 = (bf16[1024,256]{1,0:T(8,128)(2,1)S(1)}, bf16[1024,256]{1,0:T(8,128)(2,1)S(1)}, u32[]{:S(2)}, u32[]{:S(2)}) collective-permute-start(bf16[1024,256]{1,0:T(8,128)(2,1)S(1)} %get-tuple-element.12), channel_id=1, source_target_pairs={{1,2},{2,1},{3,4},{4,3},{5,6},{6,5},{7,8},{8,7},{9,10},{10,9},{11,... | collective-permute-start | bytes 1572872 | tf_op jit(solution)/shard_map/ppermute | solution.py:235
  14.6 17.3 %collective-permute-start.3 = (bf16[512,256]{1,0:T(8,128)(2,1)S(1)}, bf16[512,256]{1,0:T(8,128)(2,1)S(1)}, u32[]{:S(2)}, u32[]{:S(2)}) collective-permute-start(bf16[512,256]{1,0:T(8,128)(2,1)S(1)} %get-tuple-element.13), channel_id=1, source_target_pairs={{0,2},{1,3},{2,0},{3,1},{4,6},{5,7},{6,4},{7,5},{8,10},{9,11},{10,... | collective-permute-start | bytes 786440 | tf_op jit(solution)/shard_map/ppermute | solution.py:235
  15.9 27.2 %collective-permute-start.6 = (bf16[256,256]{1,0:T(8,128)(2,1)S(1)}, bf16[256,256]{1,0:T(8,128)(2,1)S(1)}, u32[]{:S(2)}, u32[]{:S(2)}) collective-permute-start(bf16[256,256]{1,0:T(8,128)(2,1)S(1)} %get-tuple-element.14.refs_0_), channel_id=1, source_target_pairs={{0,4},{1,5},{2,6},{3,7},{4,0},{5,1},{6,2},{7,3},{8,12},{9,13},{10,... | collective-permute-start | bytes 393224 | tf_op jit(solution)/shard_map/ppermute | solution.py:235
  17.2 25.9 %collective-permute-start.7 = (bf16[256,256]{1,0:T(8,128)(2,1)S(1)}, bf16[256,256]{1,0:T(8,128)(2,1)S(1)}, u32[]{:S(2)}, u32[]{:S(2)}) collective-permute-start(bf16[256,256]{1,0:T(8,128)(2,1)S(1)} %get-tuple-element.14.refs_0_), channel_id=1, source_target_pairs={{0,8},{1,9},{2,10},{3,11},{4,12},{5,13},{6,14},{7,15},{8,0},{9,1},... | collective-permute-start | bytes 393224 | tf_op jit(solution)/shard_map/ppermute | solution.py:235
  18.4 24.8 %collective-permute-start.8 = (bf16[256,256]{1,0:T(8,128)(2,1)S(1)}, bf16[256,256]{1,0:T(8,128)(2,1)S(1)}, u32[]{:S(2)}, u32[]{:S(2)}) collective-permute-start(bf16[256,256]{1,0:T(8,128)(2,1)S(1)} %get-tuple-element.14.refs_0_), channel_id=1, source_target_pairs={{0,12},{1,13},{2,14},{3,15},{4,8},{5,9},{6,10},{7,11},{8,4},{9,5},... | collective-permute-start | bytes 393224 | tf_op jit(solution)/shard_map/ppermute | solution.py:235
  32.0 12.4 %collective-permute-start.4 = (bf16[512,256]{1,0:T(8,128)(2,1)S(1)}, bf16[512,256]{1,0:T(8,128)(2,1)S(1)}, u32[]{:S(2)}, u32[]{:S(2)}) collective-permute-start(bf16[512,256]{1,0:T(8,128)(2,1)S(1)} %collective-permute-done.3.level_ref), channel_id=1, source_target_pairs={{0,4},{1,5},{4,8},{5,9},{6,2},{7,3},{8,12},{9,13},{10,6},{11,7},{1... | collective-permute-start | bytes 786440 | tf_op jit(solution)/shard_map/ppermute | solution.py:235
  35.2 0.7 %copy-start.7 = (s32[4,16]{1,0:T(4,128)S(1)}, s32[4,16]{1,0:T(4,128)}, u32[]{:S(2)}) copy-start(s32[4,16]{1,0:T(4,128)} %near_list_ref.1) | copy-start | bytes 772
  35.9 0.7 %copy-start.9 = (s32[4]{0:T(128)S(1)}, s32[4]{0:T(128)}, u32[]{:S(2)}) copy-start(s32[4]{0:T(128)} %count_ref.1) | copy-start | bytes 52
  36.5 10.0 %copy-start.8 = (s32[4,16]{1,0:T(4,128)S(1)}, s32[4,16]{1,0:T(4,128)}, u32[]{:S(2)}) copy-start(s32[4,16]{1,0:T(4,128)} %far_list_ref.1) | copy-start | bytes 772
  36.5 10.0 %copy-start.10 = (s32[1,8]{1,0:T(1,128)S(1)}, s32[1,8]{1,0:T(1,128)}, u32[]{:S(2)}) copy-start(s32[1,8]{1,0:T(1,128)} %coarse_list_ref.1) | copy-start | bytes 100
  43.2 3.3 %collective-permute-start.9 = (bf16[1024,256]{1,0:T(8,128)(2,1)S(1)}, bf16[1024,256]{1,0:T(8,128)(2,1)S(1)}, u32[]{:S(2)}, u32[]{:S(2)}) collective-permute-start(bf16[1024,256]{1,0:T(8,128)(2,1)S(1)} %mine.1.mine_ref), channel_id=1, source_target_pairs={{0,1},{1,0},{2,3},{3,2},{4,5},{5,4},{6,7},{7,6},{8,9},{9,8},{10,11... | collective-permute-start | bytes 1572872 | tf_op jit(solution)/shard_map/ppermute | solution.py:235
  44.9 1.6 %collective-permute-start.5 = (bf16[512,256]{1,0:T(8,128)(2,1)S(1)}, bf16[512,256]{1,0:T(8,128)(2,1)S(1)}, u32[]{:S(2)}, u32[]{:S(2)}) collective-permute-start(bf16[512,256]{1,0:T(8,128)(2,1)S(1)} %pick.1), channel_id=1, source_target_pairs={{0,1},{1,0},{2,3},{3,2},{4,5},{5,4},{6,7},{7,6},{8,9},{9,8},{10,11... | collective-permute-start | bytes 786440 | tf_op jit(solution)/shard_map/ppermute | solution.py:235

commit v7 on v5

--- a/solution.py
+++ b/solution.py
@@ -28,27 +28,27 @@
     return pl.ds(pl.multiple_of(index * rows, rows), rows)
 
 
-def up_kernel(source_ref, col_ref, transfer_ref, share_ref, lift_ref):
+def up_kernel(source_ref, col_ref, transfer_ref, share_ref, coef_ref, parent_ref):
     leaves, rows, rank = col_ref.shape
     total = None
     for leaf in range(leaves):
         panel = source_ref[pl.ds(leaf * rows, rows), :]
         share_ref[pl.ds(leaf * rows, rows), :] = panel
         coef = dot_t(col_ref[leaf], panel).astype(jnp.bfloat16)
-        lift_ref[pl.ds(leaf * rank, rank), :] = coef
+        coef_ref[pl.ds(leaf * rank, rank), :] = coef
         share_ref[pl.ds(leaves * rows + leaf * rank, rank), :] = coef
         term = dot_t(transfer_ref[leaf], coef)
         total = term if total is None else total + term
-    lift_ref[pl.ds(leaves * rank, rank), :] = total.astype(jnp.bfloat16)
-
-
-def pair_kernel(own_ref, lift_ref, share_ref, _, level_ref, pair_ref, source_ref):
-    size = level_ref.shape[0]
-    rank = own_ref.shape[0] - size
-    level_ref[...] = lift_ref[pl.ds(0, size), :]
-    pair_ref[pl.ds(0, rank), :] = own_ref[pl.ds(size, rank), :]
-    pair_ref[pl.ds(rank, rank), :] = lift_ref[pl.ds(size, rank), :]
-    source_ref[...] = share_ref[pl.ds(0, source_ref.shape[0]), :]
+    parent_ref[...] = total.astype(jnp.bfloat16)
+
+
+def join_kernel(*refs):
+    *pieces, level_ref, _, out_ref, relay_ref = refs
+    relay_ref[...] = level_ref[...]
+    at = 0
+    for ref in pieces:
+        out_ref[pl.ds(at, ref.shape[0]), :] = ref[...]
+        at += ref.shape[0]
 
 
 def pass_kernel(list_ref, *refs):
@@ -162,7 +162,7 @@
     total = None
     for slot in range(coarse_list_ref.shape[1]):
         flip = (coarse_list_ref[0, slot] & (GROUP - 1)) ^ local
-        where = rows_at(flip >> 1, rank)
+        where = rows_at((flip & 2) * 2 + (flip >> 2), rank)
         panel = jnp.where((flip & 1) == 0, mine_ref[where, :], theirs_ref[where, :])
         term = dot(coarse_coupling_ref[0, slot], panel)
         total = term if total is None else total + term
@@ -258,15 +258,17 @@
     def panel(blocks, dtype=jnp.bfloat16):
         return jax.ShapeDtypeStruct((blocks * rank, width), dtype)
 
-    share, lift = call(
+    share, coef, parent = call(
         up_kernel, "up",
-        (jax.ShapeDtypeStruct((leaves * (rows + rank), width), jnp.bfloat16), panel(leaves + 1)),
+        (jax.ShapeDtypeStruct((leaves * (rows + rank), width), jnp.bfloat16), panel(leaves), panel(1)),
         [VMEM] * 3, (source, col_basis, transfer),
         flops=2 * leaves * rank * width * (rows + rank),
         moved=2 * leaves * rows * (width + rank), limit=8,
     )
-    lift_level = send(lift, lambda d: d ^ 2)
+    layers = [send(parent, lambda d, bit=bit: d ^ bit) for bit in (4, 8, 12)]
     share_other = send(share, lambda d: d ^ 1)
+    level = send(coef, lambda d: d ^ 2)
+    across = send(source, lambda d: d + 1 if d & 1 else d - 1)
 
     picked = [
         pltpu.VMEM(near_blocks.shape, jnp.bfloat16),
@@ -284,19 +286,17 @@
         ],
         limit=48,
     )
-    level, pair, source_own = call(
-        pair_kernel, "pair", (panel(leaves), panel(2), jax.ShapeDtypeStruct(source.shape, jnp.bfloat16)),
-        [VMEM] * 3 + [ANY], (lift, lift_level, share, near),
-    )
-    across = send(source_own, lambda d: d + 1 if d & 1 else d - 1)
-    layers = [send(pair, lambda d, bit=bit: d ^ bit) for bit in (4, 8, 12)]
-    layer = send(level, lambda d: d - 4 if d & 2 else d + 4)
+    column, relay = call(
+        join_kernel, "column", (panel(GROUP // 4), panel(leaves)), [VMEM] * 5 + [ANY],
+        (parent, *layers, level, near),
+    )
+    beside = send(column, lambda d: d ^ 2)
+    layer = send(relay, lambda d: d - 4 if d & 2 else d + 4)
     mine = call(
-        pass_kernel, "pass", panel(GROUP // 2 + leaves), [SMEM] + [VMEM] * 6,
-        (near_list, pair, *layers, level, layer),
+        pass_kernel, "pass", panel(GROUP // 2 + leaves), [SMEM] + [VMEM] * 4,
+        (near_list, column, beside, level, layer),
     )
     theirs = send(mine, lambda d: d ^ 1)
-
     near = call(
         across_kernel, "across", jax.ShapeDtypeStruct((leaves, rows, width), jnp.float32),
         [SMEM] * 2 + [ANY] + [VMEM] * 2, (near_list, near_count, near_blocks, near, across),

time: 47.5 us -> 40.3 us (0.85)
  the two profiles are of different devices: /device:TPU:19 before, /device:TPU:1 now
where the time goes in v7:
time: 40.3 us; the launch traced here: 39.9 us
  starting transfers between devices  17.8 us (44%)
  Pallas kernels  14.1 us (35%)
  waiting for transfers between devices  4.48 us (11%)
  local copies, waits for them, and re-layouts  3.23 us (8%)
    ppermute x9, starting transfers between devices, send(): return lax.ppermute(value, 'row', pairs)  17.8 us
    pallas_call x6, Pallas kernels, call(): pl.pallas_call(kernel, out_shape=outs, in_specs=specs, out_specs=(VMEM,)...  14.1 us
    ppermute x9, waiting for transfers between devices, send(): return lax.ppermute(value, 'row', pairs)  4.48 us
    unnamed x24, local copies, waits for them, and re-layouts  3.23 us
  transfers between devices with their start and end apart: 9, of which 2 were waited for; matrix products, arithmetic and copies ran while one was open for 0% of the time, Pallas kernels for 23%

profile of v7, /device:TPU:1, one launch (start us, length us, event | category | flops | bytes accessed | tf_op | source)
XLA Modules:
  0.0 39.9 jit_solution(12551571497788832836)
XLA Ops:
  0.0 0.0 copy-start.1
  0.0 0.9 %copy-done.1 = bf16[4,128,128]{2,1,0:T(8,128)(2,1)S(1)} copy-done((bf16[4,128,128]{2,1,0:T(8,128)(2,1)S(1)}, bf16[4,128,128]{2,1,0:T(8,128)(2,1)}, u32[]{:S(2)}) %copy-start.1) | copy-done | bytes 131096
  0.9 0.0 copy-start.3
  0.9 0.9 %copy-done.3 = bf16[4,256,128]{2,1,0:T(8,128)(2,1)S(1)} copy-done((bf16[4,256,128]{2,1,0:T(8,128)(2,1)S(1)}, bf16[4,256,128]{2,1,0:T(8,128)(2,1)}, u32[]{:S(2)}) %copy-start.3) | copy-done | bytes 262168
  1.9 0.0 copy-start.7
  1.9 0.0 copy-start.10
  1.9 1.6 %up.1 = (bf16[1536,256]{1,0:T(8,128)(2,1)S(1)}, bf16[512,256]{1,0:T(8,128)(2,1)S(1)}, bf16[128,256]{1,0:T(8,128)(2,1)S(1)}) custom-call(bf16[1024,256]{1,0:T(8,128)(2,1)} %source_ref.1, bf16[4,256,128]{2,1,0:T(8,128)(2,1)S(1)} %copy-done.3, bf16[4,128,128]{2,1,0:T(8,128)(2,1)S(1)} %copy-done.1), custom_call_target="tpu_custom_call" | custom-call | flops 100663296 | bytes 786432 | tf_op jit(solution)/shard_map/up/pallas_call | solution.py:223
  3.4 0.1 collective-permute-start
  3.5 2.7 %collective-permute-start.2 = (bf16[512,256]{1,0:T(8,128)(2,1)S(1)}, bf16[512,256]{1,0:T(8,128)(2,1)S(1)}, u32[]{:S(2)}, u32[]{:S(2)}) collective-permute-start(bf16[512,256]{1,0:T(8,128)(2,1)S(1)} %get-tuple-element.11), channel_id=1, source_target_pairs={{0,2},{1,3},{2,0},{3,1},{4,6},{5,7},{6,4},{7,5},{8,10},{9,11},{10,... | collective-permute-start | bytes 786440 | tf_op jit(solution)/shard_map/ppermute | solution.py:256
  6.2 1.9 %collective-permute-start.1 = (bf16[1024,256]{1,0:T(8,128)(2,1)}, bf16[1024,256]{1,0:T(8,128)(2,1)S(1)}, u32[]{:S(2)}, u32[]{:S(2)}) collective-permute-start(bf16[1024,256]{1,0:T(8,128)(2,1)} %source_ref.1), channel_id=1, source_target_pairs={{1,2},{2,1},{3,4},{4,3},{5,6},{6,5},{7,8},{8,7},{9,10},{10,9},{11,... | collective-permute-start | bytes 1572872 | tf_op jit(solution)/shard_map/ppermute | solution.py:256
  8.2 3.8 %collective-permute-start.5 = (bf16[128,256]{1,0:T(8,128)(2,1)S(1)}, bf16[128,256]{1,0:T(8,128)(2,1)S(1)}, u32[]{:S(2)}, u32[]{:S(2)}) collective-permute-start(bf16[128,256]{1,0:T(8,128)(2,1)S(1)} %get-tuple-element.12.refs_0_), channel_id=1, source_target_pairs={{0,12},{1,13},{2,14},{3,15},{4,8},{5,9},{6,10},{7,11},{8,4},{9,5},... | collective-permute-start | bytes 196616 | tf_op jit(solution)/shard_map/ppermute | solution.py:256
  12.0 0.0 collective-permute-start.4
  12.0 0.0 collective-permute-done.share_ref
  12.0 0.4 collective-permute-start.3
  12.4 0.0 copy-start.6
  12.4 0.7 %copy-done.6 = s32[4,16]{1,0:T(4,128)S(1)} copy-done((s32[4,16]{1,0:T(4,128)S(1)}, s32[4,16]{1,0:T(4,128)}, u32[]{:S(2)}) %copy-start.6) | copy-done | bytes 280
  13.0 0.0 copy-start.9
  13.0 0.7 %copy-done.9 = s32[4]{0:T(128)S(1)} copy-done((s32[4]{0:T(128)S(1)}, s32[4]{0:T(128)}, u32[]{:S(2)}) %copy-start.9) | copy-done | bytes 40
  13.7 5.2 %near.1.near_ref.refs_5_ = f32[4,256,256]{2,1,0:T(8,128)S(1)} custom-call(s32[4,16]{1,0:T(4,128)S(1)} %copy-done.6, s32[4]{0:T(128)S(1)} %copy-done.9, bf16[4,16,256,256]{3,2,1,0:T(8,128)(2,1)} %blocks_hbm.3, bf16[1536,256]{1,0:T(8,128)(2,1)S(1)} %get-tuple-element.10.own_ref, bf16[1536,256]{1,0:T(8,128)(2,1)S(1)} %collective-permute-done.share_ref), custom_call_target="tpu_custom_call" | custom-call | tf_op jit(solution)/shard_map/near/pallas_call | solution.py:223
  18.9 0.0 collective-permute-done.5.refs_3_
  18.9 0.0 collective-permute-done.4.refs_2_
  19.0 0.0 collective-permute-done.3.refs_1_
  19.0 0.0 collective-permute-done.2.refs_4_.refs_2_.level_ref
  19.0 3.0 %collective-permute-start.6 = (bf16[512,256]{1,0:T(8,128)(2,1)S(1)}, bf16[512,256]{1,0:T(8,128)(2,1)S(1)}, u32[]{:S(2)}, u32[]{:S(2)}) collective-permute-start(bf16[512,256]{1,0:T(8,128)(2,1)S(1)} %get-tuple-element.13), channel_id=1, source_target_pairs={{0,4},{1,5},{4,8},{5,9},{6,2},{7,3},{8,12},{9,13},{10,6},{11,7},{1... | collective-permute-start | bytes 786440 | tf_op jit(solution)/shard_map/ppermute | solution.py:256
  22.1 0.8 %collective-permute-start.7 = (bf16[512,256]{1,0:T(8,128)(2,1)S(1)}, bf16[512,256]{1,0:T(8,128)(2,1)S(1)}, u32[]{:S(2)}, u32[]{:S(2)}) collective-permute-start(bf16[512,256]{1,0:T(8,128)(2,1)S(1)} %get-tuple-element.14.refs_0_), channel_id=1, source_target_pairs={{0,2},{1,3},{2,0},{3,1},{4,6},{5,7},{6,4},{7,5},{8,10},{9,11},{10,... | collective-permute-start | bytes 786440 | tf_op jit(solution)/shard_map/ppermute | solution.py:256
  22.9 2.5 %collective-permute-done.6.refs_3_.layer_ref = bf16[512,256]{1,0:T(8,128)(2,1)S(1)} collective-permute-done((bf16[512,256]{1,0:T(8,128)(2,1)S(1)}, bf16[512,256]{1,0:T(8,128)(2,1)S(1)}, u32[]{:S(2)}, u32[]{:S(2)}) %collective-permute-start.6) | collective-permute-done | bytes 262176 | tf_op jit(solution)/shard_map/ppermute | solution.py:256
  25.3 2.0 %collective-permute-done.7.refs_1_ = bf16[512,256]{1,0:T(8,128)(2,1)S(1)} collective-permute-done((bf16[512,256]{1,0:T(8,128)(2,1)S(1)}, bf16[512,256]{1,0:T(8,128)(2,1)S(1)}, u32[]{:S(2)}, u32[]{:S(2)}) %collective-permute-start.7) | collective-permute-done | bytes 262176 | tf_op jit(solution)/shard_map/ppermute | solution.py:256
  27.3 0.0 copy-done.7
  27.4 0.6 %pass.1.mine_ref = bf16[1536,256]{1,0:T(8,128)(2,1)S(1)} custom-call(s32[4,16]{1,0:T(4,128)S(1)} %copy-done.7, bf16[512,256]{1,0:T(8,128)(2,1)S(1)} %get-tuple-element.14.refs_0_, bf16[512,256]{1,0:T(8,128)(2,1)S(1)} %collective-permute-done.7.refs_1_, bf16[512,256]{1,0:T(8,128)(2,1)S(1)} %collective-permute-done.2.refs_4_.refs_2_.level_ref, ...), custom_call_target="tpu_custom_call" | custom-call | tf_op jit(solution)/shard_map/pass/pallas_call | solution.py:223
  28.0 0.0 copy-start
  28.0 0.0 copy-start.2
  28.0 0.0 copy-start.4
  28.0 0.0 copy-start.5
  28.0 0.0 copy-start.8
  28.0 0.0 copy-start.11
  28.1 5.0 %collective-permute-start.8 = (bf16[1536,256]{1,0:T(8,128)(2,1)S(1)}, bf16[1536,256]{1,0:T(8,128)(2,1)S(1)}, u32[]{:S(2)}, u32[]{:S(2)}) collective-permute-start(bf16[1536,256]{1,0:T(8,128)(2,1)S(1)} %pass.1.mine_ref), channel_id=1, source_target_pairs={{0,1},{1,0},{2,3},{3,2},{4,5},{5,4},{6,7},{7,6},{8,9},{9,8},{10,11... | collective-permute-start | bytes 2359304 | tf_op jit(solution)/shard_map/ppermute | solution.py:256
  33.1 0.0 collective-permute-done.1.across_ref
  33.1 0.0 copy-done.10
  33.1 3.2 %across.1.near_ref = f32[4,256,256]{2,1,0:T(8,128)S(1)} custom-call(s32[4,16]{1,0:T(4,128)S(1)} %copy-done.7, s32[4]{0:T(128)S(1)} %copy-done.10, bf16[4,16,256,256]{3,2,1,0:T(8,128)(2,1)} %blocks_hbm.3, f32[4,256,256]{2,1,0:T(8,128)S(1)} %near.1.near_ref.refs_5_, bf16[1024,256]{1,0:T(8,128)(2,1)S(1)} %collective-permute-done.1.across_ref), custom_call_target="tpu_custom_call" | custom-call | flops 17179869184 | bytes 8388608 | tf_op jit(solution)/shard_map/across/pallas_call | solution.py:223
  36.3 0.0 collective-permute-done.8.theirs_ref
  36.3 0.0 copy-done
  36.3 0.0 copy-done.2
  36.4 0.0 copy-done.4
  36.4 0.0 copy-done.5
  36.4 0.0 copy-done.8
  36.4 0.0 copy-done.11
  36.4 3.5 %down.1 = bf16[1024,256]{1,0:T(8,128)(2,1)} custom-call(s32[4,16]{1,0:T(4,128)S(1)} %copy-done.8, s32[1,8]{1,0:T(1,128)S(1)} %copy-done.11, s32[4,16]{1,0:T(4,128)S(1)} %copy-done.7, bf16[4,128,128]{2,1,0:T(8,128)(2,1)S(1)} %copy-done.2, bf16[4,16,128,128]{3,2,1,0:T(8,128)(2,1)S(1)} %copy-done, bf16[1,8,128,128]{3,2,1,0:T(8,128)(2,1)S(1)} %copy-done.4, ...), custom_call_target="tpu_custom_call" | custom-call | flops 671088640 | bytes 2097152 | tf_op jit(solution)/shard_map/down/pallas_call | solution.py:223
  (1 shorter events, 0.0 us)
Async XLA Ops:
  0.0 0.9 %copy-start.1 = (bf16[4,128,128]{2,1,0:T(8,128)(2,1)S(1)}, bf16[4,128,128]{2,1,0:T(8,128)(2,1)}, u32[]{:S(2)}) copy-start(bf16[4,128,128]{2,1,0:T(8,128)(2,1)} %transfer_ref.3) | copy-start | bytes 393220
  0.9 0.9 %copy-start.3 = (bf16[4,256,128]{2,1,0:T(8,128)(2,1)S(1)}, bf16[4,256,128]{2,1,0:T(8,128)(2,1)}, u32[]{:S(2)}) copy-start(bf16[4,256,128]{2,1,0:T(8,128)(2,1)} %col_ref.1) | copy-start | bytes 786436
  1.9 25.5 %copy-start.7 = (s32[4,16]{1,0:T(4,128)S(1)}, s32[4,16]{1,0:T(4,128)}, u32[]{:S(2)}) copy-start(s32[4,16]{1,0:T(4,128)} %near_list_ref.1) | copy-start | bytes 772
  1.9 31.2 %copy-start.10 = (s32[4]{0:T(128)S(1)}, s32[4]{0:T(128)}, u32[]{:S(2)}) copy-start(s32[4]{0:T(128)} %count_ref.3) | copy-start | bytes 52
  3.4 8.6 %collective-permute-start = (bf16[1536,256]{1,0:T(8,128)(2,1)S(1)}, bf16[1536,256]{1,0:T(8,128)(2,1)S(1)}, u32[]{:S(2)}, u32[]{:S(2)}) collective-permute-start(bf16[1536,256]{1,0:T(8,128)(2,1)S(1)} %get-tuple-element.10.own_ref), channel_id=1, source_target_pairs={{0,1},{1,0},{2,3},{3,2},{4,5},{5,4},{6,7},{7,6},{8,9},{9,8},{10,11... | collective-permute-start | bytes 2359304 | tf_op jit(solution)/shard_map/ppermute | solution.py:256
  3.5 15.4 %collective-permute-start.2 = (bf16[512,256]{1,0:T(8,128)(2,1)S(1)}, bf16[512,256]{1,0:T(8,128)(2,1)S(1)}, u32[]{:S(2)}, u32[]{:S(2)}) collective-permute-start(bf16[512,256]{1,0:T(8,128)(2,1)S(1)} %get-tuple-element.11), channel_id=1, source_target_pairs={{0,2},{1,3},{2,0},{3,1},{4,6},{5,7},{6,4},{7,5},{8,10},{9,11},{10,... | collective-permute-start | bytes 786440 | tf_op jit(solution)/shard_map/ppermute | solution.py:256
  6.2 26.8 %collective-permute-start.1 = (bf16[1024,256]{1,0:T(8,128)(2,1)}, bf16[1024,256]{1,0:T(8,128)(2,1)S(1)}, u32[]{:S(2)}, u32[]{:S(2)}) collective-permute-start(bf16[1024,256]{1,0:T(8,128)(2,1)} %source_ref.1), channel_id=1, source_target_pairs={{1,2},{2,1},{3,4},{4,3},{5,6},{6,5},{7,8},{8,7},{9,10},{10,9},{11,... | collective-permute-start | bytes 1572872 | tf_op jit(solution)/shard_map/ppermute | solution.py:256
  8.2 10.8 %collective-permute-start.5 = (bf16[128,256]{1,0:T(8,128)(2,1)S(1)}, bf16[128,256]{1,0:T(8,128)(2,1)S(1)}, u32[]{:S(2)}, u32[]{:S(2)}) collective-permute-start(bf16[128,256]{1,0:T(8,128)(2,1)S(1)} %get-tuple-element.12.refs_0_), channel_id=1, source_target_pairs={{0,12},{1,13},{2,14},{3,15},{4,8},{5,9},{6,10},{7,11},{8,4},{9,5},... | collective-permute-start | bytes 196616 | tf_op jit(solution)/shard_map/ppermute | solution.py:256
  12.0 7.0 %collective-permute-start.4 = (bf16[128,256]{1,0:T(8,128)(2,1)S(1)}, bf16[128,256]{1,0:T(8,128)(2,1)S(1)}, u32[]{:S(2)}, u32[]{:S(2)}) collective-permute-start(bf16[128,256]{1,0:T(8,128)(2,1)S(1)} %get-tuple-element.12.refs_0_), channel_id=1, source_target_pairs={{0,8},{1,9},{2,10},{3,11},{4,12},{5,13},{6,14},{7,15},{8,0},{9,1},... | collective-permute-start | bytes 196616 | tf_op jit(solution)/shard_map/ppermute | solution.py:256
  12.0 7.0 %collective-permute-start.3 = (bf16[128,256]{1,0:T(8,128)(2,1)S(1)}, bf16[128,256]{1,0:T(8,128)(2,1)S(1)}, u32[]{:S(2)}, u32[]{:S(2)}) collective-permute-start(bf16[128,256]{1,0:T(8,128)(2,1)S(1)} %get-tuple-element.12.refs_0_), channel_id=1, source_target_pairs={{0,4},{1,5},{2,6},{3,7},{4,0},{5,1},{6,2},{7,3},{8,12},{9,13},{10,... | collective-permute-start | bytes 196616 | tf_op jit(solution)/shard_map/ppermute | solution.py:256
  12.4 0.7 %copy-start.6 = (s32[4,16]{1,0:T(4,128)S(1)}, s32[4,16]{1,0:T(4,128)}, u32[]{:S(2)}) copy-start(s32[4,16]{1,0:T(4,128)} %near_list_ref.1) | copy-start | bytes 772
  13.0 0.7 %copy-start.9 = (s32[4]{0:T(128)S(1)}, s32[4]{0:T(128)}, u32[]{:S(2)}) copy-start(s32[4]{0:T(128)} %count_ref.3) | copy-start | bytes 52
  19.0 6.3 %collective-permute-start.6 = (bf16[512,256]{1,0:T(8,128)(2,1)S(1)}, bf16[512,256]{1,0:T(8,128)(2,1)S(1)}, u32[]{:S(2)}, u32[]{:S(2)}) collective-permute-start(bf16[512,256]{1,0:T(8,128)(2,1)S(1)} %get-tuple-element.13), channel_id=1, source_target_pairs={{0,4},{1,5},{4,8},{5,9},{6,2},{7,3},{8,12},{9,13},{10,6},{11,7},{1... | collective-permute-start | bytes 786440 | tf_op jit(solution)/shard_map/ppermute | solution.py:256
  22.1 5.3 %collective-permute-start.7 = (bf16[512,256]{1,0:T(8,128)(2,1)S(1)}, bf16[512,256]{1,0:T(8,128)(2,1)S(1)}, u32[]{:S(2)}, u32[]{:S(2)}) collective-permute-start(bf16[512,256]{1,0:T(8,128)(2,1)S(1)} %get-tuple-element.14.refs_0_), channel_id=1, source_target_pairs={{0,2},{1,3},{2,0},{3,1},{4,6},{5,7},{6,4},{7,5},{8,10},{9,11},{10,... | collective-permute-start | bytes 786440 | tf_op jit(solution)/shard_map/ppermute | solution.py:256
  28.0 8.4 %copy-start = (bf16[4,16,128,128]{3,2,1,0:T(8,128)(2,1)S(1)}, bf16[4,16,128,128]{3,2,1,0:T(8,128)(2,1)}, u32[]{:S(2)}) copy-start(bf16[4,16,128,128]{3,2,1,0:T(8,128)(2,1)} %coupling_ref.1) | copy-start | bytes 6291460
  28.0 8.3 %copy-start.2 = (bf16[4,128,128]{2,1,0:T(8,128)(2,1)S(1)}, bf16[4,128,128]{2,1,0:T(8,128)(2,1)}, u32[]{:S(2)}) copy-start(bf16[4,128,128]{2,1,0:T(8,128)(2,1)} %transfer_ref.3) | copy-start | bytes 393220
  28.0 8.3 %copy-start.4 = (bf16[1,8,128,128]{3,2,1,0:T(8,128)(2,1)S(1)}, bf16[1,8,128,128]{3,2,1,0:T(8,128)(2,1)}, u32[]{:S(2)}) copy-start(bf16[1,8,128,128]{3,2,1,0:T(8,128)(2,1)} %coarse_coupling_ref.1) | copy-start | bytes 786436
  28.0 8.3 %copy-start.5 = (bf16[4,256,128]{2,1,0:T(8,128)(2,1)S(1)}, bf16[4,256,128]{2,1,0:T(8,128)(2,1)}, u32[]{:S(2)}) copy-start(bf16[4,256,128]{2,1,0:T(8,128)(2,1)} %row_ref.1) | copy-start | bytes 786436
  28.0 8.3 %copy-start.8 = (s32[4,16]{1,0:T(4,128)S(1)}, s32[4,16]{1,0:T(4,128)}, u32[]{:S(2)}) copy-start(s32[4,16]{1,0:T(4,128)} %far_list_ref.1) | copy-start | bytes 772
  28.0 8.3 %copy-start.11 = (s32[1,8]{1,0:T(1,128)S(1)}, s32[1,8]{1,0:T(1,128)}, u32[]{:S(2)}) copy-start(s32[1,8]{1,0:T(1,128)} %coarse_list_ref.1) | copy-start | bytes 100
  28.1 8.3 %collective-permute-start.8 = (bf16[1536,256]{1,0:T(8,128)(2,1)S(1)}, bf16[1536,256]{1,0:T(8,128)(2,1)S(1)}, u32[]{:S(2)}, u32[]{:S(2)}) collective-permute-start(bf16[1536,256]{1,0:T(8,128)(2,1)S(1)} %pass.1.mine_ref), channel_id=1, source_target_pairs={{0,1},{1,0},{2,3},{3,2},{4,5},{5,4},{6,7},{7,6},{8,9},{9,8},{10,11... | collective-permute-start | bytes 2359304 | tf_op jit(solution)/shard_map/ppermute | solution.py:256

commit v8 on v7

--- a/solution.py
+++ b/solution.py
@@ -51,16 +51,14 @@
         at += ref.shape[0]
 
 
-def pass_kernel(list_ref, *refs):
-    *layers, level_ref, layer_ref, out_ref = refs
-    at = 0
-    for ref in layers:
-        out_ref[pl.ds(at, ref.shape[0]), :] = ref[...]
-        at += ref.shape[0]
-    place = lax.div(list_ref[0, 0], list_ref.shape[0])
-    corner = place & 3
+def pick_kernel(list_ref, level_ref, layer_ref, out_ref):
+    corner = lax.div(list_ref[0, 0], list_ref.shape[0]) & 3
     level = (corner == 0) | (corner == 3)
-    out_ref[pl.ds(at, level_ref.shape[0]), :] = jnp.where(level, level_ref[...], layer_ref[...])
+    out_ref[...] = jnp.where(level, level_ref[...], layer_ref[...])
+
+
+def hand_kernel(in_ref, _, __, out_ref):
+    out_ref[...] = in_ref[...]
 
 
 def pick_slots(list_ref, count_ref, blocks_hbm, blocks, sems, order_ref, leaf, keep):
@@ -138,59 +136,68 @@
         add_slots(near_ref, blocks_hbm, blocks, block_sems, order, leaf, found[leaf], panel_of)
 
 
-def down_kernel(
-    far_list_ref, coarse_list_ref, near_list_ref,
-    transfer_ref, coupling_ref, coarse_coupling_ref, row_ref, near_ref,
-    level_ref, layer_ref, share_ref, mine_ref, theirs_ref,
-    out_ref,
+def far_kernel(
+    list_ref, near_list_ref, coupling_ref, level_ref, layer_ref, share_ref, passed_ref,
+    far_ref,
     coefs, sems,
 ):
     leaves, slots, rank, _ = coupling_ref.shape
-    rows = row_ref.shape[1]
     size = leaves * rank
     place = lax.div(near_list_ref[0, 0], leaves)
+    beyond = jnp.where((place & 2) == 0, place - 2, place + 2)
     copies = [
         pltpu.make_async_copy(
             ref.at[pl.ds(ref.shape[0] - size, size)], coefs.at[pl.ds(n * size, size)], sems.at[n]
         )
-        for n, ref in enumerate((level_ref, layer_ref, share_ref, theirs_ref))
+        for n, ref in enumerate((level_ref, layer_ref, share_ref, passed_ref))
     ]
     for copy in copies:
         copy.start()
-
-    local = place & (GROUP - 1)
+    for copy in copies:
+        copy.wait()
+
+    def panel_of(leaf, slot):
+        column = list_ref[leaf, slot]
+        cluster = lax.div(column, leaves)
+        which = jnp.where(
+            cluster == (place ^ 2), 0,
+            jnp.where(cluster == beyond, 1, jnp.where(cluster == (place ^ 1), 2, 3)),
+        )
+        return coefs[rows_at(which * leaves + column - cluster * leaves, rank), :]
+
+    for leaf in range(leaves):
+        total = None
+        for slot in range(0, slots, 2):
+            both = jnp.concatenate([coupling_ref[leaf, slot], coupling_ref[leaf, slot + 1]], axis=1)
+            panels = jnp.concatenate([panel_of(leaf, slot), panel_of(leaf, slot + 1)], axis=0)
+            term = dot(both, panels)
+            total = term if total is None else total + term
+        far_ref[pl.ds(leaf * rank, rank), :] = total
+
+
+def down_kernel(
+    list_ref, near_list_ref, transfer_ref, coupling_ref, row_ref, near_ref, far_ref,
+    column_ref, beside_ref, their_column_ref, their_beside_ref,
+    out_ref,
+):
+    leaves, rows, rank = row_ref.shape
+    local = lax.div(near_list_ref[0, 0], leaves) & (GROUP - 1)
     total = None
-    for slot in range(coarse_list_ref.shape[1]):
-        flip = (coarse_list_ref[0, slot] & (GROUP - 1)) ^ local
-        where = rows_at((flip & 2) * 2 + (flip >> 2), rank)
-        panel = jnp.where((flip & 1) == 0, mine_ref[where, :], theirs_ref[where, :])
-        term = dot(coarse_coupling_ref[0, slot], panel)
+    for slot in range(list_ref.shape[1]):
+        flip = (list_ref[0, slot] & (GROUP - 1)) ^ local
+        where = rows_at(flip >> 2, rank)
+        mine = jnp.where((flip & 2) == 0, column_ref[where, :], beside_ref[where, :])
+        theirs = jnp.where((flip & 2) == 0, their_column_ref[where, :], their_beside_ref[where, :])
+        term = dot(coupling_ref[0, slot], jnp.where((flip & 1) == 0, mine, theirs))
         total = term if total is None else total + term
     high = total.astype(jnp.bfloat16)
     low = (total - high.astype(jnp.float32)).astype(jnp.bfloat16)
     coarse = jnp.concatenate([high, low], axis=0)
-
-    beyond = jnp.where((place & 2) == 0, place - 2, place + 2)
-    for copy in copies:
-        copy.wait()
-
-    def panel_of(leaf, slot):
-        column = far_list_ref[leaf, slot]
-        cluster = lax.div(column, leaves)
-        which = jnp.where(
-            cluster == (place ^ 2), 0,
-            jnp.where(cluster == beyond, 1, jnp.where(cluster == (place ^ 1), 2, 3)),
-        )
-        return coefs[rows_at(which * leaves + column - cluster * leaves, rank), :]
-
     for leaf in range(leaves):
         matrix = transfer_ref[leaf]
-        total = dot(jnp.concatenate([matrix, matrix], axis=1), coarse)
-        for slot in range(0, slots, 2):
-            both = jnp.concatenate([coupling_ref[leaf, slot], coupling_ref[leaf, slot + 1]], axis=1)
-            panels = jnp.concatenate([panel_of(leaf, slot), panel_of(leaf, slot + 1)], axis=0)
-            total = total + dot(both, panels)
-        result = near_ref[leaf] + dot(row_ref[leaf], total.astype(jnp.bfloat16))
+        spread = dot(jnp.concatenate([matrix, matrix], axis=1), coarse)
+        down = (far_ref[pl.ds(leaf * rank, rank), :] + spread).astype(jnp.bfloat16)
+        result = near_ref[leaf] + dot(row_ref[leaf], down)
         out_ref[pl.ds(leaf * rows, rows), :] = result.astype(jnp.bfloat16)
 
 
@@ -292,11 +299,11 @@
     )
     beside = send(column, lambda d: d ^ 2)
     layer = send(relay, lambda d: d - 4 if d & 2 else d + 4)
-    mine = call(
-        pass_kernel, "pass", panel(GROUP // 2 + leaves), [SMEM] + [VMEM] * 4,
-        (near_list, column, beside, level, layer),
-    )
-    theirs = send(mine, lambda d: d ^ 1)
+    their_column = send(column, lambda d: d ^ 1)
+    picked_coef = call(
+        pick_kernel, "pick", panel(leaves), [SMEM] + [VMEM] * 2, (near_list, level, layer)
+    )
+    passed = send(picked_coef, lambda d: d ^ 1)
     near = call(
         across_kernel, "across", jax.ShapeDtypeStruct((leaves, rows, width), jnp.float32),
         [SMEM] * 2 + [ANY] + [VMEM] * 2, (near_list, near_count, near_blocks, near, across),
@@ -304,19 +311,29 @@
         flops=16 * leaves * slots * rows * rows * width,
         moved=2 * leaves * slots * rows * rows, limit=48,
     )
-    return call(
-        down_kernel, "down", jax.ShapeDtypeStruct(source.shape, jnp.bfloat16),
-        [SMEM] * 3 + [VMEM] * 5 + [ANY] * 3 + [VMEM] * 2,
-        (
-            far_list, coarse_list, near_list, transfer, far_coupling, coarse_coupling, row_basis,
-            near, level, layer, share_other, mine, theirs,
-        ),
+    far = call(
+        far_kernel, "far", panel(leaves, jnp.float32), [SMEM] * 2 + [VMEM] + [ANY] * 4,
+        (far_list, near_list, far_coupling, level, layer, share_other, passed),
         scratch=[
             pltpu.VMEM((4 * leaves * rank, width), jnp.bfloat16),
             pltpu.SemaphoreType.DMA((4,)),
         ],
-        flops=2 * leaves * (far_slots + 4) * rank * rank * width,
-        moved=2 * leaves * far_slots * rank * rank, limit=12,
+        flops=2 * leaves * far_slots * rank * rank * width,
+        moved=2 * leaves * far_slots * rank * rank, limit=10,
+    )
+    handed = call(
+        hand_kernel, "hand", panel(GROUP // 4), [VMEM] + [ANY] * 2, (beside, far, near)
+    )
+    their_beside = send(handed, lambda d: d ^ 1)
+    return call(
+        down_kernel, "down", jax.ShapeDtypeStruct(source.shape, jnp.bfloat16),
+        [SMEM] * 2 + [VMEM] * 9,
+        (
+            coarse_list, near_list, transfer, coarse_coupling, row_basis, near, far,
+            column, handed, their_column, their_beside,
+        ),
+        flops=8 * leaves * rank * rank * width,
+        moved=4 * leaves * rows * width, limit=8,
     )
 
 

time: 40.3 us -> 41.5 us (1.030)
  starting transfers between devices: 17.8 us -> 21.5 us
  waiting for transfers between devices: 4.48 us -> 1.54 us
    ppermute x9 -> x11, starting transfers between devices: 17.8 us -> 21.5 us  [send(): return lax.ppermute(value, 'row', pairs)]
    ppermute x9 -> x11, waiting for transfers between devices: 4.48 us -> 1.54 us  [send(): return lax.ppermute(value, 'row', pairs)]
    pallas_call x6 -> x8, Pallas kernels: 14.1 us -> 14.3 us  [call(): pl.pallas_call(kernel, out_shape=outs, in_specs=specs, out_specs=(VMEM,)...]
  transfers between devices with their start and end apart: 9 -> 11, of which waited for: 2 -> 1; matrix products, arithmetic and copies ran while one was open for 0% -> 0% of each run, Pallas kernels for 23% -> 25%
where the time goes in v8:
time: 41.5 us; the launch traced here: 40.8 us
  starting transfers between devices  21.5 us (52%)
  Pallas kernels  14.3 us (34%)
  local copies, waits for them, and re-layouts  3.23 us (8%)
  waiting for transfers between devices  1.54 us (4%)
    ppermute x11, starting transfers between devices, send(): return lax.ppermute(value, 'row', pairs)  21.5 us
    pallas_call x8, Pallas kernels, call(): pl.pallas_call(kernel, out_shape=outs, in_specs=specs, out_specs=(VMEM,)...  14.3 us
    unnamed x24, local copies, waits for them, and re-layouts  3.23 us
    ppermute x11, waiting for transfers between devices, send(): return lax.ppermute(value, 'row', pairs)  1.54 us
  transfers between devices with their start and end apart: 11, of which 1 were waited for; matrix products, arithmetic and copies ran while one was open for 0% of the time, Pallas kernels for 25%

profile of v8, /device:TPU:1, one launch (start us, length us, event | category | flops | bytes accessed | tf_op | source)
XLA Modules:
  0.0 40.8 jit_solution(14767476748687073783)
XLA Ops:
  0.0 0.0 copy-start.1
  0.0 0.9 %copy-done.1 = bf16[4,128,128]{2,1,0:T(8,128)(2,1)S(1)} copy-done((bf16[4,128,128]{2,1,0:T(8,128)(2,1)S(1)}, bf16[4,128,128]{2,1,0:T(8,128)(2,1)}, u32[]{:S(2)}) %copy-start.1) | copy-done | bytes 131096
  0.9 0.0 copy-start.3
  0.9 0.9 %copy-done.3 = bf16[4,256,128]{2,1,0:T(8,128)(2,1)S(1)} copy-done((bf16[4,256,128]{2,1,0:T(8,128)(2,1)S(1)}, bf16[4,256,128]{2,1,0:T(8,128)(2,1)}, u32[]{:S(2)}) %copy-start.3) | copy-done | bytes 262168
  1.9 0.0 copy-start.7
  1.9 0.0 copy-start.10
  1.9 1.6 %up.1 = (bf16[1536,256]{1,0:T(8,128)(2,1)S(1)}, bf16[512,256]{1,0:T(8,128)(2,1)S(1)}, bf16[128,256]{1,0:T(8,128)(2,1)S(1)}) custom-call(bf16[1024,256]{1,0:T(8,128)(2,1)} %source_ref.1, bf16[4,256,128]{2,1,0:T(8,128)(2,1)S(1)} %copy-done.3, bf16[4,128,128]{2,1,0:T(8,128)(2,1)S(1)} %copy-done.1), custom_call_target="tpu_custom_call" | custom-call | flops 100663296 | bytes 786432 | tf_op jit(solution)/shard_map/up/pallas_call | solution.py:230
  3.4 0.1 collective-permute-start
  3.5 2.7 %collective-permute-start.2 = (bf16[512,256]{1,0:T(8,128)(2,1)S(1)}, bf16[512,256]{1,0:T(8,128)(2,1)S(1)}, u32[]{:S(2)}, u32[]{:S(2)}) collective-permute-start(bf16[512,256]{1,0:T(8,128)(2,1)S(1)} %get-tuple-element.11), channel_id=1, source_target_pairs={{0,2},{1,3},{2,0},{3,1},{4,6},{5,7},{6,4},{7,5},{8,10},{9,11},{10,... | collective-permute-start | bytes 786440 | tf_op jit(solution)/shard_map/ppermute | solution.py:263
  6.2 1.9 %collective-permute-start.1 = (bf16[1024,256]{1,0:T(8,128)(2,1)}, bf16[1024,256]{1,0:T(8,128)(2,1)S(1)}, u32[]{:S(2)}, u32[]{:S(2)}) collective-permute-start(bf16[1024,256]{1,0:T(8,128)(2,1)} %source_ref.1), channel_id=1, source_target_pairs={{1,2},{2,1},{3,4},{4,3},{5,6},{6,5},{7,8},{8,7},{9,10},{10,9},{11,... | collective-permute-start | bytes 1572872 | tf_op jit(solution)/shard_map/ppermute | solution.py:263
  8.2 1.8 %collective-permute-start.3 = (bf16[128,256]{1,0:T(8,128)(2,1)S(1)}, bf16[128,256]{1,0:T(8,128)(2,1)S(1)}, u32[]{:S(2)}, u32[]{:S(2)}) collective-permute-start(bf16[128,256]{1,0:T(8,128)(2,1)S(1)} %get-tuple-element.12.refs_0_), channel_id=1, source_target_pairs={{0,4},{1,5},{2,6},{3,7},{4,0},{5,1},{6,2},{7,3},{8,12},{9,13},{10,... | collective-permute-start | bytes 196616 | tf_op jit(solution)/shard_map/ppermute | solution.py:263
  10.0 2.3 %collective-permute-start.4 = (bf16[128,256]{1,0:T(8,128)(2,1)S(1)}, bf16[128,256]{1,0:T(8,128)(2,1)S(1)}, u32[]{:S(2)}, u32[]{:S(2)}) collective-permute-start(bf16[128,256]{1,0:T(8,128)(2,1)S(1)} %get-tuple-element.12.refs_0_), channel_id=1, source_target_pairs={{0,8},{1,9},{2,10},{3,11},{4,12},{5,13},{6,14},{7,15},{8,0},{9,1},... | collective-permute-start | bytes 196616 | tf_op jit(solution)/shard_map/ppermute | solution.py:263
  12.3 0.0 collective-permute-done.share_ref
  12.3 0.0 collective-permute-start.5
  12.3 0.0 copy-start.6
  12.3 0.7 %copy-done.6 = s32[4,16]{1,0:T(4,128)S(1)} copy-done((s32[4,16]{1,0:T(4,128)S(1)}, s32[4,16]{1,0:T(4,128)}, u32[]{:S(2)}) %copy-start.6) | copy-done | bytes 280
  13.0 0.0 copy-start.9
  13.0 0.7 %copy-done.9 = s32[4]{0:T(128)S(1)} copy-done((s32[4]{0:T(128)S(1)}, s32[4]{0:T(128)}, u32[]{:S(2)}) %copy-start.9) | copy-done | bytes 40
  13.6 4.4 %near.1.near_ref.refs_5_ = f32[4,256,256]{2,1,0:T(8,128)S(1)} custom-call(s32[4,16]{1,0:T(4,128)S(1)} %copy-done.6, s32[4]{0:T(128)S(1)} %copy-done.9, bf16[4,16,256,256]{3,2,1,0:T(8,128)(2,1)} %blocks_hbm.3, bf16[1536,256]{1,0:T(8,128)(2,1)S(1)} %get-tuple-element.10.own_ref, bf16[1536,256]{1,0:T(8,128)(2,1)S(1)} %collective-permute-done.share_ref), custom_call_target="tpu_custom_call" | custom-call | tf_op jit(solution)/shard_map/near/pallas_call | solution.py:230
  18.0 0.0 collective-permute-done.3.refs_1_
  18.0 0.0 collective-permute-done.4.refs_2_
  18.1 0.0 collective-permute-done.5.refs_3_
  18.1 0.0 collective-permute-done.2.refs_4_.level_ref
  18.1 1.7 %collective-permute-start.6 = (bf16[512,256]{1,0:T(8,128)(2,1)S(1)}, bf16[512,256]{1,0:T(8,128)(2,1)S(1)}, u32[]{:S(2)}, u32[]{:S(2)}) collective-permute-start(bf16[512,256]{1,0:T(8,128)(2,1)S(1)} %get-tuple-element.13), channel_id=1, source_target_pairs={{0,4},{1,5},{4,8},{5,9},{6,2},{7,3},{8,12},{9,13},{10,6},{11,7},{1... | collective-permute-start | bytes 786440 | tf_op jit(solution)/shard_map/ppermute | solution.py:263
  19.8 3.1 %collective-permute-start.8 = (bf16[512,256]{1,0:T(8,128)(2,1)S(1)}, bf16[512,256]{1,0:T(8,128)(2,1)S(1)}, u32[]{:S(2)}, u32[]{:S(2)}) collective-permute-start(bf16[512,256]{1,0:T(8,128)(2,1)S(1)} %get-tuple-element.14.column_ref), channel_id=1, source_target_pairs={{0,2},{1,3},{2,0},{3,1},{4,6},{5,7},{6,4},{7,5},{8,10},{9,11},{10,... | collective-permute-start | bytes 786440 | tf_op jit(solution)/shard_map/ppermute | solution.py:263
  22.8 4.1 %collective-permute-start.9 = (bf16[512,256]{1,0:T(8,128)(2,1)S(1)}, bf16[512,256]{1,0:T(8,128)(2,1)S(1)}, u32[]{:S(2)}, u32[]{:S(2)}) collective-permute-start(bf16[512,256]{1,0:T(8,128)(2,1)S(1)} %get-tuple-element.14.column_ref), channel_id=1, source_target_pairs={{0,1},{1,0},{2,3},{3,2},{4,5},{5,4},{6,7},{7,6},{8,9},{9,8},{10,11... | collective-permute-start | bytes 786440 | tf_op jit(solution)/shard_map/ppermute | solution.py:263
  26.9 0.0 collective-permute-done.6.layer_ref
  26.9 0.6 %pick.1 = bf16[512,256]{1,0:T(8,128)(2,1)S(1)} custom-call(s32[4,16]{1,0:T(4,128)S(1)} %copy-done.6, bf16[512,256]{1,0:T(8,128)(2,1)S(1)} %collective-permute-done.2.refs_4_.level_ref, bf16[512,256]{1,0:T(8,128)(2,1)S(1)} %collective-permute-done.6.layer_ref), custom_call_target="tpu_custom_call" | custom-call | tf_op jit(solution)/shard_map/pick/pallas_call | solution.py:230
  27.5 0.0 copy-start
  27.5 0.0 copy-start.8
  27.6 0.0 copy-start.2
  27.6 0.0 copy-start.4
  27.6 0.0 copy-start.5
  27.6 0.0 copy-start.11
  27.6 3.8 %collective-permute-start.7 = (bf16[512,256]{1,0:T(8,128)(2,1)S(1)}, bf16[512,256]{1,0:T(8,128)(2,1)S(1)}, u32[]{:S(2)}, u32[]{:S(2)}) collective-permute-start(bf16[512,256]{1,0:T(8,128)(2,1)S(1)} %pick.1), channel_id=1, source_target_pairs={{0,1},{1,0},{2,3},{3,2},{4,5},{5,4},{6,7},{7,6},{8,9},{9,8},{10,11... | collective-permute-start | bytes 786440 | tf_op jit(solution)/shard_map/ppermute | solution.py:263
  31.4 0.0 collective-permute-done.1.across_ref
  31.4 0.0 copy-done.7
  31.4 0.0 copy-done.10
  31.4 3.6 %across.1.__.near_ref = f32[4,256,256]{2,1,0:T(8,128)S(1)} custom-call(s32[4,16]{1,0:T(4,128)S(1)} %copy-done.7, s32[4]{0:T(128)S(1)} %copy-done.10, bf16[4,16,256,256]{3,2,1,0:T(8,128)(2,1)} %blocks_hbm.3, f32[4,256,256]{2,1,0:T(8,128)S(1)} %near.1.near_ref.refs_5_, bf16[1024,256]{1,0:T(8,128)(2,1)S(1)} %collective-permute-done.1.across_ref), custom_call_target="tpu_custom_call" | custom-call | flops 17179869184 | bytes 8388608 | tf_op jit(solution)/shard_map/across/pallas_call | solution.py:230
  35.0 0.0 collective-permute-done.7.passed_ref
  35.0 0.0 copy-done
  35.0 0.0 copy-done.8
  35.0 1.5 %far.1._.far_ref = f32[512,256]{1,0:T(8,128)S(1)} custom-call(s32[4,16]{1,0:T(4,128)S(1)} %copy-done.8, s32[4,16]{1,0:T(4,128)S(1)} %copy-done.7, bf16[4,16,128,128]{3,2,1,0:T(8,128)(2,1)S(1)} %copy-done, bf16[512,256]{1,0:T(8,128)(2,1)S(1)} %collective-permute-done.2.refs_4_.level_ref, bf16[512,256]{1,0:T(8,128)(2,1)S(1)} %collective-permute-done.6.layer_ref, ...), custom_call_target="tpu_custom_call" | custom-call | flops 536870912 | bytes 2097152 | tf_op jit(solution)/shard_map/far/pallas_call | solution.py:230
  36.6 0.0 collective-permute-done.8.in_ref
  36.6 0.1 collective-permute-start.10
  36.7 0.0 collective-permute-done.9.their_column_ref
  36.7 1.5 %collective-permute-done.10.their_beside_ref = bf16[512,256]{1,0:T(8,128)(2,1)S(1)} collective-permute-done((bf16[512,256]{1,0:T(8,128)(2,1)S(1)}, bf16[512,256]{1,0:T(8,128)(2,1)S(1)}, u32[]{:S(2)}, u32[]{:S(2)}) %collective-permute-start.10) | collective-permute-done | bytes 262176 | tf_op jit(solution)/shard_map/ppermute | solution.py:263
  38.2 0.0 copy-done.2
  38.2 0.0 copy-done.4
  38.2 0.0 copy-done.5
  38.2 0.0 copy-done.11
  38.2 2.6 %down.1 = bf16[1024,256]{1,0:T(8,128)(2,1)} custom-call(s32[1,8]{1,0:T(1,128)S(1)} %copy-done.11, s32[4,16]{1,0:T(4,128)S(1)} %copy-done.7, bf16[4,128,128]{2,1,0:T(8,128)(2,1)S(1)} %copy-done.2, bf16[1,8,128,128]{3,2,1,0:T(8,128)(2,1)S(1)} %copy-done.4, bf16[4,256,128]{2,1,0:T(8,128)(2,1)S(1)} %copy-done.5, f32[4,256,256]{2,1,0:T(8,128)S(1)} %across.1.__.near_ref, ...), custom_call_target="tpu_custom_call" | custom-call | flops 134217728 | bytes 1048576 | tf_op jit(solution)/shard_map/down/pallas_call | solution.py:230
  (2 shorter events, 0.1 us)
Async XLA Ops:
  0.0 0.9 %copy-start.1 = (bf16[4,128,128]{2,1,0:T(8,128)(2,1)S(1)}, bf16[4,128,128]{2,1,0:T(8,128)(2,1)}, u32[]{:S(2)}) copy-start(bf16[4,128,128]{2,1,0:T(8,128)(2,1)} %transfer_ref.3) | copy-start | bytes 393220
  0.9 0.9 %copy-start.3 = (bf16[4,256,128]{2,1,0:T(8,128)(2,1)S(1)}, bf16[4,256,128]{2,1,0:T(8,128)(2,1)}, u32[]{:S(2)}) copy-start(bf16[4,256,128]{2,1,0:T(8,128)(2,1)} %col_ref.1) | copy-start | bytes 786436
  1.9 29.5 %copy-start.7 = (s32[4,16]{1,0:T(4,128)S(1)}, s32[4,16]{1,0:T(4,128)}, u32[]{:S(2)}) copy-start(s32[4,16]{1,0:T(4,128)} %near_list_ref.3) | copy-start | bytes 772
  1.9 29.5 %copy-start.10 = (s32[4]{0:T(128)S(1)}, s32[4]{0:T(128)}, u32[]{:S(2)}) copy-start(s32[4]{0:T(128)} %count_ref.3) | copy-start | bytes 52
  3.4 8.9 %collective-permute-start = (bf16[1536,256]{1,0:T(8,128)(2,1)S(1)}, bf16[1536,256]{1,0:T(8,128)(2,1)S(1)}, u32[]{:S(2)}, u32[]{:S(2)}) collective-permute-start(bf16[1536,256]{1,0:T(8,128)(2,1)S(1)} %get-tuple-element.10.own_ref), channel_id=1, source_target_pairs={{0,1},{1,0},{2,3},{3,2},{4,5},{5,4},{6,7},{7,6},{8,9},{9,8},{10,11... | collective-permute-start | bytes 2359304 | tf_op jit(solution)/shard_map/ppermute | solution.py:263
  3.5 14.5 %collective-permute-start.2 = (bf16[512,256]{1,0:T(8,128)(2,1)S(1)}, bf16[512,256]{1,0:T(8,128)(2,1)S(1)}, u32[]{:S(2)}, u32[]{:S(2)}) collective-permute-start(bf16[512,256]{1,0:T(8,128)(2,1)S(1)} %get-tuple-element.11), channel_id=1, source_target_pairs={{0,2},{1,3},{2,0},{3,1},{4,6},{5,7},{6,4},{7,5},{8,10},{9,11},{10,... | collective-permute-start | bytes 786440 | tf_op jit(solution)/shard_map/ppermute | solution.py:263
  6.2 25.1 %collective-permute-start.1 = (bf16[1024,256]{1,0:T(8,128)(2,1)}, bf16[1024,256]{1,0:T(8,128)(2,1)S(1)}, u32[]{:S(2)}, u32[]{:S(2)}) collective-permute-start(bf16[1024,256]{1,0:T(8,128)(2,1)} %source_ref.1), channel_id=1, source_target_pairs={{1,2},{2,1},{3,4},{4,3},{5,6},{6,5},{7,8},{8,7},{9,10},{10,9},{11,... | collective-permute-start | bytes 1572872 | tf_op jit(solution)/shard_map/ppermute | solution.py:263
  8.2 9.9 %collective-permute-start.3 = (bf16[128,256]{1,0:T(8,128)(2,1)S(1)}, bf16[128,256]{1,0:T(8,128)(2,1)S(1)}, u32[]{:S(2)}, u32[]{:S(2)}) collective-permute-start(bf16[128,256]{1,0:T(8,128)(2,1)S(1)} %get-tuple-element.12.refs_0_), channel_id=1, source_target_pairs={{0,4},{1,5},{2,6},{3,7},{4,0},{5,1},{6,2},{7,3},{8,12},{9,13},{10,... | collective-permute-start | bytes 196616 | tf_op jit(solution)/shard_map/ppermute | solution.py:263
  10.0 8.1 %collective-permute-start.4 = (bf16[128,256]{1,0:T(8,128)(2,1)S(1)}, bf16[128,256]{1,0:T(8,128)(2,1)S(1)}, u32[]{:S(2)}, u32[]{:S(2)}) collective-permute-start(bf16[128,256]{1,0:T(8,128)(2,1)S(1)} %get-tuple-element.12.refs_0_), channel_id=1, source_target_pairs={{0,8},{1,9},{2,10},{3,11},{4,12},{5,13},{6,14},{7,15},{8,0},{9,1},... | collective-permute-start | bytes 196616 | tf_op jit(solution)/shard_map/ppermute | solution.py:263
  12.3 5.8 %collective-permute-start.5 = (bf16[128,256]{1,0:T(8,128)(2,1)S(1)}, bf16[128,256]{1,0:T(8,128)(2,1)S(1)}, u32[]{:S(2)}, u32[]{:S(2)}) collective-permute-start(bf16[128,256]{1,0:T(8,128)(2,1)S(1)} %get-tuple-element.12.refs_0_), channel_id=1, source_target_pairs={{0,12},{1,13},{2,14},{3,15},{4,8},{5,9},{6,10},{7,11},{8,4},{9,5},... | collective-permute-start | bytes 196616 | tf_op jit(solution)/shard_map/ppermute | solution.py:263
  12.3 0.7 %copy-start.6 = (s32[4,16]{1,0:T(4,128)S(1)}, s32[4,16]{1,0:T(4,128)}, u32[]{:S(2)}) copy-start(s32[4,16]{1,0:T(4,128)} %near_list_ref.3) | copy-start | bytes 772
  13.0 0.7 %copy-start.9 = (s32[4]{0:T(128)S(1)}, s32[4]{0:T(128)}, u32[]{:S(2)}) copy-start(s32[4]{0:T(128)} %count_ref.3) | copy-start | bytes 52
  18.1 8.8 %collective-permute-start.6 = (bf16[512,256]{1,0:T(8,128)(2,1)S(1)}, bf16[512,256]{1,0:T(8,128)(2,1)S(1)}, u32[]{:S(2)}, u32[]{:S(2)}) collective-permute-start(bf16[512,256]{1,0:T(8,128)(2,1)S(1)} %get-tuple-element.13), channel_id=1, source_target_pairs={{0,4},{1,5},{4,8},{5,9},{6,2},{7,3},{8,12},{9,13},{10,6},{11,7},{1... | collective-permute-start | bytes 786440 | tf_op jit(solution)/shard_map/ppermute | solution.py:263
  19.8 16.8 %collective-permute-start.8 = (bf16[512,256]{1,0:T(8,128)(2,1)S(1)}, bf16[512,256]{1,0:T(8,128)(2,1)S(1)}, u32[]{:S(2)}, u32[]{:S(2)}) collective-permute-start(bf16[512,256]{1,0:T(8,128)(2,1)S(1)} %get-tuple-element.14.column_ref), channel_id=1, source_target_pairs={{0,2},{1,3},{2,0},{3,1},{4,6},{5,7},{6,4},{7,5},{8,10},{9,11},{10,... | collective-permute-start | bytes 786440 | tf_op jit(solution)/shard_map/ppermute | solution.py:263
  22.8 13.8 %collective-permute-start.9 = (bf16[512,256]{1,0:T(8,128)(2,1)S(1)}, bf16[512,256]{1,0:T(8,128)(2,1)S(1)}, u32[]{:S(2)}, u32[]{:S(2)}) collective-permute-start(bf16[512,256]{1,0:T(8,128)(2,1)S(1)} %get-tuple-element.14.column_ref), channel_id=1, source_target_pairs={{0,1},{1,0},{2,3},{3,2},{4,5},{5,4},{6,7},{7,6},{8,9},{9,8},{10,11... | collective-permute-start | bytes 786440 | tf_op jit(solution)/shard_map/ppermute | solution.py:263
  27.5 7.5 %copy-start = (bf16[4,16,128,128]{3,2,1,0:T(8,128)(2,1)S(1)}, bf16[4,16,128,128]{3,2,1,0:T(8,128)(2,1)}, u32[]{:S(2)}) copy-start(bf16[4,16,128,128]{3,2,1,0:T(8,128)(2,1)} %coupling_ref.2) | copy-start | bytes 6291460
  27.5 7.5 %copy-start.8 = (s32[4,16]{1,0:T(4,128)S(1)}, s32[4,16]{1,0:T(4,128)}, u32[]{:S(2)}) copy-start(s32[4,16]{1,0:T(4,128)} %list_ref.8) | copy-start | bytes 772
  27.6 10.7 %copy-start.2 = (bf16[4,128,128]{2,1,0:T(8,128)(2,1)S(1)}, bf16[4,128,128]{2,1,0:T(8,128)(2,1)}, u32[]{:S(2)}) copy-start(bf16[4,128,128]{2,1,0:T(8,128)(2,1)} %transfer_ref.3) | copy-start | bytes 393220
  27.6 10.6 %copy-start.4 = (bf16[1,8,128,128]{3,2,1,0:T(8,128)(2,1)S(1)}, bf16[1,8,128,128]{3,2,1,0:T(8,128)(2,1)}, u32[]{:S(2)}) copy-start(bf16[1,8,128,128]{3,2,1,0:T(8,128)(2,1)} %coupling_ref.3) | copy-start | bytes 786436
  27.6 10.6 %copy-start.5 = (bf16[4,256,128]{2,1,0:T(8,128)(2,1)S(1)}, bf16[4,256,128]{2,1,0:T(8,128)(2,1)}, u32[]{:S(2)}) copy-start(bf16[4,256,128]{2,1,0:T(8,128)(2,1)} %row_ref.1) | copy-start | bytes 786436
  27.6 10.6 %copy-start.11 = (s32[1,8]{1,0:T(1,128)S(1)}, s32[1,8]{1,0:T(1,128)}, u32[]{:S(2)}) copy-start(s32[1,8]{1,0:T(1,128)} %list_ref.9) | copy-start | bytes 100
  27.6 7.4 %collective-permute-start.7 = (bf16[512,256]{1,0:T(8,128)(2,1)S(1)}, bf16[512,256]{1,0:T(8,128)(2,1)S(1)}, u32[]{:S(2)}, u32[]{:S(2)}) collective-permute-start(bf16[512,256]{1,0:T(8,128)(2,1)S(1)} %pick.1), channel_id=1, source_target_pairs={{0,1},{1,0},{2,3},{3,2},{4,5},{5,4},{6,7},{7,6},{8,9},{9,8},{10,11... | collective-permute-start | bytes 786440 | tf_op jit(solution)/shard_map/ppermute | solution.py:263
  36.6 1.6 %collective-permute-start.10 = (bf16[512,256]{1,0:T(8,128)(2,1)S(1)}, bf16[512,256]{1,0:T(8,128)(2,1)S(1)}, u32[]{:S(2)}, u32[]{:S(2)}) collective-permute-start(bf16[512,256]{1,0:T(8,128)(2,1)S(1)} %hand.1.beside_ref), channel_id=1, source_target_pairs={{0,1},{1,0},{2,3},{3,2},{4,5},{5,4},{6,7},{7,6},{8,9},{9,8},{10,11... | collective-permute-start | bytes 786440 | tf_op jit(solution)/shard_map/ppermute | solution.py:263

commit v9 on v8

--- a/solution.py
+++ b/solution.py
@@ -43,22 +43,21 @@
 
 
 def join_kernel(*refs):
-    *pieces, level_ref, _, out_ref, relay_ref = refs
-    relay_ref[...] = level_ref[...]
+    *pieces, out_ref = refs
     at = 0
     for ref in pieces:
         out_ref[pl.ds(at, ref.shape[0]), :] = ref[...]
         at += ref.shape[0]
 
 
-def pick_kernel(list_ref, level_ref, layer_ref, out_ref):
+def pick_kernel(list_ref, level_ref, layer_ref, _, out_ref):
     corner = lax.div(list_ref[0, 0], list_ref.shape[0]) & 3
     level = (corner == 0) | (corner == 3)
     out_ref[...] = jnp.where(level, level_ref[...], layer_ref[...])
 
 
-def hand_kernel(in_ref, _, __, out_ref):
-    out_ref[...] = in_ref[...]
+def hand_kernel(in_ref, _, out_ref):
+    out_ref[...] = in_ref[pl.ds(0, out_ref.shape[0]), :]
 
 
 def pick_slots(list_ref, count_ref, blocks_hbm, blocks, sems, order_ref, leaf, keep):
@@ -202,7 +201,7 @@
 
 
 def across_kernel(
-    list_ref, count_ref, blocks_hbm, near_ref, across_ref,
+    list_ref, count_ref, blocks_hbm, near_ref, across_ref, _,
     total_ref,
     blocks, order, sems,
 ):
@@ -275,7 +274,11 @@
     layers = [send(parent, lambda d, bit=bit: d ^ bit) for bit in (4, 8, 12)]
     share_other = send(share, lambda d: d ^ 1)
     level = send(coef, lambda d: d ^ 2)
-    across = send(source, lambda d: d + 1 if d & 1 else d - 1)
+    panels = call(
+        hand_kernel, "panels", jax.ShapeDtypeStruct(source.shape, jnp.bfloat16), [VMEM, ANY],
+        (share, share_other),
+    )
+    across = send(panels, lambda d: d + 1 if d & 1 else d - 1)
 
     picked = [
         pltpu.VMEM(near_blocks.shape, jnp.bfloat16),
@@ -293,24 +296,22 @@
         ],
         limit=48,
     )
-    column, relay = call(
-        join_kernel, "column", (panel(GROUP // 4), panel(leaves)), [VMEM] * 5 + [ANY],
-        (parent, *layers, level, near),
-    )
+    relay = call(hand_kernel, "relay", panel(leaves), [VMEM, ANY], (level, near))
+    layer = send(relay, lambda d: d - 4 if d & 2 else d + 4)
+    column = call(join_kernel, "column", panel(GROUP // 4), [VMEM] * 4, (parent, *layers))
     beside = send(column, lambda d: d ^ 2)
-    layer = send(relay, lambda d: d - 4 if d & 2 else d + 4)
     their_column = send(column, lambda d: d ^ 1)
-    picked_coef = call(
-        pick_kernel, "pick", panel(leaves), [SMEM] + [VMEM] * 2, (near_list, level, layer)
-    )
-    passed = send(picked_coef, lambda d: d ^ 1)
     near = call(
         across_kernel, "across", jax.ShapeDtypeStruct((leaves, rows, width), jnp.float32),
-        [SMEM] * 2 + [ANY] + [VMEM] * 2, (near_list, near_count, near_blocks, near, across),
+        [SMEM] * 2 + [ANY] + [VMEM] * 2 + [ANY],
+        (near_list, near_count, near_blocks, near, across, column),
         scratch=picked,
-        flops=16 * leaves * slots * rows * rows * width,
-        moved=2 * leaves * slots * rows * rows, limit=48,
-    )
+        flops=leaves * slots * rows * rows * width, moved=0, limit=48,
+    )
+    picked_coef = call(
+        pick_kernel, "pick", panel(leaves), [SMEM] + [VMEM] * 2 + [ANY], (near_list, level, layer, near)
+    )
+    passed = send(picked_coef, lambda d: d ^ 1)
     far = call(
         far_kernel, "far", panel(leaves, jnp.float32), [SMEM] * 2 + [VMEM] + [ANY] * 4,
         (far_list, near_list, far_coupling, level, layer, share_other, passed),
@@ -321,16 +322,13 @@
         flops=2 * leaves * far_slots * rank * rank * width,
         moved=2 * leaves * far_slots * rank * rank, limit=10,
     )
-    handed = call(
-        hand_kernel, "hand", panel(GROUP // 4), [VMEM] + [ANY] * 2, (beside, far, near)
-    )
-    their_beside = send(handed, lambda d: d ^ 1)
+    their_beside = send(beside, lambda d: d ^ 1)
     return call(
         down_kernel, "down", jax.ShapeDtypeStruct(source.shape, jnp.bfloat16),
         [SMEM] * 2 + [VMEM] * 9,
         (
             coarse_list, near_list, transfer, coarse_coupling, row_basis, near, far,
-            column, handed, their_column, their_beside,
+            column, beside, their_column, their_beside,
         ),
         flops=8 * leaves * rank * rank * width,
         moved=4 * leaves * rows * width, limit=8,

time: 41.5 us -> 44.3 us (1.067)
  waiting for transfers between devices: 1.54 us -> 9.58 us
  starting transfers between devices: 21.5 us -> 17.2 us
  Pallas kernels: 14.3 us -> 12.7 us
  local copies, waits for them, and re-layouts: 3.23 us -> 4.28 us
    ppermute x11, waiting for transfers between devices: 1.54 us -> 9.58 us  [send(): return lax.ppermute(value, 'row', pairs)]
    ppermute x11, starting transfers between devices: 21.5 us -> 17.2 us  [send(): return lax.ppermute(value, 'row', pairs)]
    pallas_call x8 -> x9, Pallas kernels: 14.3 us -> 12.7 us  [call(): pl.pallas_call(kernel, out_shape=outs, in_specs=specs, out_specs=(VMEM,)...]
    unnamed x24 -> x26, local copies, waits for them, and re-layouts: 3.23 us -> 4.28 us
  transfers between devices with their start and end apart: 11 -> 11, of which waited for: 1 -> 3; matrix products, arithmetic and copies ran while one was open for 0% -> 0% of each run, Pallas kernels for 25% -> 22%
where the time goes in v9:
time: 44.3 us; the launch traced here: 44 us
  starting transfers between devices  17.2 us (39%)
  Pallas kernels  12.7 us (29%)
  waiting for transfers between devices  9.58 us (22%)
  local copies, waits for them, and re-layouts  4.28 us (10%)
    ppermute x11, starting transfers between devices, send(): return lax.ppermute(value, 'row', pairs)  17.2 us
    pallas_call x9, Pallas kernels, call(): pl.pallas_call(kernel, out_shape=outs, in_specs=specs, out_specs=(VMEM,)...  12.7 us
    ppermute x11, waiting for transfers between devices, send(): return lax.ppermute(value, 'row', pairs)  9.58 us
    unnamed x26, local copies, waits for them, and re-layouts  4.28 us
  transfers between devices with their start and end apart: 11, of which 3 were waited for; matrix products, arithmetic and copies ran while one was open for 0% of the time, Pallas kernels for 22%

profile of v9, /device:TPU:1, one launch (start us, length us, event | category | flops | bytes accessed | tf_op | source)
XLA Modules:
  0.0 44.0 jit_solution(18154522078572688984)
XLA Ops:
  0.0 0.0 copy-start.1
  0.0 0.9 %copy-done.1 = bf16[4,128,128]{2,1,0:T(8,128)(2,1)S(1)} copy-done((bf16[4,128,128]{2,1,0:T(8,128)(2,1)S(1)}, bf16[4,128,128]{2,1,0:T(8,128)(2,1)}, u32[]{:S(2)}) %copy-start.1) | copy-done | bytes 131096
  0.9 0.0 copy-start.3
  0.9 1.0 %copy-done.3 = bf16[1024,256]{1,0:T(8,128)(2,1)S(1)} copy-done((bf16[1024,256]{1,0:T(8,128)(2,1)S(1)}, bf16[1024,256]{1,0:T(8,128)(2,1)}, u32[]{:S(2)}) %copy-start.3) | copy-done | bytes 524312
  1.9 0.0 copy-start.4
  1.9 0.9 %copy-done.4 = bf16[4,256,128]{2,1,0:T(8,128)(2,1)S(1)} copy-done((bf16[4,256,128]{2,1,0:T(8,128)(2,1)S(1)}, bf16[4,256,128]{2,1,0:T(8,128)(2,1)}, u32[]{:S(2)}) %copy-start.4) | copy-done | bytes 262168
  2.9 0.0 copy-start.8
  2.9 0.0 copy-start.11
  2.9 0.5 %up.1 = (bf16[1536,256]{1,0:T(8,128)(2,1)S(1)}, bf16[512,256]{1,0:T(8,128)(2,1)S(1)}, bf16[128,256]{1,0:T(8,128)(2,1)S(1)}) custom-call(bf16[1024,256]{1,0:T(8,128)(2,1)S(1)} %copy-done.3, bf16[4,256,128]{2,1,0:T(8,128)(2,1)S(1)} %copy-done.4, bf16[4,128,128]{2,1,0:T(8,128)(2,1)S(1)} %copy-done.1), custom_call_target="tpu_custom_call" | custom-call | flops 100663296 | bytes 786432 | tf_op jit(solution)/shard_map/up/pallas_call | solution.py:229
  3.4 0.1 collective-permute-start
  3.5 2.2 %collective-permute-done.share_ref._ = bf16[1536,256]{1,0:T(8,128)(2,1)S(1)} collective-permute-done((bf16[1536,256]{1,0:T(8,128)(2,1)S(1)}, bf16[1536,256]{1,0:T(8,128)(2,1)S(1)}, u32[]{:S(2)}, u32[]{:S(2)}) %collective-permute-start) | collective-permute-done | bytes 786464 | tf_op jit(solution)/shard_map/ppermute | solution.py:262
  5.8 4.5 %collective-permute-start.1 = (bf16[1024,256]{1,0:T(8,128)(2,1)S(1)}, bf16[1024,256]{1,0:T(8,128)(2,1)S(1)}, u32[]{:S(2)}, u32[]{:S(2)}) collective-permute-start(bf16[1024,256]{1,0:T(8,128)(2,1)S(1)} %panels.1), channel_id=1, source_target_pairs={{1,2},{2,1},{3,4},{4,3},{5,6},{6,5},{7,8},{8,7},{9,10},{10,9},{11,... | collective-permute-start | bytes 1572872 | tf_op jit(solution)/shard_map/ppermute | solution.py:262
  10.3 1.3 %collective-permute-start.5 = (bf16[512,256]{1,0:T(8,128)(2,1)S(1)}, bf16[512,256]{1,0:T(8,128)(2,1)S(1)}, u32[]{:S(2)}, u32[]{:S(2)}) collective-permute-start(bf16[512,256]{1,0:T(8,128)(2,1)S(1)} %get-tuple-element.10), channel_id=1, source_target_pairs={{0,2},{1,3},{2,0},{3,1},{4,6},{5,7},{6,4},{7,5},{8,10},{9,11},{10,... | collective-permute-start | bytes 786440 | tf_op jit(solution)/shard_map/ppermute | solution.py:262
  11.6 1.3 %collective-permute-start.2 = (bf16[128,256]{1,0:T(8,128)(2,1)S(1)}, bf16[128,256]{1,0:T(8,128)(2,1)S(1)}, u32[]{:S(2)}, u32[]{:S(2)}) collective-permute-start(bf16[128,256]{1,0:T(8,128)(2,1)S(1)} %get-tuple-element.9.refs_0_), channel_id=1, source_target_pairs={{0,4},{1,5},{2,6},{3,7},{4,0},{5,1},{6,2},{7,3},{8,12},{9,13},{10,... | collective-permute-start | bytes 196616 | tf_op jit(solution)/shard_map/ppermute | solution.py:262
  12.9 1.1 %collective-permute-start.3 = (bf16[128,256]{1,0:T(8,128)(2,1)S(1)}, bf16[128,256]{1,0:T(8,128)(2,1)S(1)}, u32[]{:S(2)}, u32[]{:S(2)}) collective-permute-start(bf16[128,256]{1,0:T(8,128)(2,1)S(1)} %get-tuple-element.9.refs_0_), channel_id=1, source_target_pairs={{0,8},{1,9},{2,10},{3,11},{4,12},{5,13},{6,14},{7,15},{8,0},{9,1},... | collective-permute-start | bytes 196616 | tf_op jit(solution)/shard_map/ppermute | solution.py:262
  14.1 1.1 %collective-permute-start.4 = (bf16[128,256]{1,0:T(8,128)(2,1)S(1)}, bf16[128,256]{1,0:T(8,128)(2,1)S(1)}, u32[]{:S(2)}, u32[]{:S(2)}) collective-permute-start(bf16[128,256]{1,0:T(8,128)(2,1)S(1)} %get-tuple-element.9.refs_0_), channel_id=1, source_target_pairs={{0,12},{1,13},{2,14},{3,15},{4,8},{5,9},{6,10},{7,11},{8,4},{9,5},... | collective-permute-start | bytes 196616 | tf_op jit(solution)/shard_map/ppermute | solution.py:262
  15.2 0.0 copy-start.7
  15.2 0.7 %copy-done.7 = s32[4,16]{1,0:T(4,128)S(1)} copy-done((s32[4,16]{1,0:T(4,128)S(1)}, s32[4,16]{1,0:T(4,128)}, u32[]{:S(2)}) %copy-start.7) | copy-done | bytes 280
  15.9 0.0 copy-start.10
  15.9 0.7 %copy-done.10 = s32[4]{0:T(128)S(1)} copy-done((s32[4]{0:T(128)S(1)}, s32[4]{0:T(128)}, u32[]{:S(2)}) %copy-start.10) | copy-done | bytes 40
  16.5 4.6 %near.1.near_ref._ = f32[4,256,256]{2,1,0:T(8,128)S(1)} custom-call(s32[4,16]{1,0:T(4,128)S(1)} %copy-done.7, s32[4]{0:T(128)S(1)} %copy-done.10, bf16[4,16,256,256]{3,2,1,0:T(8,128)(2,1)} %blocks_hbm.3, bf16[1536,256]{1,0:T(8,128)(2,1)S(1)} %get-tuple-element.8.own_ref.in_ref, bf16[1536,256]{1,0:T(8,128)(2,1)S(1)} %collective-permute-done.share_ref._), custom_call_target="tpu_custom_call" | custom-call | tf_op jit(solution)/shard_map/near/pallas_call | solution.py:229
  21.1 0.0 copy-start
  21.1 0.0 copy-start.9
  21.1 6.5 %collective-permute-done.5.in_ref.level_ref = bf16[512,256]{1,0:T(8,128)(2,1)S(1)} collective-permute-done((bf16[512,256]{1,0:T(8,128)(2,1)S(1)}, bf16[512,256]{1,0:T(8,128)(2,1)S(1)}, u32[]{:S(2)}, u32[]{:S(2)}) %collective-permute-start.5) | collective-permute-done | bytes 262176 | tf_op jit(solution)/shard_map/ppermute | solution.py:262
  27.7 3.2 %collective-permute-start.6 = (bf16[512,256]{1,0:T(8,128)(2,1)S(1)}, bf16[512,256]{1,0:T(8,128)(2,1)S(1)}, u32[]{:S(2)}, u32[]{:S(2)}) collective-permute-start(bf16[512,256]{1,0:T(8,128)(2,1)S(1)} %relay.1), channel_id=1, source_target_pairs={{0,4},{1,5},{4,8},{5,9},{6,2},{7,3},{8,12},{9,13},{10,6},{11,7},{1... | collective-permute-start | bytes 786440 | tf_op jit(solution)/shard_map/ppermute | solution.py:262
  30.9 0.0 collective-permute-done.2.refs_1_
  30.9 0.0 collective-permute-done.3.refs_2_
  30.9 0.0 collective-permute-done.4.refs_3_
  31.0 0.0 copy-start.2
  31.0 0.0 copy-start.5
  31.0 0.0 copy-start.6
  31.0 0.0 copy-start.12
  31.0 0.1 collective-permute-start.8
  31.1 0.0 collective-permute-done.1.across_ref
  31.1 0.0 copy-done.8
  31.1 0.0 copy-done.11
  31.1 2.9 %across.1._.near_ref = f32[4,256,256]{2,1,0:T(8,128)S(1)} custom-call(s32[4,16]{1,0:T(4,128)S(1)} %copy-done.8, s32[4]{0:T(128)S(1)} %copy-done.11, bf16[4,16,256,256]{3,2,1,0:T(8,128)(2,1)} %blocks_hbm.3, f32[4,256,256]{2,1,0:T(8,128)S(1)} %near.1.near_ref._, bf16[1024,256]{1,0:T(8,128)(2,1)S(1)} %collective-permute-done.1.across_ref, ...), custom_call_target="tpu_custom_call" | custom-call | flops 1073741824 | tf_op jit(solution)/shard_map/across/pallas_call | solution.py:229
  34.0 0.8 %collective-permute-done.6.layer_ref = bf16[512,256]{1,0:T(8,128)(2,1)S(1)} collective-permute-done((bf16[512,256]{1,0:T(8,128)(2,1)S(1)}, bf16[512,256]{1,0:T(8,128)(2,1)S(1)}, u32[]{:S(2)}, u32[]{:S(2)}) %collective-permute-start.6) | collective-permute-done | bytes 262176 | tf_op jit(solution)/shard_map/ppermute | solution.py:262
  34.8 0.6 %pick.1 = bf16[512,256]{1,0:T(8,128)(2,1)S(1)} custom-call(s32[4,16]{1,0:T(4,128)S(1)} %copy-done.8, bf16[512,256]{1,0:T(8,128)(2,1)S(1)} %collective-permute-done.5.in_ref.level_ref, bf16[512,256]{1,0:T(8,128)(2,1)S(1)} %collective-permute-done.6.layer_ref, f32[4,256,256]{2,1,0:T(8,128)S(1)} %across.1._.near_ref), custom_call_target="tpu_custom_call" | custom-call | tf_op jit(solution)/shard_map/pick/pallas_call | solution.py:229
  35.4 2.7 %collective-permute-start.7 = (bf16[512,256]{1,0:T(8,128)(2,1)S(1)}, bf16[512,256]{1,0:T(8,128)(2,1)S(1)}, u32[]{:S(2)}, u32[]{:S(2)}) collective-permute-start(bf16[512,256]{1,0:T(8,128)(2,1)S(1)} %pick.1), channel_id=1, source_target_pairs={{0,1},{1,0},{2,3},{3,2},{4,5},{5,4},{6,7},{7,6},{8,9},{9,8},{10,11... | collective-permute-start | bytes 786440 | tf_op jit(solution)/shard_map/ppermute | solution.py:262
  38.1 0.1 collective-permute-start.9
  38.1 0.0 collective-permute-done.8.beside_ref
  38.2 1.7 %collective-permute-start.10 = (bf16[512,256]{1,0:T(8,128)(2,1)S(1)}, bf16[512,256]{1,0:T(8,128)(2,1)S(1)}, u32[]{:S(2)}, u32[]{:S(2)}) collective-permute-start(bf16[512,256]{1,0:T(8,128)(2,1)S(1)} %collective-permute-done.8.beside_ref), channel_id=1, source_target_pairs={{0,1},{1,0},{2,3},{3,2},{4,5},{5,4},{6,7},{7,6},{8,9},{9,8},{10,11... | collective-permute-start | bytes 786440 | tf_op jit(solution)/shard_map/ppermute | solution.py:262
  39.8 0.0 collective-permute-done.7.passed_ref
  39.8 0.0 copy-done
  39.8 0.0 copy-done.9
  39.8 1.5 %far.1.far_ref = f32[512,256]{1,0:T(8,128)S(1)} custom-call(s32[4,16]{1,0:T(4,128)S(1)} %copy-done.9, s32[4,16]{1,0:T(4,128)S(1)} %copy-done.8, bf16[4,16,128,128]{3,2,1,0:T(8,128)(2,1)S(1)} %copy-done, bf16[512,256]{1,0:T(8,128)(2,1)S(1)} %collective-permute-done.5.in_ref.level_ref, bf16[512,256]{1,0:T(8,128)(2,1)S(1)} %collective-permute-done.6.layer_ref, ...), custom_call_target="tpu_custom_call" | custom-call | flops 536870912 | bytes 2097152 | tf_op jit(solution)/shard_map/far/pallas_call | solution.py:229
  41.4 0.0 collective-permute-done.9.their_column_ref
  41.4 0.0 collective-permute-done.10.their_beside_ref
  41.4 0.0 copy-done.2
  41.4 0.0 copy-done.5
  41.4 0.0 copy-done.6
  41.4 0.0 copy-done.12
  41.4 2.5 %down.1 = bf16[1024,256]{1,0:T(8,128)(2,1)} custom-call(s32[1,8]{1,0:T(1,128)S(1)} %copy-done.12, s32[4,16]{1,0:T(4,128)S(1)} %copy-done.8, bf16[4,128,128]{2,1,0:T(8,128)(2,1)S(1)} %copy-done.2, bf16[1,8,128,128]{3,2,1,0:T(8,128)(2,1)S(1)} %copy-done.5, bf16[4,256,128]{2,1,0:T(8,128)(2,1)S(1)} %copy-done.6, f32[4,256,256]{2,1,0:T(8,128)S(1)} %across.1._.near_ref, ...), custom_call_target="tpu_custom_call" | custom-call | flops 134217728 | bytes 1048576 | tf_op jit(solution)/shard_map/down/pallas_call | solution.py:229
  (3 shorter events, 0.1 us)
Async XLA Ops:
  0.0 0.9 %copy-start.1 = (bf16[4,128,128]{2,1,0:T(8,128)(2,1)S(1)}, bf16[4,128,128]{2,1,0:T(8,128)(2,1)}, u32[]{:S(2)}) copy-start(bf16[4,128,128]{2,1,0:T(8,128)(2,1)} %transfer_ref.3) | copy-start | bytes 393220
  0.9 1.0 %copy-start.3 = (bf16[1024,256]{1,0:T(8,128)(2,1)S(1)}, bf16[1024,256]{1,0:T(8,128)(2,1)}, u32[]{:S(2)}) copy-start(bf16[1024,256]{1,0:T(8,128)(2,1)} %source_ref.1) | copy-start | bytes 1572868
  1.9 0.9 %copy-start.4 = (bf16[4,256,128]{2,1,0:T(8,128)(2,1)S(1)}, bf16[4,256,128]{2,1,0:T(8,128)(2,1)}, u32[]{:S(2)}) copy-start(bf16[4,256,128]{2,1,0:T(8,128)(2,1)} %col_ref.1) | copy-start | bytes 786436
  2.9 28.2 %copy-start.8 = (s32[4,16]{1,0:T(4,128)S(1)}, s32[4,16]{1,0:T(4,128)}, u32[]{:S(2)}) copy-start(s32[4,16]{1,0:T(4,128)} %near_list_ref.3) | copy-start | bytes 772
  2.9 28.2 %copy-start.11 = (s32[4]{0:T(128)S(1)}, s32[4]{0:T(128)}, u32[]{:S(2)}) copy-start(s32[4]{0:T(128)} %count_ref.3) | copy-start | bytes 52
  3.4 2.4 %collective-permute-start = (bf16[1536,256]{1,0:T(8,128)(2,1)S(1)}, bf16[1536,256]{1,0:T(8,128)(2,1)S(1)}, u32[]{:S(2)}, u32[]{:S(2)}) collective-permute-start(bf16[1536,256]{1,0:T(8,128)(2,1)S(1)} %get-tuple-element.8.own_ref.in_ref), channel_id=1, source_target_pairs={{0,1},{1,0},{2,3},{3,2},{4,5},{5,4},{6,7},{7,6},{8,9},{9,8},{10,11... | collective-permute-start | bytes 2359304 | tf_op jit(solution)/shard_map/ppermute | solution.py:262
  5.8 25.3 %collective-permute-start.1 = (bf16[1024,256]{1,0:T(8,128)(2,1)S(1)}, bf16[1024,256]{1,0:T(8,128)(2,1)S(1)}, u32[]{:S(2)}, u32[]{:S(2)}) collective-permute-start(bf16[1024,256]{1,0:T(8,128)(2,1)S(1)} %panels.1), channel_id=1, source_target_pairs={{1,2},{2,1},{3,4},{4,3},{5,6},{6,5},{7,8},{8,7},{9,10},{10,9},{11,... | collective-permute-start | bytes 1572872 | tf_op jit(solution)/shard_map/ppermute | solution.py:262
  10.3 17.3 %collective-permute-start.5 = (bf16[512,256]{1,0:T(8,128)(2,1)S(1)}, bf16[512,256]{1,0:T(8,128)(2,1)S(1)}, u32[]{:S(2)}, u32[]{:S(2)}) collective-permute-start(bf16[512,256]{1,0:T(8,128)(2,1)S(1)} %get-tuple-element.10), channel_id=1, source_target_pairs={{0,2},{1,3},{2,0},{3,1},{4,6},{5,7},{6,4},{7,5},{8,10},{9,11},{10,... | collective-permute-start | bytes 786440 | tf_op jit(solution)/shard_map/ppermute | solution.py:262
  11.6 19.3 %collective-permute-start.2 = (bf16[128,256]{1,0:T(8,128)(2,1)S(1)}, bf16[128,256]{1,0:T(8,128)(2,1)S(1)}, u32[]{:S(2)}, u32[]{:S(2)}) collective-permute-start(bf16[128,256]{1,0:T(8,128)(2,1)S(1)} %get-tuple-element.9.refs_0_), channel_id=1, source_target_pairs={{0,4},{1,5},{2,6},{3,7},{4,0},{5,1},{6,2},{7,3},{8,12},{9,13},{10,... | collective-permute-start | bytes 196616 | tf_op jit(solution)/shard_map/ppermute | solution.py:262
  12.9 18.0 %collective-permute-start.3 = (bf16[128,256]{1,0:T(8,128)(2,1)S(1)}, bf16[128,256]{1,0:T(8,128)(2,1)S(1)}, u32[]{:S(2)}, u32[]{:S(2)}) collective-permute-start(bf16[128,256]{1,0:T(8,128)(2,1)S(1)} %get-tuple-element.9.refs_0_), channel_id=1, source_target_pairs={{0,8},{1,9},{2,10},{3,11},{4,12},{5,13},{6,14},{7,15},{8,0},{9,1},... | collective-permute-start | bytes 196616 | tf_op jit(solution)/shard_map/ppermute | solution.py:262
  14.1 16.9 %collective-permute-start.4 = (bf16[128,256]{1,0:T(8,128)(2,1)S(1)}, bf16[128,256]{1,0:T(8,128)(2,1)S(1)}, u32[]{:S(2)}, u32[]{:S(2)}) collective-permute-start(bf16[128,256]{1,0:T(8,128)(2,1)S(1)} %get-tuple-element.9.refs_0_), channel_id=1, source_target_pairs={{0,12},{1,13},{2,14},{3,15},{4,8},{5,9},{6,10},{7,11},{8,4},{9,5},... | collective-permute-start | bytes 196616 | tf_op jit(solution)/shard_map/ppermute | solution.py:262
  15.2 0.7 %copy-start.7 = (s32[4,16]{1,0:T(4,128)S(1)}, s32[4,16]{1,0:T(4,128)}, u32[]{:S(2)}) copy-start(s32[4,16]{1,0:T(4,128)} %near_list_ref.3) | copy-start | bytes 772
  15.9 0.7 %copy-start.10 = (s32[4]{0:T(128)S(1)}, s32[4]{0:T(128)}, u32[]{:S(2)}) copy-start(s32[4]{0:T(128)} %count_ref.3) | copy-start | bytes 52
  21.1 18.7 %copy-start = (bf16[4,16,128,128]{3,2,1,0:T(8,128)(2,1)S(1)}, bf16[4,16,128,128]{3,2,1,0:T(8,128)(2,1)}, u32[]{:S(2)}) copy-start(bf16[4,16,128,128]{3,2,1,0:T(8,128)(2,1)} %coupling_ref.2) | copy-start | bytes 6291460
  21.1 18.7 %copy-start.9 = (s32[4,16]{1,0:T(4,128)S(1)}, s32[4,16]{1,0:T(4,128)}, u32[]{:S(2)}) copy-start(s32[4,16]{1,0:T(4,128)} %list_ref.8) | copy-start | bytes 772
  27.7 7.1 %collective-permute-start.6 = (bf16[512,256]{1,0:T(8,128)(2,1)S(1)}, bf16[512,256]{1,0:T(8,128)(2,1)S(1)}, u32[]{:S(2)}, u32[]{:S(2)}) collective-permute-start(bf16[512,256]{1,0:T(8,128)(2,1)S(1)} %relay.1), channel_id=1, source_target_pairs={{0,4},{1,5},{4,8},{5,9},{6,2},{7,3},{8,12},{9,13},{10,6},{11,7},{1... | collective-permute-start | bytes 786440 | tf_op jit(solution)/shard_map/ppermute | solution.py:262
  31.0 10.4 %copy-start.2 = (bf16[4,128,128]{2,1,0:T(8,128)(2,1)S(1)}, bf16[4,128,128]{2,1,0:T(8,128)(2,1)}, u32[]{:S(2)}) copy-start(bf16[4,128,128]{2,1,0:T(8,128)(2,1)} %transfer_ref.3) | copy-start | bytes 393220
  31.0 10.4 %copy-start.5 = (bf16[1,8,128,128]{3,2,1,0:T(8,128)(2,1)S(1)}, bf16[1,8,128,128]{3,2,1,0:T(8,128)(2,1)}, u32[]{:S(2)}) copy-start(bf16[1,8,128,128]{3,2,1,0:T(8,128)(2,1)} %coupling_ref.3) | copy-start | bytes 786436
  31.0 10.4 %copy-start.6 = (bf16[4,256,128]{2,1,0:T(8,128)(2,1)S(1)}, bf16[4,256,128]{2,1,0:T(8,128)(2,1)}, u32[]{:S(2)}) copy-start(bf16[4,256,128]{2,1,0:T(8,128)(2,1)} %row_ref.1) | copy-start | bytes 786436
  31.0 10.4 %copy-start.12 = (s32[1,8]{1,0:T(1,128)S(1)}, s32[1,8]{1,0:T(1,128)}, u32[]{:S(2)}) copy-start(s32[1,8]{1,0:T(1,128)} %list_ref.9) | copy-start | bytes 100
  31.0 7.1 %collective-permute-start.8 = (bf16[512,256]{1,0:T(8,128)(2,1)S(1)}, bf16[512,256]{1,0:T(8,128)(2,1)S(1)}, u32[]{:S(2)}, u32[]{:S(2)}) collective-permute-start(bf16[512,256]{1,0:T(8,128)(2,1)S(1)} %column.1._.column_ref), channel_id=1, source_target_pairs={{0,2},{1,3},{2,0},{3,1},{4,6},{5,7},{6,4},{7,5},{8,10},{9,11},{10,... | collective-permute-start | bytes 786440 | tf_op jit(solution)/shard_map/ppermute | solution.py:262
  35.4 4.4 %collective-permute-start.7 = (bf16[512,256]{1,0:T(8,128)(2,1)S(1)}, bf16[512,256]{1,0:T(8,128)(2,1)S(1)}, u32[]{:S(2)}, u32[]{:S(2)}) collective-permute-start(bf16[512,256]{1,0:T(8,128)(2,1)S(1)} %pick.1), channel_id=1, source_target_pairs={{0,1},{1,0},{2,3},{3,2},{4,5},{5,4},{6,7},{7,6},{8,9},{9,8},{10,11... | collective-permute-start | bytes 786440 | tf_op jit(solution)/shard_map/ppermute | solution.py:262
  38.1 3.3 %collective-permute-start.9 = (bf16[512,256]{1,0:T(8,128)(2,1)S(1)}, bf16[512,256]{1,0:T(8,128)(2,1)S(1)}, u32[]{:S(2)}, u32[]{:S(2)}) collective-permute-start(bf16[512,256]{1,0:T(8,128)(2,1)S(1)} %column.1._.column_ref), channel_id=1, source_target_pairs={{0,1},{1,0},{2,3},{3,2},{4,5},{5,4},{6,7},{7,6},{8,9},{9,8},{10,11... | collective-permute-start | bytes 786440 | tf_op jit(solution)/shard_map/ppermute | solution.py:262
  38.2 3.2 %collective-permute-start.10 = (bf16[512,256]{1,0:T(8,128)(2,1)S(1)}, bf16[512,256]{1,0:T(8,128)(2,1)S(1)}, u32[]{:S(2)}, u32[]{:S(2)}) collective-permute-start(bf16[512,256]{1,0:T(8,128)(2,1)S(1)} %collective-permute-done.8.beside_ref), channel_id=1, source_target_pairs={{0,1},{1,0},{2,3},{3,2},{4,5},{5,4},{6,7},{7,6},{8,9},{9,8},{10,11... | collective-permute-start | bytes 786440 | tf_op jit(solution)/shard_map/ppermute | solution.py:262

commit v10 on v9

--- a/solution.py
+++ b/solution.py
@@ -7,6 +7,7 @@
 
 GROUP = 16
 CHUNK = 4
+AHEAD = 4
 MIB = 2**20
 
 VMEM = pl.BlockSpec(memory_space=pltpu.VMEM)
@@ -50,89 +51,76 @@
         at += ref.shape[0]
 
 
-def pick_kernel(list_ref, level_ref, layer_ref, _, out_ref):
+def pick_kernel(list_ref, level_ref, layer_ref, out_ref):
     corner = lax.div(list_ref[0, 0], list_ref.shape[0]) & 3
     level = (corner == 0) | (corner == 3)
     out_ref[...] = jnp.where(level, level_ref[...], layer_ref[...])
 
 
-def hand_kernel(in_ref, _, out_ref):
+def hand_kernel(in_ref, *refs):
+    out_ref = refs[-1]
     out_ref[...] = in_ref[pl.ds(0, out_ref.shape[0]), :]
 
 
-def pick_slots(list_ref, count_ref, blocks_hbm, blocks, sems, order_ref, leaf, keep):
-    leaves, _ = list_ref.shape
-
-    def step(slot, found):
-        column = list_ref[leaf, slot]
-        kept = keep(lax.div(column, leaves))
-
-        @pl.when(kept)
-        def _():
-            order_ref[leaf, found] = column
-            pltpu.make_async_copy(
-                blocks_hbm.at[leaf, slot], blocks.at[leaf, found], sems.at[leaf, found]
-            ).start()
-
-        return found + kept.astype(jnp.int32)
-
-    found = lax.fori_loop(0, count_ref[leaf], step, 0)
-    for pad in range(CHUNK):
-        order_ref[leaf, found + pad] = -1
-    return found
-
-
-def add_slots(total_ref, blocks_hbm, blocks, sems, order_ref, leaf, found, panel_of):
-    for first in range(0, blocks.shape[1], CHUNK):
-        @pl.when(first < found)
-        def _():
-            for n in range(first, first + CHUNK):
-                @pl.when(n < found)
-                def _():
-                    pltpu.make_async_copy(
-                        blocks_hbm.at[leaf, 0], blocks.at[leaf, n], sems.at[leaf, n]
-                    ).wait()
-            total = total_ref[leaf]
-            for n in range(first, first + CHUNK):
-                block = blocks[leaf, jnp.where(n < found, n, 0)]
-                total = total + dot(block, panel_of(order_ref[leaf, n]))
-            total_ref[leaf] = total
-
-
 def near_kernel(
-    list_ref, count_ref, blocks_hbm, own_ref, share_ref,
+    list_ref, count_ref, blocks_hbm, own_ref, share_ref, across_ref,
     near_ref,
-    blocks, panels, order, block_sems, panel_sems,
+    blocks, panels, block_sems, panel_sems,
 ):
-    leaves, _, rows, _ = blocks.shape
+    leaves, slots, rows, _ = blocks.shape
+    chunks = slots // CHUNK
     size = leaves * rows
     place = lax.div(list_ref[0, 0], leaves)
+
+    def live(step):
+        return step % chunks * CHUNK < count_ref[step // chunks]
+
+    def block_copy(step):
+        leaf, chunk = step // chunks, step % chunks
+        where = pl.ds(chunk * CHUNK, CHUNK)
+        return pltpu.make_async_copy(
+            blocks_hbm.at[leaf, where], blocks.at[leaf, where], block_sems.at[leaf, chunk]
+        )
+
+    def start(step):
+        if step < leaves * chunks:
+            @pl.when(live(step))
+            def _():
+                block_copy(step).start()
+
     pairs = [
         pltpu.make_async_copy(
             ref.at[pl.ds(0, size)], panels.at[pl.ds(which * size, size)], panel_sems.at[which]
         )
-        for which, ref in enumerate((own_ref, share_ref))
+        for which, ref in enumerate((own_ref, share_ref, across_ref))
     ]
     for copy in pairs:
         copy.start()
-    found = [
-        pick_slots(
-            list_ref, count_ref, blocks_hbm, blocks, block_sems, order, leaf,
-            lambda cluster: (cluster ^ place) <= 1,
-        )
-        for leaf in range(leaves)
-    ]
-    near_ref[...] = jnp.zeros(near_ref.shape, near_ref.dtype)
-    panels[pl.ds(2 * size, rows), :] = jnp.zeros((rows, panels.shape[1]), panels.dtype)
+    for step in range(AHEAD):
+        start(step)
+    panels[pl.ds(3 * size, rows), :] = jnp.zeros((rows, panels.shape[1]), panels.dtype)
     for copy in pairs:
         copy.wait()
 
-    def panel_of(column):
-        index = (lax.div(column, leaves) ^ place) * leaves + (column & (leaves - 1))
-        return panels[rows_at(jnp.where(column < 0, 2 * leaves, index), rows), :]
-
-    for leaf in range(leaves):
-        add_slots(near_ref, blocks_hbm, blocks, block_sems, order, leaf, found[leaf], panel_of)
+    def panel_of(leaf, slot):
+        column = list_ref[leaf, slot]
+        which = jnp.minimum(lax.div(column, leaves) ^ place, 2)
+        index = which * leaves + (column & (leaves - 1))
+        index = jnp.where(slot < count_ref[leaf], index, 3 * leaves)
+        return panels[rows_at(index, rows), :]
+
+    for step in range(leaves * chunks):
+        leaf, chunk = step // chunks, step % chunks
+        start(step + AHEAD)
+
+        @pl.when(live(step))
+        def _():
+            block_copy(step).wait()
+            total = None if chunk == 0 else near_ref[leaf]
+            for slot in range(chunk * CHUNK, (chunk + 1) * CHUNK):
+                term = dot(blocks[leaf, slot], panel_of(leaf, slot))
+                total = term if total is None else total + term
+            near_ref[leaf] = total
 
 
 def far_kernel(
@@ -200,30 +188,6 @@
         out_ref[pl.ds(leaf * rows, rows), :] = result.astype(jnp.bfloat16)
 
 
-def across_kernel(
-    list_ref, count_ref, blocks_hbm, near_ref, across_ref, _,
-    total_ref,
-    blocks, order, sems,
-):
-    leaves, _, rows, _ = blocks.shape
-    place = lax.div(list_ref[0, 0], leaves)
-    found = [
-        pick_slots(
-            list_ref, count_ref, blocks_hbm, blocks, sems, order, leaf,
-            lambda cluster: (cluster ^ place) > 1,
-        )
-        for leaf in range(leaves)
-    ]
-    total_ref[...] = near_ref[...]
-
-    def panel_of(column):
-        panel = across_ref[rows_at(column & (leaves - 1), rows), :]
-        return jnp.where(column < 0, jnp.zeros_like(panel), panel)
-
-    for leaf in range(leaves):
-        add_slots(total_ref, blocks_hbm, blocks, sems, order, leaf, found[leaf], panel_of)
-
-
 def call(kernel, name, outs, specs, args, scratch=(), flops=0, moved=0, limit=4):
     many = isinstance(outs, tuple)
     return pl.pallas_call(
@@ -275,41 +239,29 @@
     share_other = send(share, lambda d: d ^ 1)
     level = send(coef, lambda d: d ^ 2)
     panels = call(
-        hand_kernel, "panels", jax.ShapeDtypeStruct(source.shape, jnp.bfloat16), [VMEM, ANY],
+        hand_kernel, "panels", jax.ShapeDtypeStruct(source.shape, jnp.bfloat16), [VMEM] + [ANY] * 1,
         (share, share_other),
     )
     across = send(panels, lambda d: d + 1 if d & 1 else d - 1)
 
-    picked = [
-        pltpu.VMEM(near_blocks.shape, jnp.bfloat16),
-        pltpu.SMEM((leaves, slots + CHUNK), jnp.int32),
-        pltpu.SemaphoreType.DMA((leaves, slots)),
-    ]
-    near = call(
-        near_kernel, "near", jax.ShapeDtypeStruct((leaves, rows, width), jnp.float32),
-        [SMEM, SMEM] + [ANY] * 3, (near_list, near_count, near_blocks, share, share_other),
-        scratch=[
-            picked[0],
-            pltpu.VMEM(((2 * leaves + 1) * rows, width), jnp.bfloat16),
-            *picked[1:],
-            pltpu.SemaphoreType.DMA((2,)),
-        ],
-        limit=48,
-    )
-    relay = call(hand_kernel, "relay", panel(leaves), [VMEM, ANY], (level, near))
-    layer = send(relay, lambda d: d - 4 if d & 2 else d + 4)
+    layer = send(level, lambda d: d - 4 if d & 2 else d + 4)
     column = call(join_kernel, "column", panel(GROUP // 4), [VMEM] * 4, (parent, *layers))
     beside = send(column, lambda d: d ^ 2)
     their_column = send(column, lambda d: d ^ 1)
     near = call(
-        across_kernel, "across", jax.ShapeDtypeStruct((leaves, rows, width), jnp.float32),
-        [SMEM] * 2 + [ANY] + [VMEM] * 2 + [ANY],
-        (near_list, near_count, near_blocks, near, across, column),
-        scratch=picked,
-        flops=leaves * slots * rows * rows * width, moved=0, limit=48,
+        near_kernel, "near", jax.ShapeDtypeStruct((leaves, rows, width), jnp.float32),
+        [SMEM, SMEM] + [ANY] * 4,
+        (near_list, near_count, near_blocks, share, share_other, across),
+        scratch=[
+            pltpu.VMEM(near_blocks.shape, jnp.bfloat16),
+            pltpu.VMEM(((3 * leaves + 1) * rows, width), jnp.bfloat16),
+            pltpu.SemaphoreType.DMA((leaves, slots // CHUNK)),
+            pltpu.SemaphoreType.DMA((3,)),
+        ],
+        limit=48,
     )
     picked_coef = call(
-        pick_kernel, "pick", panel(leaves), [SMEM] + [VMEM] * 2 + [ANY], (near_list, level, layer, near)
+        pick_kernel, "pick", panel(leaves), [SMEM] + [VMEM] * 2, (near_list, level, layer)
     )
     passed = send(picked_coef, lambda d: d ^ 1)
     far = call(
@@ -322,13 +274,14 @@
         flops=2 * leaves * far_slots * rank * rank * width,
         moved=2 * leaves * far_slots * rank * rank, limit=10,
     )
-    their_beside = send(beside, lambda d: d ^ 1)
+    handed = call(hand_kernel, "hand", panel(GROUP // 4), [VMEM, ANY], (beside, near))
+    their_beside = send(handed, lambda d: d ^ 1)
     return call(
         down_kernel, "down", jax.ShapeDtypeStruct(source.shape, jnp.bfloat16),
         [SMEM] * 2 + [VMEM] * 9,
         (
             coarse_list, near_list, transfer, coarse_coupling, row_basis, near, far,
-            column, beside, their_column, their_beside,
+            column, handed, their_column, their_beside,
         ),
         flops=8 * leaves * rank * rank * width,
         moved=4 * leaves * rows * width, limit=8,

time: 44.3 us -> 39 us (0.88)
  waiting for transfers between devices: 9.58 us -> 2.54 us
  starting transfers between devices: 17.2 us -> 20.8 us
  Pallas kernels: 12.7 us -> 11.2 us
    ppermute x11, waiting for transfers between devices: 9.58 us -> 2.54 us  [send(): return lax.ppermute(value, 'row', pairs)]
    ppermute x11, starting transfers between devices: 17.2 us -> 20.8 us  [send(): return lax.ppermute(value, 'row', pairs)]
    pallas_call x9 -> x8, Pallas kernels: 12.7 us -> 11.2 us  [call(): pl.pallas_call(kernel, out_shape=outs, in_specs=specs, out_specs=(VMEM,)...]
    unnamed x26 -> x22, local copies, waits for them, and re-layouts: 4.28 us -> 4.27 us
  transfers between devices with their start and end apart: 11 -> 11, of which waited for: 3 -> 1; matrix products, arithmetic and copies ran while one was open for 0% -> 0% of each run, Pallas kernels for 22% -> 21%
where the time goes in v10:
time: 39 us; the launch traced here: 38.9 us
  starting transfers between devices  20.8 us (53%)
  Pallas kernels  11.2 us (29%)
  local copies, waits for them, and re-layouts  4.27 us (11%)
  waiting for transfers between devices  2.54 us (7%)
    ppermute x11, starting transfers between devices, send(): return lax.ppermute(value, 'row', pairs)  20.8 us
    pallas_call x8, Pallas kernels, call(): pl.pallas_call(kernel, out_shape=outs, in_specs=specs, out_specs=(VMEM,)...  11.2 us
    unnamed x22, local copies, waits for them, and re-layouts  4.27 us
    ppermute x11, waiting for transfers between devices, send(): return lax.ppermute(value, 'row', pairs)  2.54 us
  transfers between devices with their start and end apart: 11, of which 1 were waited for; matrix products, arithmetic and copies ran while one was open for 0% of the time, Pallas kernels for 21%

profile of v10, /device:TPU:1, one launch (start us, length us, event | category | flops | bytes accessed | tf_op | source)
XLA Modules:
  0.0 38.9 jit_solution(15819635611124789000)
XLA Ops:
  0.0 0.0 copy-start.1
  0.0 0.9 %copy-done.1 = bf16[4,128,128]{2,1,0:T(8,128)(2,1)S(1)} copy-done((bf16[4,128,128]{2,1,0:T(8,128)(2,1)S(1)}, bf16[4,128,128]{2,1,0:T(8,128)(2,1)}, u32[]{:S(2)}) %copy-start.1) | copy-done | bytes 131096
  0.9 0.0 copy-start.3
  0.9 1.0 %copy-done.3 = bf16[1024,256]{1,0:T(8,128)(2,1)S(1)} copy-done((bf16[1024,256]{1,0:T(8,128)(2,1)S(1)}, bf16[1024,256]{1,0:T(8,128)(2,1)}, u32[]{:S(2)}) %copy-start.3) | copy-done | bytes 524312
  1.9 0.0 copy-start.4
  1.9 0.9 %copy-done.4 = bf16[4,256,128]{2,1,0:T(8,128)(2,1)S(1)} copy-done((bf16[4,256,128]{2,1,0:T(8,128)(2,1)S(1)}, bf16[4,256,128]{2,1,0:T(8,128)(2,1)}, u32[]{:S(2)}) %copy-start.4) | copy-done | bytes 262168
  2.9 0.5 %up.1 = (bf16[1536,256]{1,0:T(8,128)(2,1)S(1)}, bf16[512,256]{1,0:T(8,128)(2,1)S(1)}, bf16[128,256]{1,0:T(8,128)(2,1)S(1)}) custom-call(bf16[1024,256]{1,0:T(8,128)(2,1)S(1)} %copy-done.3, bf16[4,256,128]{2,1,0:T(8,128)(2,1)S(1)} %copy-done.4, bf16[4,128,128]{2,1,0:T(8,128)(2,1)S(1)} %copy-done.1), custom_call_target="tpu_custom_call" | custom-call | flops 100663296 | bytes 786432 | tf_op jit(solution)/shard_map/up/pallas_call | solution.py:193
  3.4 0.0 copy-start
  3.4 0.0 copy-start.8
  3.4 0.1 collective-permute-start
  3.5 2.7 %collective-permute-start.2 = (bf16[512,256]{1,0:T(8,128)(2,1)S(1)}, bf16[512,256]{1,0:T(8,128)(2,1)S(1)}, u32[]{:S(2)}, u32[]{:S(2)}) collective-permute-start(bf16[512,256]{1,0:T(8,128)(2,1)S(1)} %get-tuple-element.9), channel_id=1, source_target_pairs={{0,2},{1,3},{2,0},{3,1},{4,6},{5,7},{6,4},{7,5},{8,10},{9,11},{10,... | collective-permute-start | bytes 786440 | tf_op jit(solution)/shard_map/ppermute | solution.py:226
  6.2 0.0 collective-permute-done.refs_0_.share_ref
  6.3 4.1 %collective-permute-start.1 = (bf16[1024,256]{1,0:T(8,128)(2,1)S(1)}, bf16[1024,256]{1,0:T(8,128)(2,1)S(1)}, u32[]{:S(2)}, u32[]{:S(2)}) collective-permute-start(bf16[1024,256]{1,0:T(8,128)(2,1)S(1)} %panels.1), channel_id=1, source_target_pairs={{1,2},{2,1},{3,4},{4,3},{5,6},{6,5},{7,8},{8,7},{9,10},{10,9},{11,... | collective-permute-start | bytes 1572872 | tf_op jit(solution)/shard_map/ppermute | solution.py:226
  10.3 1.4 %collective-permute-start.5 = (bf16[128,256]{1,0:T(8,128)(2,1)S(1)}, bf16[128,256]{1,0:T(8,128)(2,1)S(1)}, u32[]{:S(2)}, u32[]{:S(2)}) collective-permute-start(bf16[128,256]{1,0:T(8,128)(2,1)S(1)} %get-tuple-element.10.refs_0_), channel_id=1, source_target_pairs={{0,4},{1,5},{2,6},{3,7},{4,0},{5,1},{6,2},{7,3},{8,12},{9,13},{10,... | collective-permute-start | bytes 196616 | tf_op jit(solution)/shard_map/ppermute | solution.py:226
  11.7 2.3 %collective-permute-start.6 = (bf16[128,256]{1,0:T(8,128)(2,1)S(1)}, bf16[128,256]{1,0:T(8,128)(2,1)S(1)}, u32[]{:S(2)}, u32[]{:S(2)}) collective-permute-start(bf16[128,256]{1,0:T(8,128)(2,1)S(1)} %get-tuple-element.10.refs_0_), channel_id=1, source_target_pairs={{0,8},{1,9},{2,10},{3,11},{4,12},{5,13},{6,14},{7,15},{8,0},{9,1},... | collective-permute-start | bytes 196616 | tf_op jit(solution)/shard_map/ppermute | solution.py:226
  14.0 0.0 collective-permute-start.7
  14.0 0.0 collective-permute-done.2.level_ref
  14.0 3.1 %collective-permute-start.3 = (bf16[512,256]{1,0:T(8,128)(2,1)S(1)}, bf16[512,256]{1,0:T(8,128)(2,1)S(1)}, u32[]{:S(2)}, u32[]{:S(2)}) collective-permute-start(bf16[512,256]{1,0:T(8,128)(2,1)S(1)} %collective-permute-done.2.level_ref), channel_id=1, source_target_pairs={{0,4},{1,5},{4,8},{5,9},{6,2},{7,3},{8,12},{9,13},{10,6},{11,7},{1... | collective-permute-start | bytes 786440 | tf_op jit(solution)/shard_map/ppermute | solution.py:226
  17.2 0.0 collective-permute-done.5.refs_1_
  17.2 0.0 collective-permute-done.6.refs_2_
  17.2 2.5 %collective-permute-done.7.refs_3_ = bf16[128,256]{1,0:T(8,128)(2,1)S(1)} collective-permute-done((bf16[128,256]{1,0:T(8,128)(2,1)S(1)}, bf16[128,256]{1,0:T(8,128)(2,1)S(1)}, u32[]{:S(2)}, u32[]{:S(2)}) %collective-permute-start.7) | collective-permute-done | bytes 65568 | tf_op jit(solution)/shard_map/ppermute | solution.py:226
  19.7 2.3 %collective-permute-start.8 = (bf16[512,256]{1,0:T(8,128)(2,1)S(1)}, bf16[512,256]{1,0:T(8,128)(2,1)S(1)}, u32[]{:S(2)}, u32[]{:S(2)}) collective-permute-start(bf16[512,256]{1,0:T(8,128)(2,1)S(1)} %column.1.column_ref), channel_id=1, source_target_pairs={{0,2},{1,3},{2,0},{3,1},{4,6},{5,7},{6,4},{7,5},{8,10},{9,11},{10,... | collective-permute-start | bytes 786440 | tf_op jit(solution)/shard_map/ppermute | solution.py:226
  22.1 0.0 collective-permute-done.3.layer_ref
  22.1 0.0 copy-start.7
  22.1 0.7 %copy-done.7 = s32[4,16]{1,0:T(4,128)S(1)} copy-done((s32[4,16]{1,0:T(4,128)S(1)}, s32[4,16]{1,0:T(4,128)}, u32[]{:S(2)}) %copy-start.7) | copy-done | bytes 280
  22.8 0.0 copy-start.10
  22.8 0.6 %pick.1 = bf16[512,256]{1,0:T(8,128)(2,1)S(1)} custom-call(s32[4,16]{1,0:T(4,128)S(1)} %copy-done.7, bf16[512,256]{1,0:T(8,128)(2,1)S(1)} %collective-permute-done.2.level_ref, bf16[512,256]{1,0:T(8,128)(2,1)S(1)} %collective-permute-done.3.layer_ref), custom_call_target="tpu_custom_call" | custom-call | tf_op jit(solution)/shard_map/pick/pallas_call | solution.py:193
  23.4 0.0 copy-start.2
  23.4 0.0 copy-start.5
  23.4 0.0 copy-start.6
  23.4 3.5 %collective-permute-start.4 = (bf16[512,256]{1,0:T(8,128)(2,1)S(1)}, bf16[512,256]{1,0:T(8,128)(2,1)S(1)}, u32[]{:S(2)}, u32[]{:S(2)}) collective-permute-start(bf16[512,256]{1,0:T(8,128)(2,1)S(1)} %pick.1), channel_id=1, source_target_pairs={{0,1},{1,0},{2,3},{3,2},{4,5},{5,4},{6,7},{7,6},{8,9},{9,8},{10,11... | collective-permute-start | bytes 786440 | tf_op jit(solution)/shard_map/ppermute | solution.py:226
  26.9 0.1 collective-permute-start.9
  27.0 0.0 collective-permute-done.1.across_ref
  27.0 0.0 copy-start.9
  27.0 0.7 %copy-done.9 = s32[4]{0:T(128)S(1)} copy-done((s32[4]{0:T(128)S(1)}, s32[4]{0:T(128)}, u32[]{:S(2)}) %copy-start.9) | copy-done | bytes 40
  27.7 5.9 %near.1.refs_0_.near_ref = f32[4,256,256]{2,1,0:T(8,128)S(1)} custom-call(s32[4,16]{1,0:T(4,128)S(1)} %copy-done.7, s32[4]{0:T(128)S(1)} %copy-done.9, bf16[4,16,256,256]{3,2,1,0:T(8,128)(2,1)} %blocks_hbm.1, bf16[1536,256]{1,0:T(8,128)(2,1)S(1)} %get-tuple-element.8.in_ref.own_ref, bf16[1536,256]{1,0:T(8,128)(2,1)S(1)} %collective-permute-done.refs_0_.share_ref, ...), custom_call_target="tpu_custom_call" | custom-call | tf_op jit(solution)/shard_map/near/pallas_call | solution.py:193
  33.6 0.0 collective-permute-done.8.in_ref
  33.6 1.1 %collective-permute-start.10 = (bf16[512,256]{1,0:T(8,128)(2,1)S(1)}, bf16[512,256]{1,0:T(8,128)(2,1)S(1)}, u32[]{:S(2)}, u32[]{:S(2)}) collective-permute-start(bf16[512,256]{1,0:T(8,128)(2,1)S(1)} %hand.1.beside_ref), channel_id=1, source_target_pairs={{0,1},{1,0},{2,3},{3,2},{4,5},{5,4},{6,7},{7,6},{8,9},{9,8},{10,11... | collective-permute-start | bytes 786440 | tf_op jit(solution)/shard_map/ppermute | solution.py:226
  34.7 0.0 collective-permute-done.4.passed_ref
  34.7 0.0 copy-done
  34.7 0.0 copy-done.8
  34.7 1.5 %far.1.far_ref = f32[512,256]{1,0:T(8,128)S(1)} custom-call(s32[4,16]{1,0:T(4,128)S(1)} %copy-done.8, s32[4,16]{1,0:T(4,128)S(1)} %copy-done.7, bf16[4,16,128,128]{3,2,1,0:T(8,128)(2,1)S(1)} %copy-done, bf16[512,256]{1,0:T(8,128)(2,1)S(1)} %collective-permute-done.2.level_ref, bf16[512,256]{1,0:T(8,128)(2,1)S(1)} %collective-permute-done.3.layer_ref, ...), custom_call_target="tpu_custom_call" | custom-call | flops 536870912 | bytes 2097152 | tf_op jit(solution)/shard_map/far/pallas_call | solution.py:193
  36.3 0.0 collective-permute-done.9.their_column_ref
  36.3 0.0 collective-permute-done.10.their_beside_ref
  36.3 0.0 copy-done.10
  36.3 0.0 copy-done.2
  36.3 0.0 copy-done.5
  36.3 0.0 copy-done.6
  36.3 2.6 %down.1 = bf16[1024,256]{1,0:T(8,128)(2,1)} custom-call(s32[1,8]{1,0:T(1,128)S(1)} %copy-done.10, s32[4,16]{1,0:T(4,128)S(1)} %copy-done.7, bf16[4,128,128]{2,1,0:T(8,128)(2,1)S(1)} %copy-done.2, bf16[1,8,128,128]{3,2,1,0:T(8,128)(2,1)S(1)} %copy-done.5, bf16[4,256,128]{2,1,0:T(8,128)(2,1)S(1)} %copy-done.6, f32[4,256,256]{2,1,0:T(8,128)S(1)} %near.1.refs_0_.near_ref, ...), custom_call_target="tpu_custom_call" | custom-call | flops 134217728 | bytes 1048576 | tf_op jit(solution)/shard_map/down/pallas_call | solution.py:193
  (3 shorter events, 0.1 us)
Async XLA Ops:
  0.0 0.9 %copy-start.1 = (bf16[4,128,128]{2,1,0:T(8,128)(2,1)S(1)}, bf16[4,128,128]{2,1,0:T(8,128)(2,1)}, u32[]{:S(2)}) copy-start(bf16[4,128,128]{2,1,0:T(8,128)(2,1)} %transfer_ref.3) | copy-start | bytes 393220
  0.9 1.0 %copy-start.3 = (bf16[1024,256]{1,0:T(8,128)(2,1)S(1)}, bf16[1024,256]{1,0:T(8,128)(2,1)}, u32[]{:S(2)}) copy-start(bf16[1024,256]{1,0:T(8,128)(2,1)} %source_ref.1) | copy-start | bytes 1572868
  1.9 0.9 %copy-start.4 = (bf16[4,256,128]{2,1,0:T(8,128)(2,1)S(1)}, bf16[4,256,128]{2,1,0:T(8,128)(2,1)}, u32[]{:S(2)}) copy-start(bf16[4,256,128]{2,1,0:T(8,128)(2,1)} %col_ref.1) | copy-start | bytes 786436
  3.4 31.3 %copy-start = (bf16[4,16,128,128]{3,2,1,0:T(8,128)(2,1)S(1)}, bf16[4,16,128,128]{3,2,1,0:T(8,128)(2,1)}, u32[]{:S(2)}) copy-start(bf16[4,16,128,128]{3,2,1,0:T(8,128)(2,1)} %coupling_ref.2) | copy-start | bytes 6291460
  3.4 31.3 %copy-start.8 = (s32[4,16]{1,0:T(4,128)S(1)}, s32[4,16]{1,0:T(4,128)}, u32[]{:S(2)}) copy-start(s32[4,16]{1,0:T(4,128)} %list_ref.6) | copy-start | bytes 772
  3.4 2.8 %collective-permute-start = (bf16[1536,256]{1,0:T(8,128)(2,1)S(1)}, bf16[1536,256]{1,0:T(8,128)(2,1)S(1)}, u32[]{:S(2)}, u32[]{:S(2)}) collective-permute-start(bf16[1536,256]{1,0:T(8,128)(2,1)S(1)} %get-tuple-element.8.in_ref.own_ref), channel_id=1, source_target_pairs={{0,1},{1,0},{2,3},{3,2},{4,5},{5,4},{6,7},{7,6},{8,9},{9,8},{10,11... | collective-permute-start | bytes 2359304 | tf_op jit(solution)/shard_map/ppermute | solution.py:226
  3.5 10.5 %collective-permute-start.2 = (bf16[512,256]{1,0:T(8,128)(2,1)S(1)}, bf16[512,256]{1,0:T(8,128)(2,1)S(1)}, u32[]{:S(2)}, u32[]{:S(2)}) collective-permute-start(bf16[512,256]{1,0:T(8,128)(2,1)S(1)} %get-tuple-element.9), channel_id=1, source_target_pairs={{0,2},{1,3},{2,0},{3,1},{4,6},{5,7},{6,4},{7,5},{8,10},{9,11},{10,... | collective-permute-start | bytes 786440 | tf_op jit(solution)/shard_map/ppermute | solution.py:226
  6.3 20.7 %collective-permute-start.1 = (bf16[1024,256]{1,0:T(8,128)(2,1)S(1)}, bf16[1024,256]{1,0:T(8,128)(2,1)S(1)}, u32[]{:S(2)}, u32[]{:S(2)}) collective-permute-start(bf16[1024,256]{1,0:T(8,128)(2,1)S(1)} %panels.1), channel_id=1, source_target_pairs={{1,2},{2,1},{3,4},{4,3},{5,6},{6,5},{7,8},{8,7},{9,10},{10,9},{11,... | collective-permute-start | bytes 1572872 | tf_op jit(solution)/shard_map/ppermute | solution.py:226
  10.3 6.8 %collective-permute-start.5 = (bf16[128,256]{1,0:T(8,128)(2,1)S(1)}, bf16[128,256]{1,0:T(8,128)(2,1)S(1)}, u32[]{:S(2)}, u32[]{:S(2)}) collective-permute-start(bf16[128,256]{1,0:T(8,128)(2,1)S(1)} %get-tuple-element.10.refs_0_), channel_id=1, source_target_pairs={{0,4},{1,5},{2,6},{3,7},{4,0},{5,1},{6,2},{7,3},{8,12},{9,13},{10,... | collective-permute-start | bytes 196616 | tf_op jit(solution)/shard_map/ppermute | solution.py:226
  11.7 5.5 %collective-permute-start.6 = (bf16[128,256]{1,0:T(8,128)(2,1)S(1)}, bf16[128,256]{1,0:T(8,128)(2,1)S(1)}, u32[]{:S(2)}, u32[]{:S(2)}) collective-permute-start(bf16[128,256]{1,0:T(8,128)(2,1)S(1)} %get-tuple-element.10.refs_0_), channel_id=1, source_target_pairs={{0,8},{1,9},{2,10},{3,11},{4,12},{5,13},{6,14},{7,15},{8,0},{9,1},... | collective-permute-start | bytes 196616 | tf_op jit(solution)/shard_map/ppermute | solution.py:226
  14.0 5.7 %collective-permute-start.7 = (bf16[128,256]{1,0:T(8,128)(2,1)S(1)}, bf16[128,256]{1,0:T(8,128)(2,1)S(1)}, u32[]{:S(2)}, u32[]{:S(2)}) collective-permute-start(bf16[128,256]{1,0:T(8,128)(2,1)S(1)} %get-tuple-element.10.refs_0_), channel_id=1, source_target_pairs={{0,12},{1,13},{2,14},{3,15},{4,8},{5,9},{6,10},{7,11},{8,4},{9,5},... | collective-permute-start | bytes 196616 | tf_op jit(solution)/shard_map/ppermute | solution.py:226
  14.0 8.1 %collective-permute-start.3 = (bf16[512,256]{1,0:T(8,128)(2,1)S(1)}, bf16[512,256]{1,0:T(8,128)(2,1)S(1)}, u32[]{:S(2)}, u32[]{:S(2)}) collective-permute-start(bf16[512,256]{1,0:T(8,128)(2,1)S(1)} %collective-permute-done.2.level_ref), channel_id=1, source_target_pairs={{0,4},{1,5},{4,8},{5,9},{6,2},{7,3},{8,12},{9,13},{10,6},{11,7},{1... | collective-permute-start | bytes 786440 | tf_op jit(solution)/shard_map/ppermute | solution.py:226
  19.7 13.8 %collective-permute-start.8 = (bf16[512,256]{1,0:T(8,128)(2,1)S(1)}, bf16[512,256]{1,0:T(8,128)(2,1)S(1)}, u32[]{:S(2)}, u32[]{:S(2)}) collective-permute-start(bf16[512,256]{1,0:T(8,128)(2,1)S(1)} %column.1.column_ref), channel_id=1, source_target_pairs={{0,2},{1,3},{2,0},{3,1},{4,6},{5,7},{6,4},{7,5},{8,10},{9,11},{10,... | collective-permute-start | bytes 786440 | tf_op jit(solution)/shard_map/ppermute | solution.py:226
  22.1 0.7 %copy-start.7 = (s32[4,16]{1,0:T(4,128)S(1)}, s32[4,16]{1,0:T(4,128)}, u32[]{:S(2)}) copy-start(s32[4,16]{1,0:T(4,128)} %near_list_ref.3) | copy-start | bytes 772
  22.8 13.5 %copy-start.10 = (s32[1,8]{1,0:T(1,128)S(1)}, s32[1,8]{1,0:T(1,128)}, u32[]{:S(2)}) copy-start(s32[1,8]{1,0:T(1,128)} %list_ref.7) | copy-start | bytes 100
  23.4 12.9 %copy-start.2 = (bf16[4,128,128]{2,1,0:T(8,128)(2,1)S(1)}, bf16[4,128,128]{2,1,0:T(8,128)(2,1)}, u32[]{:S(2)}) copy-start(bf16[4,128,128]{2,1,0:T(8,128)(2,1)} %transfer_ref.3) | copy-start | bytes 393220
  23.4 12.9 %copy-start.5 = (bf16[1,8,128,128]{3,2,1,0:T(8,128)(2,1)S(1)}, bf16[1,8,128,128]{3,2,1,0:T(8,128)(2,1)}, u32[]{:S(2)}) copy-start(bf16[1,8,128,128]{3,2,1,0:T(8,128)(2,1)} %coupling_ref.3) | copy-start | bytes 786436
  23.4 12.9 %copy-start.6 = (bf16[4,256,128]{2,1,0:T(8,128)(2,1)S(1)}, bf16[4,256,128]{2,1,0:T(8,128)(2,1)}, u32[]{:S(2)}) copy-start(bf16[4,256,128]{2,1,0:T(8,128)(2,1)} %row_ref.1) | copy-start | bytes 786436
  23.4 11.3 %collective-permute-start.4 = (bf16[512,256]{1,0:T(8,128)(2,1)S(1)}, bf16[512,256]{1,0:T(8,128)(2,1)S(1)}, u32[]{:S(2)}, u32[]{:S(2)}) collective-permute-start(bf16[512,256]{1,0:T(8,128)(2,1)S(1)} %pick.1), channel_id=1, source_target_pairs={{0,1},{1,0},{2,3},{3,2},{4,5},{5,4},{6,7},{7,6},{8,9},{9,8},{10,11... | collective-permute-start | bytes 786440 | tf_op jit(solution)/shard_map/ppermute | solution.py:226
  26.9 9.3 %collective-permute-start.9 = (bf16[512,256]{1,0:T(8,128)(2,1)S(1)}, bf16[512,256]{1,0:T(8,128)(2,1)S(1)}, u32[]{:S(2)}, u32[]{:S(2)}) collective-permute-start(bf16[512,256]{1,0:T(8,128)(2,1)S(1)} %column.1.column_ref), channel_id=1, source_target_pairs={{0,1},{1,0},{2,3},{3,2},{4,5},{5,4},{6,7},{7,6},{8,9},{9,8},{10,11... | collective-permute-start | bytes 786440 | tf_op jit(solution)/shard_map/ppermute | solution.py:226
  27.0 0.7 %copy-start.9 = (s32[4]{0:T(128)S(1)}, s32[4]{0:T(128)}, u32[]{:S(2)}) copy-start(s32[4]{0:T(128)} %count_ref.1) | copy-start | bytes 52
  33.6 2.7 %collective-permute-start.10 = (bf16[512,256]{1,0:T(8,128)(2,1)S(1)}, bf16[512,256]{1,0:T(8,128)(2,1)S(1)}, u32[]{:S(2)}, u32[]{:S(2)}) collective-permute-start(bf16[512,256]{1,0:T(8,128)(2,1)S(1)} %hand.1.beside_ref), channel_id=1, source_target_pairs={{0,1},{1,0},{2,3},{3,2},{4,5},{5,4},{6,7},{7,6},{8,9},{9,8},{10,11... | collective-permute-start | bytes 786440 | tf_op jit(solution)/shard_map/ppermute | solution.py:226

commit v11 on v10

--- a/solution.py
+++ b/solution.py
@@ -7,7 +7,7 @@
 
 GROUP = 16
 CHUNK = 4
-AHEAD = 4
+AHEAD = 8
 MIB = 2**20
 
 VMEM = pl.BlockSpec(memory_space=pltpu.VMEM)
@@ -51,8 +51,8 @@
         at += ref.shape[0]
 
 
-def pick_kernel(list_ref, level_ref, layer_ref, out_ref):
-    corner = lax.div(list_ref[0, 0], list_ref.shape[0]) & 3
+def pick_kernel(level_ref, layer_ref, out_ref):
+    corner = lax.axis_index("row") & 3
     level = (corner == 0) | (corner == 3)
     out_ref[...] = jnp.where(level, level_ref[...], layer_ref[...])
 
@@ -70,24 +70,15 @@
     leaves, slots, rows, _ = blocks.shape
     chunks = slots // CHUNK
     size = leaves * rows
-    place = lax.div(list_ref[0, 0], leaves)
-
-    def live(step):
-        return step % chunks * CHUNK < count_ref[step // chunks]
-
-    def block_copy(step):
+    place = lax.axis_index("row")
+
+    copies = []
+    for step in range(leaves * chunks):
         leaf, chunk = step // chunks, step % chunks
         where = pl.ds(chunk * CHUNK, CHUNK)
-        return pltpu.make_async_copy(
+        copies.append(pltpu.make_async_copy(
             blocks_hbm.at[leaf, where], blocks.at[leaf, where], block_sems.at[leaf, chunk]
-        )
-
-    def start(step):
-        if step < leaves * chunks:
-            @pl.when(live(step))
-            def _():
-                block_copy(step).start()
-
+        ))
     pairs = [
         pltpu.make_async_copy(
             ref.at[pl.ds(0, size)], panels.at[pl.ds(which * size, size)], panel_sems.at[which]
@@ -96,8 +87,8 @@
     ]
     for copy in pairs:
         copy.start()
-    for step in range(AHEAD):
-        start(step)
+    for copy in copies[:AHEAD]:
+        copy.start()
     panels[pl.ds(3 * size, rows), :] = jnp.zeros((rows, panels.shape[1]), panels.dtype)
     for copy in pairs:
         copy.wait()
@@ -109,28 +100,27 @@
         index = jnp.where(slot < count_ref[leaf], index, 3 * leaves)
         return panels[rows_at(index, rows), :]
 
-    for step in range(leaves * chunks):
-        leaf, chunk = step // chunks, step % chunks
-        start(step + AHEAD)
-
-        @pl.when(live(step))
-        def _():
-            block_copy(step).wait()
-            total = None if chunk == 0 else near_ref[leaf]
-            for slot in range(chunk * CHUNK, (chunk + 1) * CHUNK):
-                term = dot(blocks[leaf, slot], panel_of(leaf, slot))
-                total = term if total is None else total + term
-            near_ref[leaf] = total
+    for leaf in range(leaves):
+        total = None
+        for slot in range(slots):
+            if slot % CHUNK == 0:
+                step = leaf * chunks + slot // CHUNK
+                if step + AHEAD < len(copies):
+                    copies[step + AHEAD].start()
+                copies[step].wait()
+            term = dot(blocks[leaf, slot], panel_of(leaf, slot))
+            total = term if total is None else total + term
+        near_ref[leaf] = total
 
 
 def far_kernel(
-    list_ref, near_list_ref, coupling_ref, level_ref, layer_ref, share_ref, passed_ref,
+    list_ref, coupling_ref, level_ref, layer_ref, share_ref, passed_ref,
     far_ref,
     coefs, sems,
 ):
     leaves, slots, rank, _ = coupling_ref.shape
     size = leaves * rank
-    place = lax.div(near_list_ref[0, 0], leaves)
+    place = lax.axis_index("row")
     beyond = jnp.where((place & 2) == 0, place - 2, place + 2)
     copies = [
         pltpu.make_async_copy(
@@ -163,12 +153,12 @@
 
 
 def down_kernel(
-    list_ref, near_list_ref, transfer_ref, coupling_ref, row_ref, near_ref, far_ref,
+    list_ref, transfer_ref, coupling_ref, row_ref, near_ref, far_ref,
     column_ref, beside_ref, their_column_ref, their_beside_ref,
     out_ref,
 ):
     leaves, rows, rank = row_ref.shape
-    local = lax.div(near_list_ref[0, 0], leaves) & (GROUP - 1)
+    local = lax.axis_index("row") & (GROUP - 1)
     total = None
     for slot in range(list_ref.shape[1]):
         flip = (list_ref[0, slot] & (GROUP - 1)) ^ local
@@ -261,12 +251,12 @@
         limit=48,
     )
     picked_coef = call(
-        pick_kernel, "pick", panel(leaves), [SMEM] + [VMEM] * 2, (near_list, level, layer)
+        pick_kernel, "pick", panel(leaves), [VMEM] * 2, (level, layer)
     )
     passed = send(picked_coef, lambda d: d ^ 1)
     far = call(
-        far_kernel, "far", panel(leaves, jnp.float32), [SMEM] * 2 + [VMEM] + [ANY] * 4,
-        (far_list, near_list, far_coupling, level, layer, share_other, passed),
+        far_kernel, "far", panel(leaves, jnp.float32), [SMEM, VMEM] + [ANY] * 4,
+        (far_list, far_coupling, level, layer, share_other, passed),
         scratch=[
             pltpu.VMEM((4 * leaves * rank, width), jnp.bfloat16),
             pltpu.SemaphoreType.DMA((4,)),
@@ -278,9 +268,9 @@
     their_beside = send(handed, lambda d: d ^ 1)
     return call(
         down_kernel, "down", jax.ShapeDtypeStruct(source.shape, jnp.bfloat16),
-        [SMEM] * 2 + [VMEM] * 9,
+        [SMEM] + [VMEM] * 9,
         (
-            coarse_list, near_list, transfer, coarse_coupling, row_basis, near, far,
+            coarse_list, transfer, coarse_coupling, row_basis, near, far,
             column, handed, their_column, their_beside,
         ),
         flops=8 * leaves * rank * rank * width,

time: 39 us -> 39.4 us (1.010)
  Pallas kernels: 11.2 us -> 11.9 us
  starting transfers between devices: 20.8 us -> 20.2 us
    pallas_call x8, Pallas kernels: 11.2 us -> 11.9 us  [call(): pl.pallas_call(kernel, out_shape=outs, in_specs=specs, out_specs=(VMEM,)...]
    ppermute x11, starting transfers between devices: 20.8 us -> 20.2 us  [send(): return lax.ppermute(value, 'row', pairs)]
  transfers between devices with their start and end apart: 11 -> 11, of which waited for: 1 -> 1; matrix products, arithmetic and copies ran while one was open for 0% -> 0% of each run, Pallas kernels for 21% -> 23%
where the time goes in v11:
time: 39.4 us; the launch traced here: 39.1 us
  starting transfers between devices  20.2 us (51%)
  Pallas kernels  11.9 us (30%)
  local copies, waits for them, and re-layouts  4.27 us (11%)
  waiting for transfers between devices  2.54 us (6%)
    ppermute x11, starting transfers between devices, send(): return lax.ppermute(value, 'row', pairs)  20.2 us
    pallas_call x8, Pallas kernels, call(): pl.pallas_call(kernel, out_shape=outs, in_specs=specs, out_specs=(VMEM,)...  11.9 us
    unnamed x22, local copies, waits for them, and re-layouts  4.27 us
    ppermute x11, waiting for transfers between devices, send(): return lax.ppermute(value, 'row', pairs)  2.54 us
  transfers between devices with their start and end apart: 11, of which 1 were waited for; matrix products, arithmetic and copies ran while one was open for 0% of the time, Pallas kernels for 23%

profile of v11, /device:TPU:1, one launch (start us, length us, event | category | flops | bytes accessed | tf_op | source)
XLA Modules:
  0.0 39.1 jit_solution(10521918494378882492)
XLA Ops:
  0.0 0.0 copy-start.1
  0.0 0.9 %copy-done.1 = bf16[4,128,128]{2,1,0:T(8,128)(2,1)S(1)} copy-done((bf16[4,128,128]{2,1,0:T(8,128)(2,1)S(1)}, bf16[4,128,128]{2,1,0:T(8,128)(2,1)}, u32[]{:S(2)}) %copy-start.1) | copy-done | bytes 131096
  0.9 0.0 copy-start.3
  0.9 1.0 %copy-done.3 = bf16[1024,256]{1,0:T(8,128)(2,1)S(1)} copy-done((bf16[1024,256]{1,0:T(8,128)(2,1)S(1)}, bf16[1024,256]{1,0:T(8,128)(2,1)}, u32[]{:S(2)}) %copy-start.3) | copy-done | bytes 524312
  1.9 0.0 copy-start.4
  1.9 0.9 %copy-done.4 = bf16[4,256,128]{2,1,0:T(8,128)(2,1)S(1)} copy-done((bf16[4,256,128]{2,1,0:T(8,128)(2,1)S(1)}, bf16[4,256,128]{2,1,0:T(8,128)(2,1)}, u32[]{:S(2)}) %copy-start.4) | copy-done | bytes 262168
  2.9 0.5 %up.1 = (bf16[1536,256]{1,0:T(8,128)(2,1)S(1)}, bf16[512,256]{1,0:T(8,128)(2,1)S(1)}, bf16[128,256]{1,0:T(8,128)(2,1)S(1)}) custom-call(bf16[1024,256]{1,0:T(8,128)(2,1)S(1)} %copy-done.3, bf16[4,256,128]{2,1,0:T(8,128)(2,1)S(1)} %copy-done.4, bf16[4,128,128]{2,1,0:T(8,128)(2,1)S(1)} %copy-done.1), custom_call_target="tpu_custom_call" | custom-call | flops 100663296 | bytes 786432 | tf_op jit(solution)/shard_map/up/pallas_call | solution.py:183
  3.4 0.0 copy-start
  3.4 0.0 copy-start.8
  3.4 0.1 collective-permute-start
  3.5 2.7 %collective-permute-start.2 = (bf16[512,256]{1,0:T(8,128)(2,1)S(1)}, bf16[512,256]{1,0:T(8,128)(2,1)S(1)}, u32[]{:S(2)}, u32[]{:S(2)}) collective-permute-start(bf16[512,256]{1,0:T(8,128)(2,1)S(1)} %get-tuple-element.9), channel_id=1, source_target_pairs={{0,2},{1,3},{2,0},{3,1},{4,6},{5,7},{6,4},{7,5},{8,10},{9,11},{10,... | collective-permute-start | bytes 786440 | tf_op jit(solution)/shard_map/ppermute | solution.py:216
  6.2 0.0 collective-permute-done.refs_0_.share_ref
  6.3 4.1 %collective-permute-start.1 = (bf16[1024,256]{1,0:T(8,128)(2,1)S(1)}, bf16[1024,256]{1,0:T(8,128)(2,1)S(1)}, u32[]{:S(2)}, u32[]{:S(2)}) collective-permute-start(bf16[1024,256]{1,0:T(8,128)(2,1)S(1)} %panels.1), channel_id=1, source_target_pairs={{1,2},{2,1},{3,4},{4,3},{5,6},{6,5},{7,8},{8,7},{9,10},{10,9},{11,... | collective-permute-start | bytes 1572872 | tf_op jit(solution)/shard_map/ppermute | solution.py:216
  10.3 1.4 %collective-permute-start.5 = (bf16[128,256]{1,0:T(8,128)(2,1)S(1)}, bf16[128,256]{1,0:T(8,128)(2,1)S(1)}, u32[]{:S(2)}, u32[]{:S(2)}) collective-permute-start(bf16[128,256]{1,0:T(8,128)(2,1)S(1)} %get-tuple-element.10.refs_0_), channel_id=1, source_target_pairs={{0,4},{1,5},{2,6},{3,7},{4,0},{5,1},{6,2},{7,3},{8,12},{9,13},{10,... | collective-permute-start | bytes 196616 | tf_op jit(solution)/shard_map/ppermute | solution.py:216
  11.7 2.3 %collective-permute-start.6 = (bf16[128,256]{1,0:T(8,128)(2,1)S(1)}, bf16[128,256]{1,0:T(8,128)(2,1)S(1)}, u32[]{:S(2)}, u32[]{:S(2)}) collective-permute-start(bf16[128,256]{1,0:T(8,128)(2,1)S(1)} %get-tuple-element.10.refs_0_), channel_id=1, source_target_pairs={{0,8},{1,9},{2,10},{3,11},{4,12},{5,13},{6,14},{7,15},{8,0},{9,1},... | collective-permute-start | bytes 196616 | tf_op jit(solution)/shard_map/ppermute | solution.py:216
  14.0 0.0 collective-permute-start.7
  14.0 0.0 collective-permute-done.2.level_ref
  14.0 3.1 %collective-permute-start.3 = (bf16[512,256]{1,0:T(8,128)(2,1)S(1)}, bf16[512,256]{1,0:T(8,128)(2,1)S(1)}, u32[]{:S(2)}, u32[]{:S(2)}) collective-permute-start(bf16[512,256]{1,0:T(8,128)(2,1)S(1)} %collective-permute-done.2.level_ref), channel_id=1, source_target_pairs={{0,4},{1,5},{4,8},{5,9},{6,2},{7,3},{8,12},{9,13},{10,6},{11,7},{1... | collective-permute-start | bytes 786440 | tf_op jit(solution)/shard_map/ppermute | solution.py:216
  17.2 0.0 collective-permute-done.5.refs_1_
  17.2 0.0 collective-permute-done.6.refs_2_
  17.2 2.5 %collective-permute-done.7.refs_3_ = bf16[128,256]{1,0:T(8,128)(2,1)S(1)} collective-permute-done((bf16[128,256]{1,0:T(8,128)(2,1)S(1)}, bf16[128,256]{1,0:T(8,128)(2,1)S(1)}, u32[]{:S(2)}, u32[]{:S(2)}) %collective-permute-start.7) | collective-permute-done | bytes 65568 | tf_op jit(solution)/shard_map/ppermute | solution.py:216
  19.7 2.3 %collective-permute-start.8 = (bf16[512,256]{1,0:T(8,128)(2,1)S(1)}, bf16[512,256]{1,0:T(8,128)(2,1)S(1)}, u32[]{:S(2)}, u32[]{:S(2)}) collective-permute-start(bf16[512,256]{1,0:T(8,128)(2,1)S(1)} %column.1.column_ref), channel_id=1, source_target_pairs={{0,2},{1,3},{2,0},{3,1},{4,6},{5,7},{6,4},{7,5},{8,10},{9,11},{10,... | collective-permute-start | bytes 786440 | tf_op jit(solution)/shard_map/ppermute | solution.py:216
  22.1 0.0 collective-permute-done.3.layer_ref
  22.1 0.0 copy-start.10
  22.1 0.0 copy-start.2
  22.1 0.0 copy-start.5
  22.1 0.0 copy-start.6
  22.2 3.5 %collective-permute-start.4 = (bf16[512,256]{1,0:T(8,128)(2,1)S(1)}, bf16[512,256]{1,0:T(8,128)(2,1)S(1)}, u32[]{:S(2)}, u32[]{:S(2)}) collective-permute-start(bf16[512,256]{1,0:T(8,128)(2,1)S(1)} %pick.1), channel_id=1, source_target_pairs={{0,1},{1,0},{2,3},{3,2},{4,5},{5,4},{6,7},{7,6},{8,9},{9,8},{10,11... | collective-permute-start | bytes 786440 | tf_op jit(solution)/shard_map/ppermute | solution.py:216
  25.7 0.1 collective-permute-start.9
  25.8 0.0 collective-permute-done.1.across_ref
  25.8 0.0 copy-start.7
  25.8 0.7 %copy-done.7 = s32[4,16]{1,0:T(4,128)S(1)} copy-done((s32[4,16]{1,0:T(4,128)S(1)}, s32[4,16]{1,0:T(4,128)}, u32[]{:S(2)}) %copy-start.7) | copy-done | bytes 280
  26.5 0.0 copy-start.9
  26.5 0.7 %copy-done.9 = s32[4]{0:T(128)S(1)} copy-done((s32[4]{0:T(128)S(1)}, s32[4]{0:T(128)}, u32[]{:S(2)}) %copy-start.9) | copy-done | bytes 40
  27.1 7.3 %near.1.refs_0_.near_ref = f32[4,256,256]{2,1,0:T(8,128)S(1)} custom-call(s32[4,16]{1,0:T(4,128)S(1)} %copy-done.7, s32[4]{0:T(128)S(1)} %copy-done.9, bf16[4,16,256,256]{3,2,1,0:T(8,128)(2,1)} %blocks_hbm.1, bf16[1536,256]{1,0:T(8,128)(2,1)S(1)} %get-tuple-element.8.in_ref.own_ref, bf16[1536,256]{1,0:T(8,128)(2,1)S(1)} %collective-permute-done.refs_0_.share_ref, ...), custom_call_target="tpu_custom_call" | custom-call | tf_op jit(solution)/shard_map/near/pallas_call | solution.py:183
  34.4 0.0 collective-permute-done.8.in_ref
  34.4 0.5 %collective-permute-start.10 = (bf16[512,256]{1,0:T(8,128)(2,1)S(1)}, bf16[512,256]{1,0:T(8,128)(2,1)S(1)}, u32[]{:S(2)}, u32[]{:S(2)}) collective-permute-start(bf16[512,256]{1,0:T(8,128)(2,1)S(1)} %hand.1.beside_ref), channel_id=1, source_target_pairs={{0,1},{1,0},{2,3},{3,2},{4,5},{5,4},{6,7},{7,6},{8,9},{9,8},{10,11... | collective-permute-start | bytes 786440 | tf_op jit(solution)/shard_map/ppermute | solution.py:216
  34.9 0.0 collective-permute-done.4.passed_ref
  34.9 0.0 copy-done
  34.9 0.0 copy-done.8
  34.9 1.5 %far.1.far_ref = f32[512,256]{1,0:T(8,128)S(1)} custom-call(s32[4,16]{1,0:T(4,128)S(1)} %copy-done.8, bf16[4,16,128,128]{3,2,1,0:T(8,128)(2,1)S(1)} %copy-done, bf16[512,256]{1,0:T(8,128)(2,1)S(1)} %collective-permute-done.2.level_ref, bf16[512,256]{1,0:T(8,128)(2,1)S(1)} %collective-permute-done.3.layer_ref, ...), custom_call_target="tpu_custom_call" | custom-call | flops 536870912 | bytes 2097152 | tf_op jit(solution)/shard_map/far/pallas_call | solution.py:183
  36.4 0.0 collective-permute-done.9.their_column_ref
  36.5 0.0 collective-permute-done.10.their_beside_ref
  36.5 0.0 copy-done.10
  36.5 0.0 copy-done.2
  36.5 0.0 copy-done.5
  36.5 0.0 copy-done.6
  36.5 2.6 %down.1 = bf16[1024,256]{1,0:T(8,128)(2,1)} custom-call(s32[1,8]{1,0:T(1,128)S(1)} %copy-done.10, bf16[4,128,128]{2,1,0:T(8,128)(2,1)S(1)} %copy-done.2, bf16[1,8,128,128]{3,2,1,0:T(8,128)(2,1)S(1)} %copy-done.5, bf16[4,256,128]{2,1,0:T(8,128)(2,1)S(1)} %copy-done.6, f32[4,256,256]{2,1,0:T(8,128)S(1)} %near.1.refs_0_.near_ref, f32[512,256]{1,0:T(8,128)S(1)} %far.1.far_ref, ...), custom_call_target="tpu_custom_call" | custom-call | flops 134217728 | bytes 1048576 | tf_op jit(solution)/shard_map/down/pallas_call | solution.py:183
  (4 shorter events, 0.1 us)
Async XLA Ops:
  0.0 0.9 %copy-start.1 = (bf16[4,128,128]{2,1,0:T(8,128)(2,1)S(1)}, bf16[4,128,128]{2,1,0:T(8,128)(2,1)}, u32[]{:S(2)}) copy-start(bf16[4,128,128]{2,1,0:T(8,128)(2,1)} %transfer_ref.3) | copy-start | bytes 393220
  0.9 1.0 %copy-start.3 = (bf16[1024,256]{1,0:T(8,128)(2,1)S(1)}, bf16[1024,256]{1,0:T(8,128)(2,1)}, u32[]{:S(2)}) copy-start(bf16[1024,256]{1,0:T(8,128)(2,1)} %source_ref.1) | copy-start | bytes 1572868
  1.9 0.9 %copy-start.4 = (bf16[4,256,128]{2,1,0:T(8,128)(2,1)S(1)}, bf16[4,256,128]{2,1,0:T(8,128)(2,1)}, u32[]{:S(2)}) copy-start(bf16[4,256,128]{2,1,0:T(8,128)(2,1)} %col_ref.1) | copy-start | bytes 786436
  3.4 31.5 %copy-start = (bf16[4,16,128,128]{3,2,1,0:T(8,128)(2,1)S(1)}, bf16[4,16,128,128]{3,2,1,0:T(8,128)(2,1)}, u32[]{:S(2)}) copy-start(bf16[4,16,128,128]{3,2,1,0:T(8,128)(2,1)} %coupling_ref.2) | copy-start | bytes 6291460
  3.4 31.5 %copy-start.8 = (s32[4,16]{1,0:T(4,128)S(1)}, s32[4,16]{1,0:T(4,128)}, u32[]{:S(2)}) copy-start(s32[4,16]{1,0:T(4,128)} %list_ref.4) | copy-start | bytes 772
  3.4 2.8 %collective-permute-start = (bf16[1536,256]{1,0:T(8,128)(2,1)S(1)}, bf16[1536,256]{1,0:T(8,128)(2,1)S(1)}, u32[]{:S(2)}, u32[]{:S(2)}) collective-permute-start(bf16[1536,256]{1,0:T(8,128)(2,1)S(1)} %get-tuple-element.8.in_ref.own_ref), channel_id=1, source_target_pairs={{0,1},{1,0},{2,3},{3,2},{4,5},{5,4},{6,7},{7,6},{8,9},{9,8},{10,11... | collective-permute-start | bytes 2359304 | tf_op jit(solution)/shard_map/ppermute | solution.py:216
  3.5 10.5 %collective-permute-start.2 = (bf16[512,256]{1,0:T(8,128)(2,1)S(1)}, bf16[512,256]{1,0:T(8,128)(2,1)S(1)}, u32[]{:S(2)}, u32[]{:S(2)}) collective-permute-start(bf16[512,256]{1,0:T(8,128)(2,1)S(1)} %get-tuple-element.9), channel_id=1, source_target_pairs={{0,2},{1,3},{2,0},{3,1},{4,6},{5,7},{6,4},{7,5},{8,10},{9,11},{10,... | collective-permute-start | bytes 786440 | tf_op jit(solution)/shard_map/ppermute | solution.py:216
  6.3 19.5 %collective-permute-start.1 = (bf16[1024,256]{1,0:T(8,128)(2,1)S(1)}, bf16[1024,256]{1,0:T(8,128)(2,1)S(1)}, u32[]{:S(2)}, u32[]{:S(2)}) collective-permute-start(bf16[1024,256]{1,0:T(8,128)(2,1)S(1)} %panels.1), channel_id=1, source_target_pairs={{1,2},{2,1},{3,4},{4,3},{5,6},{6,5},{7,8},{8,7},{9,10},{10,9},{11,... | collective-permute-start | bytes 1572872 | tf_op jit(solution)/shard_map/ppermute | solution.py:216
  10.3 6.8 %collective-permute-start.5 = (bf16[128,256]{1,0:T(8,128)(2,1)S(1)}, bf16[128,256]{1,0:T(8,128)(2,1)S(1)}, u32[]{:S(2)}, u32[]{:S(2)}) collective-permute-start(bf16[128,256]{1,0:T(8,128)(2,1)S(1)} %get-tuple-element.10.refs_0_), channel_id=1, source_target_pairs={{0,4},{1,5},{2,6},{3,7},{4,0},{5,1},{6,2},{7,3},{8,12},{9,13},{10,... | collective-permute-start | bytes 196616 | tf_op jit(solution)/shard_map/ppermute | solution.py:216
  11.7 5.5 %collective-permute-start.6 = (bf16[128,256]{1,0:T(8,128)(2,1)S(1)}, bf16[128,256]{1,0:T(8,128)(2,1)S(1)}, u32[]{:S(2)}, u32[]{:S(2)}) collective-permute-start(bf16[128,256]{1,0:T(8,128)(2,1)S(1)} %get-tuple-element.10.refs_0_), channel_id=1, source_target_pairs={{0,8},{1,9},{2,10},{3,11},{4,12},{5,13},{6,14},{7,15},{8,0},{9,1},... | collective-permute-start | bytes 196616 | tf_op jit(solution)/shard_map/ppermute | solution.py:216
  14.0 5.7 %collective-permute-start.7 = (bf16[128,256]{1,0:T(8,128)(2,1)S(1)}, bf16[128,256]{1,0:T(8,128)(2,1)S(1)}, u32[]{:S(2)}, u32[]{:S(2)}) collective-permute-start(bf16[128,256]{1,0:T(8,128)(2,1)S(1)} %get-tuple-element.10.refs_0_), channel_id=1, source_target_pairs={{0,12},{1,13},{2,14},{3,15},{4,8},{5,9},{6,10},{7,11},{8,4},{9,5},... | collective-permute-start | bytes 196616 | tf_op jit(solution)/shard_map/ppermute | solution.py:216
  14.0 8.1 %collective-permute-start.3 = (bf16[512,256]{1,0:T(8,128)(2,1)S(1)}, bf16[512,256]{1,0:T(8,128)(2,1)S(1)}, u32[]{:S(2)}, u32[]{:S(2)}) collective-permute-start(bf16[512,256]{1,0:T(8,128)(2,1)S(1)} %collective-permute-done.2.level_ref), channel_id=1, source_target_pairs={{0,4},{1,5},{4,8},{5,9},{6,2},{7,3},{8,12},{9,13},{10,6},{11,7},{1... | collective-permute-start | bytes 786440 | tf_op jit(solution)/shard_map/ppermute | solution.py:216
  19.7 14.7 %collective-permute-start.8 = (bf16[512,256]{1,0:T(8,128)(2,1)S(1)}, bf16[512,256]{1,0:T(8,128)(2,1)S(1)}, u32[]{:S(2)}, u32[]{:S(2)}) collective-permute-start(bf16[512,256]{1,0:T(8,128)(2,1)S(1)} %column.1.column_ref), channel_id=1, source_target_pairs={{0,2},{1,3},{2,0},{3,1},{4,6},{5,7},{6,4},{7,5},{8,10},{9,11},{10,... | collective-permute-start | bytes 786440 | tf_op jit(solution)/shard_map/ppermute | solution.py:216
  22.1 14.4 %copy-start.10 = (s32[1,8]{1,0:T(1,128)S(1)}, s32[1,8]{1,0:T(1,128)}, u32[]{:S(2)}) copy-start(s32[1,8]{1,0:T(1,128)} %list_ref.5) | copy-start | bytes 100
  22.1 14.4 %copy-start.2 = (bf16[4,128,128]{2,1,0:T(8,128)(2,1)S(1)}, bf16[4,128,128]{2,1,0:T(8,128)(2,1)}, u32[]{:S(2)}) copy-start(bf16[4,128,128]{2,1,0:T(8,128)(2,1)} %transfer_ref.3) | copy-start | bytes 393220
  22.1 14.4 %copy-start.5 = (bf16[1,8,128,128]{3,2,1,0:T(8,128)(2,1)S(1)}, bf16[1,8,128,128]{3,2,1,0:T(8,128)(2,1)}, u32[]{:S(2)}) copy-start(bf16[1,8,128,128]{3,2,1,0:T(8,128)(2,1)} %coupling_ref.3) | copy-start | bytes 786436
  22.1 14.4 %copy-start.6 = (bf16[4,256,128]{2,1,0:T(8,128)(2,1)S(1)}, bf16[4,256,128]{2,1,0:T(8,128)(2,1)}, u32[]{:S(2)}) copy-start(bf16[4,256,128]{2,1,0:T(8,128)(2,1)} %row_ref.1) | copy-start | bytes 786436
  22.2 12.8 %collective-permute-start.4 = (bf16[512,256]{1,0:T(8,128)(2,1)S(1)}, bf16[512,256]{1,0:T(8,128)(2,1)S(1)}, u32[]{:S(2)}, u32[]{:S(2)}) collective-permute-start(bf16[512,256]{1,0:T(8,128)(2,1)S(1)} %pick.1), channel_id=1, source_target_pairs={{0,1},{1,0},{2,3},{3,2},{4,5},{5,4},{6,7},{7,6},{8,9},{9,8},{10,11... | collective-permute-start | bytes 786440 | tf_op jit(solution)/shard_map/ppermute | solution.py:216
  25.7 10.8 %collective-permute-start.9 = (bf16[512,256]{1,0:T(8,128)(2,1)S(1)}, bf16[512,256]{1,0:T(8,128)(2,1)S(1)}, u32[]{:S(2)}, u32[]{:S(2)}) collective-permute-start(bf16[512,256]{1,0:T(8,128)(2,1)S(1)} %column.1.column_ref), channel_id=1, source_target_pairs={{0,1},{1,0},{2,3},{3,2},{4,5},{5,4},{6,7},{7,6},{8,9},{9,8},{10,11... | collective-permute-start | bytes 786440 | tf_op jit(solution)/shard_map/ppermute | solution.py:216
  25.8 0.7 %copy-start.7 = (s32[4,16]{1,0:T(4,128)S(1)}, s32[4,16]{1,0:T(4,128)}, u32[]{:S(2)}) copy-start(s32[4,16]{1,0:T(4,128)} %list_ref.3) | copy-start | bytes 772
  26.5 0.7 %copy-start.9 = (s32[4]{0:T(128)S(1)}, s32[4]{0:T(128)}, u32[]{:S(2)}) copy-start(s32[4]{0:T(128)} %count_ref.1) | copy-start | bytes 52
  34.4 2.0 %collective-permute-start.10 = (bf16[512,256]{1,0:T(8,128)(2,1)S(1)}, bf16[512,256]{1,0:T(8,128)(2,1)S(1)}, u32[]{:S(2)}, u32[]{:S(2)}) collective-permute-start(bf16[512,256]{1,0:T(8,128)(2,1)S(1)} %hand.1.beside_ref), channel_id=1, source_target_pairs={{0,1},{1,0},{2,3},{3,2},{4,5},{5,4},{6,7},{7,6},{8,9},{9,8},{10,11... | collective-permute-start | bytes 786440 | tf_op jit(solution)/shard_map/ppermute | solution.py:216

commit v12 on v10

--- a/solution.py
+++ b/solution.py
@@ -51,8 +51,8 @@
         at += ref.shape[0]
 
 
-def pick_kernel(list_ref, level_ref, layer_ref, out_ref):
-    corner = lax.div(list_ref[0, 0], list_ref.shape[0]) & 3
+def pick_kernel(level_ref, layer_ref, out_ref):
+    corner = lax.axis_index("row") & 3
     level = (corner == 0) | (corner == 3)
     out_ref[...] = jnp.where(level, level_ref[...], layer_ref[...])
 
@@ -63,17 +63,16 @@
 
 
 def near_kernel(
-    list_ref, count_ref, blocks_hbm, own_ref, share_ref, across_ref,
+    index_ref, blocks_hbm, own_ref, share_ref, across_ref,
     near_ref,
     blocks, panels, block_sems, panel_sems,
 ):
     leaves, slots, rows, _ = blocks.shape
     chunks = slots // CHUNK
     size = leaves * rows
-    place = lax.div(list_ref[0, 0], leaves)
 
     def live(step):
-        return step % chunks * CHUNK < count_ref[step // chunks]
+        return index_ref[step // chunks, step % chunks * CHUNK] < 3 * leaves
 
     def block_copy(step):
         leaf, chunk = step // chunks, step % chunks
@@ -102,35 +101,30 @@
     for copy in pairs:
         copy.wait()
 
-    def panel_of(leaf, slot):
-        column = list_ref[leaf, slot]
-        which = jnp.minimum(lax.div(column, leaves) ^ place, 2)
-        index = which * leaves + (column & (leaves - 1))
-        index = jnp.where(slot < count_ref[leaf], index, 3 * leaves)
-        return panels[rows_at(index, rows), :]
+    def term(leaf, slot):
+        return dot(blocks[leaf, slot], panels[rows_at(index_ref[leaf, slot], rows), :])
 
     for step in range(leaves * chunks):
-        leaf, chunk = step // chunks, step % chunks
+        leaf, first = step // chunks, step % chunks * CHUNK
         start(step + AHEAD)
 
         @pl.when(live(step))
         def _():
             block_copy(step).wait()
-            total = None if chunk == 0 else near_ref[leaf]
-            for slot in range(chunk * CHUNK, (chunk + 1) * CHUNK):
-                term = dot(blocks[leaf, slot], panel_of(leaf, slot))
-                total = term if total is None else total + term
-            near_ref[leaf] = total
+            even = term(leaf, first) + term(leaf, first + 2)
+            odd = term(leaf, first + 1) + term(leaf, first + 3)
+            total = even + odd
+            near_ref[leaf] = total if first == 0 else near_ref[leaf] + total
 
 
 def far_kernel(
-    list_ref, near_list_ref, coupling_ref, level_ref, layer_ref, share_ref, passed_ref,
+    list_ref, coupling_ref, level_ref, layer_ref, share_ref, passed_ref,
     far_ref,
     coefs, sems,
 ):
     leaves, slots, rank, _ = coupling_ref.shape
     size = leaves * rank
-    place = lax.div(near_list_ref[0, 0], leaves)
+    place = lax.axis_index("row")
     beyond = jnp.where((place & 2) == 0, place - 2, place + 2)
     copies = [
         pltpu.make_async_copy(
@@ -163,12 +157,12 @@
 
 
 def down_kernel(
-    list_ref, near_list_ref, transfer_ref, coupling_ref, row_ref, near_ref, far_ref,
+    list_ref, transfer_ref, coupling_ref, row_ref, near_ref, far_ref,
     column_ref, beside_ref, their_column_ref, their_beside_ref,
     out_ref,
 ):
     leaves, rows, rank = row_ref.shape
-    local = lax.div(near_list_ref[0, 0], leaves) & (GROUP - 1)
+    local = lax.axis_index("row") & (GROUP - 1)
     total = None
     for slot in range(list_ref.shape[1]):
         flip = (list_ref[0, slot] & (GROUP - 1)) ^ local
@@ -248,25 +242,28 @@
     column = call(join_kernel, "column", panel(GROUP // 4), [VMEM] * 4, (parent, *layers))
     beside = send(column, lambda d: d ^ 2)
     their_column = send(column, lambda d: d ^ 1)
+    place = lax.axis_index("row")
+    live = lax.broadcasted_iota(jnp.int32, (leaves, slots), 1) < near_count[:, None]
+    which = jnp.minimum((near_list // leaves) ^ place, 2)
+    index = jnp.where(live, which * leaves + near_list % leaves, 3 * leaves)
     near = call(
         near_kernel, "near", jax.ShapeDtypeStruct((leaves, rows, width), jnp.float32),
-        [SMEM, SMEM] + [ANY] * 4,
-        (near_list, near_count, near_blocks, share, share_other, across),
+        [SMEM] + [ANY] * 4, (index, near_blocks, share, share_other, across),
         scratch=[
             pltpu.VMEM(near_blocks.shape, jnp.bfloat16),
             pltpu.VMEM(((3 * leaves + 1) * rows, width), jnp.bfloat16),
             pltpu.SemaphoreType.DMA((leaves, slots // CHUNK)),
             pltpu.SemaphoreType.DMA((3,)),
         ],
-        limit=48,
+        flops=10**9, limit=48,
     )
     picked_coef = call(
-        pick_kernel, "pick", panel(leaves), [SMEM] + [VMEM] * 2, (near_list, level, layer)
+        pick_kernel, "pick", panel(leaves), [VMEM] * 2, (level, layer)
     )
     passed = send(picked_coef, lambda d: d ^ 1)
     far = call(
-        far_kernel, "far", panel(leaves, jnp.float32), [SMEM] * 2 + [VMEM] + [ANY] * 4,
-        (far_list, near_list, far_coupling, level, layer, share_other, passed),
+        far_kernel, "far", panel(leaves, jnp.float32), [SMEM, VMEM] + [ANY] * 4,
+        (far_list, far_coupling, level, layer, share_other, passed),
         scratch=[
             pltpu.VMEM((4 * leaves * rank, width), jnp.bfloat16),
             pltpu.SemaphoreType.DMA((4,)),
@@ -278,9 +275,9 @@
     their_beside = send(handed, lambda d: d ^ 1)
     return call(
         down_kernel, "down", jax.ShapeDtypeStruct(source.shape, jnp.bfloat16),
-        [SMEM] * 2 + [VMEM] * 9,
+        [SMEM] + [VMEM] * 9,
         (
-            coarse_list, near_list, transfer, coarse_coupling, row_basis, near, far,
+            coarse_list, transfer, coarse_coupling, row_basis, near, far,
             column, handed, their_column, their_beside,
         ),
         flops=8 * leaves * rank * rank * width,

time: 39 us -> 37.8 us (0.969)
  local copies, waits for them, and re-layouts: 4.27 us -> 2.93 us
  other arithmetic: 0 us -> 0.75 us
  starting transfers between devices: 20.8 us -> 20.3 us
  Pallas kernels: 11.2 us -> 10.8 us
    unnamed x22 -> x18, local copies, waits for them, and re-layouts: 4.27 us -> 2.93 us
    select_n x0 -> x1, other arithmetic: none -> 0.75 us  [body(): index = jnp.where(live, which * leaves + near_list % leaves, 3 * leaves)]
    ppermute x11, starting transfers between devices: 20.8 us -> 20.3 us  [send(): return lax.ppermute(value, 'row', pairs)]
  transfers between devices with their start and end apart: 11 -> 11, of which waited for: 1 -> 1; matrix products, arithmetic and copies ran while one was open for 0% -> 2% of each run, Pallas kernels for 21% -> 21%
where the time goes in v12:
time: 37.8 us; the launch traced here: 37.5 us
  starting transfers between devices  20.3 us (54%)
  Pallas kernels  10.8 us (29%)
  local copies, waits for them, and re-layouts  2.93 us (8%)
  waiting for transfers between devices  2.52 us (7%)
  other arithmetic  0.75 us (2%)
    ppermute x11, starting transfers between devices, send(): return lax.ppermute(value, 'row', pairs)  20.3 us
    pallas_call x8, Pallas kernels, call(): pl.pallas_call(kernel, out_shape=outs, in_specs=specs, out_specs=(VMEM,)...  10.8 us
    unnamed x18, local copies, waits for them, and re-layouts  2.93 us
    ppermute x11, waiting for transfers between devices, send(): return lax.ppermute(value, 'row', pairs)  2.52 us
  transfers between devices with their start and end apart: 11, of which 1 were waited for; matrix products, arithmetic and copies ran while one was open for 2% of the time, Pallas kernels for 21%

profile of v12, /device:TPU:1, one launch (start us, length us, event | category | flops | bytes accessed | tf_op | source)
XLA Modules:
  0.0 37.5 jit_solution(17333870155300136600)
XLA Ops:
  0.0 0.0 copy-start.1
  0.0 0.9 %copy-done.1 = bf16[4,128,128]{2,1,0:T(8,128)(2,1)S(1)} copy-done((bf16[4,128,128]{2,1,0:T(8,128)(2,1)S(1)}, bf16[4,128,128]{2,1,0:T(8,128)(2,1)}, u32[]{:S(2)}) %copy-start.1) | copy-done | bytes 131096
  0.9 0.0 copy-start.3
  0.9 1.0 %copy-done.3 = bf16[1024,256]{1,0:T(8,128)(2,1)S(1)} copy-done((bf16[1024,256]{1,0:T(8,128)(2,1)S(1)}, bf16[1024,256]{1,0:T(8,128)(2,1)}, u32[]{:S(2)}) %copy-start.3) | copy-done | bytes 524312
  1.9 0.0 copy-start.4
  1.9 0.9 %copy-done.4 = bf16[4,256,128]{2,1,0:T(8,128)(2,1)S(1)} copy-done((bf16[4,256,128]{2,1,0:T(8,128)(2,1)S(1)}, bf16[4,256,128]{2,1,0:T(8,128)(2,1)}, u32[]{:S(2)}) %copy-start.4) | copy-done | bytes 262168
  2.9 0.5 %up.1 = (bf16[1536,256]{1,0:T(8,128)(2,1)S(1)}, bf16[512,256]{1,0:T(8,128)(2,1)S(1)}, bf16[128,256]{1,0:T(8,128)(2,1)S(1)}) custom-call(bf16[1024,256]{1,0:T(8,128)(2,1)S(1)} %copy-done.3, bf16[4,256,128]{2,1,0:T(8,128)(2,1)S(1)} %copy-done.4, bf16[4,128,128]{2,1,0:T(8,128)(2,1)S(1)} %copy-done.1), custom_call_target="tpu_custom_call" | custom-call | flops 100663296 | bytes 786432 | tf_op jit(solution)/shard_map/up/pallas_call | solution.py:187
  3.4 0.0 copy-start.7
  3.4 0.1 collective-permute-start
  3.5 2.7 %collective-permute-start.2 = (bf16[512,256]{1,0:T(8,128)(2,1)S(1)}, bf16[512,256]{1,0:T(8,128)(2,1)S(1)}, u32[]{:S(2)}, u32[]{:S(2)}) collective-permute-start(bf16[512,256]{1,0:T(8,128)(2,1)S(1)} %get-tuple-element.9), channel_id=1, source_target_pairs={{0,2},{1,3},{2,0},{3,1},{4,6},{5,7},{6,4},{7,5},{8,10},{9,11},{10,... | collective-permute-start | bytes 786440 | tf_op jit(solution)/shard_map/ppermute | solution.py:220
  6.2 0.0 collective-permute-done.refs_0_.share_ref
  6.3 4.1 %collective-permute-start.1 = (bf16[1024,256]{1,0:T(8,128)(2,1)S(1)}, bf16[1024,256]{1,0:T(8,128)(2,1)S(1)}, u32[]{:S(2)}, u32[]{:S(2)}) collective-permute-start(bf16[1024,256]{1,0:T(8,128)(2,1)S(1)} %panels.1), channel_id=1, source_target_pairs={{1,2},{2,1},{3,4},{4,3},{5,6},{6,5},{7,8},{8,7},{9,10},{10,9},{11,... | collective-permute-start | bytes 1572872 | tf_op jit(solution)/shard_map/ppermute | solution.py:220
  10.3 1.4 %collective-permute-start.5 = (bf16[128,256]{1,0:T(8,128)(2,1)S(1)}, bf16[128,256]{1,0:T(8,128)(2,1)S(1)}, u32[]{:S(2)}, u32[]{:S(2)}) collective-permute-start(bf16[128,256]{1,0:T(8,128)(2,1)S(1)} %get-tuple-element.10.refs_0_), channel_id=1, source_target_pairs={{0,4},{1,5},{2,6},{3,7},{4,0},{5,1},{6,2},{7,3},{8,12},{9,13},{10,... | collective-permute-start | bytes 196616 | tf_op jit(solution)/shard_map/ppermute | solution.py:220
  11.7 2.3 %collective-permute-start.6 = (bf16[128,256]{1,0:T(8,128)(2,1)S(1)}, bf16[128,256]{1,0:T(8,128)(2,1)S(1)}, u32[]{:S(2)}, u32[]{:S(2)}) collective-permute-start(bf16[128,256]{1,0:T(8,128)(2,1)S(1)} %get-tuple-element.10.refs_0_), channel_id=1, source_target_pairs={{0,8},{1,9},{2,10},{3,11},{4,12},{5,13},{6,14},{7,15},{8,0},{9,1},... | collective-permute-start | bytes 196616 | tf_op jit(solution)/shard_map/ppermute | solution.py:220
  14.0 0.0 collective-permute-start.7
  14.0 0.0 collective-permute-done.2.level_ref
  14.0 3.1 %collective-permute-start.3 = (bf16[512,256]{1,0:T(8,128)(2,1)S(1)}, bf16[512,256]{1,0:T(8,128)(2,1)S(1)}, u32[]{:S(2)}, u32[]{:S(2)}) collective-permute-start(bf16[512,256]{1,0:T(8,128)(2,1)S(1)} %collective-permute-done.2.level_ref), channel_id=1, source_target_pairs={{0,4},{1,5},{4,8},{5,9},{6,2},{7,3},{8,12},{9,13},{10,6},{11,7},{1... | collective-permute-start | bytes 786440 | tf_op jit(solution)/shard_map/ppermute | solution.py:220
  17.2 0.0 copy-start
  17.2 0.0 collective-permute-done.5.refs_1_
  17.2 0.0 collective-permute-done.6.refs_2_
  17.2 2.5 %collective-permute-done.7.refs_3_ = bf16[128,256]{1,0:T(8,128)(2,1)S(1)} collective-permute-done((bf16[128,256]{1,0:T(8,128)(2,1)S(1)}, bf16[128,256]{1,0:T(8,128)(2,1)S(1)}, u32[]{:S(2)}, u32[]{:S(2)}) %collective-permute-start.7) | collective-permute-done | bytes 65568 | tf_op jit(solution)/shard_map/ppermute | solution.py:220
  19.7 2.3 %collective-permute-start.8 = (bf16[512,256]{1,0:T(8,128)(2,1)S(1)}, bf16[512,256]{1,0:T(8,128)(2,1)S(1)}, u32[]{:S(2)}, u32[]{:S(2)}) collective-permute-start(bf16[512,256]{1,0:T(8,128)(2,1)S(1)} %column.1.column_ref), channel_id=1, source_target_pairs={{0,2},{1,3},{2,0},{3,1},{4,6},{5,7},{6,4},{7,5},{8,10},{9,11},{10,... | collective-permute-start | bytes 786440 | tf_op jit(solution)/shard_map/ppermute | solution.py:220
  22.1 0.8 %fusion.4.index_ref = s32[4,16]{1,0:T(4,128)S(1)} fusion(s32[4,16]{1,0:T(4,128)} %param.13, s32[]{:T(128)S(6)} %axis_index.12, s32[4]{0:T(128)} %param.14), kind=kLoop, calls=%fused_computation.9 | loop fusion | flops 1600 | bytes 532 | tf_op jit(solution)/shard_map/jit(_where)/select_n | solution.py:248
  22.8 3.5 %collective-permute-start.9 = (bf16[512,256]{1,0:T(8,128)(2,1)S(1)}, bf16[512,256]{1,0:T(8,128)(2,1)S(1)}, u32[]{:S(2)}, u32[]{:S(2)}) collective-permute-start(bf16[512,256]{1,0:T(8,128)(2,1)S(1)} %column.1.column_ref), channel_id=1, source_target_pairs={{0,1},{1,0},{2,3},{3,2},{4,5},{5,4},{6,7},{7,6},{8,9},{9,8},{10,11... | collective-permute-start | bytes 786440 | tf_op jit(solution)/shard_map/ppermute | solution.py:220
  26.3 0.0 collective-permute-done.3.layer_ref
  26.3 0.0 copy-start.2
  26.3 0.0 copy-start.5
  26.3 0.0 copy-start.6
  26.4 0.0 copy-start.8
  26.4 0.1 collective-permute-start.4
  26.5 0.0 collective-permute-done.1.across_ref
  26.5 6.2 %near.1.refs_0_.near_ref = f32[4,256,256]{2,1,0:T(8,128)S(1)} custom-call(s32[4,16]{1,0:T(4,128)S(1)} %fusion.4.index_ref, bf16[4,16,256,256]{3,2,1,0:T(8,128)(2,1)} %blocks_hbm.1, bf16[1536,256]{1,0:T(8,128)(2,1)S(1)} %get-tuple-element.8.in_ref.own_ref, bf16[1536,256]{1,0:T(8,128)(2,1)S(1)} %collective-permute-done.refs_0_.share_ref, ...), custom_call_target="tpu_custom_call" | custom-call | flops 1000000000 | tf_op jit(solution)/shard_map/near/pallas_call | solution.py:187
  32.6 0.0 collective-permute-done.8.in_ref
  32.7 0.7 %collective-permute-start.10 = (bf16[512,256]{1,0:T(8,128)(2,1)S(1)}, bf16[512,256]{1,0:T(8,128)(2,1)S(1)}, u32[]{:S(2)}, u32[]{:S(2)}) collective-permute-start(bf16[512,256]{1,0:T(8,128)(2,1)S(1)} %hand.1.beside_ref), channel_id=1, source_target_pairs={{0,1},{1,0},{2,3},{3,2},{4,5},{5,4},{6,7},{7,6},{8,9},{9,8},{10,11... | collective-permute-start | bytes 786440 | tf_op jit(solution)/shard_map/ppermute | solution.py:220
  33.4 0.0 collective-permute-done.4.passed_ref
  33.4 0.0 copy-done.7
  33.4 0.0 copy-done
  33.4 1.5 %far.1.far_ref = f32[512,256]{1,0:T(8,128)S(1)} custom-call(s32[4,16]{1,0:T(4,128)S(1)} %copy-done.7, bf16[4,16,128,128]{3,2,1,0:T(8,128)(2,1)S(1)} %copy-done, bf16[512,256]{1,0:T(8,128)(2,1)S(1)} %collective-permute-done.2.level_ref, bf16[512,256]{1,0:T(8,128)(2,1)S(1)} %collective-permute-done.3.layer_ref, ...), custom_call_target="tpu_custom_call" | custom-call | flops 536870912 | bytes 2097152 | tf_op jit(solution)/shard_map/far/pallas_call | solution.py:187
  34.9 0.0 collective-permute-done.9.their_column_ref
  34.9 0.0 collective-permute-done.10.their_beside_ref
  34.9 0.0 copy-done.2
  34.9 0.0 copy-done.5
  34.9 0.0 copy-done.6
  34.9 0.0 copy-done.8
  35.0 2.6 %down.1 = bf16[1024,256]{1,0:T(8,128)(2,1)} custom-call(s32[1,8]{1,0:T(1,128)S(1)} %copy-done.8, bf16[4,128,128]{2,1,0:T(8,128)(2,1)S(1)} %copy-done.2, bf16[1,8,128,128]{3,2,1,0:T(8,128)(2,1)S(1)} %copy-done.5, bf16[4,256,128]{2,1,0:T(8,128)(2,1)S(1)} %copy-done.6, f32[4,256,256]{2,1,0:T(8,128)S(1)} %near.1.refs_0_.near_ref, f32[512,256]{1,0:T(8,128)S(1)} %far.1.far_ref, ...), custom_call_target="tpu_custom_call" | custom-call | flops 134217728 | bytes 1048576 | tf_op jit(solution)/shard_map/down/pallas_call | solution.py:187
  (4 shorter events, 0.1 us)
Async XLA Ops:
  0.0 0.9 %copy-start.1 = (bf16[4,128,128]{2,1,0:T(8,128)(2,1)S(1)}, bf16[4,128,128]{2,1,0:T(8,128)(2,1)}, u32[]{:S(2)}) copy-start(bf16[4,128,128]{2,1,0:T(8,128)(2,1)} %transfer_ref.3) | copy-start | bytes 393220
  0.9 1.0 %copy-start.3 = (bf16[1024,256]{1,0:T(8,128)(2,1)S(1)}, bf16[1024,256]{1,0:T(8,128)(2,1)}, u32[]{:S(2)}) copy-start(bf16[1024,256]{1,0:T(8,128)(2,1)} %source_ref.1) | copy-start | bytes 1572868
  1.9 0.9 %copy-start.4 = (bf16[4,256,128]{2,1,0:T(8,128)(2,1)S(1)}, bf16[4,256,128]{2,1,0:T(8,128)(2,1)}, u32[]{:S(2)}) copy-start(bf16[4,256,128]{2,1,0:T(8,128)(2,1)} %col_ref.1) | copy-start | bytes 786436
  3.4 30.0 %copy-start.7 = (s32[4,16]{1,0:T(4,128)S(1)}, s32[4,16]{1,0:T(4,128)}, u32[]{:S(2)}) copy-start(s32[4,16]{1,0:T(4,128)} %list_ref.2) | copy-start | bytes 772
  3.4 2.8 %collective-permute-start = (bf16[1536,256]{1,0:T(8,128)(2,1)S(1)}, bf16[1536,256]{1,0:T(8,128)(2,1)S(1)}, u32[]{:S(2)}, u32[]{:S(2)}) collective-permute-start(bf16[1536,256]{1,0:T(8,128)(2,1)S(1)} %get-tuple-element.8.in_ref.own_ref), channel_id=1, source_target_pairs={{0,1},{1,0},{2,3},{3,2},{4,5},{5,4},{6,7},{7,6},{8,9},{9,8},{10,11... | collective-permute-start | bytes 2359304 | tf_op jit(solution)/shard_map/ppermute | solution.py:220
  3.5 10.5 %collective-permute-start.2 = (bf16[512,256]{1,0:T(8,128)(2,1)S(1)}, bf16[512,256]{1,0:T(8,128)(2,1)S(1)}, u32[]{:S(2)}, u32[]{:S(2)}) collective-permute-start(bf16[512,256]{1,0:T(8,128)(2,1)S(1)} %get-tuple-element.9), channel_id=1, source_target_pairs={{0,2},{1,3},{2,0},{3,1},{4,6},{5,7},{6,4},{7,5},{8,10},{9,11},{10,... | collective-permute-start | bytes 786440 | tf_op jit(solution)/shard_map/ppermute | solution.py:220
  6.3 20.2 %collective-permute-start.1 = (bf16[1024,256]{1,0:T(8,128)(2,1)S(1)}, bf16[1024,256]{1,0:T(8,128)(2,1)S(1)}, u32[]{:S(2)}, u32[]{:S(2)}) collective-permute-start(bf16[1024,256]{1,0:T(8,128)(2,1)S(1)} %panels.1), channel_id=1, source_target_pairs={{1,2},{2,1},{3,4},{4,3},{5,6},{6,5},{7,8},{8,7},{9,10},{10,9},{11,... | collective-permute-start | bytes 1572872 | tf_op jit(solution)/shard_map/ppermute | solution.py:220
  10.3 6.8 %collective-permute-start.5 = (bf16[128,256]{1,0:T(8,128)(2,1)S(1)}, bf16[128,256]{1,0:T(8,128)(2,1)S(1)}, u32[]{:S(2)}, u32[]{:S(2)}) collective-permute-start(bf16[128,256]{1,0:T(8,128)(2,1)S(1)} %get-tuple-element.10.refs_0_), channel_id=1, source_target_pairs={{0,4},{1,5},{2,6},{3,7},{4,0},{5,1},{6,2},{7,3},{8,12},{9,13},{10,... | collective-permute-start | bytes 196616 | tf_op jit(solution)/shard_map/ppermute | solution.py:220
  11.7 5.5 %collective-permute-start.6 = (bf16[128,256]{1,0:T(8,128)(2,1)S(1)}, bf16[128,256]{1,0:T(8,128)(2,1)S(1)}, u32[]{:S(2)}, u32[]{:S(2)}) collective-permute-start(bf16[128,256]{1,0:T(8,128)(2,1)S(1)} %get-tuple-element.10.refs_0_), channel_id=1, source_target_pairs={{0,8},{1,9},{2,10},{3,11},{4,12},{5,13},{6,14},{7,15},{8,0},{9,1},... | collective-permute-start | bytes 196616 | tf_op jit(solution)/shard_map/ppermute | solution.py:220
  14.0 5.7 %collective-permute-start.7 = (bf16[128,256]{1,0:T(8,128)(2,1)S(1)}, bf16[128,256]{1,0:T(8,128)(2,1)S(1)}, u32[]{:S(2)}, u32[]{:S(2)}) collective-permute-start(bf16[128,256]{1,0:T(8,128)(2,1)S(1)} %get-tuple-element.10.refs_0_), channel_id=1, source_target_pairs={{0,12},{1,13},{2,14},{3,15},{4,8},{5,9},{6,10},{7,11},{8,4},{9,5},... | collective-permute-start | bytes 196616 | tf_op jit(solution)/shard_map/ppermute | solution.py:220
  14.0 12.3 %collective-permute-start.3 = (bf16[512,256]{1,0:T(8,128)(2,1)S(1)}, bf16[512,256]{1,0:T(8,128)(2,1)S(1)}, u32[]{:S(2)}, u32[]{:S(2)}) collective-permute-start(bf16[512,256]{1,0:T(8,128)(2,1)S(1)} %collective-permute-done.2.level_ref), channel_id=1, source_target_pairs={{0,4},{1,5},{4,8},{5,9},{6,2},{7,3},{8,12},{9,13},{10,6},{11,7},{1... | collective-permute-start | bytes 786440 | tf_op jit(solution)/shard_map/ppermute | solution.py:220
  17.2 16.2 %copy-start = (bf16[4,16,128,128]{3,2,1,0:T(8,128)(2,1)S(1)}, bf16[4,16,128,128]{3,2,1,0:T(8,128)(2,1)}, u32[]{:S(2)}) copy-start(bf16[4,16,128,128]{3,2,1,0:T(8,128)(2,1)} %coupling_ref.2) | copy-start | bytes 6291460
  19.7 12.9 %collective-permute-start.8 = (bf16[512,256]{1,0:T(8,128)(2,1)S(1)}, bf16[512,256]{1,0:T(8,128)(2,1)S(1)}, u32[]{:S(2)}, u32[]{:S(2)}) collective-permute-start(bf16[512,256]{1,0:T(8,128)(2,1)S(1)} %column.1.column_ref), channel_id=1, source_target_pairs={{0,2},{1,3},{2,0},{3,1},{4,6},{5,7},{6,4},{7,5},{8,10},{9,11},{10,... | collective-permute-start | bytes 786440 | tf_op jit(solution)/shard_map/ppermute | solution.py:220
  22.8 12.1 %collective-permute-start.9 = (bf16[512,256]{1,0:T(8,128)(2,1)S(1)}, bf16[512,256]{1,0:T(8,128)(2,1)S(1)}, u32[]{:S(2)}, u32[]{:S(2)}) collective-permute-start(bf16[512,256]{1,0:T(8,128)(2,1)S(1)} %column.1.column_ref), channel_id=1, source_target_pairs={{0,1},{1,0},{2,3},{3,2},{4,5},{5,4},{6,7},{7,6},{8,9},{9,8},{10,11... | collective-permute-start | bytes 786440 | tf_op jit(solution)/shard_map/ppermute | solution.py:220
  26.3 8.6 %copy-start.2 = (bf16[4,128,128]{2,1,0:T(8,128)(2,1)S(1)}, bf16[4,128,128]{2,1,0:T(8,128)(2,1)}, u32[]{:S(2)}) copy-start(bf16[4,128,128]{2,1,0:T(8,128)(2,1)} %transfer_ref.3) | copy-start | bytes 393220
  26.3 8.6 %copy-start.5 = (bf16[1,8,128,128]{3,2,1,0:T(8,128)(2,1)S(1)}, bf16[1,8,128,128]{3,2,1,0:T(8,128)(2,1)}, u32[]{:S(2)}) copy-start(bf16[1,8,128,128]{3,2,1,0:T(8,128)(2,1)} %coupling_ref.3) | copy-start | bytes 786436
  26.3 8.6 %copy-start.6 = (bf16[4,256,128]{2,1,0:T(8,128)(2,1)S(1)}, bf16[4,256,128]{2,1,0:T(8,128)(2,1)}, u32[]{:S(2)}) copy-start(bf16[4,256,128]{2,1,0:T(8,128)(2,1)} %row_ref.1) | copy-start | bytes 786436
  26.4 8.6 %copy-start.8 = (s32[1,8]{1,0:T(1,128)S(1)}, s32[1,8]{1,0:T(1,128)}, u32[]{:S(2)}) copy-start(s32[1,8]{1,0:T(1,128)} %list_ref.3) | copy-start | bytes 100
  26.4 7.0 %collective-permute-start.4 = (bf16[512,256]{1,0:T(8,128)(2,1)S(1)}, bf16[512,256]{1,0:T(8,128)(2,1)S(1)}, u32[]{:S(2)}, u32[]{:S(2)}) collective-permute-start(bf16[512,256]{1,0:T(8,128)(2,1)S(1)} %pick.1), channel_id=1, source_target_pairs={{0,1},{1,0},{2,3},{3,2},{4,5},{5,4},{6,7},{7,6},{8,9},{9,8},{10,11... | collective-permute-start | bytes 786440 | tf_op jit(solution)/shard_map/ppermute | solution.py:220
  32.7 2.2 %collective-permute-start.10 = (bf16[512,256]{1,0:T(8,128)(2,1)S(1)}, bf16[512,256]{1,0:T(8,128)(2,1)S(1)}, u32[]{:S(2)}, u32[]{:S(2)}) collective-permute-start(bf16[512,256]{1,0:T(8,128)(2,1)S(1)} %hand.1.beside_ref), channel_id=1, source_target_pairs={{0,1},{1,0},{2,3},{3,2},{4,5},{5,4},{6,7},{7,6},{8,9},{9,8},{10,11... | collective-permute-start | bytes 786440 | tf_op jit(solution)/shard_map/ppermute | solution.py:220
